TPU v7x, 32 devices: a whole 2x2x4 slice. The times are simulated.
32 devices in a mesh: loop: 4 (over y, x), trans: 8 (over z, core).
Axes of the slice: x: 2, y: 2, z: 4, core: 2. Of those that a mesh axis runs over, the one named last changes fastest.
Arguments:
- block_now: float32 [8, 3, 64, 4, 1024], P(None, None, None, 'loop', 'trans')
- block_prev: float32 [8, 3, 64, 4, 1024], P(None, None, None, 'loop', 'trans'), may hold values from -6 to 6
- coupling_prev: float32 [8, 8], replicated, may hold values from -3 to 3
- material: int32 [64, 4, 1024], P(None, 'loop', 'trans'), may hold values from 0 to 3
- permittivity: float32 [4], replicated, may hold values from 1 to 12
Outputs:
- block_next: float32 [8, 3, 64, 4, 1024], P(None, None, None, 'loop', 'trans')
- alpha_block: float32 [8, 8], replicated
- beta_block: float32 [8, 8], replicated
All inputs are finite; a program needn't handle non-finite values.
Results may differ from a plain program's by a relative error of at most 0.0003.
Values sent between devices are 32-bit elements; how exact they have to be, the bound alone decides.
No kernel may reach another device: no remote copies, remote signals or barrier semaphores. Data moves between devices by JAX's collectives and lax.ppermute only.
A program may use at most 64 MiB of HBM per device.

v0:
```python
import jax
import jax.numpy as jnp
from jax import lax
from jax.sharding import PartitionSpec as P


def padded(cells, sides, width):
    for axis, dim in sides:
        count = lax.axis_size(axis)
        head = lax.slice_in_dim(cells, 0, width, axis=dim)
        tail = lax.slice_in_dim(cells, cells.shape[dim] - width, cells.shape[dim], axis=dim)
        cells = jnp.concatenate(
            [
                lax.ppermute(tail, axis, [(i, (i + 1) % count) for i in range(count)]),
                cells,
                lax.ppermute(head, axis, [((i + 1) % count, i) for i in range(count)]),
            ],
            axis=dim,
        )
    return cells


def cell_scale(material, permittivity):
    levels = jnp.arange(permittivity.shape[0], dtype=jnp.int32)
    inverse = 1.0 / jnp.sqrt(permittivity)
    match = (material[None] == levels[:, None, None, None]).astype(permittivity.dtype)
    return jnp.sum(match * inverse[:, None, None, None], axis=0)


def cut_axis(field, axis, start, stop):
    return lax.slice_in_dim(field, start, field.shape[axis] + stop, axis=axis)


def ahead(field, axis):
    diff = cut_axis(field, axis, 1, 0) - cut_axis(field, axis, 0, -1)
    for other in (1, 2, 3):
        if other != axis:
            diff = cut_axis(diff, other, 0, -1)
    return diff


def behind(field, axis):
    diff = cut_axis(field, axis, 1, 0) - cut_axis(field, axis, 0, -1)
    for other in (1, 2, 3):
        if other != axis:
            diff = cut_axis(diff, other, 1, 0)
    return diff


def curl_ahead(field):
    comp_z, comp_p, comp_t = (field[:, 0], field[:, 1], field[:, 2])
    out_z = ahead(comp_t, 2) - ahead(comp_p, 3)
    out_p = ahead(comp_z, 3) - ahead(comp_t, 1)
    out_t = ahead(comp_p, 1) - ahead(comp_z, 2)
    return jnp.stack([out_z, out_p, out_t], axis=1)


def curl_behind(field):
    comp_z, comp_p, comp_t = (field[:, 0], field[:, 1], field[:, 2])
    out_z = behind(comp_t, 2) - behind(comp_p, 3)
    out_p = behind(comp_z, 3) - behind(comp_t, 1)
    out_t = behind(comp_p, 1) - behind(comp_z, 2)
    return jnp.stack([out_z, out_p, out_t], axis=1)


def local(block_now, block_prev, coupling_prev, material, permittivity):
    hp = lax.Precision.HIGHEST
    scale = cell_scale(material, permittivity)
    field = block_now * scale[None, None]
    extended = padded(field, (("loop", 3), ("trans", 4)), 1)
    trans_index = lax.axis_index("trans")
    trans_count = lax.axis_size("trans")
    low_keep = (trans_index > 0).astype(jnp.float32)[None]
    high_keep = (trans_index < trans_count - 1).astype(jnp.float32)[None]
    keep = jnp.concatenate([low_keep, jnp.ones((field.shape[4],), jnp.float32), high_keep])
    extended = extended * keep
    extended = jnp.pad(extended, ((0, 0), (0, 0), (1, 1), (0, 0), (0, 0)))
    curl_h = curl_ahead(extended)
    image = curl_behind(curl_h) * scale[None, None]
    work = image - jnp.einsum("kcxyz,bk->bcxyz", block_prev, coupling_prev, precision=hp)
    count = (
        3.0
        * block_now.shape[2]
        * block_now.shape[3]
        * block_now.shape[4]
        * lax.axis_size("loop")
        * lax.axis_size("trans")
    )
    local_project = jnp.einsum("jcxyz,bcxyz->jb", block_now, work, precision=hp)
    alpha_block = lax.psum(local_project, ("loop", "trans")) / count
    resid = work - jnp.einsum("jcxyz,jb->bcxyz", block_now, alpha_block, precision=hp)
    local_resid = jnp.einsum("jcxyz,bcxyz->jb", resid, resid, precision=hp)
    gram = lax.psum(local_resid, ("loop", "trans")) / count
    lower = jnp.linalg.cholesky(gram)
    eye = jnp.eye(lower.shape[0], dtype=lower.dtype)
    lower_inv = jax.scipy.linalg.solve_triangular(lower, eye, lower=True)
    block_next = jnp.einsum("jcxyz,bj->bcxyz", resid, lower_inv, precision=hp)
    return (block_next, alpha_block, lower.T)


def solution(mesh):
    in_specs = (
        P(None, None, None, "loop", "trans"),
        P(None, None, None, "loop", "trans"),
        P(),
        P(None, "loop", "trans"),
        P(),
    )
    out_specs = (P(None, None, None, "loop", "trans"), P(), P())
    return jax.shard_map(local, mesh=mesh, in_specs=in_specs, out_specs=out_specs, check_vma=False)
```

profile of v0, /device:TPU:0, one launch (start us, length us, event | category | flops | bytes accessed | tf_op | source)
XLA Modules:
  0.0 161.1 jit_solution(2318835881438834561)
XLA Ops:
  0.6 0.0 copy-start
  0.6 0.7 sqrt.3
  1.4 0.8 select_reduce_fusion
  2.2 1.6 copy_multiply_fusion
  3.8 0.0 copy-start.1
  3.8 3.9 %collective-permute-start.1 = (f32[8,3,64,1,128]{4,0,2,3,1:T(8,128)S(1)}, f32[8,3,64,1,128]{4,0,2,3,1:T(8,128)S(1)}, u32[]{:S(2)}, u32[]{:S(2)}) collective-permute-start(f32[8,3,64,1,128]{4,0,2,3,1:T(8,128)S(1)} %copy_multiply_fusion), channel_id=1, source_target_pairs={{8,0},{16,8},{24,16},{0,24},{9,1},{17,9},{25,17},{1,25},{10,2},{18... | collective-permute-start | bytes 2359304 | tf_op jit(solution)/shard_map/ppermute | solution.py:16
  7.8 0.0 collective-permute-start
  7.8 17.9 %collective-permute-done.1 = f32[8,3,64,1,128]{4,0,2,3,1:T(8,128)S(1)} collective-permute-done((f32[8,3,64,1,128]{4,0,2,3,1:T(8,128)S(1)}, f32[8,3,64,1,128]{4,0,2,3,1:T(8,128)S(1)}, u32[]{:S(2)}, u32[]{:S(2)}) %collective-permute-start.1) | collective-permute-done | bytes 786464 | tf_op jit(solution)/shard_map/ppermute | solution.py:16
  25.7 0.0 copy-start.3
  25.7 16.7 %collective-permute-done = f32[8,3,64,1,128]{4,0,2,3,1:T(8,128)S(1)} collective-permute-done((f32[8,3,64,1,128]{4,0,2,3,1:T(8,128)S(1)}, f32[8,3,64,1,128]{4,0,2,3,1:T(8,128)S(1)}, u32[]{:S(2)}, u32[]{:S(2)}) %collective-permute-start) | collective-permute-done | bytes 786464 | tf_op jit(solution)/shard_map/ppermute | solution.py:14
  42.4 0.0 copy-done.1
  42.4 0.0 copy-done.3
  42.4 0.0 copy-start.4
  42.4 0.9 copy-done.4
  43.3 0.2 pad_maximum_fusion
  43.5 2.2 %fusion.20 = (f32[8,3,64,3,1]{4,0,2,3,1:T(8,128)S(1)}, f32[8,3,64,3,1]{4,0,2,3,1:T(8,128)}) fusion(f32[8,3,64,3,128]{4,0,2,3,1:T(8,128)S(1)} %pad_maximum_fusion), kind=kLoop, calls=%fused_computation.57 | loop fusion | bytes 73728 | tf_op jit(solution)/shard_map/slice | solution.py:11
  45.7 2.4 %copy.34 = f32[8,3,64,3,1]{2,0,4,3,1:T(8,128)S(1)} copy(f32[8,3,64,3,1]{4,0,2,3,1:T(8,128)} %get-tuple-element.16) | data formatting | bytes 36864 | tf_op jit(solution)/shard_map/slice | solution.py:10
  48.1 2.2 %collective-permute-start.3 = (f32[8,3,64,3,1]{2,0,4,3,1:T(8,128)S(1)}, f32[8,3,64,3,1]{2,0,4,3,1:T(8,128)S(1)}, u32[]{:S(2)}, u32[]{:S(2)}) collective-permute-start(f32[8,3,64,3,1]{2,0,4,3,1:T(8,128)S(1)} %copy.34), channel_id=1, source_target_pairs={{1,0},{2,1},{3,2},{4,3},{5,4},{6,5},{7,6},{0,7},{9,8},{10,9},{11,1... | collective-permute-start | bytes 55304 | tf_op jit(solution)/shard_map/ppermute | solution.py:16
  50.3 0.8 copy.33
  51.1 0.2 collective-permute-start.2
  51.3 0.1 pad_maximum_fusion.1
  51.4 0.6 collective-permute-done.3
  52.0 0.8 copy.36
  52.9 3.6 %collective-permute-done.2 = f32[8,3,64,3,1]{2,0,4,3,1:T(8,128)S(1)} collective-permute-done((f32[8,3,64,3,1]{2,0,4,3,1:T(8,128)S(1)}, f32[8,3,64,3,1]{2,0,4,3,1:T(8,128)S(1)}, u32[]{:S(2)}, u32[]{:S(2)}) %collective-permute-start.2) | collective-permute-done | bytes 18464 | tf_op jit(solution)/shard_map/ppermute | solution.py:14
  56.5 2.2 %copy.35 = f32[8,3,64,3,1]{4,0,2,3,1:T(8,128)} copy(f32[8,3,64,3,1]{2,0,4,3,1:T(8,128)S(1)} %collective-permute-done.2) | data formatting | bytes 36864 | tf_op jit(solution)/shard_map/ppermute | solution.py:14
  58.7 4.8 %maximum_multiply_fusion = f32[8,3,64,3,130]{4,0,2,3,1:T(8,128)S(1)} fusion(f32[8,3,64,3,1]{4,0,2,3,1:T(8,128)S(1)} %copy.36, f32[8,3,64,1,128]{4,0,2,3,1:T(8,128)} %copy-done.3, f32[8,3,64,1,128]{4,0,2,3,1:T(8,128)} %copy-done.1, f32[8,3,64,1,128]{4,0,2,3,1:T(8,128)} %copy-done.4, f32[8,3,64,3,1]{4,0,2,3,1:T(8,128)} %copy.35, f32[130]{0:T(256)S(1)} %pad_maximum_fusion.1), kind=kLoop, calls=%fused_computation | loop fusion | flops 2995200 | bytes 4792840 | tf_op jit(solution)/shard_map/mul | solution.py:76
  63.4 0.5 fusion.1
  63.9 1.1 fusion.23
  65.0 0.4 fusion.22
  65.4 0.5 fusion.21
  66.0 0.3 fusion.3
  66.2 0.1 fusion.32
  66.3 0.2 fusion.29
  66.5 0.3 fusion.4
  66.9 0.2 fusion.31
  67.0 0.2 fusion.28
  67.2 0.4 fusion.5
  67.6 0.1 fusion.30
  67.8 0.1 fusion.27
  67.8 0.3 fusion.10
  68.2 0.0 copy-start.5
  68.2 0.2 fusion.12
  68.5 0.0 copy-start.2
  68.5 0.2 fusion.14
  68.7 0.0 copy-done
  68.7 0.2 copy-done.5
  68.9 1.2 convolution_subtract_fusion.1
  70.1 0.0 copy-done.2
  70.1 1.9 %convolution_bitcast_fusion.3 = f32[8,8]{0,1:T(8,128)S(1)} fusion(f32[8,3,64,128]{3,0,2,1:T(8,128)S(1)} %convolution_subtract_fusion.1, f32[8,3,64,128]{3,2,1,0:T(8,128)S(1)} %bitcast.59), kind=kOutput, calls=%fused_computation.13 | convolution fusion | flops 18874368 | bytes 1573120 | tf_op jit(solution)/shard_map/jcxyz,bcxyz->jb/dot_general | solution.py:89
  72.0 37.1 %psum.14 = f32[8,8]{0,1:T(8,128)S(1)} all-reduce(f32[8,8]{0,1:T(8,128)S(1)} %convolution_bitcast_fusion.3), channel_id=1, replica_groups=mesh['loop'=4,'trans'=8] {'loop','trans'}, use_global_device_ids=true, to_apply=%region_1.2 | all-reduce | flops 64 | bytes 512 | tf_op jit(solution)/shard_map/psum | solution.py:90
  109.1 1.1 convolution_subtract_fusion
  110.3 1.8 %convolution_bitcast_fusion.2 = f32[8,8]{0,1:T(8,128)S(1)} fusion(f32[8,3,64,128]{3,0,2,1:T(8,128)S(1)} %convolution_subtract_fusion), kind=kOutput, calls=%fused_computation.12 | convolution fusion | flops 18874368 | bytes 786688 | tf_op jit(solution)/shard_map/jcxyz,bcxyz->jb/dot_general | solution.py:92
  112.0 42.3 %psum.15 = f32[8,8]{0,1:T(8,128)S(1)} all-reduce(f32[8,8]{0,1:T(8,128)S(1)} %convolution_bitcast_fusion.2), channel_id=1, replica_groups=mesh['loop'=4,'trans'=8] {'loop','trans'}, use_global_device_ids=true, to_apply=%region_2.3 | all-reduce | flops 64 | bytes 512 | tf_op jit(solution)/shard_map/psum | solution.py:93
  154.4 0.1 copy.41
  154.4 0.7 cholesky.17
  155.2 0.6 compare_reduce_fusion
  155.8 0.6 fusion.19
  156.5 0.6 custom-call.7
  157.1 0.2 convolution_bitcast_fusion.1
  157.3 0.8 convolution_bitcast_fusion
  158.1 1.7 %copy.43 = f32[8,3,64,1,128]{4,3,2,1,0:T(1,128)} copy(f32[8,3,64,1,128]{4,0,2,1,3:T(8,128)S(1)} %convolution_bitcast_fusion) | data formatting | bytes 1572864
  159.8 0.7 copy.44
  160.4 0.7 copy.45
  (5 shorter events, 0.1 us)
Async XLA Ops:
  0.6 68.1 %copy-start = (f32[8,3,64,1,128]{4,3,2,1,0:T(1,128)S(1)}, f32[8,3,64,1,128]{4,3,2,1,0:T(1,128)}, u32[]{:S(2)}) copy-start(f32[8,3,64,1,128]{4,3,2,1,0:T(1,128)} %param.6) | copy-start | bytes 2359300
  3.8 38.6 %copy-start.1 = (f32[8,3,64,1,128]{4,0,2,3,1:T(8,128)}, f32[8,3,64,1,128]{4,0,2,3,1:T(8,128)S(1)}, u32[]{:S(2)}) copy-start(f32[8,3,64,1,128]{4,0,2,3,1:T(8,128)S(1)} %copy_multiply_fusion) | copy-start | bytes 2359300
  3.8 21.9 %collective-permute-start.1 = (f32[8,3,64,1,128]{4,0,2,3,1:T(8,128)S(1)}, f32[8,3,64,1,128]{4,0,2,3,1:T(8,128)S(1)}, u32[]{:S(2)}, u32[]{:S(2)}) collective-permute-start(f32[8,3,64,1,128]{4,0,2,3,1:T(8,128)S(1)} %copy_multiply_fusion), channel_id=1, source_target_pairs={{8,0},{16,8},{24,16},{0,24},{9,1},{17,9},{25,17},{1,25},{10,2},{18... | collective-permute-start | bytes 2359304 | tf_op jit(solution)/shard_map/ppermute | solution.py:16
  7.8 34.6 %collective-permute-start = (f32[8,3,64,1,128]{4,0,2,3,1:T(8,128)S(1)}, f32[8,3,64,1,128]{4,0,2,3,1:T(8,128)S(1)}, u32[]{:S(2)}, u32[]{:S(2)}) collective-permute-start(f32[8,3,64,1,128]{4,0,2,3,1:T(8,128)S(1)} %copy_multiply_fusion), channel_id=1, source_target_pairs={{0,8},{8,16},{16,24},{24,0},{1,9},{9,17},{17,25},{25,1},{2,10},{10... | collective-permute-start | bytes 2359304 | tf_op jit(solution)/shard_map/ppermute | solution.py:14
  25.7 16.7 %copy-start.3 = (f32[8,3,64,1,128]{4,0,2,3,1:T(8,128)}, f32[8,3,64,1,128]{4,0,2,3,1:T(8,128)S(1)}, u32[]{:S(2)}) copy-start(f32[8,3,64,1,128]{4,0,2,3,1:T(8,128)S(1)} %collective-permute-done.1) | copy-start | bytes 2359300
  42.4 0.9 copy-start.4
  48.1 3.9 %collective-permute-start.3 = (f32[8,3,64,3,1]{2,0,4,3,1:T(8,128)S(1)}, f32[8,3,64,3,1]{2,0,4,3,1:T(8,128)S(1)}, u32[]{:S(2)}, u32[]{:S(2)}) collective-permute-start(f32[8,3,64,3,1]{2,0,4,3,1:T(8,128)S(1)} %copy.34), channel_id=1, source_target_pairs={{1,0},{2,1},{3,2},{4,3},{5,4},{6,5},{7,6},{0,7},{9,8},{10,9},{11,1... | collective-permute-start | bytes 55304 | tf_op jit(solution)/shard_map/ppermute | solution.py:16
  51.1 5.4 %collective-permute-start.2 = (f32[8,3,64,3,1]{2,0,4,3,1:T(8,128)S(1)}, f32[8,3,64,3,1]{2,0,4,3,1:T(8,128)S(1)}, u32[]{:S(2)}, u32[]{:S(2)}) collective-permute-start(f32[8,3,64,3,1]{2,0,4,3,1:T(8,128)S(1)} %copy.33), channel_id=1, source_target_pairs={{0,1},{1,2},{2,3},{3,4},{4,5},{5,6},{6,7},{7,0},{8,9},{9,10},{10,1... | collective-permute-start | bytes 55304 | tf_op jit(solution)/shard_map/ppermute | solution.py:14
  68.2 0.7 copy-start.5
  68.5 1.6 %copy-start.2 = (f32[8,3,64,1,128]{4,3,2,1,0:T(1,128)S(1)}, f32[8,3,64,1,128]{4,3,2,1,0:T(1,128)}, u32[]{:S(2)}) copy-start(f32[8,3,64,1,128]{4,3,2,1,0:T(1,128)} %param.5) | copy-start | bytes 2359300
where the time goes:
time: 162 us; the launch traced here: 161 us
  blocking collectives  79.4 us (49%)
  waiting for transfers between devices  38.9 us (24%)
  local copies, waits for them, and re-layouts  16.7 us (10%)
  other arithmetic  11.9 us (7%)
  matrix products  7.01 us (4%)
  starting transfers between devices  6.37 us (4%)
    psum x1, blocking collectives, local(): gram = lax.psum(local_resid, ('loop', 'trans')) / count  42.3 us
    psum x1, blocking collectives, local(): alpha_block = lax.psum(local_project, ('loop', 'trans')) / count  37.1 us
    ppermute x2, waiting for transfers between devices, padded(): lax.ppermute(tail, axis, [(i, (i + 1) % count) for i in range(count)])  20.3 us
    ppermute x2, waiting for transfers between devices, padded(): lax.ppermute(head, axis, [((i + 1) % count, i) for i in range(count)])  18.6 us
    ppermute x2, starting transfers between devices, padded(): lax.ppermute(head, axis, [((i + 1) % count, i) for i in range(count)])  6.15 us
    mul x1, other arithmetic, local(): extended = extended * keep  4.76 us
    unnamed x15, local copies, waits for them, and re-layouts  4.1 us
  transfers between devices with their start and end apart: 4, of which 4 were waited for; matrix products, arithmetic and copies ran while one was open for 1% of the time, Pallas kernels for 0%

commit v1 on v0

v1 whole, which is shorter than its diff:
```python
import jax
import jax.numpy as jnp
from jax import lax
from jax.experimental import pallas as pl
from jax.experimental.pallas import tpu as pltpu
from jax.sharding import PartitionSpec as P

VM = pltpu.VMEM
SM = pltpu.SMEM


def lane_ids(shape):
    return lax.broadcasted_iota(jnp.int32, shape, len(shape) - 1)


def row_ids(shape):
    return lax.broadcasted_iota(jnp.int32, shape, len(shape) - 2)


def roll_by(x, shift, axis):
    return pltpu.roll(x, shift % x.shape[axis], axis)


def cell_scale(mat, eps_ref):
    eps = jnp.full(mat.shape, eps_ref[0], jnp.float32)
    for level in range(1, eps_ref.shape[0]):
        eps = jnp.where(mat == level, eps_ref[level], eps)
    return 1.0 / jnp.sqrt(eps)


def z_next(x):
    n = x.shape[0]
    return jnp.where(row_ids(x.shape) == n - 1, 0.0, roll_by(x, -1, 0))


def z_prev(x):
    return jnp.where(row_ids(x.shape) == 0, 0.0, roll_by(x, 1, 0))


def pack_kernel(eps_ref, v_ref, mat_ref, fwd_ref, bwd_ref, right_ref, left_ref, scale_ref):
    nb = v_ref.shape[0]
    scale = cell_scale(mat_ref[...], eps_ref)
    scale_ref[...] = scale
    lane = lane_ids(scale.shape)
    last = scale.shape[1] - 1
    right = jnp.zeros_like(scale)
    left = jnp.zeros_like(scale)
    for b in range(nb):
        uz = v_ref[b, 0] * scale
        up = v_ref[b, 1] * scale
        ut = v_ref[b, 2] * scale
        bwd_ref[b, 0] = uz
        bwd_ref[b, 1] = ut
        fwd_ref[b, 0] = uz + (z_next(up) - up)
        fwd_ref[b, 1] = ut + (jnp.where(lane == last, 0.0, roll_by(up, -1, 1)) - up)
        for c, u in enumerate((uz, up, ut)):
            spot = 3 * b + c
            right = jnp.where(lane == spot, roll_by(u, spot + 1, 1), right)
            left = jnp.where(lane == spot, roll_by(u, spot, 1), left)
    right_ref[...] = right
    left_ref[...] = left


def gram_sums(v_ref, w_ref, acc_ref, pairs, base, group):
    steps = v_ref.shape[1] // 8
    for first in range(0, len(pairs), group):
        part = pairs[first : first + group]

        def body(r, accs):
            rows = pl.ds(pl.multiple_of(r * 8, 8), 8)
            vs = {j: v_ref[j, rows, :] for j in sorted({p[0] for p in part})}
            ws = {b: w_ref[b, rows, :] for b in sorted({p[1] for p in part})}
            return tuple(acc + vs[j] * ws[b] for acc, (j, b) in zip(accs, part))

        zero = jnp.zeros((8, v_ref.shape[2]), jnp.float32)
        accs = lax.fori_loop(0, steps, body, tuple(zero for _ in part))
        for i, acc in enumerate(accs):
            acc_ref[base + first + i] = acc


def local_kernel(eps_ref, coup_ref, v_ref, scale_ref, q_ref, fr_ref, fl_ref, cr_ref, cl_ref, l_ref, acc_ref):
    nb = v_ref.shape[0]
    nz = scale_ref.shape[0]

    def body(b, carry):
        scale = scale_ref[...]
        lane = lane_ids(scale.shape)
        last = scale.shape[1] - 1
        uz = v_ref[b, pl.ds(0, nz), :] * scale
        up = v_ref[b, pl.ds(nz, nz), :] * scale
        ut = v_ref[b, pl.ds(2 * nz, nz), :] * scale

        def at_first(edge, c):
            return pltpu.roll(edge[...], (edge.shape[1] - (3 * b + c)) % edge.shape[1], 1)

        def at_last(edge, c):
            return pltpu.roll(edge[...], edge.shape[1] - 1 - (3 * b + c), 1)

        def prev(u, c):
            return jnp.where(lane == 0, at_first(fr_ref, c), roll_by(u, 1, 1))

        def nxt(u, c):
            return jnp.where(lane == last, at_last(fl_ref, c), roll_by(u, -1, 1))

        dt_ut = ut - prev(ut, 2)
        up_next = nxt(up, 1)
        uz_next = nxt(uz, 0)
        im_z = (z_next(up) - up) + (z_next(dt_ut) - dt_ut) + 4.0 * uz - uz_next - prev(uz, 0)
        corner_r = jnp.where(lane == 0, at_first(cr_ref, 2), 0.0)
        im_p = (
            4.0 * up - z_next(up) - z_prev(up) - up_next - prev(up, 1)
            - (uz - z_prev(uz)) - dt_ut - corner_r
        )
        corner_l = jnp.where(lane == last, at_last(cl_ref, 1), 0.0)
        im_t = (
            (uz_next - z_prev(uz_next)) - (uz - z_prev(uz)) + (up_next - up)
            + 4.0 * ut - z_next(ut) - z_prev(ut) - corner_l
        )
        for c, im in enumerate((im_z, im_p, im_t)):
            rows = pl.ds(c * nz, nz)
            out = im * scale
            for k in range(nb):
                out = out - coup_ref[b, k] * q_ref[k, rows, :]
            l_ref[b, rows, :] = out
        return carry

    lax.fori_loop(0, nb, body, 0)
    pairs = [(j, b) for b in range(nb) for j in range(nb) if j <= b]
    gram_sums(v_ref, v_ref, acc_ref, pairs, 0, 36)


def sum_kernel(v_ref, scale_ref, l_ref, acc0_ref, fwd_ref, bwd_ref, w_ref, pay_ref, acc_ref):
    nb = v_ref.shape[0]
    nz = scale_ref.shape[0]

    def body(b, carry):
        scale = scale_ref[...]
        lane = lane_ids(scale.shape)
        za = fwd_ref[b, 0]
        tb = fwd_ref[b, 1]
        uz = bwd_ref[b, 0]
        ut = bwd_ref[b, 1]
        up_prev = jnp.where(lane == 0, 0.0, roll_by(ut, 1, 1))
        w_ref[b, pl.ds(0, nz), :] = l_ref[b, pl.ds(0, nz), :] - scale * (za + uz)
        div = (uz - z_prev(uz)) + (ut - up_prev)
        w_ref[b, pl.ds(nz, nz), :] = l_ref[b, pl.ds(nz, nz), :] + scale * div
        w_ref[b, pl.ds(2 * nz, nz), :] = l_ref[b, pl.ds(2 * nz, nz), :] - scale * (tb + ut)
        return carry

    lax.fori_loop(0, nb, body, 0)
    full = [(j, b) for half in (0, 1) for b in range(nb) for j in range(half * nb // 2, (half + 1) * nb // 2)]
    tri = [(j, b) for b in range(nb) for j in range(nb) if j <= b]
    gram_sums(v_ref, w_ref, acc_ref, full, 0, nb * nb // 2)
    gram_sums(w_ref, w_ref, acc_ref, tri, len(full), len(tri))
    lane = lane_ids((8, v_ref.shape[2]))
    row = row_ids((8, v_ref.shape[2]))
    place = {}
    for i, (j, b) in enumerate(full):
        place.setdefault(("new", i), []).extend([(j, b), (b, 3 * nb + j)])
    for i, (j, b) in enumerate(tri):
        place.setdefault(("new", len(full) + i), []).extend({(j, nb + b), (b, nb + j)})
        place.setdefault(("old", i), []).extend({(j, 2 * nb + b), (b, 2 * nb + j)})
    pay = jnp.zeros((8, v_ref.shape[2]), jnp.float32)
    for (which, i), spots in place.items():
        acc = acc_ref[i] if which == "new" else acc0_ref[i]
        total = jnp.sum(jnp.sum(acc, axis=0, keepdims=True), axis=1, keepdims=True)
        hit = (row == spots[0][0]) & (lane == spots[0][1])
        for spot in spots[1:]:
            hit = hit | ((row == spot[0]) & (lane == spot[1]))
        pay = jnp.where(hit, total, pay)
    pay_ref[...] = pay


def lane_at(x, k):
    return jnp.broadcast_to(x[:, k : k + 1], x.shape)


def row_at(x, k):
    return jnp.broadcast_to(x[k : k + 1, :], x.shape)


def last_kernel(count, pay_ref, v_ref, w_ref, out_ref, alpha_ref, beta_ref, coef_ref):
    nb = v_ref.shape[0]
    pay = pay_ref[...]
    lane = lane_ids(pay.shape)
    row = row_ids(pay.shape)
    proj = pay
    alpha = proj / count
    alpha_t = roll_by(pay, -3 * nb, 1) / count
    ww = roll_by(pay, -nb, 1)
    vv = roll_by(pay, -2 * nb, 1)
    cross = jnp.zeros_like(pay)
    half = jnp.zeros_like(pay)
    for j in range(nb):
        cross = cross + lane_at(alpha_t, j) * row_at(proj, j)
        half = half + lane_at(vv, j) * row_at(alpha, j)
    quad = jnp.zeros_like(pay)
    for k in range(nb):
        quad = quad + lane_at(alpha_t, k) * row_at(half, k)
    gram = ((ww - cross) + (quad - cross)) / count
    mat = jnp.where(lane < nb, gram, jnp.where(lane - nb == row, 1.0, 0.0))
    fact = jnp.zeros_like(pay)
    for k in range(nb):
        line = row_at(mat, k)
        root = 1.0 / jnp.sqrt(lane_at(line, k))
        line = line * root
        fact = jnp.where(row == k, line, fact)
        if k < nb - 1:
            mat = mat - (lane_at(mat, k) * root) * line
    inv = roll_by(fact, -nb, 1)
    alpha_ref[...] = alpha[:, :nb]
    beta_ref[...] = jnp.where(lane >= row, fact, 0.0)[:, :nb]
    mix = jnp.zeros_like(pay)
    for j in range(nb):
        mix = mix + lane_at(inv, j) * row_at(alpha_t, j)
    for j in range(nb):
        coef_ref[j] = lane_at(inv, j)
        coef_ref[nb + j] = -lane_at(mix, j)
    step = 16

    def body(r, carry):
        rows = pl.ds(pl.multiple_of(r * step, step), step)
        xs = [w_ref[j, rows, :] for j in range(nb)] + [v_ref[j, rows, :] for j in range(nb)]
        for b in range(nb):
            acc = coef_ref[0, pl.ds(b, 1), :] * xs[0]
            for j in range(1, 2 * nb):
                acc = acc + coef_ref[j, pl.ds(b, 1), :] * xs[j]
            out_ref[b, rows, :] = acc
        return carry

    lax.fori_loop(0, v_ref.shape[1] // step, body, 0)


def shift(x, loop_by, trans_by):
    loops, trans = lax.axis_size("loop"), lax.axis_size("trans")
    pairs = []
    for i in range(loops):
        for t in range(trans):
            if 0 <= t + trans_by < trans:
                pairs.append((i * trans + t, ((i + loop_by) % loops) * trans + t + trans_by))
    return lax.ppermute(x, ("loop", "trans"), pairs)


def all_sum(x):
    sizes = {axis: lax.axis_size(axis) for axis in ("trans", "loop")}
    for axis, size in sizes.items():
        if size & (size - 1):
            x = lax.psum(x, axis)
            continue
        bit = 1
        while bit < size:
            x = x + lax.ppermute(x, axis, [(i, i ^ bit) for i in range(size)])
            bit *= 2
    return x


def local(block_now, block_prev, coupling_prev, material, permittivity):
    nb, nc, nz, _, nt = block_now.shape
    f32 = jnp.float32
    count = float(nc * nz * nt * lax.axis_size("loop") * lax.axis_size("trans"))
    v4 = block_now.reshape(nb, nc, nz, nt)
    v = block_now.reshape(nb, nc * nz, nt)
    q = block_prev.reshape(nb, nc * nz, nt)
    mat = material.reshape(nz, nt)
    vm, sm = pl.BlockSpec(memory_space=VM), pl.BlockSpec(memory_space=SM)
    params = pltpu.CompilerParams(vmem_limit_bytes=32 * 2**20)
    halo = jax.ShapeDtypeStruct((nb, 2, nz, nt), f32)
    plane = jax.ShapeDtypeStruct((nz, nt), f32)
    field = jax.ShapeDtypeStruct((nb, nc * nz, nt), f32)
    fwd, bwd, right, left, scale = pl.pallas_call(
        pack_kernel,
        out_shape=(halo, halo, plane, plane, plane),
        in_specs=[sm, vm, vm],
        out_specs=(vm,) * 5,
        compiler_params=params,
        name="pack",
    )(permittivity, v4, mat)
    fwd = shift(fwd, 1, 0)
    bwd = shift(bwd, -1, 0)
    from_left = shift(right, 0, 1)
    from_right = shift(left, 0, -1)
    corner_r = shift(right, -1, 1)
    corner_l = shift(left, 1, -1)
    npair = nb * (nb + 1) // 2
    inner, acc0 = pl.pallas_call(
        local_kernel,
        out_shape=(field, jax.ShapeDtypeStruct((npair, 8, nt), f32)),
        in_specs=[sm, sm] + [vm] * 7,
        out_specs=(vm, vm),
        compiler_params=params,
        cost_estimate=pl.CostEstimate(flops=10**7, bytes_accessed=3 * 10**6, transcendentals=0),
        name="inner",
    )(permittivity, coupling_prev, v, scale, q, from_left, from_right, corner_r, corner_l)
    w, pay = pl.pallas_call(
        sum_kernel,
        out_shape=(field, jax.ShapeDtypeStruct((8, nt), f32)),
        in_specs=[vm] * 6,
        out_specs=(vm, vm),
        scratch_shapes=[VM((nb * nb + npair, 8, nt), f32)],
        compiler_params=params,
        name="products",
    )(v, scale, inner, acc0, fwd, bwd)
    pay = all_sum(pay)
    small = jax.ShapeDtypeStruct((nb, nb), f32)
    out, alpha, beta = pl.pallas_call(
        lambda *refs: last_kernel(count, *refs),
        out_shape=(field, small, small),
        in_specs=[vm] * 3,
        out_specs=(vm,) * 3,
        scratch_shapes=[VM((2 * nb, 8, nt), f32)],
        compiler_params=params,
        name="combine",
    )(pay, v, w)
    return out.reshape(block_now.shape), alpha, beta


def solution(mesh):
    in_specs = (
        P(None, None, None, "loop", "trans"),
        P(None, None, None, "loop", "trans"),
        P(),
        P(None, "loop", "trans"),
        P(),
    )
    out_specs = (P(None, None, None, "loop", "trans"), P(), P())
    return jax.shard_map(local, mesh=mesh, in_specs=in_specs, out_specs=out_specs, check_vma=False)
```

time: 162 us -> 63.1 us (0.39)
  blocking collectives: 79.4 us -> 0 us
  starting transfers between devices: 6.37 us -> 23.3 us
  local copies, waits for them, and re-layouts: 16.7 us -> 2.55 us
  waiting for transfers between devices: 38.9 us -> 26.4 us
  other arithmetic: 11.9 us -> 0.02 us
  Pallas kernels: 0 us -> 9.82 us
  matrix products: 7.01 us -> 0 us
    psum x2 -> x0, blocking collectives: 79.4 us -> none  [the longest x1 42.3 us: local(): gram = lax.psum(local_resid, ('loop', 'trans')) / count]
    ppermute x4 -> x11, starting transfers between devices: 6.37 us -> 23.3 us  [the longest x6 13.6 us: shift(): return lax.ppermute(x, ('loop', 'trans'), pairs)]
    ppermute x4 -> x11, waiting for transfers between devices: 38.9 us -> 26.4 us  [the longest x6 17.2 us: shift(): return lax.ppermute(x, ('loop', 'trans'), pairs)]
    pallas_call x0 -> x4, Pallas kernels: none -> 9.82 us  [the longest x1 3.25 us: local(): pl.pallas_call(lambda *refs: last_kernel(count, *refs), out_shape=(field,...]
    slice x12 -> x0, local copies, waits for them, and re-layouts: 8.28 us -> none  [the longest x2 2.98 us: padded(): lax.slice_in_dim(cells, cells.shape[dim] - width, cells.shape[dim], axis=...]
    dot_general x5 -> x0, matrix products: 6.83 us -> none  [the longest x1 1.92 us: local(): local_project = jnp.einsum('jcxyz,bcxyz->jb', block_now, work, precision=hp)]
    mul x2 -> x0, other arithmetic: 6.36 us -> none  [the longest x1 4.76 us: local(): extended = extended * keep]
    ppermute x2 -> x0, local copies, waits for them, and re-layouts: 3.02 us -> none  [the longest x1 2.17 us: padded(): lax.ppermute(tail, axis, [(i, (i + 1) % count) for i in range(count)])]
  transfers between devices with their start and end apart: 4 -> 11, of which waited for: 4 -> 7; matrix products, arithmetic and copies ran while one was open for 1% -> 0% of each run, Pallas kernels for 0% -> 5%
where the time goes in v1:
time: 63.1 us; the launch traced here: 62.8 us
  waiting for transfers between devices  26.4 us (42%)
  starting transfers between devices  23.3 us (37%)
  Pallas kernels  9.82 us (16%)
  local copies, waits for them, and re-layouts  2.55 us (4%)
  between operations  0.75 us (1%)
    ppermute x6, waiting for transfers between devices, shift(): return lax.ppermute(x, ('loop', 'trans'), pairs)  17.2 us
    ppermute x6, starting transfers between devices, shift(): return lax.ppermute(x, ('loop', 'trans'), pairs)  13.6 us
    ppermute x5, starting transfers between devices, all_sum(): x = x + lax.ppermute(x, axis, [(i, i ^ bit) for i in range(size)])  9.66 us
    ppermute x5, waiting for transfers between devices, all_sum(): x = x + lax.ppermute(x, axis, [(i, i ^ bit) for i in range(size)])  9.2 us
    pallas_call x1, Pallas kernels, local(): pl.pallas_call(lambda *refs: last_kernel(count, *refs), out_shape=(field,...  3.25 us
    pallas_call x1, Pallas kernels, local(): pl.pallas_call(local_kernel, out_shape=(field, jax.ShapeDtypeStruct((npai...  2.96 us
    unnamed x12, local copies, waits for them, and re-layouts  2.55 us
    pallas_call x1, Pallas kernels, local(): pl.pallas_call(sum_kernel, out_shape=(field, jax.ShapeDtypeStruct((8, nt)...  2.51 us
  transfers between devices with their start and end apart: 11, of which 7 were waited for; matrix products, arithmetic and copies ran while one was open for 0% of the time, Pallas kernels for 5%

profile of v1, /device:TPU:0, one launch (start us, length us, event | category | flops | bytes accessed | tf_op | source)
XLA Modules:
  0.0 62.8 jit_solution(12828403164268292303)
XLA Ops:
  0.6 0.0 copy-start.5
  0.6 0.6 %copy-done.5 = f32[4]{0:T(128)S(1)} copy-done((f32[4]{0:T(128)S(1)}, f32[4]{0:T(128)}, u32[]{:S(2)}) %copy-start.5) | copy-done | bytes 40
  1.3 0.0 copy-start
  1.3 1.1 %copy-done = f32[8,3,64,1,128]{4,3,2,1,0:T(1,128)S(1)} copy-done((f32[8,3,64,1,128]{4,3,2,1,0:T(1,128)S(1)}, f32[8,3,64,1,128]{4,3,2,1,0:T(1,128)}, u32[]{:S(2)}) %copy-start) | copy-done | bytes 786456
  2.4 0.0 copy-start.3
  2.4 0.8 %copy-done.3 = s32[64,1,128]{2,1,0:T(1,128)S(1)} copy-done((s32[64,1,128]{2,1,0:T(1,128)S(1)}, s32[64,1,128]{2,1,0:T(1,128)}, u32[]{:S(2)}) %copy-start.3) | copy-done | bytes 32792
  3.2 0.0 copy-start.2
  3.2 1.1 %pack.1 = (f32[8,2,64,128]{3,2,1,0:T(8,128)S(1)}, f32[8,2,64,128]{3,2,1,0:T(8,128)S(1)}, f32[64,128]{1,0:T(8,128)S(1)}, f32[64,128]{1,0:T(8,128)S(1)}, f32[64,128]{1,0:T(8,128)S(1)}) custom-call(f32[4]{0:T(128)S(1)} %copy-done.5, f32[8,3,64,128]{3,2,1,0:T(8,128)S(1)} %bitcast.7, s32[64,128]{1,0:T(8,128)S(1)} %bitcast.12), custom_call_target="tpu_custom_call" | custom-call | tf_op jit(solution)/shard_map/pack/pallas_call | solution.py:270
  4.3 3.0 %collective-permute-start.4 = (f32[8,2,64,128]{3,2,1,0:T(8,128)S(1)}, f32[8,2,64,128]{3,2,1,0:T(8,128)S(1)}, u32[]{:S(2)}, u32[]{:S(2)}) collective-permute-start(f32[8,2,64,128]{3,2,1,0:T(8,128)S(1)} %get-tuple-element.20), channel_id=1, source_target_pairs={{0,8},{1,9},{2,10},{3,11},{4,12},{5,13},{6,14},{7,15},{8,16},{9,17... | collective-permute-start | bytes 1572872 | tf_op jit(solution)/shard_map/ppermute | solution.py:241
  7.3 1.0 %collective-permute-start.5 = (f32[8,2,64,128]{3,2,1,0:T(8,128)S(1)}, f32[8,2,64,128]{3,2,1,0:T(8,128)S(1)}, u32[]{:S(2)}, u32[]{:S(2)}) collective-permute-start(f32[8,2,64,128]{3,2,1,0:T(8,128)S(1)} %get-tuple-element.21), channel_id=1, source_target_pairs={{0,24},{1,25},{2,26},{3,27},{4,28},{5,29},{6,30},{7,31},{8,0},{9,1... | collective-permute-start | bytes 1572872 | tf_op jit(solution)/shard_map/ppermute | solution.py:241
  8.3 0.0 copy-start.4
  8.3 2.9 %collective-permute-start.2 = (f32[64,128]{1,0:T(8,128)S(1)}, f32[64,128]{1,0:T(8,128)S(1)}, u32[]{:S(2)}, u32[]{:S(2)}) collective-permute-start(f32[64,128]{1,0:T(8,128)S(1)} %get-tuple-element.16), channel_id=1, source_target_pairs={{0,25},{1,26},{2,27},{3,28},{4,29},{5,30},{6,31},{8,1},{9,2},{10,3... | collective-permute-start | bytes 98312 | tf_op jit(solution)/shard_map/ppermute | solution.py:241
  11.2 4.2 %collective-permute-start = (f32[64,128]{1,0:T(8,128)S(1)}, f32[64,128]{1,0:T(8,128)S(1)}, u32[]{:S(2)}, u32[]{:S(2)}) collective-permute-start(f32[64,128]{1,0:T(8,128)S(1)} %get-tuple-element.16), channel_id=1, source_target_pairs={{0,1},{1,2},{2,3},{3,4},{4,5},{5,6},{6,7},{8,9},{9,10},{10,11},{11... | collective-permute-start | bytes 98312 | tf_op jit(solution)/shard_map/ppermute | solution.py:241
  15.3 1.3 %collective-permute-start.3 = (f32[64,128]{1,0:T(8,128)S(1)}, f32[64,128]{1,0:T(8,128)S(1)}, u32[]{:S(2)}, u32[]{:S(2)}) collective-permute-start(f32[64,128]{1,0:T(8,128)S(1)} %get-tuple-element.17), channel_id=1, source_target_pairs={{1,8},{2,9},{3,10},{4,11},{5,12},{6,13},{7,14},{9,16},{10,17},{11,... | collective-permute-start | bytes 98312 | tf_op jit(solution)/shard_map/ppermute | solution.py:241
  16.6 14.1 %collective-permute-done.2.cr_ref = f32[64,128]{1,0:T(8,128)S(1)} collective-permute-done((f32[64,128]{1,0:T(8,128)S(1)}, f32[64,128]{1,0:T(8,128)S(1)}, u32[]{:S(2)}, u32[]{:S(2)}) %collective-permute-start.2) | collective-permute-done | bytes 32800 | tf_op jit(solution)/shard_map/ppermute | solution.py:241
  30.8 1.3 %collective-permute-start.1 = (f32[64,128]{1,0:T(8,128)S(1)}, f32[64,128]{1,0:T(8,128)S(1)}, u32[]{:S(2)}, u32[]{:S(2)}) collective-permute-start(f32[64,128]{1,0:T(8,128)S(1)} %get-tuple-element.17), channel_id=1, source_target_pairs={{1,0},{2,1},{3,2},{4,3},{5,4},{6,5},{7,6},{9,8},{10,9},{11,10},{12... | collective-permute-start | bytes 98312 | tf_op jit(solution)/shard_map/ppermute | solution.py:241
  32.0 0.0 collective-permute-done.fr_ref
  32.1 0.0 collective-permute-done.3.cl_ref
  32.1 3.0 %collective-permute-done.1.fl_ref = f32[64,128]{1,0:T(8,128)S(1)} collective-permute-done((f32[64,128]{1,0:T(8,128)S(1)}, f32[64,128]{1,0:T(8,128)S(1)}, u32[]{:S(2)}, u32[]{:S(2)}) %collective-permute-start.1) | collective-permute-done | bytes 32800 | tf_op jit(solution)/shard_map/ppermute | solution.py:241
  35.1 0.0 copy-done.2
  35.1 0.0 copy-done.4
  35.1 0.0 copy-start.1
  35.1 3.0 %inner.1 = (f32[8,192,128]{2,1,0:T(8,128)S(1)}, f32[36,8,128]{2,1,0:T(8,128)S(1)}) custom-call(f32[4]{0:T(128)S(1)} %copy-done.5, f32[8,8]{1,0:T(8,128)S(1)} %copy-done.4, f32[8,192,128]{2,1,0:T(8,128)S(1)} %bitcast.8, f32[64,128]{1,0:T(8,128)S(1)} %get-tuple-element.15.scale_ref, f32[8,192,128]{2,1,0:T(8,128)S(1)} %bitcast.11, ...), custom_call_target="tpu_custom_call" | custom-call | flops 10000000 | bytes 3000000 | tf_op jit(solution)/shard_map/inner/pallas_call | solution.py:285
  38.1 0.0 collective-permute-done.4.fwd_ref
  38.1 0.0 collective-permute-done.5.bwd_ref
  38.1 0.0 copy-done.1
  38.1 2.5 %products.1 = (f32[8,192,128]{2,1,0:T(8,128)S(1)}, f32[8,128]{1,0:T(8,128)S(1)}) custom-call(f32[8,192,128]{2,1,0:T(8,128)S(1)} %bitcast.9, f32[64,128]{1,0:T(8,128)S(1)} %get-tuple-element.15.scale_ref, f32[8,192,128]{2,1,0:T(8,128)S(1)} %get-tuple-element.18.l_ref, f32[36,8,128]{2,1,0:T(8,128)S(1)} %get-tuple-element.19.acc0_ref, ...), custom_call_target="tpu_custom_call" | custom-call | tf_op jit(solution)/shard_map/products/pallas_call | solution.py:294
  40.6 2.7 %collective-permute-start.6 = (f32[8,128]{1,0:T(8,128)S(1)}, f32[8,128]{1,0:T(8,128)S(1)}, u32[]{:S(2)}, u32[]{:S(2)}) collective-permute-start(f32[8,128]{1,0:T(8,128)S(1)} %get-tuple-element.22), channel_id=1, source_target_pairs={{0,1},{1,0},{2,3},{3,2},{4,5},{5,4},{6,7},{7,6},{8,9},{9,8},{10,11... | collective-permute-start | bytes 12296 | tf_op jit(solution)/shard_map/ppermute | solution.py:252
  43.3 0.8 %collective-permute-done.6 = f32[8,128]{1,0:T(8,128)S(1)} collective-permute-done((f32[8,128]{1,0:T(8,128)S(1)}, f32[8,128]{1,0:T(8,128)S(1)}, u32[]{:S(2)}, u32[]{:S(2)}) %collective-permute-start.6) | collective-permute-done | bytes 4128 | tf_op jit(solution)/shard_map/ppermute | solution.py:252
  44.2 1.9 %collective-permute-start.7 = (f32[8,128]{1,0:T(8,128)S(1)}, f32[8,128]{1,0:T(8,128)S(1)}, u32[]{:S(2)}, u32[]{:S(2)}) collective-permute-start(f32[8,128]{1,0:T(8,128)S(1)} %add.15), channel_id=1, source_target_pairs={{0,2},{1,3},{2,0},{3,1},{4,6},{5,7},{6,4},{7,5},{8,10},{9,11},{10,... | collective-permute-start | bytes 12296 | tf_op jit(solution)/shard_map/ppermute | solution.py:252
  46.1 1.7 %collective-permute-done.7 = f32[8,128]{1,0:T(8,128)S(1)} collective-permute-done((f32[8,128]{1,0:T(8,128)S(1)}, f32[8,128]{1,0:T(8,128)S(1)}, u32[]{:S(2)}, u32[]{:S(2)}) %collective-permute-start.7) | collective-permute-done | bytes 4128 | tf_op jit(solution)/shard_map/ppermute | solution.py:252
  47.8 2.9 %collective-permute-start.8 = (f32[8,128]{1,0:T(8,128)S(1)}, f32[8,128]{1,0:T(8,128)S(1)}, u32[]{:S(2)}, u32[]{:S(2)}) collective-permute-start(f32[8,128]{1,0:T(8,128)S(1)} %add.16), channel_id=1, source_target_pairs={{0,4},{1,5},{2,6},{3,7},{4,0},{5,1},{6,2},{7,3},{8,12},{9,13},{10,... | collective-permute-start | bytes 12296 | tf_op jit(solution)/shard_map/ppermute | solution.py:252
  50.7 1.6 %collective-permute-done.8 = f32[8,128]{1,0:T(8,128)S(1)} collective-permute-done((f32[8,128]{1,0:T(8,128)S(1)}, f32[8,128]{1,0:T(8,128)S(1)}, u32[]{:S(2)}, u32[]{:S(2)}) %collective-permute-start.8) | collective-permute-done | bytes 4128 | tf_op jit(solution)/shard_map/ppermute | solution.py:252
  52.3 1.5 %collective-permute-start.9 = (f32[8,128]{1,0:T(8,128)S(1)}, f32[8,128]{1,0:T(8,128)S(1)}, u32[]{:S(2)}, u32[]{:S(2)}) collective-permute-start(f32[8,128]{1,0:T(8,128)S(1)} %add.17), channel_id=1, source_target_pairs={{0,8},{8,0},{16,24},{24,16},{1,9},{9,1},{17,25},{25,17},{2,10},{10... | collective-permute-start | bytes 12296 | tf_op jit(solution)/shard_map/ppermute | solution.py:252
  53.8 2.1 %collective-permute-done.9 = f32[8,128]{1,0:T(8,128)S(1)} collective-permute-done((f32[8,128]{1,0:T(8,128)S(1)}, f32[8,128]{1,0:T(8,128)S(1)}, u32[]{:S(2)}, u32[]{:S(2)}) %collective-permute-start.9) | collective-permute-done | bytes 4128 | tf_op jit(solution)/shard_map/ppermute | solution.py:252
  55.9 0.6 collective-permute-start.10
  56.5 3.0 %collective-permute-done.10 = f32[8,128]{1,0:T(8,128)S(1)} collective-permute-done((f32[8,128]{1,0:T(8,128)S(1)}, f32[8,128]{1,0:T(8,128)S(1)}, u32[]{:S(2)}, u32[]{:S(2)}) %collective-permute-start.10) | collective-permute-done | bytes 4128 | tf_op jit(solution)/shard_map/ppermute | solution.py:252
  59.5 3.2 %combine.1 = (f32[8,192,128]{2,1,0:T(8,128)}, f32[8,8]{1,0:T(8,128)}, f32[8,8]{1,0:T(8,128)}) custom-call(f32[8,128]{1,0:T(8,128)S(1)} %add.19.refs_0_, f32[8,192,128]{2,1,0:T(8,128)S(1)} %bitcast.10, f32[8,192,128]{2,1,0:T(8,128)S(1)} %get-tuple-element.23.refs_2_), custom_call_target="tpu_custom_call" | custom-call | tf_op jit(solution)/shard_map/combine/pallas_call | solution.py:305
  (5 shorter events, 0.0 us)
Async XLA Ops:
  0.6 0.7 %copy-start.5 = (f32[4]{0:T(128)S(1)}, f32[4]{0:T(128)}, u32[]{:S(2)}) copy-start(f32[4]{0:T(128)} %eps_ref.3) | copy-start | bytes 52
  1.3 1.1 %copy-start = (f32[8,3,64,1,128]{4,3,2,1,0:T(1,128)S(1)}, f32[8,3,64,1,128]{4,3,2,1,0:T(1,128)}, u32[]{:S(2)}) copy-start(f32[8,3,64,1,128]{4,3,2,1,0:T(1,128)} %param.5) | copy-start | bytes 2359300
  2.4 0.8 %copy-start.3 = (s32[64,1,128]{2,1,0:T(1,128)S(1)}, s32[64,1,128]{2,1,0:T(1,128)}, u32[]{:S(2)}) copy-start(s32[64,1,128]{2,1,0:T(1,128)} %param.8) | copy-start | bytes 98308
  3.2 31.9 %copy-start.2 = (f32[8,3,64,1,128]{4,3,2,1,0:T(1,128)S(1)}, f32[8,3,64,1,128]{4,3,2,1,0:T(1,128)}, u32[]{:S(2)}) copy-start(f32[8,3,64,1,128]{4,3,2,1,0:T(1,128)} %param.6) | copy-start | bytes 2359300
  4.3 33.8 %collective-permute-start.4 = (f32[8,2,64,128]{3,2,1,0:T(8,128)S(1)}, f32[8,2,64,128]{3,2,1,0:T(8,128)S(1)}, u32[]{:S(2)}, u32[]{:S(2)}) collective-permute-start(f32[8,2,64,128]{3,2,1,0:T(8,128)S(1)} %get-tuple-element.20), channel_id=1, source_target_pairs={{0,8},{1,9},{2,10},{3,11},{4,12},{5,13},{6,14},{7,15},{8,16},{9,17... | collective-permute-start | bytes 1572872 | tf_op jit(solution)/shard_map/ppermute | solution.py:241
  7.3 30.8 %collective-permute-start.5 = (f32[8,2,64,128]{3,2,1,0:T(8,128)S(1)}, f32[8,2,64,128]{3,2,1,0:T(8,128)S(1)}, u32[]{:S(2)}, u32[]{:S(2)}) collective-permute-start(f32[8,2,64,128]{3,2,1,0:T(8,128)S(1)} %get-tuple-element.21), channel_id=1, source_target_pairs={{0,24},{1,25},{2,26},{3,27},{4,28},{5,29},{6,30},{7,31},{8,0},{9,1... | collective-permute-start | bytes 1572872 | tf_op jit(solution)/shard_map/ppermute | solution.py:241
  8.3 26.8 %copy-start.4 = (f32[8,8]{1,0:T(8,128)S(1)}, f32[8,8]{1,0:T(8,128)}, u32[]{:S(2)}) copy-start(f32[8,8]{1,0:T(8,128)} %coup_ref.1) | copy-start | bytes 772
  8.3 22.4 %collective-permute-start.2 = (f32[64,128]{1,0:T(8,128)S(1)}, f32[64,128]{1,0:T(8,128)S(1)}, u32[]{:S(2)}, u32[]{:S(2)}) collective-permute-start(f32[64,128]{1,0:T(8,128)S(1)} %get-tuple-element.16), channel_id=1, source_target_pairs={{0,25},{1,26},{2,27},{3,28},{4,29},{5,30},{6,31},{8,1},{9,2},{10,3... | collective-permute-start | bytes 98312 | tf_op jit(solution)/shard_map/ppermute | solution.py:241
  11.2 20.9 %collective-permute-start = (f32[64,128]{1,0:T(8,128)S(1)}, f32[64,128]{1,0:T(8,128)S(1)}, u32[]{:S(2)}, u32[]{:S(2)}) collective-permute-start(f32[64,128]{1,0:T(8,128)S(1)} %get-tuple-element.16), channel_id=1, source_target_pairs={{0,1},{1,2},{2,3},{3,4},{4,5},{5,6},{6,7},{8,9},{9,10},{10,11},{11... | collective-permute-start | bytes 98312 | tf_op jit(solution)/shard_map/ppermute | solution.py:241
  15.3 16.7 %collective-permute-start.3 = (f32[64,128]{1,0:T(8,128)S(1)}, f32[64,128]{1,0:T(8,128)S(1)}, u32[]{:S(2)}, u32[]{:S(2)}) collective-permute-start(f32[64,128]{1,0:T(8,128)S(1)} %get-tuple-element.17), channel_id=1, source_target_pairs={{1,8},{2,9},{3,10},{4,11},{5,12},{6,13},{7,14},{9,16},{10,17},{11,... | collective-permute-start | bytes 98312 | tf_op jit(solution)/shard_map/ppermute | solution.py:241
  30.8 4.4 %collective-permute-start.1 = (f32[64,128]{1,0:T(8,128)S(1)}, f32[64,128]{1,0:T(8,128)S(1)}, u32[]{:S(2)}, u32[]{:S(2)}) collective-permute-start(f32[64,128]{1,0:T(8,128)S(1)} %get-tuple-element.17), channel_id=1, source_target_pairs={{1,0},{2,1},{3,2},{4,3},{5,4},{6,5},{7,6},{9,8},{10,9},{11,10},{12... | collective-permute-start | bytes 98312 | tf_op jit(solution)/shard_map/ppermute | solution.py:241
  35.1 3.0 %copy-start.1 = (f32[8,3,64,1,128]{4,3,2,1,0:T(1,128)S(1)}, f32[8,3,64,1,128]{4,3,2,1,0:T(1,128)}, u32[]{:S(2)}) copy-start(f32[8,3,64,1,128]{4,3,2,1,0:T(1,128)} %param.5) | copy-start | bytes 2359300
  40.6 3.5 %collective-permute-start.6 = (f32[8,128]{1,0:T(8,128)S(1)}, f32[8,128]{1,0:T(8,128)S(1)}, u32[]{:S(2)}, u32[]{:S(2)}) collective-permute-start(f32[8,128]{1,0:T(8,128)S(1)} %get-tuple-element.22), channel_id=1, source_target_pairs={{0,1},{1,0},{2,3},{3,2},{4,5},{5,4},{6,7},{7,6},{8,9},{9,8},{10,11... | collective-permute-start | bytes 12296 | tf_op jit(solution)/shard_map/ppermute | solution.py:252
  44.2 3.6 %collective-permute-start.7 = (f32[8,128]{1,0:T(8,128)S(1)}, f32[8,128]{1,0:T(8,128)S(1)}, u32[]{:S(2)}, u32[]{:S(2)}) collective-permute-start(f32[8,128]{1,0:T(8,128)S(1)} %add.15), channel_id=1, source_target_pairs={{0,2},{1,3},{2,0},{3,1},{4,6},{5,7},{6,4},{7,5},{8,10},{9,11},{10,... | collective-permute-start | bytes 12296 | tf_op jit(solution)/shard_map/ppermute | solution.py:252
  47.8 4.5 %collective-permute-start.8 = (f32[8,128]{1,0:T(8,128)S(1)}, f32[8,128]{1,0:T(8,128)S(1)}, u32[]{:S(2)}, u32[]{:S(2)}) collective-permute-start(f32[8,128]{1,0:T(8,128)S(1)} %add.16), channel_id=1, source_target_pairs={{0,4},{1,5},{2,6},{3,7},{4,0},{5,1},{6,2},{7,3},{8,12},{9,13},{10,... | collective-permute-start | bytes 12296 | tf_op jit(solution)/shard_map/ppermute | solution.py:252
  52.3 3.6 %collective-permute-start.9 = (f32[8,128]{1,0:T(8,128)S(1)}, f32[8,128]{1,0:T(8,128)S(1)}, u32[]{:S(2)}, u32[]{:S(2)}) collective-permute-start(f32[8,128]{1,0:T(8,128)S(1)} %add.17), channel_id=1, source_target_pairs={{0,8},{8,0},{16,24},{24,16},{1,9},{9,1},{17,25},{25,17},{2,10},{10... | collective-permute-start | bytes 12296 | tf_op jit(solution)/shard_map/ppermute | solution.py:252
  55.9 3.6 %collective-permute-start.10 = (f32[8,128]{1,0:T(8,128)S(1)}, f32[8,128]{1,0:T(8,128)S(1)}, u32[]{:S(2)}, u32[]{:S(2)}) collective-permute-start(f32[8,128]{1,0:T(8,128)S(1)} %add.18), channel_id=1, source_target_pairs={{0,16},{8,24},{16,0},{24,8},{1,17},{9,25},{17,1},{25,9},{2,18},{10... | collective-permute-start | bytes 12296 | tf_op jit(solution)/shard_map/ppermute | solution.py:252

commit v2 on v1

v2 whole, which is shorter than its diff:
```python
import jax
import jax.numpy as jnp
from jax import lax
from jax.experimental import pallas as pl
from jax.experimental.pallas import tpu as pltpu
from jax.sharding import PartitionSpec as P

VM = pltpu.VMEM
SM = pltpu.SMEM


def lane_ids(shape):
    return lax.broadcasted_iota(jnp.int32, shape, len(shape) - 1)


def row_ids(shape):
    return lax.broadcasted_iota(jnp.int32, shape, len(shape) - 2)


def roll_by(x, shift, axis):
    return pltpu.roll(x, shift % x.shape[axis], axis)


def cell_scale(mat, eps_ref):
    eps = jnp.full(mat.shape, eps_ref[0], jnp.float32)
    for level in range(1, eps_ref.shape[0]):
        eps = jnp.where(mat == level, eps_ref[level], eps)
    return 1.0 / jnp.sqrt(eps)


def z_next(x):
    n = x.shape[0]
    return jnp.where(row_ids(x.shape) == n - 1, 0.0, roll_by(x, -1, 0))


def z_prev(x):
    return jnp.where(row_ids(x.shape) == 0, 0.0, roll_by(x, 1, 0))


def packed(v_ref, b, scale, fwd_ref, bwd_ref, at):
    nz = scale.shape[0]
    lane = lane_ids(scale.shape)
    last = scale.shape[1] - 1
    uz = v_ref[b, pl.ds(0, nz), :] * scale
    up = v_ref[b, pl.ds(nz, nz), :] * scale
    ut = v_ref[b, pl.ds(2 * nz, nz), :] * scale
    bwd_ref[at] = uz
    bwd_ref[at + 1] = ut
    fwd_ref[at] = uz + (z_next(up) - up)
    fwd_ref[at + 1] = ut + (jnp.where(lane == last, 0.0, roll_by(up, -1, 1)) - up)


def first_kernel(v_hbm, mat_hbm, eps_hbm, fwd_ref, bwd_ref, scale_ref, v_ref, mat_ref, eps_ref, sems):
    count = v_ref.shape[0]
    copies = [
        pltpu.make_async_copy(eps_hbm, eps_ref, sems.at[0]),
        pltpu.make_async_copy(mat_hbm, mat_ref, sems.at[1]),
    ]
    for b in range(count):
        copies.append(pltpu.make_async_copy(v_hbm.at[b], v_ref.at[b], sems.at[2 + b]))
    for copy in copies:
        copy.start()
    copies[0].wait()
    copies[1].wait()
    scale = cell_scale(mat_ref[...], eps_ref)
    scale_ref[...] = scale
    for b in range(count):
        copies[2 + b].wait()
        packed(v_ref, b, scale, fwd_ref, bwd_ref, 2 * b)


def edge_kernel(v_ref, scale_ref, right_ref, left_ref):
    scale = scale_ref[...]
    nz = scale.shape[0]
    lane = lane_ids(scale.shape)
    right = jnp.zeros_like(scale)
    left = jnp.zeros_like(scale)
    for b in range(v_ref.shape[0]):
        for c in range(3):
            u = v_ref[b, pl.ds(c * nz, nz), :] * scale
            spot = 3 * b + c
            right = jnp.where(lane == spot, roll_by(u, spot + 1, 1), right)
            left = jnp.where(lane == spot, roll_by(u, spot, 1), left)
    right_ref[...] = right
    left_ref[...] = left


def corner_kernel(begin, end, v_ref, scale_ref, fr_ref, fl_ref, fwd_ref, bwd_ref):
    scale = scale_ref[...]
    for b in range(begin, end):
        packed(v_ref, b, scale, fwd_ref, bwd_ref, 2 * (b - begin))
    fwd_ref[2 * (end - begin)] = fl_ref[...]
    bwd_ref[2 * (end - begin)] = fr_ref[...]


def more_kernel(begin, end, v_ref, scale_ref, fwd_a_ref, bwd_a_ref, fwd_ref, bwd_ref):
    scale = scale_ref[...]
    for b in range(begin, end):
        packed(v_ref, b, scale, fwd_ref, bwd_ref, 2 * (b - begin))


def gram_sums(pairs, lefts, rights, steps, group):
    out = []
    for first in range(0, len(pairs), group):
        part = pairs[first : first + group]

        def body(r, accs):
            rows = pl.ds(pl.multiple_of(r * 8, 8), 8)
            load = lambda side, i: side[i][0][side[i][1], rows, :]
            ls = {j: load(lefts, j) for j in sorted({p[0] for p in part})}
            if lefts is rights:
                rs = {b: ls[b] if b in ls else load(rights, b) for b in sorted({p[1] for p in part})}
            else:
                rs = {b: load(rights, b) for b in sorted({p[1] for p in part})}
            return tuple(acc + ls[j] * rs[b] for acc, (j, b) in zip(accs, part))

        zero = jnp.zeros((8, lefts[0][0].shape[2]), jnp.float32)
        out.extend(lax.fori_loop(0, steps, body, tuple(zero for _ in part)))
    return out


def put(rows, acc, spots):
    total = jnp.sum(jnp.sum(acc, axis=0, keepdims=True), axis=1, keepdims=True)
    lane = lane_ids(rows[0].shape)
    rows = list(rows)
    for row in {s[0] for s in spots}:
        hit = None
        for spot in spots:
            if spot[0] == row:
                here = lane == spot[1]
                hit = here if hit is None else hit | here
        rows[row] = jnp.where(hit, total, rows[row])
    return rows


def inner_kernel(coup_ref, v_ref, scale_ref, q_ref, fr_ref, fl_ref, l_ref, pay_ref):
    nb = v_ref.shape[0]
    nz = scale_ref.shape[0]

    def body(b, carry):
        scale = scale_ref[...]
        lane = lane_ids(scale.shape)
        last = scale.shape[1] - 1
        uz = v_ref[b, pl.ds(0, nz), :] * scale
        up = v_ref[b, pl.ds(nz, nz), :] * scale
        ut = v_ref[b, pl.ds(2 * nz, nz), :] * scale

        def prev(u, c):
            edge = pltpu.roll(fr_ref[...], (last + 1 - (3 * b + c)) % (last + 1), 1)
            return jnp.where(lane == 0, edge, roll_by(u, 1, 1))

        def nxt(u, c):
            edge = pltpu.roll(fl_ref[...], last - (3 * b + c), 1)
            return jnp.where(lane == last, edge, roll_by(u, -1, 1))

        dt_ut = ut - prev(ut, 2)
        up_next = nxt(up, 1)
        uz_next = nxt(uz, 0)
        im_z = (z_next(up) - up) + (z_next(dt_ut) - dt_ut) + 4.0 * uz - uz_next - prev(uz, 0)
        im_p = 4.0 * up - z_next(up) - z_prev(up) - up_next - prev(up, 1) - (uz - z_prev(uz)) - dt_ut
        im_t = (
            (uz_next - z_prev(uz_next)) - (uz - z_prev(uz)) + (up_next - up)
            + 4.0 * ut - z_next(ut) - z_prev(ut)
        )
        for c, im in enumerate((im_z, im_p, im_t)):
            rows = pl.ds(c * nz, nz)
            out = im * scale
            for k in range(nb):
                out = out - coup_ref[b, k] * q_ref[k, rows, :]
            l_ref[b, rows, :] = out
        return carry

    lax.fori_loop(0, nb, body, 0)
    pairs = [(j, b) for b in range(nb) for j in range(b + 1)]
    side = [(v_ref, j) for j in range(nb)]
    row = jnp.zeros((1, v_ref.shape[2]), jnp.float32)
    rows = [row, row]
    for (j, b), acc in zip(pairs, gram_sums(pairs, side, side, v_ref.shape[1] // 8, 36)):
        rows = put(rows, acc, {(1, nb * j + b), (1, nb * b + j)})
    pay_ref[0:1, :] = rows[0]
    pay_ref[1:2, :] = rows[1]


def sum_kernel(cuts, begin, v_ref, scale_ref, l_ref, pay_in_ref, *refs):
    nb = v_ref.shape[0]
    nz, nt = scale_ref.shape
    end = cuts[-1][1]
    halos = refs[: 2 * len(cuts) + 2]
    corner_f, corner_b = halos[-2:]
    rest = refs[2 * len(cuts) + 2 :]
    old, (w_ref, pay_ref) = rest[:-2], rest[-2:]
    scale = scale_ref[...]
    lane = lane_ids(scale.shape)
    plane_f, plane_b = corner_f.shape[0] - 1, corner_b.shape[0] - 1
    for i, (low, high) in enumerate(cuts):
        fwd_ref, bwd_ref = halos[2 * i : 2 * i + 2]

        def body(m, carry):
            b = low + m
            za = fwd_ref[2 * m]
            tb = fwd_ref[2 * m + 1]
            uz = bwd_ref[2 * m]
            ut = bwd_ref[2 * m + 1]
            edge_b = pltpu.roll(corner_b[plane_b], (nt - (3 * b + 2)) % nt, 1)
            edge_f = pltpu.roll(corner_f[plane_f], nt - 1 - (3 * b + 1), 1)
            ut_prev = jnp.where(lane == 0, edge_b, roll_by(ut, 1, 1))
            tb = tb + jnp.where(lane == nt - 1, edge_f, 0.0)
            to = b - begin
            w_ref[to, pl.ds(0, nz), :] = l_ref[b, pl.ds(0, nz), :] - scale * (za + uz)
            div = (uz - z_prev(uz)) + (ut - ut_prev)
            w_ref[to, pl.ds(nz, nz), :] = l_ref[b, pl.ds(nz, nz), :] + scale * div
            w_ref[to, pl.ds(2 * nz, nz), :] = l_ref[b, pl.ds(2 * nz, nz), :] - scale * (tb + ut)
            return carry

        lax.fori_loop(0, high - low, body, 0)
    steps = v_ref.shape[1] // 8
    vs = [(v_ref, j) for j in range(nb)]
    ws = [(old[0], b) for b in range(begin)] + [(w_ref, b - begin) for b in range(begin, end)]
    rows = [pay_in_ref[0:1, :], pay_in_ref[1:2, :]]
    for j0 in range(0, nb, nb // 2):
        pairs = [(j, b) for b in range(begin, end) for j in range(j0, j0 + nb // 2)]
        for (j, b), acc in zip(pairs, gram_sums(pairs, vs, ws, steps, 32)):
            rows = put(rows, acc, {(0, nb * j + b), (1, nb * nb + nb * b + j)})
    pairs = [(j, b) for b in range(begin, end) for j in range(b + 1)]
    for (j, b), acc in zip(pairs, gram_sums(pairs, ws, ws, steps, 36)):
        rows = put(rows, acc, {(0, nb * nb + nb * j + b), (0, nb * nb + nb * b + j)})
    pay_ref[0:1, :] = rows[0]
    pay_ref[1:2, :] = rows[1]


def lane_at(x, k):
    return jnp.broadcast_to(x[:, k : k + 1], x.shape)


def row_at(x, k):
    return jnp.broadcast_to(x[k : k + 1, :], x.shape)


def matrix_of(line, offset, nb):
    x = jnp.broadcast_to(line, (8, line.shape[1]))
    row = row_ids(x.shape)
    out = roll_by(x, -offset, 1)
    for i in range(1, nb):
        out = jnp.where(row == i, roll_by(x, -offset - nb * i, 1), out)
    return out


def last_kernel(count, pay_ref, v_ref, *refs):
    w_refs = refs[:-6]
    out_hbm, alpha_ref, beta_ref, coef_ref, out_ref, sems = refs[-6:]
    nb = v_ref.shape[0]
    total = jnp.sum(pay_ref[...], axis=0)
    proj = matrix_of(total[0:1], 0, nb)
    ww = matrix_of(total[0:1], nb * nb, nb)
    vv = matrix_of(total[1:2], 0, nb)
    alpha = proj / count
    alpha_t = matrix_of(total[1:2], nb * nb, nb) / count
    lane = lane_ids(proj.shape)
    row = row_ids(proj.shape)
    cross = jnp.zeros_like(proj)
    half = jnp.zeros_like(proj)
    for j in range(nb):
        cross = cross + lane_at(alpha_t, j) * row_at(proj, j)
        half = half + lane_at(vv, j) * row_at(alpha, j)
    quad = jnp.zeros_like(proj)
    for k in range(nb):
        quad = quad + lane_at(alpha_t, k) * row_at(half, k)
    gram = ((ww - cross) + (quad - cross)) / count
    mat = jnp.where(lane < nb, gram, jnp.where(lane - nb == row, 1.0, 0.0))
    fact = jnp.zeros_like(proj)
    for k in range(nb):
        line = row_at(mat, k)
        root = 1.0 / jnp.sqrt(lane_at(line, k))
        line = line * root
        fact = jnp.where(row == k, line, fact)
        if k < nb - 1:
            mat = mat - (lane_at(mat, k) * root) * line
    inv = roll_by(fact, -nb, 1)
    alpha_ref[...] = alpha[:, :nb]
    beta_ref[...] = jnp.where(lane >= row, fact, 0.0)[:, :nb]
    mix = jnp.zeros_like(proj)
    for j in range(nb):
        mix = mix + lane_at(inv, j) * row_at(alpha_t, j)
    for j in range(nb):
        coef_ref[j] = lane_at(inv, j)
        coef_ref[nb + j] = -lane_at(mix, j)
    step = 16
    ws = [(w, i) for w in w_refs for i in range(w.shape[0])]
    pieces = sems.shape[0]
    length = v_ref.shape[1] // pieces
    copies = []
    for piece in range(pieces):
        base = piece * length

        def body(r, carry):
            rows = pl.ds(pl.multiple_of(base + r * step, step), step)
            xs = [ref[i, rows, :] for ref, i in ws] + [v_ref[j, rows, :] for j in range(nb)]
            for b in range(nb):
                acc = coef_ref[0, pl.ds(b, 1), :] * xs[0]
                for j in range(1, 2 * nb):
                    acc = acc + coef_ref[j, pl.ds(b, 1), :] * xs[j]
                out_ref[b, rows, :] = acc
            return carry

        lax.fori_loop(0, length // step, body, 0)
        part = pl.ds(base, length)
        copy = pltpu.make_async_copy(out_ref.at[:, part, :], out_hbm.at[:, part, :], sems.at[piece])
        copy.start()
        copies.append(copy)
    for copy in copies:
        copy.wait()


def shift(x, loop_by, trans_by):
    if trans_by:
        count = lax.axis_size("trans")
        return lax.ppermute(x, "trans", [(t, t + trans_by) for t in range(count) if 0 <= t + trans_by < count])
    count = lax.axis_size("loop")
    return lax.ppermute(x, "loop", [(i, (i + loop_by) % count) for i in range(count)])


def local(block_now, block_prev, coupling_prev, material, permittivity):
    nb, nc, nz, _, nt = block_now.shape
    f32 = jnp.float32
    devices = lax.axis_size("loop") * lax.axis_size("trans")
    count = float(nc * nz * nt * devices)
    v = block_now.reshape(nb, nc * nz, nt)
    q = block_prev.reshape(nb, nc * nz, nt)
    mat = material.reshape(nz, nt)
    vm, sm = pl.BlockSpec(memory_space=VM), pl.BlockSpec(memory_space=SM)
    hbm = pl.BlockSpec(memory_space=pltpu.HBM)
    params = pltpu.CompilerParams(vmem_limit_bytes=32 * 2**20)
    wide = pltpu.CompilerParams(vmem_limit_bytes=int(62 * 2**20))
    free = pl.CostEstimate(flops=0, bytes_accessed=0, transcendentals=0)
    plane = jax.ShapeDtypeStruct((nz, nt), f32)
    pay_shape = jax.ShapeDtypeStruct((2, nt), f32)
    cut_a, cut_b, cut_c = (0, nb // 2), (nb // 2, nb * 3 // 4), (nb * 3 // 4, nb)

    def planes(n):
        return jax.ShapeDtypeStruct((n, nz, nt), f32)

    def works(n):
        return jax.ShapeDtypeStruct((n, nc * nz, nt), f32)

    size_a, size_b, size_c = (2 * (c[1] - c[0]) for c in (cut_a, cut_b, cut_c))
    fwd_a, bwd_a, scale = pl.pallas_call(
        first_kernel,
        out_shape=(planes(size_a), planes(size_a), plane),
        in_specs=[hbm] * 3,
        out_specs=(vm,) * 3,
        scratch_shapes=[
            VM((cut_a[1], nc * nz, nt), f32),
            VM((nz, nt), jnp.int32),
            SM(permittivity.shape, f32),
            pltpu.SemaphoreType.DMA((2 + cut_a[1],)),
        ],
        compiler_params=wide,
        cost_estimate=free,
        name="first",
    )(v, mat, permittivity)
    fwd_a, bwd_a = shift(fwd_a, 1, 0), shift(bwd_a, -1, 0)
    right, left = pl.pallas_call(
        edge_kernel,
        out_shape=(plane, plane),
        in_specs=[vm, vm],
        out_specs=(vm, vm),
        compiler_params=params,
        cost_estimate=free,
        name="edges",
    )(v, scale)
    from_left, from_right = shift(right, 0, 1), shift(left, 0, -1)
    fwd_b, bwd_b = pl.pallas_call(
        lambda *refs: corner_kernel(*cut_b, *refs),
        out_shape=(planes(size_b + 1), planes(size_b + 1)),
        in_specs=[vm] * 4,
        out_specs=(vm, vm),
        compiler_params=params,
        cost_estimate=free,
        name="pack_b",
    )(v, scale, from_left, from_right)
    fwd_b, bwd_b = shift(fwd_b, 1, 0), shift(bwd_b, -1, 0)
    fwd_c, bwd_c = pl.pallas_call(
        lambda *refs: more_kernel(*cut_c, *refs),
        out_shape=(planes(size_c), planes(size_c)),
        in_specs=[vm, vm, hbm, hbm],
        out_specs=(vm, vm),
        compiler_params=params,
        cost_estimate=free,
        name="pack_c",
    )(v, scale, fwd_a, bwd_a)
    fwd_c, bwd_c = shift(fwd_c, 1, 0), shift(bwd_c, -1, 0)
    inner, pay = pl.pallas_call(
        inner_kernel,
        out_shape=(works(nb), pay_shape),
        in_specs=[sm] + [vm] * 5,
        out_specs=(vm, vm),
        compiler_params=params,
        cost_estimate=free,
        name="inner",
    )(coupling_prev, v, scale, q, from_left, from_right)
    w_ab, pay = pl.pallas_call(
        lambda *refs: sum_kernel((cut_a, cut_b), 0, *refs),
        out_shape=(works(cut_b[1]), pay_shape),
        in_specs=[vm] * 10,
        out_specs=(vm, vm),
        compiler_params=params,
        cost_estimate=free,
        name="products",
    )(v, scale, inner, pay, fwd_a, bwd_a, fwd_b, bwd_b, fwd_b, bwd_b)
    w_c, pay = pl.pallas_call(
        lambda *refs: sum_kernel((cut_c,), cut_c[0], *refs),
        out_shape=(works(cut_c[1] - cut_c[0]), pay_shape),
        in_specs=[vm] * 9,
        out_specs=(vm, vm),
        compiler_params=params,
        cost_estimate=free,
        name="products_last",
    )(v, scale, inner, pay, fwd_c, bwd_c, fwd_b, bwd_b, w_ab)
    pay = jnp.broadcast_to(pay[None], (devices, 2, nt))
    pay = lax.all_to_all(pay, ("loop", "trans"), 0, 0)
    small = jax.ShapeDtypeStruct((nb, nb), f32)
    out, alpha, beta = pl.pallas_call(
        lambda *refs: last_kernel(count, *refs),
        out_shape=(works(nb), small, small),
        in_specs=[vm] * 4,
        out_specs=(hbm, vm, vm),
        scratch_shapes=[VM((2 * nb, 8, nt), f32), VM((nb, nc * nz, nt), f32), pltpu.SemaphoreType.DMA((4,))],
        compiler_params=params,
        cost_estimate=free,
        name="combine",
    )(pay, v, w_ab, w_c)
    return out.reshape(block_now.shape), alpha, beta


def solution(mesh):
    in_specs = (
        P(None, None, None, "loop", "trans"),
        P(None, None, None, "loop", "trans"),
        P(),
        P(None, "loop", "trans"),
        P(),
    )
    out_specs = (P(None, None, None, "loop", "trans"), P(), P())
    return jax.shard_map(local, mesh=mesh, in_specs=in_specs, out_specs=out_specs, check_vma=False)
```

time: 63.1 us -> 48.7 us (0.77)
  waiting for transfers between devices: 26.4 us -> 7.98 us
  blocking collectives: 0 us -> 13.7 us
  starting transfers between devices: 23.3 us -> 12.7 us
  Pallas kernels: 9.82 us -> 12.4 us
  local copies, waits for them, and re-layouts: 2.55 us -> 0.79 us
    ppermute x11 -> x8, waiting for transfers between devices: 26.4 us -> 7.98 us  [the longest x6 4.13 us: shift(): lax.ppermute(x, 'loop', [(i, (i + loop_by) % count) for i in range(count)])]
    all_to_all x0 -> x1, blocking collectives: none -> 13.7 us  [local(): pay = lax.all_to_all(pay, ('loop', 'trans'), 0, 0)]
    ppermute x11 -> x8, starting transfers between devices: 23.3 us -> 12.7 us  [the longest x6 9.96 us: shift(): lax.ppermute(x, 'loop', [(i, (i + loop_by) % count) for i in range(count)])]
    pallas_call x4 -> x8, Pallas kernels: 9.82 us -> 12.4 us  [the longest x1 3.67 us: local(): pl.pallas_call(lambda *refs: last_kernel(count, *refs), out_shape=(works(...]
    unnamed x12 -> x10, local copies, waits for them, and re-layouts: 2.55 us -> 0.78 us
  transfers between devices with their start and end apart: 11 -> 8, of which waited for: 7 -> 3; matrix products, arithmetic and copies ran while one was open for 0% -> 0% of each run, Pallas kernels for 5% -> 12%
where the time goes in v2:
time: 48.7 us; the launch traced here: 48.4 us
  blocking collectives  13.7 us (28%)
  starting transfers between devices  12.7 us (26%)
  Pallas kernels  12.4 us (25%)
  waiting for transfers between devices  7.98 us (16%)
  local copies, waits for them, and re-layouts  0.79 us (2%)
  between operations  0.76 us (2%)
    all_to_all x1, blocking collectives, local(): pay = lax.all_to_all(pay, ('loop', 'trans'), 0, 0)  13.7 us
    ppermute x6, starting transfers between devices, shift(): lax.ppermute(x, 'loop', [(i, (i + loop_by) % count) for i in range(count)])  9.96 us
    ppermute x6, waiting for transfers between devices, shift(): lax.ppermute(x, 'loop', [(i, (i + loop_by) % count) for i in range(count)])  4.13 us
    ppermute x2, waiting for transfers between devices, shift(): lax.ppermute(x, 'trans', [(t, t + trans_by) for t in range(count) if 0 <=...  3.85 us
    pallas_call x1, Pallas kernels, local(): pl.pallas_call(lambda *refs: last_kernel(count, *refs), out_shape=(works(...  3.67 us
    pallas_call x1, Pallas kernels, local(): pl.pallas_call(inner_kernel, out_shape=(works(nb), pay_shape), in_specs=[...  2.89 us
    ppermute x2, starting transfers between devices, shift(): lax.ppermute(x, 'trans', [(t, t + trans_by) for t in range(count) if 0 <=...  2.75 us
    pallas_call x1, Pallas kernels, local(): pl.pallas_call(first_kernel, out_shape=(planes(size_a), planes(size_a), p...  2.09 us
  transfers between devices with their start and end apart: 8, of which 3 were waited for; matrix products, arithmetic and copies ran while one was open for 0% of the time, Pallas kernels for 12%

profile of v2, /device:TPU:0, one launch (start us, length us, event | category | flops | bytes accessed | tf_op | source)
XLA Modules:
  0.0 48.4 jit_solution(4401866753675039129)
XLA Ops:
  0.6 0.0 copy-start
  0.6 2.1 %first.1 = (f32[8,64,128]{2,1,0:T(8,128)}, f32[8,64,128]{2,1,0:T(8,128)}, f32[64,128]{1,0:T(8,128)}) custom-call(f32[8,192,128]{2,1,0:T(8,128)} %bitcast.6, s32[64,128]{1,0:T(8,128)} %bitcast.15, f32[4]{0:T(128)} %eps_hbm.1), custom_call_target="tpu_custom_call" | custom-call | tf_op jit(solution)/shard_map/first/pallas_call | solution.py:346
  2.7 3.0 %collective-permute-start.2 = (f32[8,64,128]{2,1,0:T(8,128)}, f32[8,64,128]{2,1,0:T(8,128)S(1)}, u32[]{:S(2)}, u32[]{:S(2)}) collective-permute-start(f32[8,64,128]{2,1,0:T(8,128)} %get-tuple-element.26), channel_id=1, source_target_pairs={{0,8},{8,16},{16,24},{24,0},{1,9},{9,17},{17,25},{25,1},{2,10},{10... | collective-permute-start | bytes 786440 | tf_op jit(solution)/shard_map/ppermute | solution.py:319
  5.7 1.0 %collective-permute-start.3 = (f32[8,64,128]{2,1,0:T(8,128)}, f32[8,64,128]{2,1,0:T(8,128)S(1)}, u32[]{:S(2)}, u32[]{:S(2)}) collective-permute-start(f32[8,64,128]{2,1,0:T(8,128)} %get-tuple-element.27), channel_id=1, source_target_pairs={{0,24},{8,0},{16,8},{24,16},{1,25},{9,1},{17,9},{25,17},{2,26},{10... | collective-permute-start | bytes 786440 | tf_op jit(solution)/shard_map/ppermute | solution.py:319
  6.8 0.0 copy-done
  6.8 0.0 copy-start.1
  6.8 0.8 %copy-done.1 = f32[64,128]{1,0:T(8,128)S(1)} copy-done((f32[64,128]{1,0:T(8,128)S(1)}, f32[64,128]{1,0:T(8,128)}, u32[]{:S(2)}) %copy-start.1) | copy-done | bytes 32792
  7.5 0.5 edges.1
  8.0 1.5 %collective-permute-start = (f32[64,128]{1,0:T(8,128)S(1)}, f32[64,128]{1,0:T(8,128)S(1)}, u32[]{:S(2)}, u32[]{:S(2)}) collective-permute-start(f32[64,128]{1,0:T(8,128)S(1)} %get-tuple-element.22), channel_id=1, source_target_pairs={{0,1},{1,2},{2,3},{3,4},{4,5},{5,6},{6,7},{8,9},{9,10},{10,11},{11... | collective-permute-start | bytes 98312 | tf_op jit(solution)/shard_map/ppermute | solution.py:317
  9.5 1.3 %collective-permute-start.1 = (f32[64,128]{1,0:T(8,128)S(1)}, f32[64,128]{1,0:T(8,128)S(1)}, u32[]{:S(2)}, u32[]{:S(2)}) collective-permute-start(f32[64,128]{1,0:T(8,128)S(1)} %get-tuple-element.23), channel_id=1, source_target_pairs={{1,0},{2,1},{3,2},{4,3},{5,4},{6,5},{7,6},{9,8},{10,9},{11,10},{12... | collective-permute-start | bytes 98312 | tf_op jit(solution)/shard_map/ppermute | solution.py:317
  10.8 0.0 collective-permute-done.fr_ref.refs_2_
  10.8 3.8 %collective-permute-done.1.fl_ref.refs_3_ = f32[64,128]{1,0:T(8,128)S(1)} collective-permute-done((f32[64,128]{1,0:T(8,128)S(1)}, f32[64,128]{1,0:T(8,128)S(1)}, u32[]{:S(2)}, u32[]{:S(2)}) %collective-permute-start.1) | collective-permute-done | bytes 32800 | tf_op jit(solution)/shard_map/ppermute | solution.py:317
  14.6 0.1 pack_b.1
  14.7 0.0 copy-start.3
  14.7 0.6 %collective-permute-start.4 = (f32[5,64,128]{2,1,0:T(8,128)S(1)}, f32[5,64,128]{2,1,0:T(8,128)S(1)}, u32[]{:S(2)}, u32[]{:S(2)}) collective-permute-start(f32[5,64,128]{2,1,0:T(8,128)S(1)} %get-tuple-element.28), channel_id=1, source_target_pairs={{0,8},{8,16},{16,24},{24,0},{1,9},{9,17},{17,25},{25,1},{2,10},{10... | collective-permute-start | bytes 491528 | tf_op jit(solution)/shard_map/ppermute | solution.py:319
  15.4 0.0 copy-start.2
  15.4 2.3 %collective-permute-start.5 = (f32[5,64,128]{2,1,0:T(8,128)S(1)}, f32[5,64,128]{2,1,0:T(8,128)S(1)}, u32[]{:S(2)}, u32[]{:S(2)}) collective-permute-start(f32[5,64,128]{2,1,0:T(8,128)S(1)} %get-tuple-element.29), channel_id=1, source_target_pairs={{0,24},{8,0},{16,8},{24,16},{1,25},{9,1},{17,9},{25,17},{2,26},{10... | collective-permute-start | bytes 491528 | tf_op jit(solution)/shard_map/ppermute | solution.py:319
  17.7 0.0 collective-permute-done.2.refs_4_.refs_2_
  17.7 1.4 %collective-permute-done.3.refs_5_.refs_3_ = f32[8,64,128]{2,1,0:T(8,128)S(1)} collective-permute-done((f32[8,64,128]{2,1,0:T(8,128)}, f32[8,64,128]{2,1,0:T(8,128)S(1)}, u32[]{:S(2)}, u32[]{:S(2)}) %collective-permute-start.3) | collective-permute-done | bytes 262176 | tf_op jit(solution)/shard_map/ppermute | solution.py:319
  19.1 0.1 pack_c.1
  19.2 0.0 copy-start.4
  19.2 1.5 %collective-permute-start.6 = (f32[4,64,128]{2,1,0:T(8,128)S(1)}, f32[4,64,128]{2,1,0:T(8,128)S(1)}, u32[]{:S(2)}, u32[]{:S(2)}) collective-permute-start(f32[4,64,128]{2,1,0:T(8,128)S(1)} %get-tuple-element.31), channel_id=1, source_target_pairs={{0,8},{8,16},{16,24},{24,0},{1,9},{9,17},{17,25},{25,1},{2,10},{10... | collective-permute-start | bytes 393224 | tf_op jit(solution)/shard_map/ppermute | solution.py:319
  20.7 1.4 %collective-permute-start.7 = (f32[4,64,128]{2,1,0:T(8,128)S(1)}, f32[4,64,128]{2,1,0:T(8,128)S(1)}, u32[]{:S(2)}, u32[]{:S(2)}) collective-permute-start(f32[4,64,128]{2,1,0:T(8,128)S(1)} %get-tuple-element.32), channel_id=1, source_target_pairs={{0,24},{8,0},{16,8},{24,16},{1,25},{9,1},{17,9},{25,17},{2,26},{10... | collective-permute-start | bytes 393224 | tf_op jit(solution)/shard_map/ppermute | solution.py:319
  22.2 0.0 copy-done.3
  22.2 0.0 copy-done.2
  22.2 0.0 copy-done.4
  22.2 2.9 %inner.1 = (f32[8,192,128]{2,1,0:T(8,128)S(1)}, f32[2,128]{1,0:T(2,128)S(1)}) custom-call(f32[8,8]{1,0:T(8,128)S(1)} %copy-done.4, f32[8,192,128]{2,1,0:T(8,128)S(1)} %bitcast.10, f32[64,128]{1,0:T(8,128)S(1)} %copy-done.2, f32[8,192,128]{2,1,0:T(8,128)S(1)} %bitcast.14, f32[64,128]{1,0:T(8,128)S(1)} %collective-permute-done.fr_ref.refs_2_, ...), custom_call_target="tpu_custom_call" | custom-call | tf_op jit(solution)/shard_map/inner/pallas_call | solution.py:392
  25.1 0.0 collective-permute-done.4.refs_6_.refs_8_
  25.1 0.0 collective-permute-done.5.refs_7_.refs_9_
  25.1 2.1 %products.1 = (f32[6,192,128]{2,1,0:T(8,128)S(1)}, f32[2,128]{1,0:T(2,128)S(1)}) custom-call(f32[8,192,128]{2,1,0:T(8,128)S(1)} %bitcast.11, f32[64,128]{1,0:T(8,128)S(1)} %copy-done.2, f32[8,192,128]{2,1,0:T(8,128)S(1)} %get-tuple-element.24.refs_2_, f32[2,128]{1,0:T(2,128)S(1)} %get-tuple-element.25.refs_3_, ...), custom_call_target="tpu_custom_call" | custom-call | tf_op jit(solution)/shard_map/products/pallas_call | solution.py:401
  27.1 0.0 collective-permute-done.6.refs_4_
  27.2 2.7 %collective-permute-done.7.refs_5_ = f32[4,64,128]{2,1,0:T(8,128)S(1)} collective-permute-done((f32[4,64,128]{2,1,0:T(8,128)S(1)}, f32[4,64,128]{2,1,0:T(8,128)S(1)}, u32[]{:S(2)}, u32[]{:S(2)}) %collective-permute-start.7) | collective-permute-done | bytes 131104 | tf_op jit(solution)/shard_map/ppermute | solution.py:319
  29.9 1.1 %products_last.1 = (f32[2,192,128]{2,1,0:T(8,128)S(1)}, f32[2,128]{1,0:T(2,128)S(1)}) custom-call(f32[8,192,128]{2,1,0:T(8,128)S(1)} %bitcast.12, f32[64,128]{1,0:T(8,128)S(1)} %copy-done.2, f32[8,192,128]{2,1,0:T(8,128)S(1)} %get-tuple-element.24.refs_2_, f32[2,128]{1,0:T(2,128)S(1)} %get-tuple-element.30.refs_3_, ...), custom_call_target="tpu_custom_call" | custom-call | tf_op jit(solution)/shard_map/products_last/pallas_call | solution.py:410
  31.0 13.7 %all_to_all.5.refs_0_ = f32[32,2,128]{2,1,0:T(2,128)S(1)} all-to-all(f32[32,2,128]{2,1,0:T(2,128)S(1)} %broadcast_in_dim.2), channel_id=1, replica_groups=mesh['loop'=4,'trans'=8] {'loop','trans'}, dimensions={0} | all-to-all | bytes 65536 | tf_op jit(solution)/shard_map/all_to_all | solution.py:420
  44.8 3.7 %combine.1 = (f32[8,192,128]{2,1,0:T(8,128)}, f32[8,8]{1,0:T(8,128)}, f32[8,8]{1,0:T(8,128)}) custom-call(f32[32,2,128]{2,1,0:T(2,128)S(1)} %all_to_all.5.refs_0_, f32[8,192,128]{2,1,0:T(8,128)S(1)} %bitcast.13, f32[6,192,128]{2,1,0:T(8,128)S(1)} %get-tuple-element.33.refs_8_.refs_2_, f32[2,192,128]{2,1,0:T(8,128)S(1)} %get-tuple-element.35.refs_3_), custom_call_target="tpu_custom_call" | custom-call | tf_op jit(solution)/shard_map/combine/pallas_call | solution.py:422
  (1 shorter events, 0.0 us)
Async XLA Ops:
  0.6 6.1 %copy-start = (f32[8,3,64,1,128]{4,3,2,1,0:T(1,128)S(1)}, f32[8,3,64,1,128]{4,3,2,1,0:T(1,128)}, u32[]{:S(2)}) copy-start(f32[8,3,64,1,128]{4,3,2,1,0:T(1,128)} %param.5) | copy-start | bytes 2359300
  2.7 15.0 %collective-permute-start.2 = (f32[8,64,128]{2,1,0:T(8,128)}, f32[8,64,128]{2,1,0:T(8,128)S(1)}, u32[]{:S(2)}, u32[]{:S(2)}) collective-permute-start(f32[8,64,128]{2,1,0:T(8,128)} %get-tuple-element.26), channel_id=1, source_target_pairs={{0,8},{8,16},{16,24},{24,0},{1,9},{9,17},{17,25},{25,1},{2,10},{10... | collective-permute-start | bytes 786440 | tf_op jit(solution)/shard_map/ppermute | solution.py:319
  5.7 13.3 %collective-permute-start.3 = (f32[8,64,128]{2,1,0:T(8,128)}, f32[8,64,128]{2,1,0:T(8,128)S(1)}, u32[]{:S(2)}, u32[]{:S(2)}) collective-permute-start(f32[8,64,128]{2,1,0:T(8,128)} %get-tuple-element.27), channel_id=1, source_target_pairs={{0,24},{8,0},{16,8},{24,16},{1,25},{9,1},{17,9},{25,17},{2,26},{10... | collective-permute-start | bytes 786440 | tf_op jit(solution)/shard_map/ppermute | solution.py:319
  6.8 0.8 %copy-start.1 = (f32[64,128]{1,0:T(8,128)S(1)}, f32[64,128]{1,0:T(8,128)}, u32[]{:S(2)}) copy-start(f32[64,128]{1,0:T(8,128)} %get-tuple-element.21.scale_ref.refs_1_) | copy-start | bytes 98308
  8.0 2.8 %collective-permute-start = (f32[64,128]{1,0:T(8,128)S(1)}, f32[64,128]{1,0:T(8,128)S(1)}, u32[]{:S(2)}, u32[]{:S(2)}) collective-permute-start(f32[64,128]{1,0:T(8,128)S(1)} %get-tuple-element.22), channel_id=1, source_target_pairs={{0,1},{1,2},{2,3},{3,4},{4,5},{5,6},{6,7},{8,9},{9,10},{10,11},{11... | collective-permute-start | bytes 98312 | tf_op jit(solution)/shard_map/ppermute | solution.py:317
  9.5 5.2 %collective-permute-start.1 = (f32[64,128]{1,0:T(8,128)S(1)}, f32[64,128]{1,0:T(8,128)S(1)}, u32[]{:S(2)}, u32[]{:S(2)}) collective-permute-start(f32[64,128]{1,0:T(8,128)S(1)} %get-tuple-element.23), channel_id=1, source_target_pairs={{1,0},{2,1},{3,2},{4,3},{5,4},{6,5},{7,6},{9,8},{10,9},{11,10},{12... | collective-permute-start | bytes 98312 | tf_op jit(solution)/shard_map/ppermute | solution.py:317
  14.7 7.5 %copy-start.3 = (f32[8,3,64,1,128]{4,3,2,1,0:T(1,128)S(1)}, f32[8,3,64,1,128]{4,3,2,1,0:T(1,128)}, u32[]{:S(2)}) copy-start(f32[8,3,64,1,128]{4,3,2,1,0:T(1,128)} %param.6) | copy-start | bytes 2359300
  14.7 10.3 %collective-permute-start.4 = (f32[5,64,128]{2,1,0:T(8,128)S(1)}, f32[5,64,128]{2,1,0:T(8,128)S(1)}, u32[]{:S(2)}, u32[]{:S(2)}) collective-permute-start(f32[5,64,128]{2,1,0:T(8,128)S(1)} %get-tuple-element.28), channel_id=1, source_target_pairs={{0,8},{8,16},{16,24},{24,0},{1,9},{9,17},{17,25},{25,1},{2,10},{10... | collective-permute-start | bytes 491528 | tf_op jit(solution)/shard_map/ppermute | solution.py:319
  15.4 6.8 %copy-start.2 = (f32[64,128]{1,0:T(8,128)S(1)}, f32[64,128]{1,0:T(8,128)}, u32[]{:S(2)}) copy-start(f32[64,128]{1,0:T(8,128)} %get-tuple-element.21.scale_ref.refs_1_) | copy-start | bytes 98308
  15.4 9.7 %collective-permute-start.5 = (f32[5,64,128]{2,1,0:T(8,128)S(1)}, f32[5,64,128]{2,1,0:T(8,128)S(1)}, u32[]{:S(2)}, u32[]{:S(2)}) collective-permute-start(f32[5,64,128]{2,1,0:T(8,128)S(1)} %get-tuple-element.29), channel_id=1, source_target_pairs={{0,24},{8,0},{16,8},{24,16},{1,25},{9,1},{17,9},{25,17},{2,26},{10... | collective-permute-start | bytes 491528 | tf_op jit(solution)/shard_map/ppermute | solution.py:319
  19.2 3.0 %copy-start.4 = (f32[8,8]{1,0:T(8,128)S(1)}, f32[8,8]{1,0:T(8,128)}, u32[]{:S(2)}) copy-start(f32[8,8]{1,0:T(8,128)} %coup_ref.1) | copy-start | bytes 772
  19.2 8.0 %collective-permute-start.6 = (f32[4,64,128]{2,1,0:T(8,128)S(1)}, f32[4,64,128]{2,1,0:T(8,128)S(1)}, u32[]{:S(2)}, u32[]{:S(2)}) collective-permute-start(f32[4,64,128]{2,1,0:T(8,128)S(1)} %get-tuple-element.31), channel_id=1, source_target_pairs={{0,8},{8,16},{16,24},{24,0},{1,9},{9,17},{17,25},{25,1},{2,10},{10... | collective-permute-start | bytes 393224 | tf_op jit(solution)/shard_map/ppermute | solution.py:319
  20.7 9.2 %collective-permute-start.7 = (f32[4,64,128]{2,1,0:T(8,128)S(1)}, f32[4,64,128]{2,1,0:T(8,128)S(1)}, u32[]{:S(2)}, u32[]{:S(2)}) collective-permute-start(f32[4,64,128]{2,1,0:T(8,128)S(1)} %get-tuple-element.32), channel_id=1, source_target_pairs={{0,24},{8,0},{16,8},{24,16},{1,25},{9,1},{17,9},{25,17},{2,26},{10... | collective-permute-start | bytes 393224 | tf_op jit(solution)/shard_map/ppermute | solution.py:319

commit v3 on v2

--- a/solution.py
+++ b/solution.py
@@ -44,10 +44,11 @@
     uz = v_ref[b, pl.ds(0, nz), :] * scale
     up = v_ref[b, pl.ds(nz, nz), :] * scale
     ut = v_ref[b, pl.ds(2 * nz, nz), :] * scale
-    bwd_ref[at] = uz
-    bwd_ref[at + 1] = ut
-    fwd_ref[at] = uz + (z_next(up) - up)
-    fwd_ref[at + 1] = ut + (jnp.where(lane == last, 0.0, roll_by(up, -1, 1)) - up)
+    one, two = pl.ds(at * nz, nz), pl.ds((at + 1) * nz, nz)
+    bwd_ref[one, :] = uz
+    bwd_ref[two, :] = ut
+    fwd_ref[one, :] = uz + (z_next(up) - up)
+    fwd_ref[two, :] = ut + (jnp.where(lane == last, 0.0, roll_by(up, -1, 1)) - up)
 
 
 def first_kernel(v_hbm, mat_hbm, eps_hbm, fwd_ref, bwd_ref, scale_ref, v_ref, mat_ref, eps_ref, sems):
@@ -78,19 +79,26 @@
     for b in range(v_ref.shape[0]):
         for c in range(3):
             u = v_ref[b, pl.ds(c * nz, nz), :] * scale
-            spot = 3 * b + c
+            spot = v_ref.shape[0] * c + b
             right = jnp.where(lane == spot, roll_by(u, spot + 1, 1), right)
             left = jnp.where(lane == spot, roll_by(u, spot, 1), left)
     right_ref[...] = right
     left_ref[...] = left
 
 
+def turned(x):
+    pad = jnp.zeros((x.shape[1] - x.shape[0], x.shape[1]), x.dtype)
+    return jnp.concatenate([x, pad], axis=0).T
+
+
 def corner_kernel(begin, end, v_ref, scale_ref, fr_ref, fl_ref, fwd_ref, bwd_ref):
     scale = scale_ref[...]
     for b in range(begin, end):
         packed(v_ref, b, scale, fwd_ref, bwd_ref, 2 * (b - begin))
-    fwd_ref[2 * (end - begin)] = fl_ref[...]
-    bwd_ref[2 * (end - begin)] = fr_ref[...]
+    nb = v_ref.shape[0]
+    rows = pl.ds(2 * (end - begin) * scale.shape[0], nb)
+    fwd_ref[rows, :] = turned(fl_ref[...])[nb : 2 * nb, :]
+    bwd_ref[rows, :] = turned(fr_ref[...])[2 * nb : 3 * nb, :]
 
 
 def more_kernel(begin, end, v_ref, scale_ref, fwd_a_ref, bwd_a_ref, fwd_ref, bwd_ref):
@@ -99,38 +107,59 @@
         packed(v_ref, b, scale, fwd_ref, bwd_ref, 2 * (b - begin))
 
 
-def gram_sums(pairs, lefts, rights, steps, group):
-    out = []
+def merge(a, b, dist):
+    low = (row_ids(a.shape) & dist) == 0
+    other = jnp.where(low, b, a)
+    swapped = roll_by(other, dist, 0)
+    if 2 * dist != a.shape[0]:
+        swapped = jnp.where(low, roll_by(other, -dist, 0), swapped)
+    return jnp.where(low, a, b) + swapped
+
+
+def add_products(pairs, steps, group, pays, unroll=1):
+    shape = pays[0].shape
+    lane, row = lane_ids(shape), row_ids(shape)
+    zero = jnp.zeros(shape, jnp.float32)
     for first in range(0, len(pairs), group):
         part = pairs[first : first + group]
 
         def body(r, accs):
             rows = pl.ds(pl.multiple_of(r * 8, 8), 8)
-            load = lambda side, i: side[i][0][side[i][1], rows, :]
-            ls = {j: load(lefts, j) for j in sorted({p[0] for p in part})}
-            if lefts is rights:
-                rs = {b: ls[b] if b in ls else load(rights, b) for b in sorted({p[1] for p in part})}
-            else:
-                rs = {b: load(rights, b) for b in sorted({p[1] for p in part})}
-            return tuple(acc + ls[j] * rs[b] for acc, (j, b) in zip(accs, part))
-
-        zero = jnp.zeros((8, lefts[0][0].shape[2]), jnp.float32)
-        out.extend(lax.fori_loop(0, steps, body, tuple(zero for _ in part)))
-    return out
-
-
-def put(rows, acc, spots):
-    total = jnp.sum(jnp.sum(acc, axis=0, keepdims=True), axis=1, keepdims=True)
-    lane = lane_ids(rows[0].shape)
-    rows = list(rows)
-    for row in {s[0] for s in spots}:
-        hit = None
-        for spot in spots:
-            if spot[0] == row:
-                here = lane == spot[1]
-                hit = here if hit is None else hit | here
-        rows[row] = jnp.where(hit, total, rows[row])
-    return rows
+            got = {}
+            for left, j, right, b, _ in part:
+                for ref, i in ((left, j), (right, b)):
+                    if (id(ref), i) not in got:
+                        got[(id(ref), i)] = ref[i, rows, :]
+            return tuple(
+                acc + got[(id(left), j)] * got[(id(right), b)]
+                for acc, (left, j, right, b, _) in zip(accs, part)
+            )
+
+        accs = list(lax.fori_loop(0, steps, body, tuple(zero for _ in part), unroll=unroll))
+        for at in range(0, len(part), 8):
+            eight = accs[at : at + 8]
+            eight = eight + [zero] * (8 - len(eight))
+            four = [merge(eight[i], eight[i + 4], 4) for i in range(4)]
+            two = [merge(four[i], four[i + 2], 2) for i in range(2)]
+            sums = jnp.sum(merge(two[0], two[1], 1), axis=1, keepdims=True)
+            for line in range(len(pays)):
+                hit = None
+                for i, pair in enumerate(part[at : at + 8]):
+                    for spot in sorted(pair[4]):
+                        if spot[0] == line:
+                            here = (row == i) & (lane == spot[1])
+                            hit = here if hit is None else hit | here
+                if hit is not None:
+                    pays[line] = pays[line] + jnp.where(hit, sums, 0.0)
+    return pays
+
+
+def store_pays(pay_ref, pays, before=None):
+    for line, pay in enumerate(pays):
+        total = jnp.sum(pay, axis=0, keepdims=True)
+        if before is not None:
+            total = total + before[line : line + 1, :]
+        pay_ref[line : line + 1, :] = total
 
 
 def inner_kernel(coup_ref, v_ref, scale_ref, q_ref, fr_ref, fl_ref, l_ref, pay_ref):
@@ -146,11 +175,11 @@
         ut = v_ref[b, pl.ds(2 * nz, nz), :] * scale
 
         def prev(u, c):
-            edge = pltpu.roll(fr_ref[...], (last + 1 - (3 * b + c)) % (last + 1), 1)
+            edge = pltpu.roll(fr_ref[...], (last + 1 - (nb * c + b)) % (last + 1), 1)
             return jnp.where(lane == 0, edge, roll_by(u, 1, 1))
 
         def nxt(u, c):
-            edge = pltpu.roll(fl_ref[...], last - (3 * b + c), 1)
+            edge = pltpu.roll(fl_ref[...], last - (nb * c + b), 1)
             return jnp.where(lane == last, edge, roll_by(u, -1, 1))
 
         dt_ut = ut - prev(ut, 2)
@@ -171,14 +200,9 @@
         return carry
 
     lax.fori_loop(0, nb, body, 0)
-    pairs = [(j, b) for b in range(nb) for j in range(b + 1)]
-    side = [(v_ref, j) for j in range(nb)]
-    row = jnp.zeros((1, v_ref.shape[2]), jnp.float32)
-    rows = [row, row]
-    for (j, b), acc in zip(pairs, gram_sums(pairs, side, side, v_ref.shape[1] // 8, 36)):
-        rows = put(rows, acc, {(1, nb * j + b), (1, nb * b + j)})
-    pay_ref[0:1, :] = rows[0]
-    pay_ref[1:2, :] = rows[1]
+    zero = jnp.zeros((8, v_ref.shape[2]), jnp.float32)
+    pairs = [(v_ref, j, v_ref, b, {(1, nb * j + b), (1, nb * b + j)}) for b in range(nb) for j in range(b + 1)]
+    store_pays(pay_ref, add_products(pairs, v_ref.shape[1] // 8, 36, [zero, zero]))
 
 
 def sum_kernel(cuts, begin, v_ref, scale_ref, l_ref, pay_in_ref, *refs):
@@ -191,18 +215,18 @@
     old, (w_ref, pay_ref) = rest[:-2], rest[-2:]
     scale = scale_ref[...]
     lane = lane_ids(scale.shape)
-    plane_f, plane_b = corner_f.shape[0] - 1, corner_b.shape[0] - 1
+    columns_f = turned(corner_f[pl.ds(corner_f.shape[0] - nb, nb), :])[:nz, :]
+    columns_b = turned(corner_b[pl.ds(corner_b.shape[0] - nb, nb), :])[:nz, :]
     for i, (low, high) in enumerate(cuts):
         fwd_ref, bwd_ref = halos[2 * i : 2 * i + 2]
 
-        def body(m, carry):
+        for m in range(high - low):
             b = low + m
-            za = fwd_ref[2 * m]
-            tb = fwd_ref[2 * m + 1]
-            uz = bwd_ref[2 * m]
-            ut = bwd_ref[2 * m + 1]
-            edge_b = pltpu.roll(corner_b[plane_b], (nt - (3 * b + 2)) % nt, 1)
-            edge_f = pltpu.roll(corner_f[plane_f], nt - 1 - (3 * b + 1), 1)
+            one, two = pl.ds(2 * m * nz, nz), pl.ds((2 * m + 1) * nz, nz)
+            za, tb = fwd_ref[one, :], fwd_ref[two, :]
+            uz, ut = bwd_ref[one, :], bwd_ref[two, :]
+            edge_b = roll_by(columns_b, -b, 1)
+            edge_f = roll_by(columns_f, nt - 1 - b, 1)
             ut_prev = jnp.where(lane == 0, edge_b, roll_by(ut, 1, 1))
             tb = tb + jnp.where(lane == nt - 1, edge_f, 0.0)
             to = b - begin
@@ -210,22 +234,14 @@
             div = (uz - z_prev(uz)) + (ut - ut_prev)
             w_ref[to, pl.ds(nz, nz), :] = l_ref[b, pl.ds(nz, nz), :] + scale * div
             w_ref[to, pl.ds(2 * nz, nz), :] = l_ref[b, pl.ds(2 * nz, nz), :] - scale * (tb + ut)
-            return carry
-
-        lax.fori_loop(0, high - low, body, 0)
-    steps = v_ref.shape[1] // 8
-    vs = [(v_ref, j) for j in range(nb)]
+
     ws = [(old[0], b) for b in range(begin)] + [(w_ref, b - begin) for b in range(begin, end)]
-    rows = [pay_in_ref[0:1, :], pay_in_ref[1:2, :]]
-    for j0 in range(0, nb, nb // 2):
-        pairs = [(j, b) for b in range(begin, end) for j in range(j0, j0 + nb // 2)]
-        for (j, b), acc in zip(pairs, gram_sums(pairs, vs, ws, steps, 32)):
-            rows = put(rows, acc, {(0, nb * j + b), (1, nb * nb + nb * b + j)})
-    pairs = [(j, b) for b in range(begin, end) for j in range(b + 1)]
-    for (j, b), acc in zip(pairs, gram_sums(pairs, ws, ws, steps, 36)):
-        rows = put(rows, acc, {(0, nb * nb + nb * j + b), (0, nb * nb + nb * b + j)})
-    pay_ref[0:1, :] = rows[0]
-    pay_ref[1:2, :] = rows[1]
+    pairs = []
+    for b in range(begin, end):
+        pairs += [(v_ref, j, *ws[b], {(0, nb * j + b), (1, nb * nb + nb * b + j)}) for j in range(nb)]
+        pairs += [(*ws[j], *ws[b], {(0, nb * nb + nb * j + b), (0, nb * nb + nb * b + j)}) for j in range(b + 1)]
+    zero = jnp.zeros((8, nt), jnp.float32)
+    store_pays(pay_ref, add_products(pairs, v_ref.shape[1] // 8, 36, [zero, zero]), pay_in_ref)
 
 
 def lane_at(x, k):
@@ -266,26 +282,34 @@
     for k in range(nb):
         quad = quad + lane_at(alpha_t, k) * row_at(half, k)
     gram = ((ww - cross) + (quad - cross)) / count
+    ws = [(w, i) for w in w_refs for i in range(w.shape[0])]
+    for j in range(nb):
+        coef_ref[j] = lane_at(alpha_t, j)
+    blocks = v_ref.shape[1] // 8
     mat = jnp.where(lane < nb, gram, jnp.where(lane - nb == row, 1.0, 0.0))
     fact = jnp.zeros_like(proj)
     for k in range(nb):
         line = row_at(mat, k)
-        root = 1.0 / jnp.sqrt(lane_at(line, k))
+        root = lane_at(line, k)
+        root = 1.0 / jnp.sqrt(root)
         line = line * root
         fact = jnp.where(row == k, line, fact)
         if k < nb - 1:
             mat = mat - (lane_at(mat, k) * root) * line
+        for r in range(k * blocks // nb, (k + 1) * blocks // nb):
+            rows = pl.ds(8 * r, 8)
+            vs = [v_ref[j, rows, :] for j in range(nb)]
+            for b, (w_ref, i) in enumerate(ws):
+                acc = w_ref[i, rows, :]
+                for j in range(nb):
+                    acc = acc - coef_ref[j, pl.ds(b, 1), :] * vs[j]
+                out_ref[b, rows, :] = acc
     inv = roll_by(fact, -nb, 1)
     alpha_ref[...] = alpha[:, :nb]
     beta_ref[...] = jnp.where(lane >= row, fact, 0.0)[:, :nb]
-    mix = jnp.zeros_like(proj)
     for j in range(nb):
-        mix = mix + lane_at(inv, j) * row_at(alpha_t, j)
-    for j in range(nb):
-        coef_ref[j] = lane_at(inv, j)
-        coef_ref[nb + j] = -lane_at(mix, j)
+        coef_ref[nb + j] = lane_at(inv, j)
     step = 16
-    ws = [(w, i) for w in w_refs for i in range(w.shape[0])]
     pieces = sems.shape[0]
     length = v_ref.shape[1] // pieces
     copies = []
@@ -294,11 +318,11 @@
 
         def body(r, carry):
             rows = pl.ds(pl.multiple_of(base + r * step, step), step)
-            xs = [ref[i, rows, :] for ref, i in ws] + [v_ref[j, rows, :] for j in range(nb)]
+            xs = [out_ref[j, rows, :] for j in range(nb)]
             for b in range(nb):
-                acc = coef_ref[0, pl.ds(b, 1), :] * xs[0]
-                for j in range(1, 2 * nb):
-                    acc = acc + coef_ref[j, pl.ds(b, 1), :] * xs[j]
+                acc = coef_ref[nb, pl.ds(b, 1), :] * xs[0]
+                for j in range(1, b + 1):
+                    acc = acc + coef_ref[nb + j, pl.ds(b, 1), :] * xs[j]
                 out_ref[b, rows, :] = acc
             return carry
 
@@ -336,8 +360,8 @@
     pay_shape = jax.ShapeDtypeStruct((2, nt), f32)
     cut_a, cut_b, cut_c = (0, nb // 2), (nb // 2, nb * 3 // 4), (nb * 3 // 4, nb)
 
-    def planes(n):
-        return jax.ShapeDtypeStruct((n, nz, nt), f32)
+    def planes(n, more=0):
+        return jax.ShapeDtypeStruct((n * nz + more, nt), f32)
 
     def works(n):
         return jax.ShapeDtypeStruct((n, nc * nz, nt), f32)
@@ -371,7 +395,7 @@
     from_left, from_right = shift(right, 0, 1), shift(left, 0, -1)
     fwd_b, bwd_b = pl.pallas_call(
         lambda *refs: corner_kernel(*cut_b, *refs),
-        out_shape=(planes(size_b + 1), planes(size_b + 1)),
+        out_shape=(planes(size_b, nb), planes(size_b, nb)),
         in_specs=[vm] * 4,
         out_specs=(vm, vm),
         compiler_params=params,

time: 48.7 us -> 47.1 us (0.967)
  Pallas kernels: 12.4 us -> 11.6 us
  waiting for transfers between devices: 7.98 us -> 7.3 us
    ppermute x6, waiting for transfers between devices: 4.13 us -> 3.45 us  [shift(): lax.ppermute(x, 'loop', [(i, (i + loop_by) % count) for i in range(count)])]
  transfers between devices with their start and end apart: 8 -> 8, of which waited for: 3 -> 3; matrix products, arithmetic and copies ran while one was open for 0% -> 0% of each run, Pallas kernels for 12% -> 11%
where the time goes in v3:
time: 47.1 us; the launch traced here: 46.9 us
  blocking collectives  13.7 us (29%)
  starting transfers between devices  12.7 us (27%)
  Pallas kernels  11.6 us (25%)
  waiting for transfers between devices  7.3 us (15%)
  local copies, waits for them, and re-layouts  0.79 us (2%)
  between operations  0.73 us (2%)
    all_to_all x1, blocking collectives, local(): pay = lax.all_to_all(pay, ('loop', 'trans'), 0, 0)  13.7 us
    ppermute x6, starting transfers between devices, shift(): lax.ppermute(x, 'loop', [(i, (i + loop_by) % count) for i in range(count)])  9.96 us
    ppermute x2, waiting for transfers between devices, shift(): lax.ppermute(x, 'trans', [(t, t + trans_by) for t in range(count) if 0 <=...  3.85 us
    pallas_call x1, Pallas kernels, local(): pl.pallas_call(lambda *refs: last_kernel(count, *refs), out_shape=(works(...  3.59 us
    ppermute x6, waiting for transfers between devices, shift(): lax.ppermute(x, 'loop', [(i, (i + loop_by) % count) for i in range(count)])  3.45 us
    pallas_call x1, Pallas kernels, local(): pl.pallas_call(inner_kernel, out_shape=(works(nb), pay_shape), in_specs=[...  2.82 us
    ppermute x2, starting transfers between devices, shift(): lax.ppermute(x, 'trans', [(t, t + trans_by) for t in range(count) if 0 <=...  2.75 us
    pallas_call x1, Pallas kernels, local(): pl.pallas_call(first_kernel, out_shape=(planes(size_a), planes(size_a), p...  2.09 us
  transfers between devices with their start and end apart: 8, of which 3 were waited for; matrix products, arithmetic and copies ran while one was open for 0% of the time, Pallas kernels for 11%

profile of v3, /device:TPU:0, one launch (start us, length us, event | category | flops | bytes accessed | tf_op | source)
XLA Modules:
  0.0 46.9 jit_solution(5627160898612098596)
XLA Ops:
  0.6 0.0 copy-start
  0.6 2.1 %first.1 = (f32[512,128]{1,0:T(8,128)}, f32[512,128]{1,0:T(8,128)}, f32[64,128]{1,0:T(8,128)}) custom-call(f32[8,192,128]{2,1,0:T(8,128)} %bitcast.6, s32[64,128]{1,0:T(8,128)} %bitcast.15, f32[4]{0:T(128)} %eps_hbm.1), custom_call_target="tpu_custom_call" | custom-call | tf_op jit(solution)/shard_map/first/pallas_call | solution.py:370
  2.7 3.0 %collective-permute-start.2 = (f32[512,128]{1,0:T(8,128)}, f32[512,128]{1,0:T(8,128)S(1)}, u32[]{:S(2)}, u32[]{:S(2)}) collective-permute-start(f32[512,128]{1,0:T(8,128)} %get-tuple-element.26), channel_id=1, source_target_pairs={{0,8},{8,16},{16,24},{24,0},{1,9},{9,17},{17,25},{25,1},{2,10},{10... | collective-permute-start | bytes 786440 | tf_op jit(solution)/shard_map/ppermute | solution.py:343
  5.7 1.0 %collective-permute-start.3 = (f32[512,128]{1,0:T(8,128)}, f32[512,128]{1,0:T(8,128)S(1)}, u32[]{:S(2)}, u32[]{:S(2)}) collective-permute-start(f32[512,128]{1,0:T(8,128)} %get-tuple-element.27), channel_id=1, source_target_pairs={{0,24},{8,0},{16,8},{24,16},{1,25},{9,1},{17,9},{25,17},{2,26},{10... | collective-permute-start | bytes 786440 | tf_op jit(solution)/shard_map/ppermute | solution.py:343
  6.8 0.0 copy-done
  6.8 0.0 copy-start.1
  6.8 0.8 %copy-done.1 = f32[64,128]{1,0:T(8,128)S(1)} copy-done((f32[64,128]{1,0:T(8,128)S(1)}, f32[64,128]{1,0:T(8,128)}, u32[]{:S(2)}) %copy-start.1) | copy-done | bytes 32792
  7.5 0.5 edges.1
  8.0 1.5 %collective-permute-start = (f32[64,128]{1,0:T(8,128)S(1)}, f32[64,128]{1,0:T(8,128)S(1)}, u32[]{:S(2)}, u32[]{:S(2)}) collective-permute-start(f32[64,128]{1,0:T(8,128)S(1)} %get-tuple-element.22), channel_id=1, source_target_pairs={{0,1},{1,2},{2,3},{3,4},{4,5},{5,6},{6,7},{8,9},{9,10},{10,11},{11... | collective-permute-start | bytes 98312 | tf_op jit(solution)/shard_map/ppermute | solution.py:341
  9.5 1.3 %collective-permute-start.1 = (f32[64,128]{1,0:T(8,128)S(1)}, f32[64,128]{1,0:T(8,128)S(1)}, u32[]{:S(2)}, u32[]{:S(2)}) collective-permute-start(f32[64,128]{1,0:T(8,128)S(1)} %get-tuple-element.23), channel_id=1, source_target_pairs={{1,0},{2,1},{3,2},{4,3},{5,4},{6,5},{7,6},{9,8},{10,9},{11,10},{12... | collective-permute-start | bytes 98312 | tf_op jit(solution)/shard_map/ppermute | solution.py:341
  10.8 0.0 collective-permute-done.fr_ref.refs_2_
  10.8 3.8 %collective-permute-done.1.fl_ref.refs_3_ = f32[64,128]{1,0:T(8,128)S(1)} collective-permute-done((f32[64,128]{1,0:T(8,128)S(1)}, f32[64,128]{1,0:T(8,128)S(1)}, u32[]{:S(2)}, u32[]{:S(2)}) %collective-permute-start.1) | collective-permute-done | bytes 32800 | tf_op jit(solution)/shard_map/ppermute | solution.py:341
  14.6 0.1 pack_b.1
  14.7 0.0 copy-start.3
  14.7 0.6 %collective-permute-start.4 = (f32[264,128]{1,0:T(8,128)S(1)}, f32[264,128]{1,0:T(8,128)S(1)}, u32[]{:S(2)}, u32[]{:S(2)}) collective-permute-start(f32[264,128]{1,0:T(8,128)S(1)} %get-tuple-element.28), channel_id=1, source_target_pairs={{0,8},{8,16},{16,24},{24,0},{1,9},{9,17},{17,25},{25,1},{2,10},{10... | collective-permute-start | bytes 405512 | tf_op jit(solution)/shard_map/ppermute | solution.py:343
  15.4 0.0 copy-start.2
  15.4 2.3 %collective-permute-start.5 = (f32[264,128]{1,0:T(8,128)S(1)}, f32[264,128]{1,0:T(8,128)S(1)}, u32[]{:S(2)}, u32[]{:S(2)}) collective-permute-start(f32[264,128]{1,0:T(8,128)S(1)} %get-tuple-element.29), channel_id=1, source_target_pairs={{0,24},{8,0},{16,8},{24,16},{1,25},{9,1},{17,9},{25,17},{2,26},{10... | collective-permute-start | bytes 405512 | tf_op jit(solution)/shard_map/ppermute | solution.py:343
  17.7 0.0 collective-permute-done.2.refs_4_.refs_2_
  17.7 1.4 %collective-permute-done.3.refs_5_.refs_3_ = f32[512,128]{1,0:T(8,128)S(1)} collective-permute-done((f32[512,128]{1,0:T(8,128)}, f32[512,128]{1,0:T(8,128)S(1)}, u32[]{:S(2)}, u32[]{:S(2)}) %collective-permute-start.3) | collective-permute-done | bytes 262176 | tf_op jit(solution)/shard_map/ppermute | solution.py:343
  19.1 0.1 pack_c.1
  19.2 0.0 copy-start.4
  19.2 1.5 %collective-permute-start.6 = (f32[256,128]{1,0:T(8,128)S(1)}, f32[256,128]{1,0:T(8,128)S(1)}, u32[]{:S(2)}, u32[]{:S(2)}) collective-permute-start(f32[256,128]{1,0:T(8,128)S(1)} %get-tuple-element.31), channel_id=1, source_target_pairs={{0,8},{8,16},{16,24},{24,0},{1,9},{9,17},{17,25},{25,1},{2,10},{10... | collective-permute-start | bytes 393224 | tf_op jit(solution)/shard_map/ppermute | solution.py:343
  20.7 1.4 %collective-permute-start.7 = (f32[256,128]{1,0:T(8,128)S(1)}, f32[256,128]{1,0:T(8,128)S(1)}, u32[]{:S(2)}, u32[]{:S(2)}) collective-permute-start(f32[256,128]{1,0:T(8,128)S(1)} %get-tuple-element.32), channel_id=1, source_target_pairs={{0,24},{8,0},{16,8},{24,16},{1,25},{9,1},{17,9},{25,17},{2,26},{10... | collective-permute-start | bytes 393224 | tf_op jit(solution)/shard_map/ppermute | solution.py:343
  22.2 0.0 copy-done.3
  22.2 0.0 copy-done.2
  22.2 0.0 copy-done.4
  22.2 2.8 %inner.1 = (f32[8,192,128]{2,1,0:T(8,128)S(1)}, f32[2,128]{1,0:T(2,128)S(1)}) custom-call(f32[8,8]{1,0:T(8,128)S(1)} %copy-done.4, f32[8,192,128]{2,1,0:T(8,128)S(1)} %bitcast.10, f32[64,128]{1,0:T(8,128)S(1)} %copy-done.2, f32[8,192,128]{2,1,0:T(8,128)S(1)} %bitcast.14, f32[64,128]{1,0:T(8,128)S(1)} %collective-permute-done.fr_ref.refs_2_, ...), custom_call_target="tpu_custom_call" | custom-call | tf_op jit(solution)/shard_map/inner/pallas_call | solution.py:416
  25.0 0.0 collective-permute-done.4.refs_6_.refs_8_
  25.0 0.0 collective-permute-done.5.refs_7_.refs_9_
  25.0 1.6 %products.1 = (f32[6,192,128]{2,1,0:T(8,128)S(1)}, f32[2,128]{1,0:T(2,128)S(1)}) custom-call(f32[8,192,128]{2,1,0:T(8,128)S(1)} %bitcast.11, f32[64,128]{1,0:T(8,128)S(1)} %copy-done.2, f32[8,192,128]{2,1,0:T(8,128)S(1)} %get-tuple-element.24.refs_2_, f32[2,128]{1,0:T(2,128)S(1)} %get-tuple-element.25.refs_3_, ...), custom_call_target="tpu_custom_call" | custom-call | tf_op jit(solution)/shard_map/products/pallas_call | solution.py:425
  26.6 0.0 collective-permute-done.6.refs_4_
  26.6 2.1 %collective-permute-done.7.refs_5_ = f32[256,128]{1,0:T(8,128)S(1)} collective-permute-done((f32[256,128]{1,0:T(8,128)S(1)}, f32[256,128]{1,0:T(8,128)S(1)}, u32[]{:S(2)}, u32[]{:S(2)}) %collective-permute-start.7) | collective-permute-done | bytes 131104 | tf_op jit(solution)/shard_map/ppermute | solution.py:343
  28.7 0.8 %products_last.1 = (f32[2,192,128]{2,1,0:T(8,128)S(1)}, f32[2,128]{1,0:T(2,128)S(1)}) custom-call(f32[8,192,128]{2,1,0:T(8,128)S(1)} %bitcast.12, f32[64,128]{1,0:T(8,128)S(1)} %copy-done.2, f32[8,192,128]{2,1,0:T(8,128)S(1)} %get-tuple-element.24.refs_2_, f32[2,128]{1,0:T(2,128)S(1)} %get-tuple-element.30.refs_3_, ...), custom_call_target="tpu_custom_call" | custom-call | tf_op jit(solution)/shard_map/products_last/pallas_call | solution.py:434
  29.5 13.7 %all_to_all.5.refs_0_ = f32[32,2,128]{2,1,0:T(2,128)S(1)} all-to-all(f32[32,2,128]{2,1,0:T(2,128)S(1)} %broadcast_in_dim.2), channel_id=1, replica_groups=mesh['loop'=4,'trans'=8] {'loop','trans'}, dimensions={0} | all-to-all | bytes 65536 | tf_op jit(solution)/shard_map/all_to_all | solution.py:444
  43.3 3.6 %combine.1 = (f32[8,192,128]{2,1,0:T(8,128)}, f32[8,8]{1,0:T(8,128)}, f32[8,8]{1,0:T(8,128)}) custom-call(f32[32,2,128]{2,1,0:T(2,128)S(1)} %all_to_all.5.refs_0_, f32[8,192,128]{2,1,0:T(8,128)S(1)} %bitcast.13, f32[6,192,128]{2,1,0:T(8,128)S(1)} %get-tuple-element.33.refs_8_.refs_2_, f32[2,192,128]{2,1,0:T(8,128)S(1)} %get-tuple-element.35.refs_3_), custom_call_target="tpu_custom_call" | custom-call | tf_op jit(solution)/shard_map/combine/pallas_call | solution.py:446
  (1 shorter events, 0.0 us)
Async XLA Ops:
  0.6 6.1 %copy-start = (f32[8,3,64,1,128]{4,3,2,1,0:T(1,128)S(1)}, f32[8,3,64,1,128]{4,3,2,1,0:T(1,128)}, u32[]{:S(2)}) copy-start(f32[8,3,64,1,128]{4,3,2,1,0:T(1,128)} %param.5) | copy-start | bytes 2359300
  2.7 15.0 %collective-permute-start.2 = (f32[512,128]{1,0:T(8,128)}, f32[512,128]{1,0:T(8,128)S(1)}, u32[]{:S(2)}, u32[]{:S(2)}) collective-permute-start(f32[512,128]{1,0:T(8,128)} %get-tuple-element.26), channel_id=1, source_target_pairs={{0,8},{8,16},{16,24},{24,0},{1,9},{9,17},{17,25},{25,1},{2,10},{10... | collective-permute-start | bytes 786440 | tf_op jit(solution)/shard_map/ppermute | solution.py:343
  5.7 13.3 %collective-permute-start.3 = (f32[512,128]{1,0:T(8,128)}, f32[512,128]{1,0:T(8,128)S(1)}, u32[]{:S(2)}, u32[]{:S(2)}) collective-permute-start(f32[512,128]{1,0:T(8,128)} %get-tuple-element.27), channel_id=1, source_target_pairs={{0,24},{8,0},{16,8},{24,16},{1,25},{9,1},{17,9},{25,17},{2,26},{10... | collective-permute-start | bytes 786440 | tf_op jit(solution)/shard_map/ppermute | solution.py:343
  6.8 0.8 %copy-start.1 = (f32[64,128]{1,0:T(8,128)S(1)}, f32[64,128]{1,0:T(8,128)}, u32[]{:S(2)}) copy-start(f32[64,128]{1,0:T(8,128)} %get-tuple-element.21.scale_ref.refs_1_) | copy-start | bytes 98308
  8.0 2.8 %collective-permute-start = (f32[64,128]{1,0:T(8,128)S(1)}, f32[64,128]{1,0:T(8,128)S(1)}, u32[]{:S(2)}, u32[]{:S(2)}) collective-permute-start(f32[64,128]{1,0:T(8,128)S(1)} %get-tuple-element.22), channel_id=1, source_target_pairs={{0,1},{1,2},{2,3},{3,4},{4,5},{5,6},{6,7},{8,9},{9,10},{10,11},{11... | collective-permute-start | bytes 98312 | tf_op jit(solution)/shard_map/ppermute | solution.py:341
  9.5 5.2 %collective-permute-start.1 = (f32[64,128]{1,0:T(8,128)S(1)}, f32[64,128]{1,0:T(8,128)S(1)}, u32[]{:S(2)}, u32[]{:S(2)}) collective-permute-start(f32[64,128]{1,0:T(8,128)S(1)} %get-tuple-element.23), channel_id=1, source_target_pairs={{1,0},{2,1},{3,2},{4,3},{5,4},{6,5},{7,6},{9,8},{10,9},{11,10},{12... | collective-permute-start | bytes 98312 | tf_op jit(solution)/shard_map/ppermute | solution.py:341
  14.7 7.5 %copy-start.3 = (f32[8,3,64,1,128]{4,3,2,1,0:T(1,128)S(1)}, f32[8,3,64,1,128]{4,3,2,1,0:T(1,128)}, u32[]{:S(2)}) copy-start(f32[8,3,64,1,128]{4,3,2,1,0:T(1,128)} %param.6) | copy-start | bytes 2359300
  14.7 10.3 %collective-permute-start.4 = (f32[264,128]{1,0:T(8,128)S(1)}, f32[264,128]{1,0:T(8,128)S(1)}, u32[]{:S(2)}, u32[]{:S(2)}) collective-permute-start(f32[264,128]{1,0:T(8,128)S(1)} %get-tuple-element.28), channel_id=1, source_target_pairs={{0,8},{8,16},{16,24},{24,0},{1,9},{9,17},{17,25},{25,1},{2,10},{10... | collective-permute-start | bytes 405512 | tf_op jit(solution)/shard_map/ppermute | solution.py:343
  15.4 6.8 %copy-start.2 = (f32[64,128]{1,0:T(8,128)S(1)}, f32[64,128]{1,0:T(8,128)}, u32[]{:S(2)}) copy-start(f32[64,128]{1,0:T(8,128)} %get-tuple-element.21.scale_ref.refs_1_) | copy-start | bytes 98308
  15.4 9.6 %collective-permute-start.5 = (f32[264,128]{1,0:T(8,128)S(1)}, f32[264,128]{1,0:T(8,128)S(1)}, u32[]{:S(2)}, u32[]{:S(2)}) collective-permute-start(f32[264,128]{1,0:T(8,128)S(1)} %get-tuple-element.29), channel_id=1, source_target_pairs={{0,24},{8,0},{16,8},{24,16},{1,25},{9,1},{17,9},{25,17},{2,26},{10... | collective-permute-start | bytes 405512 | tf_op jit(solution)/shard_map/ppermute | solution.py:343
  19.2 3.0 %copy-start.4 = (f32[8,8]{1,0:T(8,128)S(1)}, f32[8,8]{1,0:T(8,128)}, u32[]{:S(2)}) copy-start(f32[8,8]{1,0:T(8,128)} %coup_ref.1) | copy-start | bytes 772
  19.2 7.4 %collective-permute-start.6 = (f32[256,128]{1,0:T(8,128)S(1)}, f32[256,128]{1,0:T(8,128)S(1)}, u32[]{:S(2)}, u32[]{:S(2)}) collective-permute-start(f32[256,128]{1,0:T(8,128)S(1)} %get-tuple-element.31), channel_id=1, source_target_pairs={{0,8},{8,16},{16,24},{24,0},{1,9},{9,17},{17,25},{25,1},{2,10},{10... | collective-permute-start | bytes 393224 | tf_op jit(solution)/shard_map/ppermute | solution.py:343
  20.7 8.0 %collective-permute-start.7 = (f32[256,128]{1,0:T(8,128)S(1)}, f32[256,128]{1,0:T(8,128)S(1)}, u32[]{:S(2)}, u32[]{:S(2)}) collective-permute-start(f32[256,128]{1,0:T(8,128)S(1)} %get-tuple-element.32), channel_id=1, source_target_pairs={{0,24},{8,0},{16,8},{24,16},{1,25},{9,1},{17,9},{25,17},{2,26},{10... | collective-permute-start | bytes 393224 | tf_op jit(solution)/shard_map/ppermute | solution.py:343

commit v4 on v3

--- a/solution.py
+++ b/solution.py
@@ -209,14 +209,18 @@
     nb = v_ref.shape[0]
     nz, nt = scale_ref.shape
     end = cuts[-1][1]
-    halos = refs[: 2 * len(cuts) + 2]
-    corner_f, corner_b = halos[-2:]
-    rest = refs[2 * len(cuts) + 2 :]
-    old, (w_ref, pay_ref) = rest[:-2], rest[-2:]
+    halos = refs[: 2 * len(cuts)]
+    corners = refs[2 * len(cuts) : 2 * len(cuts) + 2]
+    if begin == 0:
+        w_ref, pay_ref, columns_f_ref, columns_b_ref = refs[-4:]
+        for corner, columns_ref in zip(corners, (columns_f_ref, columns_b_ref)):
+            columns_ref[...] = turned(corner[pl.ds(corner.shape[0] - nb, nb), :])[:nz, :]
+    else:
+        columns_f_ref, columns_b_ref = corners
+        old, w_ref, pay_ref = refs[-3:]
+    columns_f, columns_b = columns_f_ref[...], columns_b_ref[...]
     scale = scale_ref[...]
     lane = lane_ids(scale.shape)
-    columns_f = turned(corner_f[pl.ds(corner_f.shape[0] - nb, nb), :])[:nz, :]
-    columns_b = turned(corner_b[pl.ds(corner_b.shape[0] - nb, nb), :])[:nz, :]
     for i, (low, high) in enumerate(cuts):
         fwd_ref, bwd_ref = halos[2 * i : 2 * i + 2]
 
@@ -235,7 +239,7 @@
             w_ref[to, pl.ds(nz, nz), :] = l_ref[b, pl.ds(nz, nz), :] + scale * div
             w_ref[to, pl.ds(2 * nz, nz), :] = l_ref[b, pl.ds(2 * nz, nz), :] - scale * (tb + ut)
 
-    ws = [(old[0], b) for b in range(begin)] + [(w_ref, b - begin) for b in range(begin, end)]
+    ws = [(old, b) for b in range(begin)] + [(w_ref, b - begin) for b in range(begin, end)]
     pairs = []
     for b in range(begin, end):
         pairs += [(v_ref, j, *ws[b], {(0, nb * j + b), (1, nb * nb + nb * b + j)}) for j in range(nb)]
@@ -262,8 +266,8 @@
 
 
 def last_kernel(count, pay_ref, v_ref, *refs):
-    w_refs = refs[:-6]
-    out_hbm, alpha_ref, beta_ref, coef_ref, out_ref, sems = refs[-6:]
+    w_refs = refs[:-8]
+    out_hbm, alpha_hbm, beta_hbm, coef_ref, out_ref, alpha_ref, beta_ref, sems = refs[-8:]
     nb = v_ref.shape[0]
     total = jnp.sum(pay_ref[...], axis=0)
     proj = matrix_of(total[0:1], 0, nb)
@@ -271,11 +275,15 @@
     vv = matrix_of(total[1:2], 0, nb)
     alpha = proj / count
     alpha_t = matrix_of(total[1:2], nb * nb, nb) / count
+    alpha_ref[...] = alpha[:, :nb]
+    copies = [pltpu.make_async_copy(alpha_ref, alpha_hbm, sems.at[0])]
+    copies[0].start()
     lane = lane_ids(proj.shape)
     row = row_ids(proj.shape)
     cross = jnp.zeros_like(proj)
     half = jnp.zeros_like(proj)
     for j in range(nb):
+        coef_ref[j] = lane_at(alpha_t, j)
         cross = cross + lane_at(alpha_t, j) * row_at(proj, j)
         half = half + lane_at(vv, j) * row_at(alpha, j)
     quad = jnp.zeros_like(proj)
@@ -283,19 +291,32 @@
         quad = quad + lane_at(alpha_t, k) * row_at(half, k)
     gram = ((ww - cross) + (quad - cross)) / count
     ws = [(w, i) for w in w_refs for i in range(w.shape[0])]
-    for j in range(nb):
-        coef_ref[j] = lane_at(alpha_t, j)
     blocks = v_ref.shape[1] // 8
-    mat = jnp.where(lane < nb, gram, jnp.where(lane - nb == row, 1.0, 0.0))
-    fact = jnp.zeros_like(proj)
+    mat = {}
+    for i in range(nb):
+        line = row_at(gram, i)
+        for j in range(i + 1):
+            mat[i, j] = lane_at(line, j)
+    low, inv = {}, {}
+    beta = jnp.zeros_like(proj)
     for k in range(nb):
-        line = row_at(mat, k)
-        root = lane_at(line, k)
-        root = 1.0 / jnp.sqrt(root)
-        line = line * root
-        fact = jnp.where(row == k, line, fact)
-        if k < nb - 1:
-            mat = mat - (lane_at(mat, k) * root) * line
+        root = lax.rsqrt(mat[k, k])
+        low[k, k] = mat[k, k] * root
+        for i in range(k + 1, nb):
+            low[i, k] = mat[i, k] * root
+        for i in range(k + 1, nb):
+            for j in range(k + 1, i + 1):
+                mat[i, j] = mat[i, j] - low[i, k] * low[j, k]
+        for i in range(k, nb):
+            beta = jnp.where((row == k) & (lane == i), low[i, k], beta)
+        inv[k, k] = root
+        for j in range(k):
+            acc = low[k, j] * inv[j, j]
+            for q in range(j + 1, k):
+                acc = acc + low[k, q] * inv[q, j]
+            inv[k, j] = -(root * acc)
+        for j in range(k + 1):
+            coef_ref[nb + k * (k + 1) // 2 + j] = inv[k, j]
         for r in range(k * blocks // nb, (k + 1) * blocks // nb):
             rows = pl.ds(8 * r, 8)
             vs = [v_ref[j, rows, :] for j in range(nb)]
@@ -304,15 +325,12 @@
                 for j in range(nb):
                     acc = acc - coef_ref[j, pl.ds(b, 1), :] * vs[j]
                 out_ref[b, rows, :] = acc
-    inv = roll_by(fact, -nb, 1)
-    alpha_ref[...] = alpha[:, :nb]
-    beta_ref[...] = jnp.where(lane >= row, fact, 0.0)[:, :nb]
-    for j in range(nb):
-        coef_ref[nb + j] = lane_at(inv, j)
+    beta_ref[...] = beta[:, :nb]
+    copies.append(pltpu.make_async_copy(beta_ref, beta_hbm, sems.at[1]))
+    copies[1].start()
     step = 16
-    pieces = sems.shape[0]
+    pieces = sems.shape[0] - 2
     length = v_ref.shape[1] // pieces
-    copies = []
     for piece in range(pieces):
         base = piece * length
 
@@ -320,15 +338,16 @@
             rows = pl.ds(pl.multiple_of(base + r * step, step), step)
             xs = [out_ref[j, rows, :] for j in range(nb)]
             for b in range(nb):
-                acc = coef_ref[nb, pl.ds(b, 1), :] * xs[0]
+                at = nb + b * (b + 1) // 2
+                acc = coef_ref[at, pl.ds(0, 1), :] * xs[0]
                 for j in range(1, b + 1):
-                    acc = acc + coef_ref[nb + j, pl.ds(b, 1), :] * xs[j]
+                    acc = acc + coef_ref[at + j, pl.ds(0, 1), :] * xs[j]
                 out_ref[b, rows, :] = acc
             return carry
 
         lax.fori_loop(0, length // step, body, 0)
         part = pl.ds(base, length)
-        copy = pltpu.make_async_copy(out_ref.at[:, part, :], out_hbm.at[:, part, :], sems.at[piece])
+        copy = pltpu.make_async_copy(out_ref.at[:, part, :], out_hbm.at[:, part, :], sems.at[2 + piece])
         copy.start()
         copies.append(copy)
     for copy in copies:
@@ -358,7 +377,7 @@
     free = pl.CostEstimate(flops=0, bytes_accessed=0, transcendentals=0)
     plane = jax.ShapeDtypeStruct((nz, nt), f32)
     pay_shape = jax.ShapeDtypeStruct((2, nt), f32)
-    cut_a, cut_b, cut_c = (0, nb // 2), (nb // 2, nb * 3 // 4), (nb * 3 // 4, nb)
+    cut_a, cut_b, cut_c = (0, nb // 2), (nb // 2, nb - 1), (nb - 1, nb)
 
     def planes(n, more=0):
         return jax.ShapeDtypeStruct((n * nz + more, nt), f32)
@@ -422,11 +441,11 @@
         cost_estimate=free,
         name="inner",
     )(coupling_prev, v, scale, q, from_left, from_right)
-    w_ab, pay = pl.pallas_call(
+    w_ab, pay, columns_f, columns_b = pl.pallas_call(
         lambda *refs: sum_kernel((cut_a, cut_b), 0, *refs),
-        out_shape=(works(cut_b[1]), pay_shape),
+        out_shape=(works(cut_b[1]), pay_shape, plane, plane),
         in_specs=[vm] * 10,
-        out_specs=(vm, vm),
+        out_specs=(vm,) * 4,
         compiler_params=params,
         cost_estimate=free,
         name="products",
@@ -439,7 +458,7 @@
         compiler_params=params,
         cost_estimate=free,
         name="products_last",
-    )(v, scale, inner, pay, fwd_c, bwd_c, fwd_b, bwd_b, w_ab)
+    )(v, scale, inner, pay, fwd_c, bwd_c, columns_f, columns_b, w_ab)
     pay = jnp.broadcast_to(pay[None], (devices, 2, nt))
     pay = lax.all_to_all(pay, ("loop", "trans"), 0, 0)
     small = jax.ShapeDtypeStruct((nb, nb), f32)
@@ -447,8 +466,14 @@
         lambda *refs: last_kernel(count, *refs),
         out_shape=(works(nb), small, small),
         in_specs=[vm] * 4,
-        out_specs=(hbm, vm, vm),
-        scratch_shapes=[VM((2 * nb, 8, nt), f32), VM((nb, nc * nz, nt), f32), pltpu.SemaphoreType.DMA((4,))],
+        out_specs=(hbm,) * 3,
+        scratch_shapes=[
+            VM((nb + nb * (nb + 1) // 2, 8, nt), f32),
+            VM((nb, nc * nz, nt), f32),
+            VM((nb, nb), f32),
+            VM((nb, nb), f32),
+            pltpu.SemaphoreType.DMA((6,)),
+        ],
         compiler_params=params,
         cost_estimate=free,
         name="combine",

time: 47.1 us -> 45.7 us (0.970)
  Pallas kernels: 11.6 us -> 10.3 us
    pallas_call x1, Pallas kernels: 3.59 us -> 2.17 us  [local(): pl.pallas_call(lambda *refs: last_kernel(count, *refs), out_shape=(works(...]
  transfers between devices with their start and end apart: 8 -> 8, of which waited for: 3 -> 4; matrix products, arithmetic and copies ran while one was open for 0% -> 0% of each run, Pallas kernels for 11% -> 12%
where the time goes in v4:
time: 45.7 us; the launch traced here: 45.5 us
  blocking collectives  14.1 us (31%)
  starting transfers between devices  12.7 us (28%)
  Pallas kernels  10.3 us (23%)
  waiting for transfers between devices  6.85 us (15%)
  local copies, waits for them, and re-layouts  0.79 us (2%)
  between operations  0.73 us (2%)
    all_to_all x1, blocking collectives, local(): pay = lax.all_to_all(pay, ('loop', 'trans'), 0, 0)  14.1 us
    ppermute x6, starting transfers between devices, shift(): lax.ppermute(x, 'loop', [(i, (i + loop_by) % count) for i in range(count)])  9.96 us
    ppermute x2, waiting for transfers between devices, shift(): lax.ppermute(x, 'trans', [(t, t + trans_by) for t in range(count) if 0 <=...  3.85 us
    ppermute x6, waiting for transfers between devices, shift(): lax.ppermute(x, 'loop', [(i, (i + loop_by) % count) for i in range(count)])  3 us
    pallas_call x1, Pallas kernels, local(): pl.pallas_call(inner_kernel, out_shape=(works(nb), pay_shape), in_specs=[...  2.87 us
    ppermute x2, starting transfers between devices, shift(): lax.ppermute(x, 'trans', [(t, t + trans_by) for t in range(count) if 0 <=...  2.75 us
    pallas_call x1, Pallas kernels, local(): pl.pallas_call(lambda *refs: last_kernel(count, *refs), out_shape=(works(...  2.17 us
    pallas_call x1, Pallas kernels, local(): pl.pallas_call(first_kernel, out_shape=(planes(size_a), planes(size_a), p...  2.09 us
  transfers between devices with their start and end apart: 8, of which 4 were waited for; matrix products, arithmetic and copies ran while one was open for 0% of the time, Pallas kernels for 12%

profile of v4, /device:TPU:0, one launch (start us, length us, event | category | flops | bytes accessed | tf_op | source)
XLA Modules:
  0.0 45.5 jit_solution(14778719383715851714)
XLA Ops:
  0.6 0.0 copy-start
  0.6 2.1 %first.1 = (f32[512,128]{1,0:T(8,128)}, f32[512,128]{1,0:T(8,128)}, f32[64,128]{1,0:T(8,128)}) custom-call(f32[8,192,128]{2,1,0:T(8,128)} %bitcast.6, s32[64,128]{1,0:T(8,128)} %bitcast.15, f32[4]{0:T(128)} %eps_hbm.1), custom_call_target="tpu_custom_call" | custom-call | tf_op jit(solution)/shard_map/first/pallas_call | solution.py:389
  2.7 3.0 %collective-permute-start.2 = (f32[512,128]{1,0:T(8,128)}, f32[512,128]{1,0:T(8,128)S(1)}, u32[]{:S(2)}, u32[]{:S(2)}) collective-permute-start(f32[512,128]{1,0:T(8,128)} %get-tuple-element.28), channel_id=1, source_target_pairs={{0,8},{8,16},{16,24},{24,0},{1,9},{9,17},{17,25},{25,1},{2,10},{10... | collective-permute-start | bytes 786440 | tf_op jit(solution)/shard_map/ppermute | solution.py:362
  5.7 1.0 %collective-permute-start.3 = (f32[512,128]{1,0:T(8,128)}, f32[512,128]{1,0:T(8,128)S(1)}, u32[]{:S(2)}, u32[]{:S(2)}) collective-permute-start(f32[512,128]{1,0:T(8,128)} %get-tuple-element.29), channel_id=1, source_target_pairs={{0,24},{8,0},{16,8},{24,16},{1,25},{9,1},{17,9},{25,17},{2,26},{10... | collective-permute-start | bytes 786440 | tf_op jit(solution)/shard_map/ppermute | solution.py:362
  6.8 0.0 copy-done
  6.8 0.0 copy-start.1
  6.8 0.8 %copy-done.1 = f32[64,128]{1,0:T(8,128)S(1)} copy-done((f32[64,128]{1,0:T(8,128)S(1)}, f32[64,128]{1,0:T(8,128)}, u32[]{:S(2)}) %copy-start.1) | copy-done | bytes 32792
  7.5 0.5 %edges.1 = (f32[64,128]{1,0:T(8,128)S(1)}, f32[64,128]{1,0:T(8,128)S(1)}) custom-call(f32[8,192,128]{2,1,0:T(8,128)S(1)} %bitcast.7, f32[64,128]{1,0:T(8,128)S(1)} %copy-done.1), custom_call_target="tpu_custom_call" | custom-call | tf_op jit(solution)/shard_map/edges/pallas_call | solution.py:405
  8.0 1.5 %collective-permute-start = (f32[64,128]{1,0:T(8,128)S(1)}, f32[64,128]{1,0:T(8,128)S(1)}, u32[]{:S(2)}, u32[]{:S(2)}) collective-permute-start(f32[64,128]{1,0:T(8,128)S(1)} %get-tuple-element.24), channel_id=1, source_target_pairs={{0,1},{1,2},{2,3},{3,4},{4,5},{5,6},{6,7},{8,9},{9,10},{10,11},{11... | collective-permute-start | bytes 98312 | tf_op jit(solution)/shard_map/ppermute | solution.py:360
  9.5 1.3 %collective-permute-start.1 = (f32[64,128]{1,0:T(8,128)S(1)}, f32[64,128]{1,0:T(8,128)S(1)}, u32[]{:S(2)}, u32[]{:S(2)}) collective-permute-start(f32[64,128]{1,0:T(8,128)S(1)} %get-tuple-element.25), channel_id=1, source_target_pairs={{1,0},{2,1},{3,2},{4,3},{5,4},{6,5},{7,6},{9,8},{10,9},{11,10},{12... | collective-permute-start | bytes 98312 | tf_op jit(solution)/shard_map/ppermute | solution.py:360
  10.8 0.0 collective-permute-done.fr_ref.refs_2_
  10.8 3.8 %collective-permute-done.1.fl_ref.refs_3_ = f32[64,128]{1,0:T(8,128)S(1)} collective-permute-done((f32[64,128]{1,0:T(8,128)S(1)}, f32[64,128]{1,0:T(8,128)S(1)}, u32[]{:S(2)}, u32[]{:S(2)}) %collective-permute-start.1) | collective-permute-done | bytes 32800 | tf_op jit(solution)/shard_map/ppermute | solution.py:360
  14.6 0.1 pack_b.1
  14.7 0.0 copy-start.3
  14.7 0.6 %collective-permute-start.4 = (f32[392,128]{1,0:T(8,128)S(1)}, f32[392,128]{1,0:T(8,128)S(1)}, u32[]{:S(2)}, u32[]{:S(2)}) collective-permute-start(f32[392,128]{1,0:T(8,128)S(1)} %get-tuple-element.30), channel_id=1, source_target_pairs={{0,8},{8,16},{16,24},{24,0},{1,9},{9,17},{17,25},{25,1},{2,10},{10... | collective-permute-start | bytes 602120 | tf_op jit(solution)/shard_map/ppermute | solution.py:362
  15.4 0.0 copy-start.2
  15.4 2.3 %collective-permute-start.5 = (f32[392,128]{1,0:T(8,128)S(1)}, f32[392,128]{1,0:T(8,128)S(1)}, u32[]{:S(2)}, u32[]{:S(2)}) collective-permute-start(f32[392,128]{1,0:T(8,128)S(1)} %get-tuple-element.31), channel_id=1, source_target_pairs={{0,24},{8,0},{16,8},{24,16},{1,25},{9,1},{17,9},{25,17},{2,26},{10... | collective-permute-start | bytes 602120 | tf_op jit(solution)/shard_map/ppermute | solution.py:362
  17.7 0.0 collective-permute-done.2.refs_4_.refs_2_
  17.7 1.4 %collective-permute-done.3.refs_5_.refs_3_ = f32[512,128]{1,0:T(8,128)S(1)} collective-permute-done((f32[512,128]{1,0:T(8,128)}, f32[512,128]{1,0:T(8,128)S(1)}, u32[]{:S(2)}, u32[]{:S(2)}) %collective-permute-start.3) | collective-permute-done | bytes 262176 | tf_op jit(solution)/shard_map/ppermute | solution.py:362
  19.1 0.1 pack_c.1
  19.2 0.0 copy-start.4
  19.2 1.5 %collective-permute-start.6 = (f32[128,128]{1,0:T(8,128)S(1)}, f32[128,128]{1,0:T(8,128)S(1)}, u32[]{:S(2)}, u32[]{:S(2)}) collective-permute-start(f32[128,128]{1,0:T(8,128)S(1)} %get-tuple-element.33), channel_id=1, source_target_pairs={{0,8},{8,16},{16,24},{24,0},{1,9},{9,17},{17,25},{25,1},{2,10},{10... | collective-permute-start | bytes 196616 | tf_op jit(solution)/shard_map/ppermute | solution.py:362
  20.7 1.4 %collective-permute-start.7 = (f32[128,128]{1,0:T(8,128)S(1)}, f32[128,128]{1,0:T(8,128)S(1)}, u32[]{:S(2)}, u32[]{:S(2)}) collective-permute-start(f32[128,128]{1,0:T(8,128)S(1)} %get-tuple-element.34), channel_id=1, source_target_pairs={{0,24},{8,0},{16,8},{24,16},{1,25},{9,1},{17,9},{25,17},{2,26},{10... | collective-permute-start | bytes 196616 | tf_op jit(solution)/shard_map/ppermute | solution.py:362
  22.1 0.0 copy-done.3
  22.1 0.0 copy-done.2
  22.1 0.0 copy-done.4
  22.1 2.9 %inner.1 = (f32[8,192,128]{2,1,0:T(8,128)S(1)}, f32[2,128]{1,0:T(2,128)S(1)}) custom-call(f32[8,8]{1,0:T(8,128)S(1)} %copy-done.4, f32[8,192,128]{2,1,0:T(8,128)S(1)} %bitcast.10, f32[64,128]{1,0:T(8,128)S(1)} %copy-done.2, f32[8,192,128]{2,1,0:T(8,128)S(1)} %bitcast.14, f32[64,128]{1,0:T(8,128)S(1)} %collective-permute-done.fr_ref.refs_2_, ...), custom_call_target="tpu_custom_call" | custom-call | tf_op jit(solution)/shard_map/inner/pallas_call | solution.py:435
  25.0 0.0 collective-permute-done.4.refs_6_.refs_8_
  25.0 0.8 %collective-permute-done.5.refs_7_.refs_9_ = f32[392,128]{1,0:T(8,128)S(1)} collective-permute-done((f32[392,128]{1,0:T(8,128)S(1)}, f32[392,128]{1,0:T(8,128)S(1)}, u32[]{:S(2)}, u32[]{:S(2)}) %collective-permute-start.5) | collective-permute-done | bytes 200736 | tf_op jit(solution)/shard_map/ppermute | solution.py:362
  25.9 2.0 %products.1 = (f32[7,192,128]{2,1,0:T(8,128)S(1)}, f32[2,128]{1,0:T(2,128)S(1)}, f32[64,128]{1,0:T(8,128)S(1)}, f32[64,128]{1,0:T(8,128)S(1)}) custom-call(f32[8,192,128]{2,1,0:T(8,128)S(1)} %bitcast.11, f32[64,128]{1,0:T(8,128)S(1)} %copy-done.2, f32[8,192,128]{2,1,0:T(8,128)S(1)} %get-tuple-element.26.refs_2_, f32[2,128]{1,0:T(2,128)S(1)} %get-tuple-element.27.refs_3_, ...), custom_call_target="tpu_custom_call" | custom-call | tf_op jit(solution)/shard_map/products/pallas_call | solution.py:444
  27.9 0.0 collective-permute-done.6.refs_4_
  27.9 0.8 %collective-permute-done.7.refs_5_ = f32[128,128]{1,0:T(8,128)S(1)} collective-permute-done((f32[128,128]{1,0:T(8,128)S(1)}, f32[128,128]{1,0:T(8,128)S(1)}, u32[]{:S(2)}, u32[]{:S(2)}) %collective-permute-start.7) | collective-permute-done | bytes 65568 | tf_op jit(solution)/shard_map/ppermute | solution.py:362
  28.7 0.5 %products_last.1 = (f32[1,192,128]{2,1,0:T(8,128)S(1)}, f32[2,128]{1,0:T(2,128)S(1)}) custom-call(f32[8,192,128]{2,1,0:T(8,128)S(1)} %bitcast.12, f32[64,128]{1,0:T(8,128)S(1)} %copy-done.2, f32[8,192,128]{2,1,0:T(8,128)S(1)} %get-tuple-element.26.refs_2_, f32[2,128]{1,0:T(2,128)S(1)} %get-tuple-element.32.refs_3_, ...), custom_call_target="tpu_custom_call" | custom-call | tf_op jit(solution)/shard_map/products_last/pallas_call | solution.py:453
  29.2 14.1 %all_to_all.5.refs_0_ = f32[32,2,128]{2,1,0:T(2,128)S(1)} all-to-all(f32[32,2,128]{2,1,0:T(2,128)S(1)} %broadcast_in_dim.2), channel_id=1, replica_groups=mesh['loop'=4,'trans'=8] {'loop','trans'}, dimensions={0} | all-to-all | bytes 65536 | tf_op jit(solution)/shard_map/all_to_all | solution.py:463
  43.3 2.2 %combine.1 = (f32[8,192,128]{2,1,0:T(8,128)}, f32[8,8]{1,0:T(8,128)}, f32[8,8]{1,0:T(8,128)}) custom-call(f32[32,2,128]{2,1,0:T(2,128)S(1)} %all_to_all.5.refs_0_, f32[8,192,128]{2,1,0:T(8,128)S(1)} %bitcast.13, f32[7,192,128]{2,1,0:T(8,128)S(1)} %get-tuple-element.37.refs_8_.refs_2_, f32[1,192,128]{2,1,0:T(8,128)S(1)} %get-tuple-element.39.refs_3_), custom_call_target="tpu_custom_call" | custom-call | tf_op jit(solution)/shard_map/combine/pallas_call | solution.py:465
  (1 shorter events, 0.0 us)
Async XLA Ops:
  0.6 6.1 %copy-start = (f32[8,3,64,1,128]{4,3,2,1,0:T(1,128)S(1)}, f32[8,3,64,1,128]{4,3,2,1,0:T(1,128)}, u32[]{:S(2)}) copy-start(f32[8,3,64,1,128]{4,3,2,1,0:T(1,128)} %param.5) | copy-start | bytes 2359300
  2.7 15.0 %collective-permute-start.2 = (f32[512,128]{1,0:T(8,128)}, f32[512,128]{1,0:T(8,128)S(1)}, u32[]{:S(2)}, u32[]{:S(2)}) collective-permute-start(f32[512,128]{1,0:T(8,128)} %get-tuple-element.28), channel_id=1, source_target_pairs={{0,8},{8,16},{16,24},{24,0},{1,9},{9,17},{17,25},{25,1},{2,10},{10... | collective-permute-start | bytes 786440 | tf_op jit(solution)/shard_map/ppermute | solution.py:362
  5.7 13.3 %collective-permute-start.3 = (f32[512,128]{1,0:T(8,128)}, f32[512,128]{1,0:T(8,128)S(1)}, u32[]{:S(2)}, u32[]{:S(2)}) collective-permute-start(f32[512,128]{1,0:T(8,128)} %get-tuple-element.29), channel_id=1, source_target_pairs={{0,24},{8,0},{16,8},{24,16},{1,25},{9,1},{17,9},{25,17},{2,26},{10... | collective-permute-start | bytes 786440 | tf_op jit(solution)/shard_map/ppermute | solution.py:362
  6.8 0.8 %copy-start.1 = (f32[64,128]{1,0:T(8,128)S(1)}, f32[64,128]{1,0:T(8,128)}, u32[]{:S(2)}) copy-start(f32[64,128]{1,0:T(8,128)} %get-tuple-element.23.scale_ref.refs_1_) | copy-start | bytes 98308
  8.0 2.8 %collective-permute-start = (f32[64,128]{1,0:T(8,128)S(1)}, f32[64,128]{1,0:T(8,128)S(1)}, u32[]{:S(2)}, u32[]{:S(2)}) collective-permute-start(f32[64,128]{1,0:T(8,128)S(1)} %get-tuple-element.24), channel_id=1, source_target_pairs={{0,1},{1,2},{2,3},{3,4},{4,5},{5,6},{6,7},{8,9},{9,10},{10,11},{11... | collective-permute-start | bytes 98312 | tf_op jit(solution)/shard_map/ppermute | solution.py:360
  9.5 5.2 %collective-permute-start.1 = (f32[64,128]{1,0:T(8,128)S(1)}, f32[64,128]{1,0:T(8,128)S(1)}, u32[]{:S(2)}, u32[]{:S(2)}) collective-permute-start(f32[64,128]{1,0:T(8,128)S(1)} %get-tuple-element.25), channel_id=1, source_target_pairs={{1,0},{2,1},{3,2},{4,3},{5,4},{6,5},{7,6},{9,8},{10,9},{11,10},{12... | collective-permute-start | bytes 98312 | tf_op jit(solution)/shard_map/ppermute | solution.py:360
  14.7 7.4 %copy-start.3 = (f32[8,3,64,1,128]{4,3,2,1,0:T(1,128)S(1)}, f32[8,3,64,1,128]{4,3,2,1,0:T(1,128)}, u32[]{:S(2)}) copy-start(f32[8,3,64,1,128]{4,3,2,1,0:T(1,128)} %param.6) | copy-start | bytes 2359300
  14.7 10.3 %collective-permute-start.4 = (f32[392,128]{1,0:T(8,128)S(1)}, f32[392,128]{1,0:T(8,128)S(1)}, u32[]{:S(2)}, u32[]{:S(2)}) collective-permute-start(f32[392,128]{1,0:T(8,128)S(1)} %get-tuple-element.30), channel_id=1, source_target_pairs={{0,8},{8,16},{16,24},{24,0},{1,9},{9,17},{17,25},{25,1},{2,10},{10... | collective-permute-start | bytes 602120 | tf_op jit(solution)/shard_map/ppermute | solution.py:362
  15.4 6.8 %copy-start.2 = (f32[64,128]{1,0:T(8,128)S(1)}, f32[64,128]{1,0:T(8,128)}, u32[]{:S(2)}) copy-start(f32[64,128]{1,0:T(8,128)} %get-tuple-element.23.scale_ref.refs_1_) | copy-start | bytes 98308
  15.4 10.5 %collective-permute-start.5 = (f32[392,128]{1,0:T(8,128)S(1)}, f32[392,128]{1,0:T(8,128)S(1)}, u32[]{:S(2)}, u32[]{:S(2)}) collective-permute-start(f32[392,128]{1,0:T(8,128)S(1)} %get-tuple-element.31), channel_id=1, source_target_pairs={{0,24},{8,0},{16,8},{24,16},{1,25},{9,1},{17,9},{25,17},{2,26},{10... | collective-permute-start | bytes 602120 | tf_op jit(solution)/shard_map/ppermute | solution.py:362
  19.2 3.0 %copy-start.4 = (f32[8,8]{1,0:T(8,128)S(1)}, f32[8,8]{1,0:T(8,128)}, u32[]{:S(2)}) copy-start(f32[8,8]{1,0:T(8,128)} %coup_ref.1) | copy-start | bytes 772
  19.2 8.7 %collective-permute-start.6 = (f32[128,128]{1,0:T(8,128)S(1)}, f32[128,128]{1,0:T(8,128)S(1)}, u32[]{:S(2)}, u32[]{:S(2)}) collective-permute-start(f32[128,128]{1,0:T(8,128)S(1)} %get-tuple-element.33), channel_id=1, source_target_pairs={{0,8},{8,16},{16,24},{24,0},{1,9},{9,17},{17,25},{25,1},{2,10},{10... | collective-permute-start | bytes 196616 | tf_op jit(solution)/shard_map/ppermute | solution.py:362
  20.7 8.0 %collective-permute-start.7 = (f32[128,128]{1,0:T(8,128)S(1)}, f32[128,128]{1,0:T(8,128)S(1)}, u32[]{:S(2)}, u32[]{:S(2)}) collective-permute-start(f32[128,128]{1,0:T(8,128)S(1)} %get-tuple-element.34), channel_id=1, source_target_pairs={{0,24},{8,0},{16,8},{24,16},{1,25},{9,1},{17,9},{25,17},{2,26},{10... | collective-permute-start | bytes 196616 | tf_op jit(solution)/shard_map/ppermute | solution.py:362

commit v5 on v4

--- a/solution.py
+++ b/solution.py
@@ -116,7 +116,7 @@
     return jnp.where(low, a, b) + swapped
 
 
-def add_products(pairs, steps, group, pays, unroll=1):
+def add_products(pairs, steps, group, pays, unroll=8):
     shape = pays[0].shape
     lane, row = lane_ids(shape), row_ids(shape)
     zero = jnp.zeros(shape, jnp.float32)
@@ -245,7 +245,7 @@
         pairs += [(v_ref, j, *ws[b], {(0, nb * j + b), (1, nb * nb + nb * b + j)}) for j in range(nb)]
         pairs += [(*ws[j], *ws[b], {(0, nb * nb + nb * j + b), (0, nb * nb + nb * b + j)}) for j in range(b + 1)]
     zero = jnp.zeros((8, nt), jnp.float32)
-    store_pays(pay_ref, add_products(pairs, v_ref.shape[1] // 8, 36, [zero, zero]), pay_in_ref)
+    store_pays(pay_ref, add_products(pairs, v_ref.shape[1] // 8, 42, [zero, zero]), pay_in_ref)
 
 
 def lane_at(x, k):
@@ -373,7 +373,6 @@
     vm, sm = pl.BlockSpec(memory_space=VM), pl.BlockSpec(memory_space=SM)
     hbm = pl.BlockSpec(memory_space=pltpu.HBM)
     params = pltpu.CompilerParams(vmem_limit_bytes=32 * 2**20)
-    wide = pltpu.CompilerParams(vmem_limit_bytes=int(62 * 2**20))
     free = pl.CostEstimate(flops=0, bytes_accessed=0, transcendentals=0)
     plane = jax.ShapeDtypeStruct((nz, nt), f32)
     pay_shape = jax.ShapeDtypeStruct((2, nt), f32)
@@ -397,10 +396,10 @@
             SM(permittivity.shape, f32),
             pltpu.SemaphoreType.DMA((2 + cut_a[1],)),
         ],
-        compiler_params=wide,
+        compiler_params=params,
         cost_estimate=free,
         name="first",
-    )(v, mat, permittivity)
+    )(*(pltpu.with_memory_space_constraint(x, pltpu.HBM) for x in (v, mat, permittivity)))
     fwd_a, bwd_a = shift(fwd_a, 1, 0), shift(bwd_a, -1, 0)
     right, left = pl.pallas_call(
         edge_kernel,

time: 45.7 us -> 44.2 us (0.967)
  Pallas kernels: 10.3 us -> 8.27 us
  waiting for transfers between devices: 6.85 us -> 8.58 us
  local copies, waits for them, and re-layouts: 0.79 us -> 0.03 us
    ppermute x6, waiting for transfers between devices: 3 us -> 4.73 us  [shift(): lax.ppermute(x, 'loop', [(i, (i + loop_by) % count) for i in range(count)])]
    pallas_call x1, Pallas kernels: 2.02 us -> 1.2 us  [local(): pl.pallas_call(lambda *refs: sum_kernel((cut_a, cut_b), 0, *refs), out_sh...]
    unnamed x10 -> x6, local copies, waits for them, and re-layouts: 0.78 us -> 0.02 us
    pallas_call x1, Pallas kernels: 2.09 us -> 1.36 us  [local(): pl.pallas_call(first_kernel, out_shape=(planes(size_a), planes(size_a), p...]
    all_to_all x1, blocking collectives: 14.1 us -> 13.7 us  [local(): pay = lax.all_to_all(pay, ('loop', 'trans'), 0, 0)]
  transfers between devices with their start and end apart: 8 -> 8, of which waited for: 4 -> 4; matrix products, arithmetic and copies ran while one was open for 0% -> 0% of each run, Pallas kernels for 12% -> 10%
where the time goes in v5:
time: 44.2 us; the launch traced here: 44 us
  blocking collectives  13.7 us (31%)
  starting transfers between devices  12.7 us (29%)
  waiting for transfers between devices  8.58 us (19%)
  Pallas kernels  8.27 us (19%)
  between operations  0.74 us (2%)
    all_to_all x1, blocking collectives, local(): pay = lax.all_to_all(pay, ('loop', 'trans'), 0, 0)  13.7 us
    ppermute x6, starting transfers between devices, shift(): lax.ppermute(x, 'loop', [(i, (i + loop_by) % count) for i in range(count)])  9.97 us
    ppermute x6, waiting for transfers between devices, shift(): lax.ppermute(x, 'loop', [(i, (i + loop_by) % count) for i in range(count)])  4.73 us
    ppermute x2, waiting for transfers between devices, shift(): lax.ppermute(x, 'trans', [(t, t + trans_by) for t in range(count) if 0 <=...  3.85 us
    ppermute x2, starting transfers between devices, shift(): lax.ppermute(x, 'trans', [(t, t + trans_by) for t in range(count) if 0 <=...  2.75 us
    pallas_call x1, Pallas kernels, local(): pl.pallas_call(inner_kernel, out_shape=(works(nb), pay_shape), in_specs=[...  2.58 us
    pallas_call x1, Pallas kernels, local(): pl.pallas_call(lambda *refs: last_kernel(count, *refs), out_shape=(works(...  2.17 us
    pallas_call x1, Pallas kernels, local(): pl.pallas_call(first_kernel, out_shape=(planes(size_a), planes(size_a), p...  1.36 us
  transfers between devices with their start and end apart: 8, of which 4 were waited for; matrix products, arithmetic and copies ran while one was open for 0% of the time, Pallas kernels for 10%

profile of v5, /device:TPU:0, one launch (start us, length us, event | category | flops | bytes accessed | tf_op | source)
XLA Modules:
  0.0 44.0 jit_solution(11861206621019675674)
XLA Ops:
  0.6 0.0 copy-start
  0.6 1.4 %first.1 = (f32[512,128]{1,0:T(8,128)S(1)}, f32[512,128]{1,0:T(8,128)S(1)}, f32[64,128]{1,0:T(8,128)S(1)}) custom-call(f32[8,192,128]{2,1,0:T(8,128)} %bitcast.6, s32[64,128]{1,0:T(8,128)} %bitcast.15, f32[4]{0:T(128)} %eps_hbm.1), custom_call_target="tpu_custom_call" | custom-call | tf_op jit(solution)/shard_map/first/pallas_call | solution.py:388
  2.0 3.0 %collective-permute-start.2 = (f32[512,128]{1,0:T(8,128)S(1)}, f32[512,128]{1,0:T(8,128)S(1)}, u32[]{:S(2)}, u32[]{:S(2)}) collective-permute-start(f32[512,128]{1,0:T(8,128)S(1)} %get-tuple-element.28), channel_id=1, source_target_pairs={{0,8},{8,16},{16,24},{24,0},{1,9},{9,17},{17,25},{25,1},{2,10},{10... | collective-permute-start | bytes 786440 | tf_op jit(solution)/shard_map/ppermute | solution.py:362
  5.0 1.0 %collective-permute-start.3 = (f32[512,128]{1,0:T(8,128)S(1)}, f32[512,128]{1,0:T(8,128)S(1)}, u32[]{:S(2)}, u32[]{:S(2)}) collective-permute-start(f32[512,128]{1,0:T(8,128)S(1)} %get-tuple-element.29), channel_id=1, source_target_pairs={{0,24},{8,0},{16,8},{24,16},{1,25},{9,1},{17,9},{25,17},{2,26},{10... | collective-permute-start | bytes 786440 | tf_op jit(solution)/shard_map/ppermute | solution.py:362
  6.0 0.0 copy-done
  6.0 0.5 %edges.1 = (f32[64,128]{1,0:T(8,128)S(1)}, f32[64,128]{1,0:T(8,128)S(1)}) custom-call(f32[8,192,128]{2,1,0:T(8,128)S(1)} %bitcast.7, f32[64,128]{1,0:T(8,128)S(1)} %get-tuple-element.23.scale_ref.refs_1_), custom_call_target="tpu_custom_call" | custom-call | tf_op jit(solution)/shard_map/edges/pallas_call | solution.py:404
  6.5 1.5 %collective-permute-start = (f32[64,128]{1,0:T(8,128)S(1)}, f32[64,128]{1,0:T(8,128)S(1)}, u32[]{:S(2)}, u32[]{:S(2)}) collective-permute-start(f32[64,128]{1,0:T(8,128)S(1)} %get-tuple-element.24), channel_id=1, source_target_pairs={{0,1},{1,2},{2,3},{3,4},{4,5},{5,6},{6,7},{8,9},{9,10},{10,11},{11... | collective-permute-start | bytes 98312 | tf_op jit(solution)/shard_map/ppermute | solution.py:360
  8.0 1.3 %collective-permute-start.1 = (f32[64,128]{1,0:T(8,128)S(1)}, f32[64,128]{1,0:T(8,128)S(1)}, u32[]{:S(2)}, u32[]{:S(2)}) collective-permute-start(f32[64,128]{1,0:T(8,128)S(1)} %get-tuple-element.25), channel_id=1, source_target_pairs={{1,0},{2,1},{3,2},{4,3},{5,4},{6,5},{7,6},{9,8},{10,9},{11,10},{12... | collective-permute-start | bytes 98312 | tf_op jit(solution)/shard_map/ppermute | solution.py:360
  9.3 0.0 collective-permute-done.fr_ref.refs_2_
  9.3 3.8 %collective-permute-done.1.fl_ref.refs_3_ = f32[64,128]{1,0:T(8,128)S(1)} collective-permute-done((f32[64,128]{1,0:T(8,128)S(1)}, f32[64,128]{1,0:T(8,128)S(1)}, u32[]{:S(2)}, u32[]{:S(2)}) %collective-permute-start.1) | collective-permute-done | bytes 32800 | tf_op jit(solution)/shard_map/ppermute | solution.py:360
  13.1 0.1 pack_b.1
  13.2 0.0 copy-start.1
  13.2 0.6 %collective-permute-start.4 = (f32[392,128]{1,0:T(8,128)S(1)}, f32[392,128]{1,0:T(8,128)S(1)}, u32[]{:S(2)}, u32[]{:S(2)}) collective-permute-start(f32[392,128]{1,0:T(8,128)S(1)} %get-tuple-element.30), channel_id=1, source_target_pairs={{0,8},{8,16},{16,24},{24,0},{1,9},{9,17},{17,25},{25,1},{2,10},{10... | collective-permute-start | bytes 602120 | tf_op jit(solution)/shard_map/ppermute | solution.py:362
  13.9 2.3 %collective-permute-start.5 = (f32[392,128]{1,0:T(8,128)S(1)}, f32[392,128]{1,0:T(8,128)S(1)}, u32[]{:S(2)}, u32[]{:S(2)}) collective-permute-start(f32[392,128]{1,0:T(8,128)S(1)} %get-tuple-element.31), channel_id=1, source_target_pairs={{0,24},{8,0},{16,8},{24,16},{1,25},{9,1},{17,9},{25,17},{2,26},{10... | collective-permute-start | bytes 602120 | tf_op jit(solution)/shard_map/ppermute | solution.py:362
  16.2 0.0 collective-permute-done.2.refs_4_.refs_2_
  16.2 1.9 %collective-permute-done.3.refs_5_.refs_3_ = f32[512,128]{1,0:T(8,128)S(1)} collective-permute-done((f32[512,128]{1,0:T(8,128)S(1)}, f32[512,128]{1,0:T(8,128)S(1)}, u32[]{:S(2)}, u32[]{:S(2)}) %collective-permute-start.3) | collective-permute-done | bytes 262176 | tf_op jit(solution)/shard_map/ppermute | solution.py:362
  18.1 0.1 pack_c.1
  18.2 0.0 copy-start.2
  18.2 1.5 %collective-permute-start.6 = (f32[128,128]{1,0:T(8,128)S(1)}, f32[128,128]{1,0:T(8,128)S(1)}, u32[]{:S(2)}, u32[]{:S(2)}) collective-permute-start(f32[128,128]{1,0:T(8,128)S(1)} %get-tuple-element.33), channel_id=1, source_target_pairs={{0,8},{8,16},{16,24},{24,0},{1,9},{9,17},{17,25},{25,1},{2,10},{10... | collective-permute-start | bytes 196616 | tf_op jit(solution)/shard_map/ppermute | solution.py:362
  19.8 1.4 %collective-permute-start.7 = (f32[128,128]{1,0:T(8,128)S(1)}, f32[128,128]{1,0:T(8,128)S(1)}, u32[]{:S(2)}, u32[]{:S(2)}) collective-permute-start(f32[128,128]{1,0:T(8,128)S(1)} %get-tuple-element.34), channel_id=1, source_target_pairs={{0,24},{8,0},{16,8},{24,16},{1,25},{9,1},{17,9},{25,17},{2,26},{10... | collective-permute-start | bytes 196616 | tf_op jit(solution)/shard_map/ppermute | solution.py:362
  21.2 0.0 copy-done.1
  21.2 0.0 copy-done.2
  21.2 2.6 %inner.1 = (f32[8,192,128]{2,1,0:T(8,128)S(1)}, f32[2,128]{1,0:T(2,128)S(1)}) custom-call(f32[8,8]{1,0:T(8,128)S(1)} %copy-done.2, f32[8,192,128]{2,1,0:T(8,128)S(1)} %bitcast.10, f32[64,128]{1,0:T(8,128)S(1)} %get-tuple-element.23.scale_ref.refs_1_, f32[8,192,128]{2,1,0:T(8,128)S(1)} %bitcast.14, f32[64,128]{1,0:T(8,128)S(1)} %collective-permute-done.fr_ref.refs_2_, ...), custom_call_target="tpu_custom_call" | custom-call | tf_op jit(solution)/shard_map/inner/pallas_call | solution.py:434
  23.8 0.0 collective-permute-done.4.refs_6_.refs_8_
  23.8 1.2 %collective-permute-done.5.refs_7_.refs_9_ = f32[392,128]{1,0:T(8,128)S(1)} collective-permute-done((f32[392,128]{1,0:T(8,128)S(1)}, f32[392,128]{1,0:T(8,128)S(1)}, u32[]{:S(2)}, u32[]{:S(2)}) %collective-permute-start.5) | collective-permute-done | bytes 200736 | tf_op jit(solution)/shard_map/ppermute | solution.py:362
  25.0 1.2 %products.1 = (f32[7,192,128]{2,1,0:T(8,128)S(1)}, f32[2,128]{1,0:T(2,128)S(1)}, f32[64,128]{1,0:T(8,128)S(1)}, f32[64,128]{1,0:T(8,128)S(1)}) custom-call(f32[8,192,128]{2,1,0:T(8,128)S(1)} %bitcast.11, f32[64,128]{1,0:T(8,128)S(1)} %get-tuple-element.23.scale_ref.refs_1_, f32[8,192,128]{2,1,0:T(8,128)S(1)} %get-tuple-element.26.refs_2_, ...), custom_call_target="tpu_custom_call" | custom-call | tf_op jit(solution)/shard_map/products/pallas_call | solution.py:443
  26.2 0.0 collective-permute-done.6.refs_4_
  26.2 1.6 %collective-permute-done.7.refs_5_ = f32[128,128]{1,0:T(8,128)S(1)} collective-permute-done((f32[128,128]{1,0:T(8,128)S(1)}, f32[128,128]{1,0:T(8,128)S(1)}, u32[]{:S(2)}, u32[]{:S(2)}) %collective-permute-start.7) | collective-permute-done | bytes 65568 | tf_op jit(solution)/shard_map/ppermute | solution.py:362
  27.8 0.3 products_last.1
  28.2 13.7 %all_to_all.5.refs_0_ = f32[32,2,128]{2,1,0:T(2,128)S(1)} all-to-all(f32[32,2,128]{2,1,0:T(2,128)S(1)} %broadcast_in_dim.2), channel_id=1, replica_groups=mesh['loop'=4,'trans'=8] {'loop','trans'}, dimensions={0} | all-to-all | bytes 65536 | tf_op jit(solution)/shard_map/all_to_all | solution.py:462
  41.8 2.2 %combine.1 = (f32[8,192,128]{2,1,0:T(8,128)}, f32[8,8]{1,0:T(8,128)}, f32[8,8]{1,0:T(8,128)}) custom-call(f32[32,2,128]{2,1,0:T(2,128)S(1)} %all_to_all.5.refs_0_, f32[8,192,128]{2,1,0:T(8,128)S(1)} %bitcast.13, f32[7,192,128]{2,1,0:T(8,128)S(1)} %get-tuple-element.37.refs_8_.refs_2_, f32[1,192,128]{2,1,0:T(8,128)S(1)} %get-tuple-element.39.refs_3_), custom_call_target="tpu_custom_call" | custom-call | tf_op jit(solution)/shard_map/combine/pallas_call | solution.py:464
  (1 shorter events, 0.0 us)
Async XLA Ops:
  0.6 5.4 %copy-start = (f32[8,3,64,1,128]{4,3,2,1,0:T(1,128)S(1)}, f32[8,3,64,1,128]{4,3,2,1,0:T(1,128)}, u32[]{:S(2)}) copy-start(f32[8,3,64,1,128]{4,3,2,1,0:T(1,128)} %param.5) | copy-start | bytes 2359300
  2.0 14.2 %collective-permute-start.2 = (f32[512,128]{1,0:T(8,128)S(1)}, f32[512,128]{1,0:T(8,128)S(1)}, u32[]{:S(2)}, u32[]{:S(2)}) collective-permute-start(f32[512,128]{1,0:T(8,128)S(1)} %get-tuple-element.28), channel_id=1, source_target_pairs={{0,8},{8,16},{16,24},{24,0},{1,9},{9,17},{17,25},{25,1},{2,10},{10... | collective-permute-start | bytes 786440 | tf_op jit(solution)/shard_map/ppermute | solution.py:362
  5.0 13.1 %collective-permute-start.3 = (f32[512,128]{1,0:T(8,128)S(1)}, f32[512,128]{1,0:T(8,128)S(1)}, u32[]{:S(2)}, u32[]{:S(2)}) collective-permute-start(f32[512,128]{1,0:T(8,128)S(1)} %get-tuple-element.29), channel_id=1, source_target_pairs={{0,24},{8,0},{16,8},{24,16},{1,25},{9,1},{17,9},{25,17},{2,26},{10... | collective-permute-start | bytes 786440 | tf_op jit(solution)/shard_map/ppermute | solution.py:362
  6.5 2.8 %collective-permute-start = (f32[64,128]{1,0:T(8,128)S(1)}, f32[64,128]{1,0:T(8,128)S(1)}, u32[]{:S(2)}, u32[]{:S(2)}) collective-permute-start(f32[64,128]{1,0:T(8,128)S(1)} %get-tuple-element.24), channel_id=1, source_target_pairs={{0,1},{1,2},{2,3},{3,4},{4,5},{5,6},{6,7},{8,9},{9,10},{10,11},{11... | collective-permute-start | bytes 98312 | tf_op jit(solution)/shard_map/ppermute | solution.py:360
  8.0 5.2 %collective-permute-start.1 = (f32[64,128]{1,0:T(8,128)S(1)}, f32[64,128]{1,0:T(8,128)S(1)}, u32[]{:S(2)}, u32[]{:S(2)}) collective-permute-start(f32[64,128]{1,0:T(8,128)S(1)} %get-tuple-element.25), channel_id=1, source_target_pairs={{1,0},{2,1},{3,2},{4,3},{5,4},{6,5},{7,6},{9,8},{10,9},{11,10},{12... | collective-permute-start | bytes 98312 | tf_op jit(solution)/shard_map/ppermute | solution.py:360
  13.2 8.0 %copy-start.1 = (f32[8,3,64,1,128]{4,3,2,1,0:T(1,128)S(1)}, f32[8,3,64,1,128]{4,3,2,1,0:T(1,128)}, u32[]{:S(2)}) copy-start(f32[8,3,64,1,128]{4,3,2,1,0:T(1,128)} %param.6) | copy-start | bytes 2359300
  13.2 10.5 %collective-permute-start.4 = (f32[392,128]{1,0:T(8,128)S(1)}, f32[392,128]{1,0:T(8,128)S(1)}, u32[]{:S(2)}, u32[]{:S(2)}) collective-permute-start(f32[392,128]{1,0:T(8,128)S(1)} %get-tuple-element.30), channel_id=1, source_target_pairs={{0,8},{8,16},{16,24},{24,0},{1,9},{9,17},{17,25},{25,1},{2,10},{10... | collective-permute-start | bytes 602120 | tf_op jit(solution)/shard_map/ppermute | solution.py:362
  13.9 11.1 %collective-permute-start.5 = (f32[392,128]{1,0:T(8,128)S(1)}, f32[392,128]{1,0:T(8,128)S(1)}, u32[]{:S(2)}, u32[]{:S(2)}) collective-permute-start(f32[392,128]{1,0:T(8,128)S(1)} %get-tuple-element.31), channel_id=1, source_target_pairs={{0,24},{8,0},{16,8},{24,16},{1,25},{9,1},{17,9},{25,17},{2,26},{10... | collective-permute-start | bytes 602120 | tf_op jit(solution)/shard_map/ppermute | solution.py:362
  18.2 3.0 %copy-start.2 = (f32[8,8]{1,0:T(8,128)S(1)}, f32[8,8]{1,0:T(8,128)}, u32[]{:S(2)}) copy-start(f32[8,8]{1,0:T(8,128)} %coup_ref.1) | copy-start | bytes 772
  18.2 8.0 %collective-permute-start.6 = (f32[128,128]{1,0:T(8,128)S(1)}, f32[128,128]{1,0:T(8,128)S(1)}, u32[]{:S(2)}, u32[]{:S(2)}) collective-permute-start(f32[128,128]{1,0:T(8,128)S(1)} %get-tuple-element.33), channel_id=1, source_target_pairs={{0,8},{8,16},{16,24},{24,0},{1,9},{9,17},{17,25},{25,1},{2,10},{10... | collective-permute-start | bytes 196616 | tf_op jit(solution)/shard_map/ppermute | solution.py:362
  19.8 8.1 %collective-permute-start.7 = (f32[128,128]{1,0:T(8,128)S(1)}, f32[128,128]{1,0:T(8,128)S(1)}, u32[]{:S(2)}, u32[]{:S(2)}) collective-permute-start(f32[128,128]{1,0:T(8,128)S(1)} %get-tuple-element.34), channel_id=1, source_target_pairs={{0,24},{8,0},{16,8},{24,16},{1,25},{9,1},{17,9},{25,17},{2,26},{10... | collective-permute-start | bytes 196616 | tf_op jit(solution)/shard_map/ppermute | solution.py:362

commit v6 on v5

--- a/solution.py
+++ b/solution.py
@@ -39,25 +39,22 @@
 
 def packed(v_ref, b, scale, fwd_ref, bwd_ref, at):
     nz = scale.shape[0]
-    lane = lane_ids(scale.shape)
-    last = scale.shape[1] - 1
     uz = v_ref[b, pl.ds(0, nz), :] * scale
     up = v_ref[b, pl.ds(nz, nz), :] * scale
     ut = v_ref[b, pl.ds(2 * nz, nz), :] * scale
     one, two = pl.ds(at * nz, nz), pl.ds((at + 1) * nz, nz)
     bwd_ref[one, :] = uz
     bwd_ref[two, :] = ut
-    fwd_ref[one, :] = uz + (z_next(up) - up)
-    fwd_ref[two, :] = ut + (jnp.where(lane == last, 0.0, roll_by(up, -1, 1)) - up)
-
-
-def first_kernel(v_hbm, mat_hbm, eps_hbm, fwd_ref, bwd_ref, scale_ref, v_ref, mat_ref, eps_ref, sems):
-    count = v_ref.shape[0]
+    fwd_ref[one, :], fwd_ref[two, :] = forward_pair(uz, up, ut)
+
+
+def first_kernel(cuts, v_hbm, mat_hbm, eps_hbm, *refs):
+    outs, (scale_ref, v_ref, mat_ref, eps_ref, sems) = refs[: len(cuts)], refs[len(cuts) :]
     copies = [
         pltpu.make_async_copy(eps_hbm, eps_ref, sems.at[0]),
         pltpu.make_async_copy(mat_hbm, mat_ref, sems.at[1]),
     ]
-    for b in range(count):
+    for b in range(v_ref.shape[0]):
         copies.append(pltpu.make_async_copy(v_hbm.at[b], v_ref.at[b], sems.at[2 + b]))
     for copy in copies:
         copy.start()
@@ -65,9 +62,13 @@
     copies[1].wait()
     scale = cell_scale(mat_ref[...], eps_ref)
     scale_ref[...] = scale
-    for b in range(count):
-        copies[2 + b].wait()
-        packed(v_ref, b, scale, fwd_ref, bwd_ref, 2 * b)
+    nz = scale.shape[0]
+    for (begin, end), out_ref in zip(cuts, outs):
+        for b in range(begin, end):
+            copies[2 + b].wait()
+            for c in range(3):
+                rows = pl.ds((3 * (b - begin) + c) * nz, nz)
+                out_ref[rows, :] = v_ref[b, pl.ds(c * nz, nz), :] * scale
 
 
 def edge_kernel(v_ref, scale_ref, right_ref, left_ref):
@@ -91,20 +92,60 @@
     return jnp.concatenate([x, pad], axis=0).T
 
 
-def corner_kernel(begin, end, v_ref, scale_ref, fr_ref, fl_ref, fwd_ref, bwd_ref):
+def forward_pair(uz, up, ut):
+    lane = lane_ids(up.shape)
+    up_next = jnp.where(lane == up.shape[1] - 1, 0.0, roll_by(up, -1, 1))
+    return uz + (z_next(up) - up), ut + (up_next - up)
+
+
+def odd_loop():
+    return lax.rem(lax.axis_index("loop"), 2) == 1
+
+
+def relay_kernel(nz, x_ref, *refs):
+    y_ref = refs[-1]
+    odd = odd_loop()
+    count = x_ref.shape[0] // (3 * nz)
+
+    def comps(m):
+        return [x_ref[pl.ds((3 * m + c) * nz, nz), :] for c in range(3)]
+
+    def store(m, pair):
+        y_ref[pl.ds(2 * m * nz, nz), :] = pair[0]
+        y_ref[pl.ds((2 * m + 1) * nz, nz), :] = pair[1]
+
+    @pl.when(odd)
+    def _():
+        for m in range(count):
+            store(m, comps(m)[::2])
+
+    @pl.when(jnp.logical_not(odd))
+    def _():
+        for m in range(count):
+            store(m, forward_pair(*comps(m)))
+
+
+def direct_kernel(begin, end, v_ref, scale_ref, fr_ref, fl_ref, fwd_ref, bwd_ref):
+    nb = v_ref.shape[0]
     scale = scale_ref[...]
     for b in range(begin, end):
         packed(v_ref, b, scale, fwd_ref, bwd_ref, 2 * (b - begin))
-    nb = v_ref.shape[0]
     rows = pl.ds(2 * (end - begin) * scale.shape[0], nb)
     fwd_ref[rows, :] = turned(fl_ref[...])[nb : 2 * nb, :]
     bwd_ref[rows, :] = turned(fr_ref[...])[2 * nb : 3 * nb, :]
 
 
-def more_kernel(begin, end, v_ref, scale_ref, fwd_a_ref, bwd_a_ref, fwd_ref, bwd_ref):
-    scale = scale_ref[...]
-    for b in range(begin, end):
-        packed(v_ref, b, scale, fwd_ref, bwd_ref, 2 * (b - begin))
+def column_rows(block, count, nz, nt):
+    lane = lane_ids((nz, nt))
+    first = last = jnp.zeros((nz, nt), jnp.float32)
+    for b in range(count):
+        first = jnp.where(lane == b, roll_by(block(b, 1), b, 1), first)
+        last = jnp.where(lane == b, roll_by(block(b, 2), b + 1, 1), last)
+    return side_by_side(turned(first)[:8, :], turned(last)[:8, :], nz)
+
+
+def side_by_side(first, last, nz):
+    return first + roll_by(last, nz, 1)
 
 
 def merge(a, b, dist):
@@ -205,47 +246,95 @@
     store_pays(pay_ref, add_products(pairs, v_ref.shape[1] // 8, 36, [zero, zero]))
 
 
-def sum_kernel(cuts, begin, v_ref, scale_ref, l_ref, pay_in_ref, *refs):
+def works_of(b, pairs, l_ref, scale, w_ref, to, columns=None):
+    nz, nt = scale.shape
+    lane = lane_ids(scale.shape)
+    za, tb, uz, ut = pairs
+    ut_prev = roll_by(ut, 1, 1)
+    if columns is None:
+        ut_prev = jnp.where(lane == 0, 0.0, ut_prev)
+    else:
+        edge_f, edge_b = columns[0], columns[1]
+        ut_prev = jnp.where(lane == 0, roll_by(edge_b, -b, 1), ut_prev)
+        tb = tb + jnp.where(lane == nt - 1, roll_by(edge_f, nt - 1 - b, 1), 0.0)
+    w_ref[to, pl.ds(0, nz), :] = l_ref[b, pl.ds(0, nz), :] - scale * (za + uz)
+    div = (uz - z_prev(uz)) + (ut - ut_prev)
+    w_ref[to, pl.ds(nz, nz), :] = l_ref[b, pl.ds(nz, nz), :] + scale * div
+    w_ref[to, pl.ds(2 * nz, nz), :] = l_ref[b, pl.ds(2 * nz, nz), :] - scale * (tb + ut)
+
+
+def product_pairs(v_ref, ws, begin, end):
     nb = v_ref.shape[0]
-    nz, nt = scale_ref.shape
-    end = cuts[-1][1]
-    halos = refs[: 2 * len(cuts)]
-    corners = refs[2 * len(cuts) : 2 * len(cuts) + 2]
-    if begin == 0:
-        w_ref, pay_ref, columns_f_ref, columns_b_ref = refs[-4:]
-        for corner, columns_ref in zip(corners, (columns_f_ref, columns_b_ref)):
-            columns_ref[...] = turned(corner[pl.ds(corner.shape[0] - nb, nb), :])[:nz, :]
-    else:
-        columns_f_ref, columns_b_ref = corners
-        old, w_ref, pay_ref = refs[-3:]
-    columns_f, columns_b = columns_f_ref[...], columns_b_ref[...]
-    scale = scale_ref[...]
-    lane = lane_ids(scale.shape)
-    for i, (low, high) in enumerate(cuts):
-        fwd_ref, bwd_ref = halos[2 * i : 2 * i + 2]
-
-        for m in range(high - low):
-            b = low + m
-            one, two = pl.ds(2 * m * nz, nz), pl.ds((2 * m + 1) * nz, nz)
-            za, tb = fwd_ref[one, :], fwd_ref[two, :]
-            uz, ut = bwd_ref[one, :], bwd_ref[two, :]
-            edge_b = roll_by(columns_b, -b, 1)
-            edge_f = roll_by(columns_f, nt - 1 - b, 1)
-            ut_prev = jnp.where(lane == 0, edge_b, roll_by(ut, 1, 1))
-            tb = tb + jnp.where(lane == nt - 1, edge_f, 0.0)
-            to = b - begin
-            w_ref[to, pl.ds(0, nz), :] = l_ref[b, pl.ds(0, nz), :] - scale * (za + uz)
-            div = (uz - z_prev(uz)) + (ut - ut_prev)
-            w_ref[to, pl.ds(nz, nz), :] = l_ref[b, pl.ds(nz, nz), :] + scale * div
-            w_ref[to, pl.ds(2 * nz, nz), :] = l_ref[b, pl.ds(2 * nz, nz), :] - scale * (tb + ut)
-
-    ws = [(old, b) for b in range(begin)] + [(w_ref, b - begin) for b in range(begin, end)]
     pairs = []
     for b in range(begin, end):
         pairs += [(v_ref, j, *ws[b], {(0, nb * j + b), (1, nb * nb + nb * b + j)}) for j in range(nb)]
         pairs += [(*ws[j], *ws[b], {(0, nb * nb + nb * j + b), (0, nb * nb + nb * b + j)}) for j in range(b + 1)]
+    return pairs
+
+
+def relayed_kernel(cuts, v_ref, scale_ref, l_ref, pay_in_ref, *refs):
+    halos, (w_ref, pay_ref, cols_ref) = refs[:-3], refs[-3:]
+    nb = v_ref.shape[0]
+    nz, nt = scale_ref.shape
+    end = cuts[-1][1]
+    scale = scale_ref[...]
+    odd = odd_loop()
+    for i, (low, high) in enumerate(cuts):
+        x_ref, y_ref = halos[2 * i : 2 * i + 2]
+        for m in range(high - low):
+            xz, xp, xt = (x_ref[pl.ds((3 * m + c) * nz, nz), :] for c in range(3))
+            y0, y1 = (y_ref[pl.ds((2 * m + c) * nz, nz), :] for c in range(2))
+            f0, f1 = forward_pair(xz, xp, xt)
+            pairs = (
+                jnp.where(odd, f0, y0), jnp.where(odd, f1, y1), jnp.where(odd, y0, xz), jnp.where(odd, y1, xt)
+            )
+            works_of(low + m, pairs, l_ref, scale, w_ref, low + m)
     zero = jnp.zeros((8, nt), jnp.float32)
+    pairs = product_pairs(v_ref, [(w_ref, b) for b in range(end)], 0, end)
     store_pays(pay_ref, add_products(pairs, v_ref.shape[1] // 8, 42, [zero, zero]), pay_in_ref)
+    cols_ref[0:8, :] = column_rows(lambda b, c: v_ref[b, pl.ds(c * nz, nz), :], nb, nz, nt)
+    cols_ref[8:16, :] = column_rows(lambda b, c: w_ref[b, pl.ds(c * nz, nz), :], end, nz, nt)
+    turned_scale = turned(scale)
+    scale_row = side_by_side(turned_scale[0:1, :], turned_scale[nt - 1 : nt, :], nz)
+    cols_ref[16:24, :] = jnp.broadcast_to(scale_row, (8, nt))
+
+
+def direct_sum_kernel(begin, end, v_ref, scale_ref, l_ref, pay_in_ref, fwd_ref, bwd_ref, old_ref, cols_ref, w0_ref, w_ref, pay_ref):
+    nb = v_ref.shape[0]
+    nz, nt = scale_ref.shape
+    scale = scale_ref[...]
+    lane = lane_ids(scale.shape)
+    rows = pl.ds(fwd_ref.shape[0] - nb, nb)
+    rows_f, rows_b = fwd_ref[rows, :], bwd_ref[rows, :]
+    columns = (turned(rows_f)[:nz, :], turned(rows_b)[:nz, :])
+    scale_first = jnp.broadcast_to(scale[:, 0:1], scale.shape)
+    scale_last = jnp.broadcast_to(scale[:, nt - 1 : nt], scale.shape)
+    add_f, add_b = scale_last * columns[0], scale_first * columns[1]
+    for b in range(begin):
+        w0_ref[b, pl.ds(0, nz), :] = old_ref[b, pl.ds(0, nz), :]
+        first = jnp.where(lane == 0, roll_by(add_b, -b, 1), 0.0)
+        w0_ref[b, pl.ds(nz, nz), :] = old_ref[b, pl.ds(nz, nz), :] - first
+        last = jnp.where(lane == nt - 1, roll_by(add_f, nt - 1 - b, 1), 0.0)
+        w0_ref[b, pl.ds(2 * nz, nz), :] = old_ref[b, pl.ds(2 * nz, nz), :] - last
+    for b in range(begin, end):
+        m = b - begin
+        za, tb = (fwd_ref[pl.ds((2 * m + c) * nz, nz), :] for c in range(2))
+        uz, ut = (bwd_ref[pl.ds((2 * m + c) * nz, nz), :] for c in range(2))
+        works_of(b, (za, tb, uz, ut), l_ref, scale, w_ref, m, columns)
+    zero = jnp.zeros((8, nt), jnp.float32)
+    ws = [(w0_ref, b) for b in range(begin)] + [(w_ref, b - begin) for b in range(begin, end)]
+    pays = add_products(product_pairs(v_ref, ws, begin, end), v_ref.shape[1] // 8, 45, [zero, zero])
+    row, col = row_ids((8, nt)), lane_ids((8, nt))
+    v_cols, w_cols, scale_cols = cols_ref[0:8, :], cols_ref[8:16, :], cols_ref[16:24, :]
+    delta = jnp.where(row < begin, -scale_cols * side_by_side(rows_b, rows_f, nz), 0.0)
+    fixed = w_cols + delta
+    for b in range(begin):
+        proj = jnp.sum(v_cols * row_at(delta, b), axis=1, keepdims=True)
+        pays[0] = pays[0] + jnp.where(col == nb * row + b, proj, 0.0)
+        pays[1] = pays[1] + jnp.where(col == nb * nb + nb * b + row, proj, 0.0)
+        work = jnp.sum(fixed * row_at(fixed, b) - w_cols * row_at(w_cols, b), axis=1, keepdims=True)
+        pays[0] = pays[0] + jnp.where(col == nb * nb + nb * row + b, work, 0.0)
+    store_pays(pay_ref, pays, pay_in_ref)
 
 
 def lane_at(x, k):
@@ -362,6 +451,15 @@
     return lax.ppermute(x, "loop", [(i, (i + loop_by) % count) for i in range(count)])
 
 
+def swap(x):
+    return lax.ppermute(x, "loop", [(i, i ^ 1) for i in range(lax.axis_size("loop"))])
+
+
+def relay(x):
+    count = lax.axis_size("loop")
+    return lax.ppermute(x, "loop", [(i, (i + (-2 if i % 2 else 2)) % count) for i in range(count)])
+
+
 def local(block_now, block_prev, coupling_prev, material, permittivity):
     nb, nc, nz, _, nt = block_now.shape
     f32 = jnp.float32
@@ -376,7 +474,8 @@
     free = pl.CostEstimate(flops=0, bytes_accessed=0, transcendentals=0)
     plane = jax.ShapeDtypeStruct((nz, nt), f32)
     pay_shape = jax.ShapeDtypeStruct((2, nt), f32)
-    cut_a, cut_b, cut_c = (0, nb // 2), (nb // 2, nb - 1), (nb - 1, nb)
+    assert lax.axis_size("loop") % 2 == 0
+    cut_a, cut_b, cut_c = (0, nb * 3 // 8), (nb * 3 // 8, nb * 5 // 8), (nb * 5 // 8, nb)
 
     def planes(n, more=0):
         return jax.ShapeDtypeStruct((n * nz + more, nt), f32)
@@ -384,23 +483,23 @@
     def works(n):
         return jax.ShapeDtypeStruct((n, nc * nz, nt), f32)
 
-    size_a, size_b, size_c = (2 * (c[1] - c[0]) for c in (cut_a, cut_b, cut_c))
-    fwd_a, bwd_a, scale = pl.pallas_call(
-        first_kernel,
-        out_shape=(planes(size_a), planes(size_a), plane),
+    size_a, size_b, size_c = (c[1] - c[0] for c in (cut_a, cut_b, cut_c))
+    x_a, x_b, scale = pl.pallas_call(
+        lambda *refs: first_kernel((cut_a, cut_b), *refs),
+        out_shape=(planes(3 * size_a), planes(3 * size_b), plane),
         in_specs=[hbm] * 3,
         out_specs=(vm,) * 3,
         scratch_shapes=[
-            VM((cut_a[1], nc * nz, nt), f32),
+            VM((cut_b[1], nc * nz, nt), f32),
             VM((nz, nt), jnp.int32),
             SM(permittivity.shape, f32),
-            pltpu.SemaphoreType.DMA((2 + cut_a[1],)),
+            pltpu.SemaphoreType.DMA((2 + cut_b[1],)),
         ],
         compiler_params=params,
         cost_estimate=free,
         name="first",
     )(*(pltpu.with_memory_space_constraint(x, pltpu.HBM) for x in (v, mat, permittivity)))
-    fwd_a, bwd_a = shift(fwd_a, 1, 0), shift(bwd_a, -1, 0)
+    x_a, x_b = swap(x_a), swap(x_b)
     right, left = pl.pallas_call(
         edge_kernel,
         out_shape=(plane, plane),
@@ -411,26 +510,32 @@
         name="edges",
     )(v, scale)
     from_left, from_right = shift(right, 0, 1), shift(left, 0, -1)
-    fwd_b, bwd_b = pl.pallas_call(
-        lambda *refs: corner_kernel(*cut_b, *refs),
-        out_shape=(planes(size_b, nb), planes(size_b, nb)),
+
+    def relay_pair(x, size, name, *after):
+        return relay(
+            pl.pallas_call(
+                lambda *refs: relay_kernel(nz, *refs),
+                out_shape=planes(2 * size),
+                in_specs=[vm] * (1 + len(after)),
+                out_specs=vm,
+                compiler_params=params,
+                cost_estimate=free,
+                name=name,
+            )(x, *after)
+        )
+
+    y_a = relay_pair(x_a, size_a, "relay_a", right, left)
+    own_f, own_b = pl.pallas_call(
+        lambda *refs: direct_kernel(*cut_c, *refs),
+        out_shape=(planes(2 * size_c, nb), planes(2 * size_c, nb)),
         in_specs=[vm] * 4,
         out_specs=(vm, vm),
         compiler_params=params,
         cost_estimate=free,
-        name="pack_b",
+        name="direct",
     )(v, scale, from_left, from_right)
-    fwd_b, bwd_b = shift(fwd_b, 1, 0), shift(bwd_b, -1, 0)
-    fwd_c, bwd_c = pl.pallas_call(
-        lambda *refs: more_kernel(*cut_c, *refs),
-        out_shape=(planes(size_c), planes(size_c)),
-        in_specs=[vm, vm, hbm, hbm],
-        out_specs=(vm, vm),
-        compiler_params=params,
-        cost_estimate=free,
-        name="pack_c",
-    )(v, scale, fwd_a, bwd_a)
-    fwd_c, bwd_c = shift(fwd_c, 1, 0), shift(bwd_c, -1, 0)
+    fwd_c, bwd_c = shift(own_f, 1, 0), shift(own_b, -1, 0)
+    y_b = relay_pair(x_b, size_b, "relay_b", own_f, own_b)
     inner, pay = pl.pallas_call(
         inner_kernel,
         out_shape=(works(nb), pay_shape),
@@ -440,24 +545,24 @@
         cost_estimate=free,
         name="inner",
     )(coupling_prev, v, scale, q, from_left, from_right)
-    w_ab, pay, columns_f, columns_b = pl.pallas_call(
-        lambda *refs: sum_kernel((cut_a, cut_b), 0, *refs),
-        out_shape=(works(cut_b[1]), pay_shape, plane, plane),
-        in_specs=[vm] * 10,
-        out_specs=(vm,) * 4,
+    w_ab, pay, cols = pl.pallas_call(
+        lambda *refs: relayed_kernel((cut_a, cut_b), *refs),
+        out_shape=(works(cut_b[1]), pay_shape, jax.ShapeDtypeStruct((24, nt), f32)),
+        in_specs=[vm] * 8,
+        out_specs=(vm,) * 3,
         compiler_params=params,
         cost_estimate=free,
         name="products",
-    )(v, scale, inner, pay, fwd_a, bwd_a, fwd_b, bwd_b, fwd_b, bwd_b)
-    w_c, pay = pl.pallas_call(
-        lambda *refs: sum_kernel((cut_c,), cut_c[0], *refs),
-        out_shape=(works(cut_c[1] - cut_c[0]), pay_shape),
-        in_specs=[vm] * 9,
-        out_specs=(vm, vm),
+    )(v, scale, inner, pay, x_a, y_a, x_b, y_b)
+    w_ab, w_c, pay = pl.pallas_call(
+        lambda *refs: direct_sum_kernel(*cut_c, *refs),
+        out_shape=(works(cut_b[1]), works(size_c), pay_shape),
+        in_specs=[vm] * 8,
+        out_specs=(vm,) * 3,
         compiler_params=params,
         cost_estimate=free,
         name="products_last",
-    )(v, scale, inner, pay, fwd_c, bwd_c, columns_f, columns_b, w_ab)
+    )(v, scale, inner, pay, fwd_c, bwd_c, w_ab, cols)
     pay = jnp.broadcast_to(pay[None], (devices, 2, nt))
     pay = lax.all_to_all(pay, ("loop", "trans"), 0, 0)
     small = jax.ShapeDtypeStruct((nb, nb), f32)

time: 44.2 us -> 46.4 us (1.050)
  waiting for transfers between devices: 8.58 us -> 11.8 us
  starting transfers between devices: 12.7 us -> 11.4 us
  Pallas kernels: 8.27 us -> 9.01 us
  blocking collectives: 13.7 us -> 13.2 us
    ppermute x0 -> x4, waiting for transfers between devices: none -> 7.88 us  [the longest x2 7.87 us: relay(): lax.ppermute(x, 'loop', [(i, (i + (-2 if i % 2 else 2)) % count) for i in...]
    ppermute x6 -> x2, starting transfers between devices: 9.97 us -> 2.98 us  [shift(): lax.ppermute(x, 'loop', [(i, (i + loop_by) % count) for i in range(count)])]
    ppermute x0 -> x4, starting transfers between devices: none -> 5.71 us  [the longest x2 3.08 us: swap(): lax.ppermute(x, 'loop', [(i, i ^ 1) for i in range(lax.axis_size('loop'))])]
    ppermute x6 -> x2, waiting for transfers between devices: 4.73 us -> 0.01 us  [shift(): lax.ppermute(x, 'loop', [(i, (i + loop_by) % count) for i in range(count)])]
    pallas_call x5 -> x6, Pallas kernels: 3.06 us -> 3.73 us  [the longest x1 1.28 us: local(): pl.pallas_call(lambda *refs: relayed_kernel((cut_a, cut_b), *refs), out_s...]
  transfers between devices with their start and end apart: 8 -> 8, of which waited for: 4 -> 2; matrix products, arithmetic and copies ran while one was open for 0% -> 0% of each run, Pallas kernels for 10% -> 10%
where the time goes in v6:
time: 46.4 us; the launch traced here: 46.2 us
  blocking collectives  13.2 us (28%)
  waiting for transfers between devices  11.8 us (25%)
  starting transfers between devices  11.4 us (25%)
  Pallas kernels  9.01 us (19%)
  between operations  0.72 us (2%)
    all_to_all x1, blocking collectives, local(): pay = lax.all_to_all(pay, ('loop', 'trans'), 0, 0)  13.2 us
    ppermute x2, waiting for transfers between devices, relay(): lax.ppermute(x, 'loop', [(i, (i + (-2 if i % 2 else 2)) % count) for i in...  7.87 us
    ppermute x2, waiting for transfers between devices, shift(): lax.ppermute(x, 'trans', [(t, t + trans_by) for t in range(count) if 0 <=...  3.89 us
    ppermute x2, starting transfers between devices, swap(): lax.ppermute(x, 'loop', [(i, i ^ 1) for i in range(lax.axis_size('loop'))])  3.08 us
    ppermute x2, starting transfers between devices, shift(): lax.ppermute(x, 'loop', [(i, (i + loop_by) % count) for i in range(count)])  2.98 us
    ppermute x2, starting transfers between devices, shift(): lax.ppermute(x, 'trans', [(t, t + trans_by) for t in range(count) if 0 <=...  2.75 us
    ppermute x2, starting transfers between devices, relay(): lax.ppermute(x, 'loop', [(i, (i + (-2 if i % 2 else 2)) % count) for i in...  2.63 us
    pallas_call x1, Pallas kernels, local(): pl.pallas_call(inner_kernel, out_shape=(works(nb), pay_shape), in_specs=[...  2.63 us
  transfers between devices with their start and end apart: 8, of which 2 were waited for; matrix products, arithmetic and copies ran while one was open for 0% of the time, Pallas kernels for 10%

profile of v6, /device:TPU:0, one launch (start us, length us, event | category | flops | bytes accessed | tf_op | source)
XLA Modules:
  0.0 46.2 jit_solution(17422103235114051351)
XLA Ops:
  0.6 0.0 copy-start
  0.6 1.2 %first.1 = (f32[576,128]{1,0:T(8,128)S(1)}, f32[384,128]{1,0:T(8,128)S(1)}, f32[64,128]{1,0:T(8,128)S(1)}) custom-call(f32[8,192,128]{2,1,0:T(8,128)} %bitcast.6, s32[64,128]{1,0:T(8,128)} %bitcast.14, f32[4]{0:T(128)} %refs_2_.1), custom_call_target="tpu_custom_call" | custom-call | tf_op jit(solution)/shard_map/first/pallas_call | solution.py:487
  1.9 3.0 %collective-permute-start.2 = (f32[576,128]{1,0:T(8,128)S(1)}, f32[576,128]{1,0:T(8,128)S(1)}, u32[]{:S(2)}, u32[]{:S(2)}) collective-permute-start(f32[576,128]{1,0:T(8,128)S(1)} %get-tuple-element.26), channel_id=1, source_target_pairs={{0,8},{8,0},{16,24},{24,16},{1,9},{9,1},{17,25},{25,17},{2,10},{10... | collective-permute-start | bytes 884744 | tf_op jit(solution)/shard_map/ppermute | solution.py:455
  4.9 0.1 collective-permute-start.4
  5.0 0.0 copy-done
  5.0 0.5 %edges.1 = (f32[64,128]{1,0:T(8,128)S(1)}, f32[64,128]{1,0:T(8,128)S(1)}) custom-call(f32[8,192,128]{2,1,0:T(8,128)S(1)} %bitcast.7, f32[64,128]{1,0:T(8,128)S(1)} %get-tuple-element.21.scale_ref.refs_1_), custom_call_target="tpu_custom_call" | custom-call | tf_op jit(solution)/shard_map/edges/pallas_call | solution.py:503
  5.5 1.5 %collective-permute-start = (f32[64,128]{1,0:T(8,128)S(1)}, f32[64,128]{1,0:T(8,128)S(1)}, u32[]{:S(2)}, u32[]{:S(2)}) collective-permute-start(f32[64,128]{1,0:T(8,128)S(1)} %get-tuple-element.22.refs_1_), channel_id=1, source_target_pairs={{0,1},{1,2},{2,3},{3,4},{4,5},{5,6},{6,7},{8,9},{9,10},{10,11},{11... | collective-permute-start | bytes 98312 | tf_op jit(solution)/shard_map/ppermute | solution.py:449
  6.9 1.3 %collective-permute-start.1 = (f32[64,128]{1,0:T(8,128)S(1)}, f32[64,128]{1,0:T(8,128)S(1)}, u32[]{:S(2)}, u32[]{:S(2)}) collective-permute-start(f32[64,128]{1,0:T(8,128)S(1)} %get-tuple-element.23.refs_2_), channel_id=1, source_target_pairs={{1,0},{2,1},{3,2},{4,3},{5,4},{6,5},{7,6},{9,8},{10,9},{11,10},{12... | collective-permute-start | bytes 98312 | tf_op jit(solution)/shard_map/ppermute | solution.py:449
  8.2 0.0 collective-permute-done.fr_ref.refs_2_
  8.2 3.9 %collective-permute-done.1.fl_ref.refs_3_ = f32[64,128]{1,0:T(8,128)S(1)} collective-permute-done((f32[64,128]{1,0:T(8,128)S(1)}, f32[64,128]{1,0:T(8,128)S(1)}, u32[]{:S(2)}, u32[]{:S(2)}) %collective-permute-start.1) | collective-permute-done | bytes 32800 | tf_op jit(solution)/shard_map/ppermute | solution.py:449
  12.1 0.1 direct.1
  12.2 0.0 copy-start.1
  12.2 1.5 %collective-permute-start.6 = (f32[392,128]{1,0:T(8,128)S(1)}, f32[392,128]{1,0:T(8,128)S(1)}, u32[]{:S(2)}, u32[]{:S(2)}) collective-permute-start(f32[392,128]{1,0:T(8,128)S(1)} %get-tuple-element.28.refs_1_), channel_id=1, source_target_pairs={{0,8},{8,16},{16,24},{24,0},{1,9},{9,17},{17,25},{25,1},{2,10},{10... | collective-permute-start | bytes 602120 | tf_op jit(solution)/shard_map/ppermute | solution.py:451
  13.8 1.4 %collective-permute-start.7 = (f32[392,128]{1,0:T(8,128)S(1)}, f32[392,128]{1,0:T(8,128)S(1)}, u32[]{:S(2)}, u32[]{:S(2)}) collective-permute-start(f32[392,128]{1,0:T(8,128)S(1)} %get-tuple-element.29.refs_2_), channel_id=1, source_target_pairs={{0,24},{8,0},{16,8},{24,16},{1,25},{9,1},{17,9},{25,17},{2,26},{10... | collective-permute-start | bytes 602120 | tf_op jit(solution)/shard_map/ppermute | solution.py:451
  15.2 0.0 collective-permute-done.2.refs_0_.refs_4_
  15.2 0.1 relay_a.1
  15.3 1.6 %collective-permute-start.3 = (f32[384,128]{1,0:T(8,128)S(1)}, f32[384,128]{1,0:T(8,128)S(1)}, u32[]{:S(2)}, u32[]{:S(2)}) collective-permute-start(f32[384,128]{1,0:T(8,128)S(1)} %relay_a.1), channel_id=1, source_target_pairs={{0,16},{8,24},{16,0},{24,8},{1,17},{9,25},{17,1},{25,9},{2,18},{10... | collective-permute-start | bytes 589832 | tf_op jit(solution)/shard_map/ppermute | solution.py:460
  16.9 0.0 collective-permute-done.4.refs_0_.refs_6_
  16.9 0.0 copy-start.2
  16.9 0.1 relay_b.1
  17.0 1.0 %collective-permute-start.5 = (f32[256,128]{1,0:T(8,128)S(1)}, f32[256,128]{1,0:T(8,128)S(1)}, u32[]{:S(2)}, u32[]{:S(2)}) collective-permute-start(f32[256,128]{1,0:T(8,128)S(1)} %relay_b.1), channel_id=1, source_target_pairs={{0,16},{8,24},{16,0},{24,8},{1,17},{9,25},{17,1},{25,9},{2,18},{10... | collective-permute-start | bytes 393224 | tf_op jit(solution)/shard_map/ppermute | solution.py:460
  18.0 0.0 copy-done.1
  18.0 0.0 copy-done.2
  18.0 2.6 %inner.1 = (f32[8,192,128]{2,1,0:T(8,128)S(1)}, f32[2,128]{1,0:T(2,128)S(1)}) custom-call(f32[8,8]{1,0:T(8,128)S(1)} %copy-done.2, f32[8,192,128]{2,1,0:T(8,128)S(1)} %bitcast.9, f32[64,128]{1,0:T(8,128)S(1)} %get-tuple-element.21.scale_ref.refs_1_, f32[8,192,128]{2,1,0:T(8,128)S(1)} %bitcast.13, f32[64,128]{1,0:T(8,128)S(1)} %collective-permute-done.fr_ref.refs_2_, ...), custom_call_target="tpu_custom_call" | custom-call | tf_op jit(solution)/shard_map/inner/pallas_call | solution.py:539
  20.7 7.9 %collective-permute-done.5.refs_7_ = f32[256,128]{1,0:T(8,128)S(1)} collective-permute-done((f32[256,128]{1,0:T(8,128)S(1)}, f32[256,128]{1,0:T(8,128)S(1)}, u32[]{:S(2)}, u32[]{:S(2)}) %collective-permute-start.5) | collective-permute-done | bytes 131104 | tf_op jit(solution)/shard_map/ppermute | solution.py:460
  28.5 0.0 collective-permute-done.3.refs_5_
  28.5 1.3 %products.1 = (f32[5,192,128]{2,1,0:T(8,128)S(1)}, f32[2,128]{1,0:T(2,128)S(1)}, f32[24,128]{1,0:T(8,128)S(1)}) custom-call(f32[8,192,128]{2,1,0:T(8,128)S(1)} %bitcast.10, f32[64,128]{1,0:T(8,128)S(1)} %get-tuple-element.21.scale_ref.refs_1_, f32[8,192,128]{2,1,0:T(8,128)S(1)} %get-tuple-element.24.refs_2_, f32[2,128]{1,0:T(2,128)S(1)} %get-tuple-element.25.refs_3_, ...), custom_call_target="tpu_custom_call" | custom-call | tf_op jit(solution)/shard_map/products/pallas_call | solution.py:548
  29.8 0.0 collective-permute-done.6.refs_4_
  29.8 0.0 collective-permute-done.7.refs_5_
  29.8 0.9 %products_last.1 = (f32[5,192,128]{2,1,0:T(8,128)S(1)}, f32[3,192,128]{2,1,0:T(8,128)S(1)}, f32[2,128]{1,0:T(2,128)S(1)}) custom-call(f32[8,192,128]{2,1,0:T(8,128)S(1)} %bitcast.11, f32[64,128]{1,0:T(8,128)S(1)} %get-tuple-element.21.scale_ref.refs_1_, f32[8,192,128]{2,1,0:T(8,128)S(1)} %get-tuple-element.24.refs_2_, ...), custom_call_target="tpu_custom_call" | custom-call | tf_op jit(solution)/shard_map/products_last/pallas_call | solution.py:557
  30.8 13.2 %all_to_all.5.refs_0_ = f32[32,2,128]{2,1,0:T(2,128)S(1)} all-to-all(f32[32,2,128]{2,1,0:T(2,128)S(1)} %broadcast_in_dim.2), channel_id=1, replica_groups=mesh['loop'=4,'trans'=8] {'loop','trans'}, dimensions={0} | all-to-all | bytes 65536 | tf_op jit(solution)/shard_map/all_to_all | solution.py:567
  44.0 2.2 %combine.1 = (f32[8,192,128]{2,1,0:T(8,128)}, f32[8,8]{1,0:T(8,128)}, f32[8,8]{1,0:T(8,128)}) custom-call(f32[32,2,128]{2,1,0:T(2,128)S(1)} %all_to_all.5.refs_0_, f32[8,192,128]{2,1,0:T(8,128)S(1)} %bitcast.12, f32[5,192,128]{2,1,0:T(8,128)S(1)} %get-tuple-element.34.refs_2_, f32[3,192,128]{2,1,0:T(8,128)S(1)} %get-tuple-element.35.refs_3_), custom_call_target="tpu_custom_call" | custom-call | tf_op jit(solution)/shard_map/combine/pallas_call | solution.py:569
  (1 shorter events, 0.0 us)
Async XLA Ops:
  0.6 4.3 %copy-start = (f32[8,3,64,1,128]{4,3,2,1,0:T(1,128)S(1)}, f32[8,3,64,1,128]{4,3,2,1,0:T(1,128)}, u32[]{:S(2)}) copy-start(f32[8,3,64,1,128]{4,3,2,1,0:T(1,128)} %param.5) | copy-start | bytes 2359300
  1.9 13.3 %collective-permute-start.2 = (f32[576,128]{1,0:T(8,128)S(1)}, f32[576,128]{1,0:T(8,128)S(1)}, u32[]{:S(2)}, u32[]{:S(2)}) collective-permute-start(f32[576,128]{1,0:T(8,128)S(1)} %get-tuple-element.26), channel_id=1, source_target_pairs={{0,8},{8,0},{16,24},{24,16},{1,9},{9,1},{17,25},{25,17},{2,10},{10... | collective-permute-start | bytes 884744 | tf_op jit(solution)/shard_map/ppermute | solution.py:455
  4.9 12.0 %collective-permute-start.4 = (f32[384,128]{1,0:T(8,128)S(1)}, f32[384,128]{1,0:T(8,128)S(1)}, u32[]{:S(2)}, u32[]{:S(2)}) collective-permute-start(f32[384,128]{1,0:T(8,128)S(1)} %get-tuple-element.27), channel_id=1, source_target_pairs={{0,8},{8,0},{16,24},{24,16},{1,9},{9,1},{17,25},{25,17},{2,10},{10... | collective-permute-start | bytes 589832 | tf_op jit(solution)/shard_map/ppermute | solution.py:455
  5.5 2.8 %collective-permute-start = (f32[64,128]{1,0:T(8,128)S(1)}, f32[64,128]{1,0:T(8,128)S(1)}, u32[]{:S(2)}, u32[]{:S(2)}) collective-permute-start(f32[64,128]{1,0:T(8,128)S(1)} %get-tuple-element.22.refs_1_), channel_id=1, source_target_pairs={{0,1},{1,2},{2,3},{3,4},{4,5},{5,6},{6,7},{8,9},{9,10},{10,11},{11... | collective-permute-start | bytes 98312 | tf_op jit(solution)/shard_map/ppermute | solution.py:449
  6.9 5.2 %collective-permute-start.1 = (f32[64,128]{1,0:T(8,128)S(1)}, f32[64,128]{1,0:T(8,128)S(1)}, u32[]{:S(2)}, u32[]{:S(2)}) collective-permute-start(f32[64,128]{1,0:T(8,128)S(1)} %get-tuple-element.23.refs_2_), channel_id=1, source_target_pairs={{1,0},{2,1},{3,2},{4,3},{5,4},{6,5},{7,6},{9,8},{10,9},{11,10},{12... | collective-permute-start | bytes 98312 | tf_op jit(solution)/shard_map/ppermute | solution.py:449
  12.2 5.8 %copy-start.1 = (f32[8,3,64,1,128]{4,3,2,1,0:T(1,128)S(1)}, f32[8,3,64,1,128]{4,3,2,1,0:T(1,128)}, u32[]{:S(2)}) copy-start(f32[8,3,64,1,128]{4,3,2,1,0:T(1,128)} %param.6) | copy-start | bytes 2359300
  12.2 17.6 %collective-permute-start.6 = (f32[392,128]{1,0:T(8,128)S(1)}, f32[392,128]{1,0:T(8,128)S(1)}, u32[]{:S(2)}, u32[]{:S(2)}) collective-permute-start(f32[392,128]{1,0:T(8,128)S(1)} %get-tuple-element.28.refs_1_), channel_id=1, source_target_pairs={{0,8},{8,16},{16,24},{24,0},{1,9},{9,17},{17,25},{25,1},{2,10},{10... | collective-permute-start | bytes 602120 | tf_op jit(solution)/shard_map/ppermute | solution.py:451
  13.8 16.0 %collective-permute-start.7 = (f32[392,128]{1,0:T(8,128)S(1)}, f32[392,128]{1,0:T(8,128)S(1)}, u32[]{:S(2)}, u32[]{:S(2)}) collective-permute-start(f32[392,128]{1,0:T(8,128)S(1)} %get-tuple-element.29.refs_2_), channel_id=1, source_target_pairs={{0,24},{8,0},{16,8},{24,16},{1,25},{9,1},{17,9},{25,17},{2,26},{10... | collective-permute-start | bytes 602120 | tf_op jit(solution)/shard_map/ppermute | solution.py:451
  15.3 13.2 %collective-permute-start.3 = (f32[384,128]{1,0:T(8,128)S(1)}, f32[384,128]{1,0:T(8,128)S(1)}, u32[]{:S(2)}, u32[]{:S(2)}) collective-permute-start(f32[384,128]{1,0:T(8,128)S(1)} %relay_a.1), channel_id=1, source_target_pairs={{0,16},{8,24},{16,0},{24,8},{1,17},{9,25},{17,1},{25,9},{2,18},{10... | collective-permute-start | bytes 589832 | tf_op jit(solution)/shard_map/ppermute | solution.py:460
  16.9 1.1 %copy-start.2 = (f32[8,8]{1,0:T(8,128)S(1)}, f32[8,8]{1,0:T(8,128)}, u32[]{:S(2)}) copy-start(f32[8,8]{1,0:T(8,128)} %coup_ref.1) | copy-start | bytes 772
  17.0 11.5 %collective-permute-start.5 = (f32[256,128]{1,0:T(8,128)S(1)}, f32[256,128]{1,0:T(8,128)S(1)}, u32[]{:S(2)}, u32[]{:S(2)}) collective-permute-start(f32[256,128]{1,0:T(8,128)S(1)} %relay_b.1), channel_id=1, source_target_pairs={{0,16},{8,24},{16,0},{24,8},{1,17},{9,25},{17,1},{25,9},{2,18},{10... | collective-permute-start | bytes 393224 | tf_op jit(solution)/shard_map/ppermute | solution.py:460

commit v7 on v5

--- a/solution.py
+++ b/solution.py
@@ -37,27 +37,35 @@
     return jnp.where(row_ids(x.shape) == 0, 0.0, roll_by(x, 1, 0))
 
 
+def forward_pair(uz, up, ut):
+    lane = lane_ids(up.shape)
+    up_next = jnp.where(lane == up.shape[1] - 1, 0.0, roll_by(up, -1, 1))
+    return uz + (z_next(up) - up), ut + (up_next - up)
+
+
+def odd_loop():
+    return lax.rem(lax.axis_index("loop"), 2) == 1
+
+
 def packed(v_ref, b, scale, fwd_ref, bwd_ref, at):
     nz = scale.shape[0]
-    lane = lane_ids(scale.shape)
-    last = scale.shape[1] - 1
     uz = v_ref[b, pl.ds(0, nz), :] * scale
     up = v_ref[b, pl.ds(nz, nz), :] * scale
     ut = v_ref[b, pl.ds(2 * nz, nz), :] * scale
     one, two = pl.ds(at * nz, nz), pl.ds((at + 1) * nz, nz)
     bwd_ref[one, :] = uz
     bwd_ref[two, :] = ut
-    fwd_ref[one, :] = uz + (z_next(up) - up)
-    fwd_ref[two, :] = ut + (jnp.where(lane == last, 0.0, roll_by(up, -1, 1)) - up)
-
-
-def first_kernel(v_hbm, mat_hbm, eps_hbm, fwd_ref, bwd_ref, scale_ref, v_ref, mat_ref, eps_ref, sems):
-    count = v_ref.shape[0]
+    fwd_ref[one, :], fwd_ref[two, :] = forward_pair(uz, up, ut)
+
+
+def first_kernel(
+    cut_r, cut_a, v_hbm, mat_hbm, eps_hbm, x_ref, fwd_ref, bwd_ref, scale_ref, v_ref, mat_ref, eps_ref, sems
+):
     copies = [
         pltpu.make_async_copy(eps_hbm, eps_ref, sems.at[0]),
         pltpu.make_async_copy(mat_hbm, mat_ref, sems.at[1]),
     ]
-    for b in range(count):
+    for b in range(v_ref.shape[0]):
         copies.append(pltpu.make_async_copy(v_hbm.at[b], v_ref.at[b], sems.at[2 + b]))
     for copy in copies:
         copy.start()
@@ -65,9 +73,36 @@
     copies[1].wait()
     scale = cell_scale(mat_ref[...], eps_ref)
     scale_ref[...] = scale
-    for b in range(count):
+    nz = scale.shape[0]
+    for m, b in enumerate(range(*cut_r)):
         copies[2 + b].wait()
-        packed(v_ref, b, scale, fwd_ref, bwd_ref, 2 * b)
+        for c in range(3):
+            x_ref[pl.ds((3 * m + c) * nz, nz), :] = v_ref[b, pl.ds(c * nz, nz), :] * scale
+    for m, b in enumerate(range(*cut_a)):
+        copies[2 + b].wait()
+        packed(v_ref, b, scale, fwd_ref, bwd_ref, 2 * m)
+
+
+def relay_kernel(nz, x_ref, after_f_ref, after_b_ref, y_ref):
+    odd = odd_loop()
+    count = x_ref.shape[0] // (3 * nz)
+
+    def comps(m):
+        return [x_ref[pl.ds((3 * m + c) * nz, nz), :] for c in range(3)]
+
+    def store(m, pair):
+        y_ref[pl.ds(2 * m * nz, nz), :] = pair[0]
+        y_ref[pl.ds((2 * m + 1) * nz, nz), :] = pair[1]
+
+    @pl.when(odd)
+    def _():
+        for m in range(count):
+            store(m, comps(m)[::2])
+
+    @pl.when(jnp.logical_not(odd))
+    def _():
+        for m in range(count):
+            store(m, forward_pair(*comps(m)))
 
 
 def edge_kernel(v_ref, scale_ref, right_ref, left_ref):
@@ -221,14 +256,22 @@
     columns_f, columns_b = columns_f_ref[...], columns_b_ref[...]
     scale = scale_ref[...]
     lane = lane_ids(scale.shape)
-    for i, (low, high) in enumerate(cuts):
+    odd = odd_loop()
+    for i, (low, high, relayed) in enumerate(cuts):
         fwd_ref, bwd_ref = halos[2 * i : 2 * i + 2]
 
         for m in range(high - low):
             b = low + m
             one, two = pl.ds(2 * m * nz, nz), pl.ds((2 * m + 1) * nz, nz)
-            za, tb = fwd_ref[one, :], fwd_ref[two, :]
-            uz, ut = bwd_ref[one, :], bwd_ref[two, :]
+            if relayed:
+                xz, xp, xt = (fwd_ref[pl.ds((3 * m + c) * nz, nz), :] for c in range(3))
+                y0, y1 = bwd_ref[one, :], bwd_ref[two, :]
+                f0, f1 = forward_pair(xz, xp, xt)
+                za, tb = jnp.where(odd, f0, y0), jnp.where(odd, f1, y1)
+                uz, ut = jnp.where(odd, y0, xz), jnp.where(odd, y1, xt)
+            else:
+                za, tb = fwd_ref[one, :], fwd_ref[two, :]
+                uz, ut = bwd_ref[one, :], bwd_ref[two, :]
             edge_b = roll_by(columns_b, -b, 1)
             edge_f = roll_by(columns_f, nt - 1 - b, 1)
             ut_prev = jnp.where(lane == 0, edge_b, roll_by(ut, 1, 1))
@@ -362,6 +405,15 @@
     return lax.ppermute(x, "loop", [(i, (i + loop_by) % count) for i in range(count)])
 
 
+def swap(x):
+    return lax.ppermute(x, "loop", [(i, i ^ 1) for i in range(lax.axis_size("loop"))])
+
+
+def relay(x):
+    count = lax.axis_size("loop")
+    return lax.ppermute(x, "loop", [(i, (i + (-2 if i % 2 else 2)) % count) for i in range(count)])
+
+
 def local(block_now, block_prev, coupling_prev, material, permittivity):
     nb, nc, nz, _, nt = block_now.shape
     f32 = jnp.float32
@@ -376,7 +428,9 @@
     free = pl.CostEstimate(flops=0, bytes_accessed=0, transcendentals=0)
     plane = jax.ShapeDtypeStruct((nz, nt), f32)
     pay_shape = jax.ShapeDtypeStruct((2, nt), f32)
-    cut_a, cut_b, cut_c = (0, nb // 2), (nb // 2, nb - 1), (nb - 1, nb)
+    assert lax.axis_size("loop") % 2 == 0
+    marks = (0, nb * 3 // 8, nb * 5 // 8, nb - 1, nb)
+    cut_r, cut_a, cut_b, cut_c = zip(marks[:-1], marks[1:])
 
     def planes(n, more=0):
         return jax.ShapeDtypeStruct((n * nz + more, nt), f32)
@@ -384,12 +438,12 @@
     def works(n):
         return jax.ShapeDtypeStruct((n, nc * nz, nt), f32)
 
-    size_a, size_b, size_c = (2 * (c[1] - c[0]) for c in (cut_a, cut_b, cut_c))
-    fwd_a, bwd_a, scale = pl.pallas_call(
-        first_kernel,
-        out_shape=(planes(size_a), planes(size_a), plane),
+    size_r, size_a, size_b, size_c = (2 * (c[1] - c[0]) for c in (cut_r, cut_a, cut_b, cut_c))
+    x_r, fwd_a, bwd_a, scale = pl.pallas_call(
+        lambda *refs: first_kernel(cut_r, cut_a, *refs),
+        out_shape=(planes(size_r * 3 // 2), planes(size_a), planes(size_a), plane),
         in_specs=[hbm] * 3,
-        out_specs=(vm,) * 3,
+        out_specs=(vm,) * 4,
         scratch_shapes=[
             VM((cut_a[1], nc * nz, nt), f32),
             VM((nz, nt), jnp.int32),
@@ -400,6 +454,7 @@
         cost_estimate=free,
         name="first",
     )(*(pltpu.with_memory_space_constraint(x, pltpu.HBM) for x in (v, mat, permittivity)))
+    x_r = swap(x_r)
     fwd_a, bwd_a = shift(fwd_a, 1, 0), shift(bwd_a, -1, 0)
     right, left = pl.pallas_call(
         edge_kernel,
@@ -411,7 +466,7 @@
         name="edges",
     )(v, scale)
     from_left, from_right = shift(right, 0, 1), shift(left, 0, -1)
-    fwd_b, bwd_b = pl.pallas_call(
+    own_f, own_b = pl.pallas_call(
         lambda *refs: corner_kernel(*cut_b, *refs),
         out_shape=(planes(size_b, nb), planes(size_b, nb)),
         in_specs=[vm] * 4,
@@ -420,7 +475,18 @@
         cost_estimate=free,
         name="pack_b",
     )(v, scale, from_left, from_right)
-    fwd_b, bwd_b = shift(fwd_b, 1, 0), shift(bwd_b, -1, 0)
+    fwd_b, bwd_b = shift(own_f, 1, 0), shift(own_b, -1, 0)
+    y_r = relay(
+        pl.pallas_call(
+            lambda *refs: relay_kernel(nz, *refs),
+            out_shape=planes(size_r),
+            in_specs=[vm, hbm, hbm],
+            out_specs=vm,
+            compiler_params=params,
+            cost_estimate=free,
+            name="relay",
+        )(x_r, own_f, own_b)
+    )
     fwd_c, bwd_c = pl.pallas_call(
         lambda *refs: more_kernel(*cut_c, *refs),
         out_shape=(planes(size_c), planes(size_c)),
@@ -441,16 +507,16 @@
         name="inner",
     )(coupling_prev, v, scale, q, from_left, from_right)
     w_ab, pay, columns_f, columns_b = pl.pallas_call(
-        lambda *refs: sum_kernel((cut_a, cut_b), 0, *refs),
+        lambda *refs: sum_kernel(((*cut_r, True), (*cut_a, False), (*cut_b, False)), 0, *refs),
         out_shape=(works(cut_b[1]), pay_shape, plane, plane),
-        in_specs=[vm] * 10,
+        in_specs=[vm] * 12,
         out_specs=(vm,) * 4,
         compiler_params=params,
         cost_estimate=free,
         name="products",
-    )(v, scale, inner, pay, fwd_a, bwd_a, fwd_b, bwd_b, fwd_b, bwd_b)
+    )(v, scale, inner, pay, x_r, y_r, fwd_a, bwd_a, fwd_b, bwd_b, fwd_b, bwd_b)
     w_c, pay = pl.pallas_call(
-        lambda *refs: sum_kernel((cut_c,), cut_c[0], *refs),
+        lambda *refs: sum_kernel(((*cut_c, False),), cut_c[0], *refs),
         out_shape=(works(cut_c[1] - cut_c[0]), pay_shape),
         in_specs=[vm] * 9,
         out_specs=(vm, vm),

time: 44.2 us -> 42.7 us (0.966)
  waiting for transfers between devices: 8.58 us -> 2.64 us
  starting transfers between devices: 12.7 us -> 16.6 us
  blocking collectives: 13.7 us -> 14.2 us
    ppermute x0 -> x2, starting transfers between devices: none -> 4.84 us  [the longest x1 3 us: swap(): lax.ppermute(x, 'loop', [(i, i ^ 1) for i in range(lax.axis_size('loop'))])]
    ppermute x2, waiting for transfers between devices: 3.85 us -> 0.46 us  [shift(): lax.ppermute(x, 'trans', [(t, t + trans_by) for t in range(count) if 0 <=...]
    ppermute x6, waiting for transfers between devices: 4.73 us -> 1.95 us  [shift(): lax.ppermute(x, 'loop', [(i, (i + loop_by) % count) for i in range(count)])]
    ppermute x6, starting transfers between devices: 9.97 us -> 9 us  [shift(): lax.ppermute(x, 'loop', [(i, (i + loop_by) % count) for i in range(count)])]
    all_to_all x1, blocking collectives: 13.7 us -> 14.2 us  [local(): pay = lax.all_to_all(pay, ('loop', 'trans'), 0, 0)]
    pallas_call x3 -> x4, Pallas kernels: 2.87 us -> 2.98 us  [the longest x1 1.35 us: local(): pl.pallas_call(lambda *refs: first_kernel(cut_r, cut_a, *refs), out_shape...]
  transfers between devices with their start and end apart: 8 -> 10, of which waited for: 4 -> 5; matrix products, arithmetic and copies ran while one was open for 0% -> 0% of each run, Pallas kernels for 10% -> 11%
where the time goes in v7:
time: 42.7 us; the launch traced here: 42.5 us
  starting transfers between devices  16.6 us (39%)
  blocking collectives  14.2 us (33%)
  Pallas kernels  8.38 us (20%)
  waiting for transfers between devices  2.64 us (6%)
  between operations  0.73 us (2%)
    all_to_all x1, blocking collectives, local(): pay = lax.all_to_all(pay, ('loop', 'trans'), 0, 0)  14.2 us
    ppermute x6, starting transfers between devices, shift(): lax.ppermute(x, 'loop', [(i, (i + loop_by) % count) for i in range(count)])  9 us
    ppermute x1, starting transfers between devices, swap(): lax.ppermute(x, 'loop', [(i, i ^ 1) for i in range(lax.axis_size('loop'))])  3 us
    ppermute x2, starting transfers between devices, shift(): lax.ppermute(x, 'trans', [(t, t + trans_by) for t in range(count) if 0 <=...  2.75 us
    pallas_call x1, Pallas kernels, local(): pl.pallas_call(inner_kernel, out_shape=(works(nb), pay_shape), in_specs=[...  2.61 us
    pallas_call x1, Pallas kernels, local(): pl.pallas_call(lambda *refs: last_kernel(count, *refs), out_shape=(works(...  2.16 us
    ppermute x6, waiting for transfers between devices, shift(): lax.ppermute(x, 'loop', [(i, (i + loop_by) % count) for i in range(count)])  1.95 us
    ppermute x1, starting transfers between devices, relay(): lax.ppermute(x, 'loop', [(i, (i + (-2 if i % 2 else 2)) % count) for i in...  1.83 us
  transfers between devices with their start and end apart: 10, of which 5 were waited for; matrix products, arithmetic and copies ran while one was open for 0% of the time, Pallas kernels for 11%

profile of v7, /device:TPU:0, one launch (start us, length us, event | category | flops | bytes accessed | tf_op | source)
XLA Modules:
  0.0 42.5 jit_solution(1963002869253972252)
XLA Ops:
  0.6 0.0 copy-start
  0.6 1.3 %first.1 = (f32[576,128]{1,0:T(8,128)S(1)}, f32[256,128]{1,0:T(8,128)S(1)}, f32[256,128]{1,0:T(8,128)S(1)}, f32[64,128]{1,0:T(8,128)S(1)}) custom-call(f32[8,192,128]{2,1,0:T(8,128)} %bitcast.6, s32[64,128]{1,0:T(8,128)} %bitcast.15, f32[4]{0:T(128)} %refs_2_.1), custom_call_target="tpu_custom_call" | custom-call | tf_op jit(solution)/shard_map/first/pallas_call | solution.py:442
  2.0 3.0 %collective-permute-start.2 = (f32[576,128]{1,0:T(8,128)S(1)}, f32[576,128]{1,0:T(8,128)S(1)}, u32[]{:S(2)}, u32[]{:S(2)}) collective-permute-start(f32[576,128]{1,0:T(8,128)S(1)} %get-tuple-element.29), channel_id=1, source_target_pairs={{0,8},{8,0},{16,24},{24,16},{1,9},{9,1},{17,25},{25,17},{2,10},{10... | collective-permute-start | bytes 884744 | tf_op jit(solution)/shard_map/ppermute | solution.py:409
  5.0 0.0 copy-done
  5.0 0.5 %edges.1 = (f32[64,128]{1,0:T(8,128)S(1)}, f32[64,128]{1,0:T(8,128)S(1)}) custom-call(f32[8,192,128]{2,1,0:T(8,128)S(1)} %bitcast.7, f32[64,128]{1,0:T(8,128)S(1)} %get-tuple-element.24.scale_ref.refs_1_), custom_call_target="tpu_custom_call" | custom-call | tf_op jit(solution)/shard_map/edges/pallas_call | solution.py:459
  5.5 1.5 %collective-permute-start = (f32[64,128]{1,0:T(8,128)S(1)}, f32[64,128]{1,0:T(8,128)S(1)}, u32[]{:S(2)}, u32[]{:S(2)}) collective-permute-start(f32[64,128]{1,0:T(8,128)S(1)} %get-tuple-element.25), channel_id=1, source_target_pairs={{0,1},{1,2},{2,3},{3,4},{4,5},{5,6},{6,7},{8,9},{9,10},{10,11},{11... | collective-permute-start | bytes 98312 | tf_op jit(solution)/shard_map/ppermute | solution.py:403
  6.9 1.3 %collective-permute-start.1 = (f32[64,128]{1,0:T(8,128)S(1)}, f32[64,128]{1,0:T(8,128)S(1)}, u32[]{:S(2)}, u32[]{:S(2)}) collective-permute-start(f32[64,128]{1,0:T(8,128)S(1)} %get-tuple-element.26), channel_id=1, source_target_pairs={{1,0},{2,1},{3,2},{4,3},{5,4},{6,5},{7,6},{9,8},{10,9},{11,10},{12... | collective-permute-start | bytes 98312 | tf_op jit(solution)/shard_map/ppermute | solution.py:403
  8.2 0.4 collective-permute-start.4
  8.6 2.6 %collective-permute-start.5 = (f32[256,128]{1,0:T(8,128)S(1)}, f32[256,128]{1,0:T(8,128)S(1)}, u32[]{:S(2)}, u32[]{:S(2)}) collective-permute-start(f32[256,128]{1,0:T(8,128)S(1)} %get-tuple-element.33), channel_id=1, source_target_pairs={{0,24},{8,0},{16,8},{24,16},{1,25},{9,1},{17,9},{25,17},{2,26},{10... | collective-permute-start | bytes 393224 | tf_op jit(solution)/shard_map/ppermute | solution.py:405
  11.2 0.0 collective-permute-done.fr_ref.refs_2_
  11.2 0.5 %collective-permute-done.1.fl_ref.refs_3_ = f32[64,128]{1,0:T(8,128)S(1)} collective-permute-done((f32[64,128]{1,0:T(8,128)S(1)}, f32[64,128]{1,0:T(8,128)S(1)}, u32[]{:S(2)}, u32[]{:S(2)}) %collective-permute-start.1) | collective-permute-done | bytes 32800 | tf_op jit(solution)/shard_map/ppermute | solution.py:403
  11.7 0.1 pack_b.1
  11.8 0.2 collective-permute-done.2.refs_0_.refs_4_
  12.0 0.0 copy-start.1
  12.0 0.1 relay.1
  12.1 1.8 %collective-permute-start.3 = (f32[384,128]{1,0:T(8,128)S(1)}, f32[384,128]{1,0:T(8,128)S(1)}, u32[]{:S(2)}, u32[]{:S(2)}) collective-permute-start(f32[384,128]{1,0:T(8,128)S(1)} %relay.1), channel_id=1, source_target_pairs={{0,16},{8,24},{16,0},{24,8},{1,17},{9,25},{17,1},{25,9},{2,18},{10... | collective-permute-start | bytes 589832 | tf_op jit(solution)/shard_map/ppermute | solution.py:414
  13.9 1.4 %collective-permute-start.6 = (f32[264,128]{1,0:T(8,128)S(1)}, f32[264,128]{1,0:T(8,128)S(1)}, u32[]{:S(2)}, u32[]{:S(2)}) collective-permute-start(f32[264,128]{1,0:T(8,128)S(1)} %get-tuple-element.30.refs_1_), channel_id=1, source_target_pairs={{0,8},{8,16},{16,24},{24,0},{1,9},{9,17},{17,25},{25,1},{2,10},{10... | collective-permute-start | bytes 405512 | tf_op jit(solution)/shard_map/ppermute | solution.py:405
  15.4 1.5 %collective-permute-start.7 = (f32[264,128]{1,0:T(8,128)S(1)}, f32[264,128]{1,0:T(8,128)S(1)}, u32[]{:S(2)}, u32[]{:S(2)}) collective-permute-start(f32[264,128]{1,0:T(8,128)S(1)} %get-tuple-element.31.refs_2_), channel_id=1, source_target_pairs={{0,24},{8,0},{16,8},{24,16},{1,25},{9,1},{17,9},{25,17},{2,26},{10... | collective-permute-start | bytes 405512 | tf_op jit(solution)/shard_map/ppermute | solution.py:405
  16.9 0.0 collective-permute-done.4.refs_6_.refs_2_
  16.9 0.0 collective-permute-done.5.refs_7_.refs_3_
  16.9 0.1 pack_c.1
  17.0 0.0 copy-start.2
  17.0 3.1 %collective-permute-start.8 = (f32[128,128]{1,0:T(8,128)S(1)}, f32[128,128]{1,0:T(8,128)S(1)}, u32[]{:S(2)}, u32[]{:S(2)}) collective-permute-start(f32[128,128]{1,0:T(8,128)S(1)} %get-tuple-element.35), channel_id=1, source_target_pairs={{0,8},{8,16},{16,24},{24,0},{1,9},{9,17},{17,25},{25,1},{2,10},{10... | collective-permute-start | bytes 196616 | tf_op jit(solution)/shard_map/ppermute | solution.py:405
  20.1 0.0 collective-permute-start.9
  20.1 0.0 copy-done.1
  20.1 0.0 copy-done.2
  20.1 2.6 %inner.1 = (f32[8,192,128]{2,1,0:T(8,128)S(1)}, f32[2,128]{1,0:T(2,128)S(1)}) custom-call(f32[8,8]{1,0:T(8,128)S(1)} %copy-done.2, f32[8,192,128]{2,1,0:T(8,128)S(1)} %bitcast.10, f32[64,128]{1,0:T(8,128)S(1)} %get-tuple-element.24.scale_ref.refs_1_, f32[8,192,128]{2,1,0:T(8,128)S(1)} %bitcast.14, f32[64,128]{1,0:T(8,128)S(1)} %collective-permute-done.fr_ref.refs_2_, ...), custom_call_target="tpu_custom_call" | custom-call | tf_op jit(solution)/shard_map/inner/pallas_call | solution.py:500
  22.7 0.0 collective-permute-done.6.refs_8_.refs_10_
  22.7 0.4 collective-permute-done.7.refs_9_.refs_11_
  23.1 0.0 collective-permute-done.3.refs_5_
  23.1 1.2 %products.1 = (f32[7,192,128]{2,1,0:T(8,128)S(1)}, f32[2,128]{1,0:T(2,128)S(1)}, f32[64,128]{1,0:T(8,128)S(1)}, f32[64,128]{1,0:T(8,128)S(1)}) custom-call(f32[8,192,128]{2,1,0:T(8,128)S(1)} %bitcast.11, f32[64,128]{1,0:T(8,128)S(1)} %get-tuple-element.24.scale_ref.refs_1_, f32[8,192,128]{2,1,0:T(8,128)S(1)} %get-tuple-element.27.refs_2_, ...), custom_call_target="tpu_custom_call" | custom-call | tf_op jit(solution)/shard_map/products/pallas_call | solution.py:509
  24.3 0.9 %collective-permute-done.8.refs_4_ = f32[128,128]{1,0:T(8,128)S(1)} collective-permute-done((f32[128,128]{1,0:T(8,128)S(1)}, f32[128,128]{1,0:T(8,128)S(1)}, u32[]{:S(2)}, u32[]{:S(2)}) %collective-permute-start.8) | collective-permute-done | bytes 65568 | tf_op jit(solution)/shard_map/ppermute | solution.py:405
  25.2 0.6 %collective-permute-done.9.refs_5_ = f32[128,128]{1,0:T(8,128)S(1)} collective-permute-done((f32[128,128]{1,0:T(8,128)S(1)}, f32[128,128]{1,0:T(8,128)S(1)}, u32[]{:S(2)}, u32[]{:S(2)}) %collective-permute-start.9) | collective-permute-done | bytes 65568 | tf_op jit(solution)/shard_map/ppermute | solution.py:405
  25.9 0.3 products_last.1
  26.2 14.2 %all_to_all.5.refs_0_ = f32[32,2,128]{2,1,0:T(2,128)S(1)} all-to-all(f32[32,2,128]{2,1,0:T(2,128)S(1)} %broadcast_in_dim.2), channel_id=1, replica_groups=mesh['loop'=4,'trans'=8] {'loop','trans'}, dimensions={0} | all-to-all | bytes 65536 | tf_op jit(solution)/shard_map/all_to_all | solution.py:528
  40.4 2.2 %combine.1 = (f32[8,192,128]{2,1,0:T(8,128)}, f32[8,8]{1,0:T(8,128)}, f32[8,8]{1,0:T(8,128)}) custom-call(f32[32,2,128]{2,1,0:T(2,128)S(1)} %all_to_all.5.refs_0_, f32[8,192,128]{2,1,0:T(8,128)S(1)} %bitcast.13, f32[7,192,128]{2,1,0:T(8,128)S(1)} %get-tuple-element.39.refs_8_.refs_2_, f32[1,192,128]{2,1,0:T(8,128)S(1)} %get-tuple-element.41.refs_3_), custom_call_target="tpu_custom_call" | custom-call | tf_op jit(solution)/shard_map/combine/pallas_call | solution.py:530
  (1 shorter events, 0.0 us)
Async XLA Ops:
  0.6 4.4 %copy-start = (f32[8,3,64,1,128]{4,3,2,1,0:T(1,128)S(1)}, f32[8,3,64,1,128]{4,3,2,1,0:T(1,128)}, u32[]{:S(2)}) copy-start(f32[8,3,64,1,128]{4,3,2,1,0:T(1,128)} %param.5) | copy-start | bytes 2359300
  2.0 10.0 %collective-permute-start.2 = (f32[576,128]{1,0:T(8,128)S(1)}, f32[576,128]{1,0:T(8,128)S(1)}, u32[]{:S(2)}, u32[]{:S(2)}) collective-permute-start(f32[576,128]{1,0:T(8,128)S(1)} %get-tuple-element.29), channel_id=1, source_target_pairs={{0,8},{8,0},{16,24},{24,16},{1,9},{9,1},{17,25},{25,17},{2,10},{10... | collective-permute-start | bytes 884744 | tf_op jit(solution)/shard_map/ppermute | solution.py:409
  5.5 5.7 %collective-permute-start = (f32[64,128]{1,0:T(8,128)S(1)}, f32[64,128]{1,0:T(8,128)S(1)}, u32[]{:S(2)}, u32[]{:S(2)}) collective-permute-start(f32[64,128]{1,0:T(8,128)S(1)} %get-tuple-element.25), channel_id=1, source_target_pairs={{0,1},{1,2},{2,3},{3,4},{4,5},{5,6},{6,7},{8,9},{9,10},{10,11},{11... | collective-permute-start | bytes 98312 | tf_op jit(solution)/shard_map/ppermute | solution.py:403
  6.9 4.7 %collective-permute-start.1 = (f32[64,128]{1,0:T(8,128)S(1)}, f32[64,128]{1,0:T(8,128)S(1)}, u32[]{:S(2)}, u32[]{:S(2)}) collective-permute-start(f32[64,128]{1,0:T(8,128)S(1)} %get-tuple-element.26), channel_id=1, source_target_pairs={{1,0},{2,1},{3,2},{4,3},{5,4},{6,5},{7,6},{9,8},{10,9},{11,10},{12... | collective-permute-start | bytes 98312 | tf_op jit(solution)/shard_map/ppermute | solution.py:403
  8.2 8.6 %collective-permute-start.4 = (f32[256,128]{1,0:T(8,128)S(1)}, f32[256,128]{1,0:T(8,128)S(1)}, u32[]{:S(2)}, u32[]{:S(2)}) collective-permute-start(f32[256,128]{1,0:T(8,128)S(1)} %get-tuple-element.32), channel_id=1, source_target_pairs={{0,8},{8,16},{16,24},{24,0},{1,9},{9,17},{17,25},{25,1},{2,10},{10... | collective-permute-start | bytes 393224 | tf_op jit(solution)/shard_map/ppermute | solution.py:405
  8.6 8.3 %collective-permute-start.5 = (f32[256,128]{1,0:T(8,128)S(1)}, f32[256,128]{1,0:T(8,128)S(1)}, u32[]{:S(2)}, u32[]{:S(2)}) collective-permute-start(f32[256,128]{1,0:T(8,128)S(1)} %get-tuple-element.33), channel_id=1, source_target_pairs={{0,24},{8,0},{16,8},{24,16},{1,25},{9,1},{17,9},{25,17},{2,26},{10... | collective-permute-start | bytes 393224 | tf_op jit(solution)/shard_map/ppermute | solution.py:405
  12.0 8.1 %copy-start.1 = (f32[8,3,64,1,128]{4,3,2,1,0:T(1,128)S(1)}, f32[8,3,64,1,128]{4,3,2,1,0:T(1,128)}, u32[]{:S(2)}) copy-start(f32[8,3,64,1,128]{4,3,2,1,0:T(1,128)} %param.6) | copy-start | bytes 2359300
  12.1 10.9 %collective-permute-start.3 = (f32[384,128]{1,0:T(8,128)S(1)}, f32[384,128]{1,0:T(8,128)S(1)}, u32[]{:S(2)}, u32[]{:S(2)}) collective-permute-start(f32[384,128]{1,0:T(8,128)S(1)} %relay.1), channel_id=1, source_target_pairs={{0,16},{8,24},{16,0},{24,8},{1,17},{9,25},{17,1},{25,9},{2,18},{10... | collective-permute-start | bytes 589832 | tf_op jit(solution)/shard_map/ppermute | solution.py:414
  13.9 8.7 %collective-permute-start.6 = (f32[264,128]{1,0:T(8,128)S(1)}, f32[264,128]{1,0:T(8,128)S(1)}, u32[]{:S(2)}, u32[]{:S(2)}) collective-permute-start(f32[264,128]{1,0:T(8,128)S(1)} %get-tuple-element.30.refs_1_), channel_id=1, source_target_pairs={{0,8},{8,16},{16,24},{24,0},{1,9},{9,17},{17,25},{25,1},{2,10},{10... | collective-permute-start | bytes 405512 | tf_op jit(solution)/shard_map/ppermute | solution.py:405
  15.4 7.7 %collective-permute-start.7 = (f32[264,128]{1,0:T(8,128)S(1)}, f32[264,128]{1,0:T(8,128)S(1)}, u32[]{:S(2)}, u32[]{:S(2)}) collective-permute-start(f32[264,128]{1,0:T(8,128)S(1)} %get-tuple-element.31.refs_2_), channel_id=1, source_target_pairs={{0,24},{8,0},{16,8},{24,16},{1,25},{9,1},{17,9},{25,17},{2,26},{10... | collective-permute-start | bytes 405512 | tf_op jit(solution)/shard_map/ppermute | solution.py:405
  17.0 3.1 %copy-start.2 = (f32[8,8]{1,0:T(8,128)S(1)}, f32[8,8]{1,0:T(8,128)}, u32[]{:S(2)}) copy-start(f32[8,8]{1,0:T(8,128)} %coup_ref.1) | copy-start | bytes 772
  17.0 8.3 %collective-permute-start.8 = (f32[128,128]{1,0:T(8,128)S(1)}, f32[128,128]{1,0:T(8,128)S(1)}, u32[]{:S(2)}, u32[]{:S(2)}) collective-permute-start(f32[128,128]{1,0:T(8,128)S(1)} %get-tuple-element.35), channel_id=1, source_target_pairs={{0,8},{8,16},{16,24},{24,0},{1,9},{9,17},{17,25},{25,1},{2,10},{10... | collective-permute-start | bytes 196616 | tf_op jit(solution)/shard_map/ppermute | solution.py:405
  20.1 5.8 %collective-permute-start.9 = (f32[128,128]{1,0:T(8,128)S(1)}, f32[128,128]{1,0:T(8,128)S(1)}, u32[]{:S(2)}, u32[]{:S(2)}) collective-permute-start(f32[128,128]{1,0:T(8,128)S(1)} %get-tuple-element.36), channel_id=1, source_target_pairs={{0,24},{8,0},{16,8},{24,16},{1,25},{9,1},{17,9},{25,17},{2,26},{10... | collective-permute-start | bytes 196616 | tf_op jit(solution)/shard_map/ppermute | solution.py:405

commit v8 on v7

--- a/solution.py
+++ b/solution.py
@@ -41,6 +41,10 @@
     lane = lane_ids(up.shape)
     up_next = jnp.where(lane == up.shape[1] - 1, 0.0, roll_by(up, -1, 1))
     return uz + (z_next(up) - up), ut + (up_next - up)
+
+
+def even_trans():
+    return lax.rem(lax.axis_index("trans"), 2) == 0
 
 
 def odd_loop():
@@ -105,7 +109,7 @@
             store(m, forward_pair(*comps(m)))
 
 
-def edge_kernel(v_ref, scale_ref, right_ref, left_ref):
+def edge_kernel(v_ref, scale_ref, near_ref, far_ref):
     scale = scale_ref[...]
     nz = scale.shape[0]
     lane = lane_ids(scale.shape)
@@ -117,8 +121,9 @@
             spot = v_ref.shape[0] * c + b
             right = jnp.where(lane == spot, roll_by(u, spot + 1, 1), right)
             left = jnp.where(lane == spot, roll_by(u, spot, 1), left)
-    right_ref[...] = right
-    left_ref[...] = left
+    even = even_trans()
+    near_ref[...] = jnp.where(even, right, left)
+    far_ref[...] = jnp.where(even, left, right)
 
 
 def turned(x):
@@ -126,14 +131,19 @@
     return jnp.concatenate([x, pad], axis=0).T
 
 
-def corner_kernel(begin, end, v_ref, scale_ref, fr_ref, fl_ref, fwd_ref, bwd_ref):
+def corner_kernel(begin, end, v_ref, scale_ref, near_ref, far_ref, fwd_ref, bwd_ref, fr_ref, fl_ref):
     scale = scale_ref[...]
     for b in range(begin, end):
         packed(v_ref, b, scale, fwd_ref, bwd_ref, 2 * (b - begin))
     nb = v_ref.shape[0]
+    even = even_trans()
+    near, far = near_ref[...], far_ref[...]
+    from_left, from_right = jnp.where(even, far, near), jnp.where(even, near, far)
+    fr_ref[...] = from_left
+    fl_ref[...] = from_right
     rows = pl.ds(2 * (end - begin) * scale.shape[0], nb)
-    fwd_ref[rows, :] = turned(fl_ref[...])[nb : 2 * nb, :]
-    bwd_ref[rows, :] = turned(fr_ref[...])[2 * nb : 3 * nb, :]
+    fwd_ref[rows, :] = turned(from_right)[nb : 2 * nb, :]
+    bwd_ref[rows, :] = turned(from_left)[2 * nb : 3 * nb, :]
 
 
 def more_kernel(begin, end, v_ref, scale_ref, fwd_a_ref, bwd_a_ref, fwd_ref, bwd_ref):
@@ -397,12 +407,15 @@
         copy.wait()
 
 
-def shift(x, loop_by, trans_by):
-    if trans_by:
-        count = lax.axis_size("trans")
-        return lax.ppermute(x, "trans", [(t, t + trans_by) for t in range(count) if 0 <= t + trans_by < count])
+def shift(x, loop_by):
     count = lax.axis_size("loop")
     return lax.ppermute(x, "loop", [(i, (i + loop_by) % count) for i in range(count)])
+
+
+def trans_swaps(near, far):
+    count = lax.axis_size("trans")
+    pairs = [(t, t + (-1 if t % 2 == 0 else 1)) for t in range(1, count - 1)]
+    return lax.ppermute(near, "trans", [(t, t ^ 1) for t in range(count)]), lax.ppermute(far, "trans", pairs)
 
 
 def swap(x):
@@ -428,7 +441,7 @@
     free = pl.CostEstimate(flops=0, bytes_accessed=0, transcendentals=0)
     plane = jax.ShapeDtypeStruct((nz, nt), f32)
     pay_shape = jax.ShapeDtypeStruct((2, nt), f32)
-    assert lax.axis_size("loop") % 2 == 0
+    assert lax.axis_size("loop") % 2 == 0 and lax.axis_size("trans") % 2 == 0
     marks = (0, nb * 3 // 8, nb * 5 // 8, nb - 1, nb)
     cut_r, cut_a, cut_b, cut_c = zip(marks[:-1], marks[1:])
 
@@ -455,8 +468,8 @@
         name="first",
     )(*(pltpu.with_memory_space_constraint(x, pltpu.HBM) for x in (v, mat, permittivity)))
     x_r = swap(x_r)
-    fwd_a, bwd_a = shift(fwd_a, 1, 0), shift(bwd_a, -1, 0)
-    right, left = pl.pallas_call(
+    fwd_a, bwd_a = shift(fwd_a, 1), shift(bwd_a, -1)
+    near, far = pl.pallas_call(
         edge_kernel,
         out_shape=(plane, plane),
         in_specs=[vm, vm],
@@ -465,17 +478,17 @@
         cost_estimate=free,
         name="edges",
     )(v, scale)
-    from_left, from_right = shift(right, 0, 1), shift(left, 0, -1)
-    own_f, own_b = pl.pallas_call(
+    near, far = trans_swaps(near, far)
+    own_f, own_b, from_left, from_right = pl.pallas_call(
         lambda *refs: corner_kernel(*cut_b, *refs),
-        out_shape=(planes(size_b, nb), planes(size_b, nb)),
+        out_shape=(planes(size_b, nb), planes(size_b, nb), plane, plane),
         in_specs=[vm] * 4,
-        out_specs=(vm, vm),
+        out_specs=(vm,) * 4,
         compiler_params=params,
         cost_estimate=free,
         name="pack_b",
-    )(v, scale, from_left, from_right)
-    fwd_b, bwd_b = shift(own_f, 1, 0), shift(own_b, -1, 0)
+    )(v, scale, near, far)
+    fwd_b, bwd_b = shift(own_f, 1), shift(own_b, -1)
     y_r = relay(
         pl.pallas_call(
             lambda *refs: relay_kernel(nz, *refs),
@@ -496,7 +509,7 @@
         cost_estimate=free,
         name="pack_c",
     )(v, scale, fwd_a, bwd_a)
-    fwd_c, bwd_c = shift(fwd_c, 1, 0), shift(bwd_c, -1, 0)
+    fwd_c, bwd_c = shift(fwd_c, 1), shift(bwd_c, -1)
     inner, pay = pl.pallas_call(
         inner_kernel,
         out_shape=(works(nb), pay_shape),

time: 42.7 us -> 42 us (0.984)
  waiting for transfers between devices: 2.64 us -> 4.85 us
  starting transfers between devices: 16.6 us -> 15 us
  blocking collectives: 14.2 us -> 12.9 us
    ppermute x1, waiting for transfers between devices: 0.22 us -> 3.11 us  [swap(): lax.ppermute(x, 'loop', [(i, i ^ 1) for i in range(lax.axis_size('loop'))])]
    ppermute x2, starting transfers between devices: 2.75 us -> 0.73 us  [the longest x1 0.66 us: trans_swaps(): lax.ppermute(far, 'trans', pairs)]
    all_to_all x1, blocking collectives: 14.2 us -> 12.9 us  [local(): pay = lax.all_to_all(pay, ('loop', 'trans'), 0, 0)]
    ppermute x2, waiting for transfers between devices: 0.46 us -> 0.01 us  [the longest x1 0.01 us: trans_swaps(): lax.ppermute(near, 'trans', [(t, t ^ 1) for t in range(count)])]
  transfers between devices with their start and end apart: 10 -> 10, of which waited for: 5 -> 3; matrix products, arithmetic and copies ran while one was open for 0% -> 0% of each run, Pallas kernels for 11% -> 11%
where the time goes in v8:
time: 42 us; the launch traced here: 41.9 us
  starting transfers between devices  15 us (36%)
  blocking collectives  12.9 us (31%)
  Pallas kernels  8.39 us (20%)
  waiting for transfers between devices  4.85 us (12%)
  between operations  0.74 us (2%)
    all_to_all x1, blocking collectives, local(): pay = lax.all_to_all(pay, ('loop', 'trans'), 0, 0)  12.9 us
    ppermute x6, starting transfers between devices, shift(): lax.ppermute(x, 'loop', [(i, (i + loop_by) % count) for i in range(count)])  9.4 us
    ppermute x1, waiting for transfers between devices, swap(): lax.ppermute(x, 'loop', [(i, i ^ 1) for i in range(lax.axis_size('loop'))])  3.11 us
    ppermute x1, starting transfers between devices, swap(): lax.ppermute(x, 'loop', [(i, i ^ 1) for i in range(lax.axis_size('loop'))])  3 us
    pallas_call x1, Pallas kernels, local(): pl.pallas_call(inner_kernel, out_shape=(works(nb), pay_shape), in_specs=[...  2.61 us
    pallas_call x1, Pallas kernels, local(): pl.pallas_call(lambda *refs: last_kernel(count, *refs), out_shape=(works(...  2.16 us
    ppermute x1, starting transfers between devices, relay(): lax.ppermute(x, 'loop', [(i, (i + (-2 if i % 2 else 2)) % count) for i in...  1.87 us
    ppermute x6, waiting for transfers between devices, shift(): lax.ppermute(x, 'loop', [(i, (i + loop_by) % count) for i in range(count)])  1.74 us
  transfers between devices with their start and end apart: 10, of which 3 were waited for; matrix products, arithmetic and copies ran while one was open for 0% of the time, Pallas kernels for 11%

profile of v8, /device:TPU:0, one launch (start us, length us, event | category | flops | bytes accessed | tf_op | source)
XLA Modules:
  0.0 41.9 jit_solution(5780856350903526932)
XLA Ops:
  0.6 0.0 copy-start
  0.6 1.3 %first.1 = (f32[576,128]{1,0:T(8,128)S(1)}, f32[256,128]{1,0:T(8,128)S(1)}, f32[256,128]{1,0:T(8,128)S(1)}, f32[64,128]{1,0:T(8,128)S(1)}) custom-call(f32[8,192,128]{2,1,0:T(8,128)} %bitcast.6, s32[64,128]{1,0:T(8,128)} %bitcast.15, f32[4]{0:T(128)} %refs_2_.1), custom_call_target="tpu_custom_call" | custom-call | tf_op jit(solution)/shard_map/first/pallas_call | solution.py:455
  2.0 3.0 %collective-permute-start.2 = (f32[576,128]{1,0:T(8,128)S(1)}, f32[576,128]{1,0:T(8,128)S(1)}, u32[]{:S(2)}, u32[]{:S(2)}) collective-permute-start(f32[576,128]{1,0:T(8,128)S(1)} %get-tuple-element.33), channel_id=1, source_target_pairs={{0,8},{8,0},{16,24},{24,16},{1,9},{9,1},{17,25},{25,17},{2,10},{10... | collective-permute-start | bytes 884744 | tf_op jit(solution)/shard_map/ppermute | solution.py:422
  5.0 0.0 copy-done
  5.0 0.5 %edges.1 = (f32[64,128]{1,0:T(8,128)S(1)}, f32[64,128]{1,0:T(8,128)S(1)}) custom-call(f32[8,192,128]{2,1,0:T(8,128)S(1)} %bitcast.7, f32[64,128]{1,0:T(8,128)S(1)} %get-tuple-element.26.scale_ref.refs_1_), custom_call_target="tpu_custom_call" | custom-call | tf_op jit(solution)/shard_map/edges/pallas_call | solution.py:472
  5.5 0.1 collective-permute-start
  5.6 0.7 %collective-permute-start.1 = (f32[64,128]{1,0:T(8,128)S(1)}, f32[64,128]{1,0:T(8,128)S(1)}, u32[]{:S(2)}, u32[]{:S(2)}) collective-permute-start(f32[64,128]{1,0:T(8,128)S(1)} %get-tuple-element.28), channel_id=1, source_target_pairs={{1,2},{2,1},{3,4},{4,3},{5,6},{6,5},{9,10},{10,9},{11,12},{12,11},... | collective-permute-start | bytes 98312 | tf_op jit(solution)/shard_map/ppermute | solution.py:418
  6.2 0.1 collective-permute-start.4
  6.3 2.9 %collective-permute-start.5 = (f32[256,128]{1,0:T(8,128)S(1)}, f32[256,128]{1,0:T(8,128)S(1)}, u32[]{:S(2)}, u32[]{:S(2)}) collective-permute-start(f32[256,128]{1,0:T(8,128)S(1)} %get-tuple-element.37), channel_id=1, source_target_pairs={{0,24},{8,0},{16,8},{24,16},{1,25},{9,1},{17,9},{25,17},{2,26},{10... | collective-permute-start | bytes 393224 | tf_op jit(solution)/shard_map/ppermute | solution.py:412
  9.2 0.0 collective-permute-done.refs_2_
  9.2 0.0 collective-permute-done.1.refs_3_
  9.2 0.1 pack_b.1
  9.3 3.1 %collective-permute-done.2.refs_0_.refs_4_ = f32[576,128]{1,0:T(8,128)S(1)} collective-permute-done((f32[576,128]{1,0:T(8,128)S(1)}, f32[576,128]{1,0:T(8,128)S(1)}, u32[]{:S(2)}, u32[]{:S(2)}) %collective-permute-start.2) | collective-permute-done | bytes 294944 | tf_op jit(solution)/shard_map/ppermute | solution.py:422
  12.4 0.0 copy-start.1
  12.4 0.1 relay.1
  12.5 1.9 %collective-permute-start.3 = (f32[384,128]{1,0:T(8,128)S(1)}, f32[384,128]{1,0:T(8,128)S(1)}, u32[]{:S(2)}, u32[]{:S(2)}) collective-permute-start(f32[384,128]{1,0:T(8,128)S(1)} %relay.1), channel_id=1, source_target_pairs={{0,16},{8,24},{16,0},{24,8},{1,17},{9,25},{17,1},{25,9},{2,18},{10... | collective-permute-start | bytes 589832 | tf_op jit(solution)/shard_map/ppermute | solution.py:427
  14.4 2.1 %collective-permute-start.6 = (f32[264,128]{1,0:T(8,128)S(1)}, f32[264,128]{1,0:T(8,128)S(1)}, u32[]{:S(2)}, u32[]{:S(2)}) collective-permute-start(f32[264,128]{1,0:T(8,128)S(1)} %get-tuple-element.34.refs_1_), channel_id=1, source_target_pairs={{0,8},{8,16},{16,24},{24,0},{1,9},{9,17},{17,25},{25,1},{2,10},{10... | collective-permute-start | bytes 405512 | tf_op jit(solution)/shard_map/ppermute | solution.py:412
  16.5 0.8 %collective-permute-start.7 = (f32[264,128]{1,0:T(8,128)S(1)}, f32[264,128]{1,0:T(8,128)S(1)}, u32[]{:S(2)}, u32[]{:S(2)}) collective-permute-start(f32[264,128]{1,0:T(8,128)S(1)} %get-tuple-element.35.refs_2_), channel_id=1, source_target_pairs={{0,24},{8,0},{16,8},{24,16},{1,25},{9,1},{17,9},{25,17},{2,26},{10... | collective-permute-start | bytes 405512 | tf_op jit(solution)/shard_map/ppermute | solution.py:412
  17.3 0.0 collective-permute-done.4.refs_6_.refs_2_
  17.3 0.7 %collective-permute-done.5.refs_7_.refs_3_ = f32[256,128]{1,0:T(8,128)S(1)} collective-permute-done((f32[256,128]{1,0:T(8,128)S(1)}, f32[256,128]{1,0:T(8,128)S(1)}, u32[]{:S(2)}, u32[]{:S(2)}) %collective-permute-start.5) | collective-permute-done | bytes 131104 | tf_op jit(solution)/shard_map/ppermute | solution.py:412
  18.0 0.1 pack_c.1
  18.1 0.0 copy-start.2
  18.1 3.5 %collective-permute-start.8 = (f32[128,128]{1,0:T(8,128)S(1)}, f32[128,128]{1,0:T(8,128)S(1)}, u32[]{:S(2)}, u32[]{:S(2)}) collective-permute-start(f32[128,128]{1,0:T(8,128)S(1)} %get-tuple-element.39), channel_id=1, source_target_pairs={{0,8},{8,16},{16,24},{24,0},{1,9},{9,17},{17,25},{25,1},{2,10},{10... | collective-permute-start | bytes 196616 | tf_op jit(solution)/shard_map/ppermute | solution.py:412
  21.6 0.0 collective-permute-start.9
  21.6 0.0 copy-done.1
  21.6 0.0 copy-done.2
  21.6 2.6 %inner.1 = (f32[8,192,128]{2,1,0:T(8,128)S(1)}, f32[2,128]{1,0:T(2,128)S(1)}) custom-call(f32[8,8]{1,0:T(8,128)S(1)} %copy-done.2, f32[8,192,128]{2,1,0:T(8,128)S(1)} %bitcast.10, f32[64,128]{1,0:T(8,128)S(1)} %get-tuple-element.26.scale_ref.refs_1_, f32[8,192,128]{2,1,0:T(8,128)S(1)} %bitcast.14, f32[64,128]{1,0:T(8,128)S(1)} %get-tuple-element.29.fr_ref, ...), custom_call_target="tpu_custom_call" | custom-call | tf_op jit(solution)/shard_map/inner/pallas_call | solution.py:513
  24.2 0.0 collective-permute-done.6.refs_8_.refs_10_
  24.3 0.0 collective-permute-done.7.refs_9_.refs_11_
  24.3 0.0 collective-permute-done.3.refs_5_
  24.3 1.2 %products.1 = (f32[7,192,128]{2,1,0:T(8,128)S(1)}, f32[2,128]{1,0:T(2,128)S(1)}, f32[64,128]{1,0:T(8,128)S(1)}, f32[64,128]{1,0:T(8,128)S(1)}) custom-call(f32[8,192,128]{2,1,0:T(8,128)S(1)} %bitcast.11, f32[64,128]{1,0:T(8,128)S(1)} %get-tuple-element.26.scale_ref.refs_1_, f32[8,192,128]{2,1,0:T(8,128)S(1)} %get-tuple-element.31.refs_2_, ...), custom_call_target="tpu_custom_call" | custom-call | tf_op jit(solution)/shard_map/products/pallas_call | solution.py:522
  25.5 1.0 %collective-permute-done.8.refs_4_ = f32[128,128]{1,0:T(8,128)S(1)} collective-permute-done((f32[128,128]{1,0:T(8,128)S(1)}, f32[128,128]{1,0:T(8,128)S(1)}, u32[]{:S(2)}, u32[]{:S(2)}) %collective-permute-start.8) | collective-permute-done | bytes 65568 | tf_op jit(solution)/shard_map/ppermute | solution.py:412
  26.5 0.0 collective-permute-done.9.refs_5_
  26.5 0.3 products_last.1
  26.9 12.9 %all_to_all.5.refs_0_ = f32[32,2,128]{2,1,0:T(2,128)S(1)} all-to-all(f32[32,2,128]{2,1,0:T(2,128)S(1)} %broadcast_in_dim.2), channel_id=1, replica_groups=mesh['loop'=4,'trans'=8] {'loop','trans'}, dimensions={0} | all-to-all | bytes 65536 | tf_op jit(solution)/shard_map/all_to_all | solution.py:541
  39.7 2.2 %combine.1 = (f32[8,192,128]{2,1,0:T(8,128)}, f32[8,8]{1,0:T(8,128)}, f32[8,8]{1,0:T(8,128)}) custom-call(f32[32,2,128]{2,1,0:T(2,128)S(1)} %all_to_all.5.refs_0_, f32[8,192,128]{2,1,0:T(8,128)S(1)} %bitcast.13, f32[7,192,128]{2,1,0:T(8,128)S(1)} %get-tuple-element.43.refs_8_.refs_2_, f32[1,192,128]{2,1,0:T(8,128)S(1)} %get-tuple-element.45.refs_3_), custom_call_target="tpu_custom_call" | custom-call | tf_op jit(solution)/shard_map/combine/pallas_call | solution.py:543
  (1 shorter events, 0.0 us)
Async XLA Ops:
  0.6 4.4 %copy-start = (f32[8,3,64,1,128]{4,3,2,1,0:T(1,128)S(1)}, f32[8,3,64,1,128]{4,3,2,1,0:T(1,128)}, u32[]{:S(2)}) copy-start(f32[8,3,64,1,128]{4,3,2,1,0:T(1,128)} %param.5) | copy-start | bytes 2359300
  2.0 10.4 %collective-permute-start.2 = (f32[576,128]{1,0:T(8,128)S(1)}, f32[576,128]{1,0:T(8,128)S(1)}, u32[]{:S(2)}, u32[]{:S(2)}) collective-permute-start(f32[576,128]{1,0:T(8,128)S(1)} %get-tuple-element.33), channel_id=1, source_target_pairs={{0,8},{8,0},{16,24},{24,16},{1,9},{9,1},{17,25},{25,17},{2,10},{10... | collective-permute-start | bytes 884744 | tf_op jit(solution)/shard_map/ppermute | solution.py:422
  5.5 3.7 %collective-permute-start = (f32[64,128]{1,0:T(8,128)S(1)}, f32[64,128]{1,0:T(8,128)S(1)}, u32[]{:S(2)}, u32[]{:S(2)}) collective-permute-start(f32[64,128]{1,0:T(8,128)S(1)} %get-tuple-element.27), channel_id=1, source_target_pairs={{0,1},{1,0},{2,3},{3,2},{4,5},{5,4},{6,7},{7,6},{8,9},{9,8},{10,11... | collective-permute-start | bytes 98312 | tf_op jit(solution)/shard_map/ppermute | solution.py:418
  5.6 3.7 %collective-permute-start.1 = (f32[64,128]{1,0:T(8,128)S(1)}, f32[64,128]{1,0:T(8,128)S(1)}, u32[]{:S(2)}, u32[]{:S(2)}) collective-permute-start(f32[64,128]{1,0:T(8,128)S(1)} %get-tuple-element.28), channel_id=1, source_target_pairs={{1,2},{2,1},{3,4},{4,3},{5,6},{6,5},{9,10},{10,9},{11,12},{12,11},... | collective-permute-start | bytes 98312 | tf_op jit(solution)/shard_map/ppermute | solution.py:418
  6.2 11.1 %collective-permute-start.4 = (f32[256,128]{1,0:T(8,128)S(1)}, f32[256,128]{1,0:T(8,128)S(1)}, u32[]{:S(2)}, u32[]{:S(2)}) collective-permute-start(f32[256,128]{1,0:T(8,128)S(1)} %get-tuple-element.36), channel_id=1, source_target_pairs={{0,8},{8,16},{16,24},{24,0},{1,9},{9,17},{17,25},{25,1},{2,10},{10... | collective-permute-start | bytes 393224 | tf_op jit(solution)/shard_map/ppermute | solution.py:412
  6.3 11.7 %collective-permute-start.5 = (f32[256,128]{1,0:T(8,128)S(1)}, f32[256,128]{1,0:T(8,128)S(1)}, u32[]{:S(2)}, u32[]{:S(2)}) collective-permute-start(f32[256,128]{1,0:T(8,128)S(1)} %get-tuple-element.37), channel_id=1, source_target_pairs={{0,24},{8,0},{16,8},{24,16},{1,25},{9,1},{17,9},{25,17},{2,26},{10... | collective-permute-start | bytes 393224 | tf_op jit(solution)/shard_map/ppermute | solution.py:412
  12.4 9.2 %copy-start.1 = (f32[8,3,64,1,128]{4,3,2,1,0:T(1,128)S(1)}, f32[8,3,64,1,128]{4,3,2,1,0:T(1,128)}, u32[]{:S(2)}) copy-start(f32[8,3,64,1,128]{4,3,2,1,0:T(1,128)} %param.6) | copy-start | bytes 2359300
  12.5 11.8 %collective-permute-start.3 = (f32[384,128]{1,0:T(8,128)S(1)}, f32[384,128]{1,0:T(8,128)S(1)}, u32[]{:S(2)}, u32[]{:S(2)}) collective-permute-start(f32[384,128]{1,0:T(8,128)S(1)} %relay.1), channel_id=1, source_target_pairs={{0,16},{8,24},{16,0},{24,8},{1,17},{9,25},{17,1},{25,9},{2,18},{10... | collective-permute-start | bytes 589832 | tf_op jit(solution)/shard_map/ppermute | solution.py:427
  14.4 9.9 %collective-permute-start.6 = (f32[264,128]{1,0:T(8,128)S(1)}, f32[264,128]{1,0:T(8,128)S(1)}, u32[]{:S(2)}, u32[]{:S(2)}) collective-permute-start(f32[264,128]{1,0:T(8,128)S(1)} %get-tuple-element.34.refs_1_), channel_id=1, source_target_pairs={{0,8},{8,16},{16,24},{24,0},{1,9},{9,17},{17,25},{25,1},{2,10},{10... | collective-permute-start | bytes 405512 | tf_op jit(solution)/shard_map/ppermute | solution.py:412
  16.5 7.7 %collective-permute-start.7 = (f32[264,128]{1,0:T(8,128)S(1)}, f32[264,128]{1,0:T(8,128)S(1)}, u32[]{:S(2)}, u32[]{:S(2)}) collective-permute-start(f32[264,128]{1,0:T(8,128)S(1)} %get-tuple-element.35.refs_2_), channel_id=1, source_target_pairs={{0,24},{8,0},{16,8},{24,16},{1,25},{9,1},{17,9},{25,17},{2,26},{10... | collective-permute-start | bytes 405512 | tf_op jit(solution)/shard_map/ppermute | solution.py:412
  18.1 3.5 %copy-start.2 = (f32[8,8]{1,0:T(8,128)S(1)}, f32[8,8]{1,0:T(8,128)}, u32[]{:S(2)}) copy-start(f32[8,8]{1,0:T(8,128)} %coup_ref.1) | copy-start | bytes 772
  18.1 8.4 %collective-permute-start.8 = (f32[128,128]{1,0:T(8,128)S(1)}, f32[128,128]{1,0:T(8,128)S(1)}, u32[]{:S(2)}, u32[]{:S(2)}) collective-permute-start(f32[128,128]{1,0:T(8,128)S(1)} %get-tuple-element.39), channel_id=1, source_target_pairs={{0,8},{8,16},{16,24},{24,0},{1,9},{9,17},{17,25},{25,1},{2,10},{10... | collective-permute-start | bytes 196616 | tf_op jit(solution)/shard_map/ppermute | solution.py:412
  21.6 4.9 %collective-permute-start.9 = (f32[128,128]{1,0:T(8,128)S(1)}, f32[128,128]{1,0:T(8,128)S(1)}, u32[]{:S(2)}, u32[]{:S(2)}) collective-permute-start(f32[128,128]{1,0:T(8,128)S(1)} %get-tuple-element.40), channel_id=1, source_target_pairs={{0,24},{8,0},{16,8},{24,16},{1,25},{9,1},{17,9},{25,17},{2,26},{10... | collective-permute-start | bytes 196616 | tf_op jit(solution)/shard_map/ppermute | solution.py:412

commit v9 on v8

--- a/solution.py
+++ b/solution.py
@@ -62,9 +62,14 @@
     fwd_ref[one, :], fwd_ref[two, :] = forward_pair(uz, up, ut)
 
 
-def first_kernel(
-    cut_r, cut_a, v_hbm, mat_hbm, eps_hbm, x_ref, fwd_ref, bwd_ref, scale_ref, v_ref, mat_ref, eps_ref, sems
-):
+def raw(v_ref, b, scale, out_ref, at):
+    nz = scale.shape[0]
+    for c in range(3):
+        out_ref[pl.ds((at + c) * nz, nz), :] = v_ref[b, pl.ds(c * nz, nz), :] * scale
+
+
+def first_kernel(cuts, v_hbm, mat_hbm, eps_hbm, *refs):
+    outs, (scale_ref, v_ref, mat_ref, eps_ref, sems) = refs[: len(cuts)], refs[len(cuts) :]
     copies = [
         pltpu.make_async_copy(eps_hbm, eps_ref, sems.at[0]),
         pltpu.make_async_copy(mat_hbm, mat_ref, sems.at[1]),
@@ -77,36 +82,35 @@
     copies[1].wait()
     scale = cell_scale(mat_ref[...], eps_ref)
     scale_ref[...] = scale
-    nz = scale.shape[0]
-    for m, b in enumerate(range(*cut_r)):
-        copies[2 + b].wait()
-        for c in range(3):
-            x_ref[pl.ds((3 * m + c) * nz, nz), :] = v_ref[b, pl.ds(c * nz, nz), :] * scale
-    for m, b in enumerate(range(*cut_a)):
-        copies[2 + b].wait()
-        packed(v_ref, b, scale, fwd_ref, bwd_ref, 2 * m)
-
-
-def relay_kernel(nz, x_ref, after_f_ref, after_b_ref, y_ref):
+    for cut, out_ref in zip(cuts, outs):
+        for m, b in enumerate(range(*cut)):
+            copies[2 + b].wait()
+            raw(v_ref, b, scale, out_ref, 3 * m)
+
+
+def relay_kernel(nz, nb, x_ref, *refs):
+    y_ref = refs[-1]
     odd = odd_loop()
     count = x_ref.shape[0] // (3 * nz)
+    with_rows = x_ref.shape[0] > 3 * nz * count
 
     def comps(m):
         return [x_ref[pl.ds((3 * m + c) * nz, nz), :] for c in range(3)]
 
-    def store(m, pair):
-        y_ref[pl.ds(2 * m * nz, nz), :] = pair[0]
-        y_ref[pl.ds((2 * m + 1) * nz, nz), :] = pair[1]
+    def store(pairs, side):
+        for m, pair in enumerate(pairs):
+            y_ref[pl.ds(2 * m * nz, nz), :] = pair[0]
+            y_ref[pl.ds((2 * m + 1) * nz, nz), :] = pair[1]
+        if with_rows:
+            y_ref[pl.ds(2 * count * nz, nb), :] = x_ref[pl.ds(3 * count * nz + side * nb, nb), :]
 
     @pl.when(odd)
     def _():
-        for m in range(count):
-            store(m, comps(m)[::2])
+        store((comps(m)[::2] for m in range(count)), 1)
 
     @pl.when(jnp.logical_not(odd))
     def _():
-        for m in range(count):
-            store(m, forward_pair(*comps(m)))
+        store((forward_pair(*comps(m)) for m in range(count)), 0)
 
 
 def edge_kernel(v_ref, scale_ref, near_ref, far_ref):
@@ -131,22 +135,22 @@
     return jnp.concatenate([x, pad], axis=0).T
 
 
-def corner_kernel(begin, end, v_ref, scale_ref, near_ref, far_ref, fwd_ref, bwd_ref, fr_ref, fl_ref):
+def corner_kernel(begin, end, v_ref, scale_ref, near_ref, far_ref, x_ref, fr_ref, fl_ref):
     scale = scale_ref[...]
-    for b in range(begin, end):
-        packed(v_ref, b, scale, fwd_ref, bwd_ref, 2 * (b - begin))
     nb = v_ref.shape[0]
+    for m, b in enumerate(range(begin, end)):
+        raw(v_ref, b, scale, x_ref, 3 * m)
     even = even_trans()
     near, far = near_ref[...], far_ref[...]
     from_left, from_right = jnp.where(even, far, near), jnp.where(even, near, far)
     fr_ref[...] = from_left
     fl_ref[...] = from_right
-    rows = pl.ds(2 * (end - begin) * scale.shape[0], nb)
-    fwd_ref[rows, :] = turned(from_right)[nb : 2 * nb, :]
-    bwd_ref[rows, :] = turned(from_left)[2 * nb : 3 * nb, :]
-
-
-def more_kernel(begin, end, v_ref, scale_ref, fwd_a_ref, bwd_a_ref, fwd_ref, bwd_ref):
+    at = 3 * (end - begin) * scale.shape[0]
+    x_ref[pl.ds(at, nb), :] = turned(from_right)[nb : 2 * nb, :]
+    x_ref[pl.ds(at + nb, nb), :] = turned(from_left)[2 * nb : 3 * nb, :]
+
+
+def direct_kernel(begin, end, v_ref, scale_ref, after_ref, fwd_ref, bwd_ref):
     scale = scale_ref[...]
     for b in range(begin, end):
         packed(v_ref, b, scale, fwd_ref, bwd_ref, 2 * (b - begin))
@@ -256,17 +260,18 @@
     end = cuts[-1][1]
     halos = refs[: 2 * len(cuts)]
     corners = refs[2 * len(cuts) : 2 * len(cuts) + 2]
+    odd = odd_loop()
     if begin == 0:
         w_ref, pay_ref, columns_f_ref, columns_b_ref = refs[-4:]
-        for corner, columns_ref in zip(corners, (columns_f_ref, columns_b_ref)):
-            columns_ref[...] = turned(corner[pl.ds(corner.shape[0] - nb, nb), :])[:nz, :]
+        near, far = (ref[pl.ds(ref.shape[0] - n, n), :] for ref, n in zip(corners, (2 * nb, nb)))
+        columns_f_ref[...] = turned(jnp.where(odd, near[:nb], far))[:nz, :]
+        columns_b_ref[...] = turned(jnp.where(odd, far, near[nb:]))[:nz, :]
     else:
         columns_f_ref, columns_b_ref = corners
         old, w_ref, pay_ref = refs[-3:]
     columns_f, columns_b = columns_f_ref[...], columns_b_ref[...]
     scale = scale_ref[...]
     lane = lane_ids(scale.shape)
-    odd = odd_loop()
     for i, (low, high, relayed) in enumerate(cuts):
         fwd_ref, bwd_ref = halos[2 * i : 2 * i + 2]
 
@@ -442,8 +447,8 @@
     plane = jax.ShapeDtypeStruct((nz, nt), f32)
     pay_shape = jax.ShapeDtypeStruct((2, nt), f32)
     assert lax.axis_size("loop") % 2 == 0 and lax.axis_size("trans") % 2 == 0
-    marks = (0, nb * 3 // 8, nb * 5 // 8, nb - 1, nb)
-    cut_r, cut_a, cut_b, cut_c = zip(marks[:-1], marks[1:])
+    marks = (0, nb * 3 // 8, nb * 5 // 8, nb)
+    cut_a, cut_c, cut_d = zip(marks[:-1], marks[1:])
 
     def planes(n, more=0):
         return jax.ShapeDtypeStruct((n * nz + more, nt), f32)
@@ -451,12 +456,12 @@
     def works(n):
         return jax.ShapeDtypeStruct((n, nc * nz, nt), f32)
 
-    size_r, size_a, size_b, size_c = (2 * (c[1] - c[0]) for c in (cut_r, cut_a, cut_b, cut_c))
-    x_r, fwd_a, bwd_a, scale = pl.pallas_call(
-        lambda *refs: first_kernel(cut_r, cut_a, *refs),
-        out_shape=(planes(size_r * 3 // 2), planes(size_a), planes(size_a), plane),
+    size_a, size_c, size_d = (c[1] - c[0] for c in (cut_a, cut_c, cut_d))
+    x_a, scale = pl.pallas_call(
+        lambda *refs: first_kernel((cut_a,), *refs),
+        out_shape=(planes(3 * size_a), plane),
         in_specs=[hbm] * 3,
-        out_specs=(vm,) * 4,
+        out_specs=(vm,) * 2,
         scratch_shapes=[
             VM((cut_a[1], nc * nz, nt), f32),
             VM((nz, nt), jnp.int32),
@@ -467,8 +472,7 @@
         cost_estimate=free,
         name="first",
     )(*(pltpu.with_memory_space_constraint(x, pltpu.HBM) for x in (v, mat, permittivity)))
-    x_r = swap(x_r)
-    fwd_a, bwd_a = shift(fwd_a, 1), shift(bwd_a, -1)
+    x_a = swap(x_a)
     near, far = pl.pallas_call(
         edge_kernel,
         out_shape=(plane, plane),
@@ -479,37 +483,41 @@
         name="edges",
     )(v, scale)
     near, far = trans_swaps(near, far)
-    own_f, own_b, from_left, from_right = pl.pallas_call(
-        lambda *refs: corner_kernel(*cut_b, *refs),
-        out_shape=(planes(size_b, nb), planes(size_b, nb), plane, plane),
+    own_c, from_left, from_right = pl.pallas_call(
+        lambda *refs: corner_kernel(*cut_c, *refs),
+        out_shape=(planes(3 * size_c, 2 * nb), plane, plane),
         in_specs=[vm] * 4,
-        out_specs=(vm,) * 4,
-        compiler_params=params,
-        cost_estimate=free,
-        name="pack_b",
+        out_specs=(vm,) * 3,
+        compiler_params=params,
+        cost_estimate=free,
+        name="corners",
     )(v, scale, near, far)
-    fwd_b, bwd_b = shift(own_f, 1), shift(own_b, -1)
-    y_r = relay(
-        pl.pallas_call(
-            lambda *refs: relay_kernel(nz, *refs),
-            out_shape=planes(size_r),
-            in_specs=[vm, hbm, hbm],
+    x_c = swap(own_c)
+
+    def relay_pair(x, size, rows, name, *after):
+        return pl.pallas_call(
+            lambda *refs: relay_kernel(nz, nb, *refs),
+            out_shape=planes(2 * size, rows),
+            in_specs=[vm] + [hbm] * len(after),
             out_specs=vm,
             compiler_params=params,
             cost_estimate=free,
-            name="relay",
-        )(x_r, own_f, own_b)
-    )
-    fwd_c, bwd_c = pl.pallas_call(
-        lambda *refs: more_kernel(*cut_c, *refs),
-        out_shape=(planes(size_c), planes(size_c)),
-        in_specs=[vm, vm, hbm, hbm],
+            name=name,
+        )(x, *after)
+
+    pair_a = relay_pair(x_a, size_a, 0, "relay_a", own_c)
+    y_a = relay(pair_a)
+    own_f, own_b = pl.pallas_call(
+        lambda *refs: direct_kernel(*cut_d, *refs),
+        out_shape=(planes(2 * size_d), planes(2 * size_d)),
+        in_specs=[vm, vm, hbm],
         out_specs=(vm, vm),
         compiler_params=params,
         cost_estimate=free,
-        name="pack_c",
-    )(v, scale, fwd_a, bwd_a)
-    fwd_c, bwd_c = shift(fwd_c, 1), shift(bwd_c, -1)
+        name="direct",
+    )(v, scale, pair_a)
+    fwd_d, bwd_d = shift(own_f, 1), shift(own_b, -1)
+    y_c = relay(relay_pair(x_c, size_c, nb, "relay_c", own_f, own_b))
     inner, pay = pl.pallas_call(
         inner_kernel,
         out_shape=(works(nb), pay_shape),
@@ -519,24 +527,24 @@
         cost_estimate=free,
         name="inner",
     )(coupling_prev, v, scale, q, from_left, from_right)
-    w_ab, pay, columns_f, columns_b = pl.pallas_call(
-        lambda *refs: sum_kernel(((*cut_r, True), (*cut_a, False), (*cut_b, False)), 0, *refs),
-        out_shape=(works(cut_b[1]), pay_shape, plane, plane),
-        in_specs=[vm] * 12,
+    w_ac, pay, columns_f, columns_b = pl.pallas_call(
+        lambda *refs: sum_kernel(((*cut_a, True), (*cut_c, True)), 0, *refs),
+        out_shape=(works(cut_c[1]), pay_shape, plane, plane),
+        in_specs=[vm] * 10,
         out_specs=(vm,) * 4,
         compiler_params=params,
         cost_estimate=free,
         name="products",
-    )(v, scale, inner, pay, x_r, y_r, fwd_a, bwd_a, fwd_b, bwd_b, fwd_b, bwd_b)
-    w_c, pay = pl.pallas_call(
-        lambda *refs: sum_kernel(((*cut_c, False),), cut_c[0], *refs),
-        out_shape=(works(cut_c[1] - cut_c[0]), pay_shape),
+    )(v, scale, inner, pay, x_a, y_a, x_c, y_c, x_c, y_c)
+    w_d, pay = pl.pallas_call(
+        lambda *refs: sum_kernel(((*cut_d, False),), cut_d[0], *refs),
+        out_shape=(works(size_d), pay_shape),
         in_specs=[vm] * 9,
         out_specs=(vm, vm),
         compiler_params=params,
         cost_estimate=free,
         name="products_last",
-    )(v, scale, inner, pay, fwd_c, bwd_c, columns_f, columns_b, w_ab)
+    )(v, scale, inner, pay, fwd_d, bwd_d, columns_f, columns_b, w_ac)
     pay = jnp.broadcast_to(pay[None], (devices, 2, nt))
     pay = lax.all_to_all(pay, ("loop", "trans"), 0, 0)
     small = jax.ShapeDtypeStruct((nb, nb), f32)
@@ -555,7 +563,7 @@
         compiler_params=params,
         cost_estimate=free,
         name="combine",
-    )(pay, v, w_ab, w_c)
+    )(pay, v, w_ac, w_d)
     return out.reshape(block_now.shape), alpha, beta
 
 

time: 42 us -> 43.2 us (1.029)
  waiting for transfers between devices: 4.85 us -> 11 us
  starting transfers between devices: 15 us -> 9.01 us
  blocking collectives: 12.9 us -> 13.5 us
    ppermute x6 -> x2, starting transfers between devices: 9.4 us -> 2.98 us  [shift(): lax.ppermute(x, 'loop', [(i, (i + loop_by) % count) for i in range(count)])]
    ppermute x1 -> x2, waiting for transfers between devices: 0.01 us -> 5.42 us  [relay(): lax.ppermute(x, 'loop', [(i, (i + (-2 if i % 2 else 2)) % count) for i in...]
    ppermute x1 -> x2, waiting for transfers between devices: 3.11 us -> 5.08 us  [swap(): lax.ppermute(x, 'loop', [(i, i ^ 1) for i in range(lax.axis_size('loop'))])]
    ppermute x6 -> x2, waiting for transfers between devices: 1.74 us -> 0.01 us  [shift(): lax.ppermute(x, 'loop', [(i, (i + loop_by) % count) for i in range(count)])]
    all_to_all x1, blocking collectives: 12.9 us -> 13.5 us  [local(): pay = lax.all_to_all(pay, ('loop', 'trans'), 0, 0)]
    ppermute x1, waiting for transfers between devices: 0.01 us -> 0.52 us  [trans_swaps(): lax.ppermute(near, 'trans', [(t, t ^ 1) for t in range(count)])]
    ppermute x1 -> x2, starting transfers between devices: 1.87 us -> 2.16 us  [relay(): lax.ppermute(x, 'loop', [(i, (i + (-2 if i % 2 else 2)) % count) for i in...]
    ppermute x1 -> x2, starting transfers between devices: 3 us -> 3.14 us  [swap(): lax.ppermute(x, 'loop', [(i, i ^ 1) for i in range(lax.axis_size('loop'))])]
  transfers between devices with their start and end apart: 10 -> 8, of which waited for: 3 -> 3; matrix products, arithmetic and copies ran while one was open for 0% -> 0% of each run, Pallas kernels for 11% -> 10%
where the time goes in v9:
time: 43.2 us; the launch traced here: 43 us
  blocking collectives  13.5 us (31%)
  waiting for transfers between devices  11 us (25%)
  starting transfers between devices  9.01 us (21%)
  Pallas kernels  8.38 us (19%)
  between operations  0.72 us (2%)
    all_to_all x1, blocking collectives, local(): pay = lax.all_to_all(pay, ('loop', 'trans'), 0, 0)  13.5 us
    ppermute x2, waiting for transfers between devices, relay(): lax.ppermute(x, 'loop', [(i, (i + (-2 if i % 2 else 2)) % count) for i in...  5.42 us
    ppermute x2, waiting for transfers between devices, swap(): lax.ppermute(x, 'loop', [(i, i ^ 1) for i in range(lax.axis_size('loop'))])  5.08 us
    ppermute x2, starting transfers between devices, swap(): lax.ppermute(x, 'loop', [(i, i ^ 1) for i in range(lax.axis_size('loop'))])  3.14 us
    ppermute x2, starting transfers between devices, shift(): lax.ppermute(x, 'loop', [(i, (i + loop_by) % count) for i in range(count)])  2.98 us
    pallas_call x1, Pallas kernels, local(): pl.pallas_call(inner_kernel, out_shape=(works(nb), pay_shape), in_specs=[...  2.57 us
    pallas_call x1, Pallas kernels, local(): pl.pallas_call(lambda *refs: last_kernel(count, *refs), out_shape=(works(...  2.19 us
    ppermute x2, starting transfers between devices, relay(): lax.ppermute(x, 'loop', [(i, (i + (-2 if i % 2 else 2)) % count) for i in...  2.16 us
  transfers between devices with their start and end apart: 8, of which 3 were waited for; matrix products, arithmetic and copies ran while one was open for 0% of the time, Pallas kernels for 10%

profile of v9, /device:TPU:0, one launch (start us, length us, event | category | flops | bytes accessed | tf_op | source)
XLA Modules:
  0.0 43.0 jit_solution(10983417851386609988)
XLA Ops:
  0.6 0.0 copy-start
  0.6 1.1 %first.1 = (f32[576,128]{1,0:T(8,128)S(1)}, f32[64,128]{1,0:T(8,128)S(1)}) custom-call(f32[8,192,128]{2,1,0:T(8,128)} %bitcast.6, s32[64,128]{1,0:T(8,128)} %bitcast.15, f32[4]{0:T(128)} %refs_2_.1), custom_call_target="tpu_custom_call" | custom-call | tf_op jit(solution)/shard_map/first/pallas_call | solution.py:460
  1.8 3.0 %collective-permute-start.2 = (f32[576,128]{1,0:T(8,128)S(1)}, f32[576,128]{1,0:T(8,128)S(1)}, u32[]{:S(2)}, u32[]{:S(2)}) collective-permute-start(f32[576,128]{1,0:T(8,128)S(1)} %get-tuple-element.30), channel_id=1, source_target_pairs={{0,8},{8,0},{16,24},{24,16},{1,9},{9,1},{17,25},{25,17},{2,10},{10... | collective-permute-start | bytes 884744 | tf_op jit(solution)/shard_map/ppermute | solution.py:427
  4.8 0.0 copy-done
  4.8 0.5 %edges.1 = (f32[64,128]{1,0:T(8,128)S(1)}, f32[64,128]{1,0:T(8,128)S(1)}) custom-call(f32[8,192,128]{2,1,0:T(8,128)S(1)} %bitcast.7, f32[64,128]{1,0:T(8,128)S(1)} %get-tuple-element.23.scale_ref.refs_1_), custom_call_target="tpu_custom_call" | custom-call | tf_op jit(solution)/shard_map/edges/pallas_call | solution.py:476
  5.3 0.1 collective-permute-start
  5.3 0.7 %collective-permute-start.1 = (f32[64,128]{1,0:T(8,128)S(1)}, f32[64,128]{1,0:T(8,128)S(1)}, u32[]{:S(2)}, u32[]{:S(2)}) collective-permute-start(f32[64,128]{1,0:T(8,128)S(1)} %get-tuple-element.25), channel_id=1, source_target_pairs={{1,2},{2,1},{3,4},{4,3},{5,6},{6,5},{9,10},{10,9},{11,12},{12,11},... | collective-permute-start | bytes 98312 | tf_op jit(solution)/shard_map/ppermute | solution.py:423
  6.0 0.5 %collective-permute-done.refs_2_ = f32[64,128]{1,0:T(8,128)S(1)} collective-permute-done((f32[64,128]{1,0:T(8,128)S(1)}, f32[64,128]{1,0:T(8,128)S(1)}, u32[]{:S(2)}, u32[]{:S(2)}) %collective-permute-start) | collective-permute-done | bytes 32800 | tf_op jit(solution)/shard_map/ppermute | solution.py:423
  6.5 0.0 collective-permute-done.1.refs_3_
  6.6 0.1 collective-permute-start.4
  6.7 5.1 %collective-permute-done.2.refs_0_.refs_4_ = f32[576,128]{1,0:T(8,128)S(1)} collective-permute-done((f32[576,128]{1,0:T(8,128)S(1)}, f32[576,128]{1,0:T(8,128)S(1)}, u32[]{:S(2)}, u32[]{:S(2)}) %collective-permute-start.2) | collective-permute-done | bytes 294944 | tf_op jit(solution)/shard_map/ppermute | solution.py:427
  11.8 0.1 relay_a.1.refs_2_
  11.9 0.0 copy-start.1
  11.9 1.8 %collective-permute-start.3 = (f32[384,128]{1,0:T(8,128)S(1)}, f32[384,128]{1,0:T(8,128)S(1)}, u32[]{:S(2)}, u32[]{:S(2)}) collective-permute-start(f32[384,128]{1,0:T(8,128)S(1)} %relay_a.1.refs_2_), channel_id=1, source_target_pairs={{0,16},{8,24},{16,0},{24,8},{1,17},{9,25},{17,1},{25,9},{2,18},{10... | collective-permute-start | bytes 589832 | tf_op jit(solution)/shard_map/ppermute | solution.py:432
  13.7 0.1 direct.1
  13.8 1.5 %collective-permute-start.6 = (f32[384,128]{1,0:T(8,128)S(1)}, f32[384,128]{1,0:T(8,128)S(1)}, u32[]{:S(2)}, u32[]{:S(2)}) collective-permute-start(f32[384,128]{1,0:T(8,128)S(1)} %get-tuple-element.32.refs_1_), channel_id=1, source_target_pairs={{0,8},{8,16},{16,24},{24,0},{1,9},{9,17},{17,25},{25,1},{2,10},{10... | collective-permute-start | bytes 589832 | tf_op jit(solution)/shard_map/ppermute | solution.py:417
  15.3 1.5 %collective-permute-start.7 = (f32[384,128]{1,0:T(8,128)S(1)}, f32[384,128]{1,0:T(8,128)S(1)}, u32[]{:S(2)}, u32[]{:S(2)}) collective-permute-start(f32[384,128]{1,0:T(8,128)S(1)} %get-tuple-element.33.refs_2_), channel_id=1, source_target_pairs={{0,24},{8,0},{16,8},{24,16},{1,25},{9,1},{17,9},{25,17},{2,26},{10... | collective-permute-start | bytes 589832 | tf_op jit(solution)/shard_map/ppermute | solution.py:417
  16.8 0.0 collective-permute-done.4.refs_0_.refs_6_.refs_8_
  16.8 0.1 relay_c.1
  16.9 0.0 copy-start.2
  16.9 0.3 collective-permute-start.5
  17.2 0.0 copy-done.1
  17.2 0.4 copy-done.2
  17.6 2.6 %inner.1 = (f32[8,192,128]{2,1,0:T(8,128)S(1)}, f32[2,128]{1,0:T(2,128)S(1)}) custom-call(f32[8,8]{1,0:T(8,128)S(1)} %copy-done.2, f32[8,192,128]{2,1,0:T(8,128)S(1)} %bitcast.10, f32[64,128]{1,0:T(8,128)S(1)} %get-tuple-element.23.scale_ref.refs_1_, f32[8,192,128]{2,1,0:T(8,128)S(1)} %bitcast.14, f32[64,128]{1,0:T(8,128)S(1)} %get-tuple-element.26.fr_ref, ...), custom_call_target="tpu_custom_call" | custom-call | tf_op jit(solution)/shard_map/inner/pallas_call | solution.py:521
  20.2 5.4 %collective-permute-done.5.refs_7_.refs_9_ = f32[264,128]{1,0:T(8,128)S(1)} collective-permute-done((f32[264,128]{1,0:T(8,128)S(1)}, f32[264,128]{1,0:T(8,128)S(1)}, u32[]{:S(2)}, u32[]{:S(2)}) %collective-permute-start.5) | collective-permute-done | bytes 135200 | tf_op jit(solution)/shard_map/ppermute | solution.py:432
  25.6 0.0 collective-permute-done.3.refs_5_
  25.6 1.0 %products.1 = (f32[5,192,128]{2,1,0:T(8,128)S(1)}, f32[2,128]{1,0:T(2,128)S(1)}, f32[64,128]{1,0:T(8,128)S(1)}, f32[64,128]{1,0:T(8,128)S(1)}) custom-call(f32[8,192,128]{2,1,0:T(8,128)S(1)} %bitcast.11, f32[64,128]{1,0:T(8,128)S(1)} %get-tuple-element.23.scale_ref.refs_1_, f32[8,192,128]{2,1,0:T(8,128)S(1)} %get-tuple-element.28.refs_2_, ...), custom_call_target="tpu_custom_call" | custom-call | tf_op jit(solution)/shard_map/products/pallas_call | solution.py:530
  26.6 0.0 collective-permute-done.6.refs_4_
  26.6 0.0 collective-permute-done.7.refs_5_
  26.6 0.7 %products_last.1 = (f32[3,192,128]{2,1,0:T(8,128)S(1)}, f32[2,128]{1,0:T(2,128)S(1)}) custom-call(f32[8,192,128]{2,1,0:T(8,128)S(1)} %bitcast.12, f32[64,128]{1,0:T(8,128)S(1)} %get-tuple-element.23.scale_ref.refs_1_, f32[8,192,128]{2,1,0:T(8,128)S(1)} %get-tuple-element.28.refs_2_, f32[2,128]{1,0:T(2,128)S(1)} %get-tuple-element.34.refs_3_, ...), custom_call_target="tpu_custom_call" | custom-call | tf_op jit(solution)/shard_map/products_last/pallas_call | solution.py:539
  27.3 13.5 %all_to_all.5.refs_0_ = f32[32,2,128]{2,1,0:T(2,128)S(1)} all-to-all(f32[32,2,128]{2,1,0:T(2,128)S(1)} %broadcast_in_dim.2), channel_id=1, replica_groups=mesh['loop'=4,'trans'=8] {'loop','trans'}, dimensions={0} | all-to-all | bytes 65536 | tf_op jit(solution)/shard_map/all_to_all | solution.py:549
  40.8 2.2 %combine.1 = (f32[8,192,128]{2,1,0:T(8,128)}, f32[8,8]{1,0:T(8,128)}, f32[8,8]{1,0:T(8,128)}) custom-call(f32[32,2,128]{2,1,0:T(2,128)S(1)} %all_to_all.5.refs_0_, f32[8,192,128]{2,1,0:T(8,128)S(1)} %bitcast.13, f32[5,192,128]{2,1,0:T(8,128)S(1)} %get-tuple-element.37.refs_8_.refs_2_, f32[3,192,128]{2,1,0:T(8,128)S(1)} %get-tuple-element.39.refs_3_), custom_call_target="tpu_custom_call" | custom-call | tf_op jit(solution)/shard_map/combine/pallas_call | solution.py:551
  (2 shorter events, 0.0 us)
Async XLA Ops:
  0.6 4.2 %copy-start = (f32[8,3,64,1,128]{4,3,2,1,0:T(1,128)S(1)}, f32[8,3,64,1,128]{4,3,2,1,0:T(1,128)}, u32[]{:S(2)}) copy-start(f32[8,3,64,1,128]{4,3,2,1,0:T(1,128)} %param.5) | copy-start | bytes 2359300
  1.8 10.0 %collective-permute-start.2 = (f32[576,128]{1,0:T(8,128)S(1)}, f32[576,128]{1,0:T(8,128)S(1)}, u32[]{:S(2)}, u32[]{:S(2)}) collective-permute-start(f32[576,128]{1,0:T(8,128)S(1)} %get-tuple-element.30), channel_id=1, source_target_pairs={{0,8},{8,0},{16,24},{24,16},{1,9},{9,1},{17,25},{25,17},{2,10},{10... | collective-permute-start | bytes 884744 | tf_op jit(solution)/shard_map/ppermute | solution.py:427
  5.3 1.3 %collective-permute-start = (f32[64,128]{1,0:T(8,128)S(1)}, f32[64,128]{1,0:T(8,128)S(1)}, u32[]{:S(2)}, u32[]{:S(2)}) collective-permute-start(f32[64,128]{1,0:T(8,128)S(1)} %get-tuple-element.24), channel_id=1, source_target_pairs={{0,1},{1,0},{2,3},{3,2},{4,5},{5,4},{6,7},{7,6},{8,9},{9,8},{10,11... | collective-permute-start | bytes 98312 | tf_op jit(solution)/shard_map/ppermute | solution.py:423
  5.3 1.2 %collective-permute-start.1 = (f32[64,128]{1,0:T(8,128)S(1)}, f32[64,128]{1,0:T(8,128)S(1)}, u32[]{:S(2)}, u32[]{:S(2)}) collective-permute-start(f32[64,128]{1,0:T(8,128)S(1)} %get-tuple-element.25), channel_id=1, source_target_pairs={{1,2},{2,1},{3,4},{4,3},{5,6},{6,5},{9,10},{10,9},{11,12},{12,11},... | collective-permute-start | bytes 98312 | tf_op jit(solution)/shard_map/ppermute | solution.py:423
  6.6 10.2 %collective-permute-start.4 = (f32[400,128]{1,0:T(8,128)S(1)}, f32[400,128]{1,0:T(8,128)S(1)}, u32[]{:S(2)}, u32[]{:S(2)}) collective-permute-start(f32[400,128]{1,0:T(8,128)S(1)} %get-tuple-element.31.refs_1_), channel_id=1, source_target_pairs={{0,8},{8,0},{16,24},{24,16},{1,9},{9,1},{17,25},{25,17},{2,10},{10... | collective-permute-start | bytes 614408 | tf_op jit(solution)/shard_map/ppermute | solution.py:427
  11.9 5.4 %copy-start.1 = (f32[8,3,64,1,128]{4,3,2,1,0:T(1,128)S(1)}, f32[8,3,64,1,128]{4,3,2,1,0:T(1,128)}, u32[]{:S(2)}) copy-start(f32[8,3,64,1,128]{4,3,2,1,0:T(1,128)} %param.6) | copy-start | bytes 2359300
  11.9 13.7 %collective-permute-start.3 = (f32[384,128]{1,0:T(8,128)S(1)}, f32[384,128]{1,0:T(8,128)S(1)}, u32[]{:S(2)}, u32[]{:S(2)}) collective-permute-start(f32[384,128]{1,0:T(8,128)S(1)} %relay_a.1.refs_2_), channel_id=1, source_target_pairs={{0,16},{8,24},{16,0},{24,8},{1,17},{9,25},{17,1},{25,9},{2,18},{10... | collective-permute-start | bytes 589832 | tf_op jit(solution)/shard_map/ppermute | solution.py:432
  13.8 12.7 %collective-permute-start.6 = (f32[384,128]{1,0:T(8,128)S(1)}, f32[384,128]{1,0:T(8,128)S(1)}, u32[]{:S(2)}, u32[]{:S(2)}) collective-permute-start(f32[384,128]{1,0:T(8,128)S(1)} %get-tuple-element.32.refs_1_), channel_id=1, source_target_pairs={{0,8},{8,16},{16,24},{24,0},{1,9},{9,17},{17,25},{25,1},{2,10},{10... | collective-permute-start | bytes 589832 | tf_op jit(solution)/shard_map/ppermute | solution.py:417
  15.3 11.3 %collective-permute-start.7 = (f32[384,128]{1,0:T(8,128)S(1)}, f32[384,128]{1,0:T(8,128)S(1)}, u32[]{:S(2)}, u32[]{:S(2)}) collective-permute-start(f32[384,128]{1,0:T(8,128)S(1)} %get-tuple-element.33.refs_2_), channel_id=1, source_target_pairs={{0,24},{8,0},{16,8},{24,16},{1,25},{9,1},{17,9},{25,17},{2,26},{10... | collective-permute-start | bytes 589832 | tf_op jit(solution)/shard_map/ppermute | solution.py:417
  16.9 0.7 %copy-start.2 = (f32[8,8]{1,0:T(8,128)S(1)}, f32[8,8]{1,0:T(8,128)}, u32[]{:S(2)}) copy-start(f32[8,8]{1,0:T(8,128)} %coup_ref.1) | copy-start | bytes 772
  16.9 8.7 %collective-permute-start.5 = (f32[264,128]{1,0:T(8,128)S(1)}, f32[264,128]{1,0:T(8,128)S(1)}, u32[]{:S(2)}, u32[]{:S(2)}) collective-permute-start(f32[264,128]{1,0:T(8,128)S(1)} %relay_c.1), channel_id=1, source_target_pairs={{0,16},{8,24},{16,0},{24,8},{1,17},{9,25},{17,1},{25,9},{2,18},{10... | collective-permute-start | bytes 405512 | tf_op jit(solution)/shard_map/ppermute | solution.py:432

commit v10 on v8

--- a/solution.py
+++ b/solution.py
@@ -62,9 +62,7 @@
     fwd_ref[one, :], fwd_ref[two, :] = forward_pair(uz, up, ut)
 
 
-def first_kernel(
-    cut_r, cut_a, v_hbm, mat_hbm, eps_hbm, x_ref, fwd_ref, bwd_ref, scale_ref, v_ref, mat_ref, eps_ref, sems
-):
+def first_kernel(cut_r, v_hbm, mat_hbm, eps_hbm, x_ref, scale_ref, v_ref, mat_ref, eps_ref, sems):
     copies = [
         pltpu.make_async_copy(eps_hbm, eps_ref, sems.at[0]),
         pltpu.make_async_copy(mat_hbm, mat_ref, sems.at[1]),
@@ -82,9 +80,6 @@
         copies[2 + b].wait()
         for c in range(3):
             x_ref[pl.ds((3 * m + c) * nz, nz), :] = v_ref[b, pl.ds(c * nz, nz), :] * scale
-    for m, b in enumerate(range(*cut_a)):
-        copies[2 + b].wait()
-        packed(v_ref, b, scale, fwd_ref, bwd_ref, 2 * m)
 
 
 def relay_kernel(nz, x_ref, after_f_ref, after_b_ref, y_ref):
@@ -109,7 +104,7 @@
             store(m, forward_pair(*comps(m)))
 
 
-def edge_kernel(v_ref, scale_ref, near_ref, far_ref):
+def edge_kernel(cut, v_ref, scale_ref, near_ref, far_ref, fwd_ref, bwd_ref):
     scale = scale_ref[...]
     nz = scale.shape[0]
     lane = lane_ids(scale.shape)
@@ -124,6 +119,8 @@
     even = even_trans()
     near_ref[...] = jnp.where(even, right, left)
     far_ref[...] = jnp.where(even, left, right)
+    for m, b in enumerate(range(*cut)):
+        packed(v_ref, b, scale, fwd_ref, bwd_ref, 2 * m)
 
 
 def turned(x):
@@ -326,8 +323,8 @@
     proj = matrix_of(total[0:1], 0, nb)
     ww = matrix_of(total[0:1], nb * nb, nb)
     vv = matrix_of(total[1:2], 0, nb)
-    alpha = proj / count
-    alpha_t = matrix_of(total[1:2], nb * nb, nb) / count
+    alpha = proj * (1.0 / count)
+    alpha_t = matrix_of(total[1:2], nb * nb, nb) * (1.0 / count)
     alpha_ref[...] = alpha[:, :nb]
     copies = [pltpu.make_async_copy(alpha_ref, alpha_hbm, sems.at[0])]
     copies[0].start()
@@ -342,7 +339,7 @@
     quad = jnp.zeros_like(proj)
     for k in range(nb):
         quad = quad + lane_at(alpha_t, k) * row_at(half, k)
-    gram = ((ww - cross) + (quad - cross)) / count
+    gram = ((ww - cross) + (quad - cross)) * (1.0 / count)
     ws = [(w, i) for w in w_refs for i in range(w.shape[0])]
     blocks = v_ref.shape[1] // 8
     mat = {}
@@ -398,7 +395,7 @@
                 out_ref[b, rows, :] = acc
             return carry
 
-        lax.fori_loop(0, length // step, body, 0)
+        lax.fori_loop(0, length // step, body, 0, unroll=True)
         part = pl.ds(base, length)
         copy = pltpu.make_async_copy(out_ref.at[:, part, :], out_hbm.at[:, part, :], sems.at[2 + piece])
         copy.start()
@@ -452,33 +449,33 @@
         return jax.ShapeDtypeStruct((n, nc * nz, nt), f32)
 
     size_r, size_a, size_b, size_c = (2 * (c[1] - c[0]) for c in (cut_r, cut_a, cut_b, cut_c))
-    x_r, fwd_a, bwd_a, scale = pl.pallas_call(
-        lambda *refs: first_kernel(cut_r, cut_a, *refs),
-        out_shape=(planes(size_r * 3 // 2), planes(size_a), planes(size_a), plane),
+    x_r, scale = pl.pallas_call(
+        lambda *refs: first_kernel(cut_r, *refs),
+        out_shape=(planes(size_r * 3 // 2), plane),
         in_specs=[hbm] * 3,
-        out_specs=(vm,) * 4,
+        out_specs=(vm,) * 2,
         scratch_shapes=[
-            VM((cut_a[1], nc * nz, nt), f32),
+            VM((cut_r[1], nc * nz, nt), f32),
             VM((nz, nt), jnp.int32),
             SM(permittivity.shape, f32),
-            pltpu.SemaphoreType.DMA((2 + cut_a[1],)),
+            pltpu.SemaphoreType.DMA((2 + cut_r[1],)),
         ],
         compiler_params=params,
         cost_estimate=free,
         name="first",
     )(*(pltpu.with_memory_space_constraint(x, pltpu.HBM) for x in (v, mat, permittivity)))
     x_r = swap(x_r)
-    fwd_a, bwd_a = shift(fwd_a, 1), shift(bwd_a, -1)
-    near, far = pl.pallas_call(
-        edge_kernel,
-        out_shape=(plane, plane),
+    near, far, fwd_a, bwd_a = pl.pallas_call(
+        lambda *refs: edge_kernel(cut_a, *refs),
+        out_shape=(plane, plane, planes(size_a), planes(size_a)),
         in_specs=[vm, vm],
-        out_specs=(vm, vm),
+        out_specs=(vm,) * 4,
         compiler_params=params,
         cost_estimate=free,
         name="edges",
     )(v, scale)
     near, far = trans_swaps(near, far)
+    fwd_a, bwd_a = shift(fwd_a, 1), shift(bwd_a, -1)
     own_f, own_b, from_left, from_right = pl.pallas_call(
         lambda *refs: corner_kernel(*cut_b, *refs),
         out_shape=(planes(size_b, nb), planes(size_b, nb), plane, plane),

time: 42 us -> 41.6 us (level)
  Pallas kernels: 8.39 us -> 7.94 us
where the time goes in v10:
time: 41.6 us; the launch traced here: 41.4 us
  starting transfers between devices  15 us (36%)
  blocking collectives  12.9 us (31%)
  Pallas kernels  7.94 us (19%)
  waiting for transfers between devices  4.83 us (12%)
  between operations  0.74 us (2%)
    all_to_all x1, blocking collectives, local(): pay = lax.all_to_all(pay, ('loop', 'trans'), 0, 0)  12.9 us
    ppermute x6, starting transfers between devices, shift(): lax.ppermute(x, 'loop', [(i, (i + loop_by) % count) for i in range(count)])  9.4 us
    ppermute x1, waiting for transfers between devices, swap(): lax.ppermute(x, 'loop', [(i, i ^ 1) for i in range(lax.axis_size('loop'))])  3.08 us
    ppermute x1, starting transfers between devices, swap(): lax.ppermute(x, 'loop', [(i, i ^ 1) for i in range(lax.axis_size('loop'))])  3 us
    pallas_call x1, Pallas kernels, local(): pl.pallas_call(inner_kernel, out_shape=(works(nb), pay_shape), in_specs=[...  2.61 us
    pallas_call x1, Pallas kernels, local(): pl.pallas_call(lambda *refs: last_kernel(count, *refs), out_shape=(works(...  1.9 us
    ppermute x1, starting transfers between devices, relay(): lax.ppermute(x, 'loop', [(i, (i + (-2 if i % 2 else 2)) % count) for i in...  1.84 us
    ppermute x6, waiting for transfers between devices, shift(): lax.ppermute(x, 'loop', [(i, (i + loop_by) % count) for i in range(count)])  1.74 us
  transfers between devices with their start and end apart: 10, of which 3 were waited for; matrix products, arithmetic and copies ran while one was open for 0% of the time, Pallas kernels for 11%

profile of v10, /device:TPU:0, one launch (start us, length us, event | category | flops | bytes accessed | tf_op | source)
XLA Modules:
  0.0 41.4 jit_solution(2229632569569206934)
XLA Ops:
  0.6 0.0 copy-start
  0.6 1.1 %first.1 = (f32[576,128]{1,0:T(8,128)S(1)}, f32[64,128]{1,0:T(8,128)S(1)}) custom-call(f32[8,192,128]{2,1,0:T(8,128)} %bitcast.6, s32[64,128]{1,0:T(8,128)} %bitcast.15, f32[4]{0:T(128)} %refs_2_.1), custom_call_target="tpu_custom_call" | custom-call | tf_op jit(solution)/shard_map/first/pallas_call | solution.py:452
  1.8 3.0 %collective-permute-start.2 = (f32[576,128]{1,0:T(8,128)S(1)}, f32[576,128]{1,0:T(8,128)S(1)}, u32[]{:S(2)}, u32[]{:S(2)}) collective-permute-start(f32[576,128]{1,0:T(8,128)S(1)} %get-tuple-element.33), channel_id=1, source_target_pairs={{0,8},{8,0},{16,24},{24,16},{1,9},{9,1},{17,25},{25,17},{2,10},{10... | collective-permute-start | bytes 884744 | tf_op jit(solution)/shard_map/ppermute | solution.py:419
  4.8 0.0 copy-done
  4.8 0.5 %edges.1 = (f32[64,128]{1,0:T(8,128)S(1)}, f32[64,128]{1,0:T(8,128)S(1)}, f32[256,128]{1,0:T(8,128)S(1)}, f32[256,128]{1,0:T(8,128)S(1)}) custom-call(f32[8,192,128]{2,1,0:T(8,128)S(1)} %bitcast.7, f32[64,128]{1,0:T(8,128)S(1)} %get-tuple-element.26.refs_1_.scale_ref), custom_call_target="tpu_custom_call" | custom-call | tf_op jit(solution)/shard_map/edges/pallas_call | solution.py:468
  5.3 0.1 collective-permute-start
  5.4 0.7 %collective-permute-start.1 = (f32[64,128]{1,0:T(8,128)S(1)}, f32[64,128]{1,0:T(8,128)S(1)}, u32[]{:S(2)}, u32[]{:S(2)}) collective-permute-start(f32[64,128]{1,0:T(8,128)S(1)} %get-tuple-element.28), channel_id=1, source_target_pairs={{1,2},{2,1},{3,4},{4,3},{5,6},{6,5},{9,10},{10,9},{11,12},{12,11},... | collective-permute-start | bytes 98312 | tf_op jit(solution)/shard_map/ppermute | solution.py:415
  6.0 0.1 collective-permute-start.4
  6.2 2.9 %collective-permute-start.5 = (f32[256,128]{1,0:T(8,128)S(1)}, f32[256,128]{1,0:T(8,128)S(1)}, u32[]{:S(2)}, u32[]{:S(2)}) collective-permute-start(f32[256,128]{1,0:T(8,128)S(1)} %get-tuple-element.37), channel_id=1, source_target_pairs={{0,24},{8,0},{16,8},{24,16},{1,25},{9,1},{17,9},{25,17},{2,26},{10... | collective-permute-start | bytes 393224 | tf_op jit(solution)/shard_map/ppermute | solution.py:409
  9.0 0.0 collective-permute-done.refs_2_
  9.0 0.0 collective-permute-done.1.refs_3_
  9.0 0.1 pack_b.1
  9.1 3.1 %collective-permute-done.2.refs_0_.refs_4_ = f32[576,128]{1,0:T(8,128)S(1)} collective-permute-done((f32[576,128]{1,0:T(8,128)S(1)}, f32[576,128]{1,0:T(8,128)S(1)}, u32[]{:S(2)}, u32[]{:S(2)}) %collective-permute-start.2) | collective-permute-done | bytes 294944 | tf_op jit(solution)/shard_map/ppermute | solution.py:419
  12.2 0.0 copy-start.1
  12.2 0.1 relay.1
  12.3 1.8 %collective-permute-start.3 = (f32[384,128]{1,0:T(8,128)S(1)}, f32[384,128]{1,0:T(8,128)S(1)}, u32[]{:S(2)}, u32[]{:S(2)}) collective-permute-start(f32[384,128]{1,0:T(8,128)S(1)} %relay.1), channel_id=1, source_target_pairs={{0,16},{8,24},{16,0},{24,8},{1,17},{9,25},{17,1},{25,9},{2,18},{10... | collective-permute-start | bytes 589832 | tf_op jit(solution)/shard_map/ppermute | solution.py:424
  14.1 2.2 %collective-permute-start.6 = (f32[264,128]{1,0:T(8,128)S(1)}, f32[264,128]{1,0:T(8,128)S(1)}, u32[]{:S(2)}, u32[]{:S(2)}) collective-permute-start(f32[264,128]{1,0:T(8,128)S(1)} %get-tuple-element.34.refs_1_), channel_id=1, source_target_pairs={{0,8},{8,16},{16,24},{24,0},{1,9},{9,17},{17,25},{25,1},{2,10},{10... | collective-permute-start | bytes 405512 | tf_op jit(solution)/shard_map/ppermute | solution.py:409
  16.3 0.8 %collective-permute-start.7 = (f32[264,128]{1,0:T(8,128)S(1)}, f32[264,128]{1,0:T(8,128)S(1)}, u32[]{:S(2)}, u32[]{:S(2)}) collective-permute-start(f32[264,128]{1,0:T(8,128)S(1)} %get-tuple-element.35.refs_2_), channel_id=1, source_target_pairs={{0,24},{8,0},{16,8},{24,16},{1,25},{9,1},{17,9},{25,17},{2,26},{10... | collective-permute-start | bytes 405512 | tf_op jit(solution)/shard_map/ppermute | solution.py:409
  17.1 0.0 collective-permute-done.4.refs_6_.refs_2_
  17.1 0.8 %collective-permute-done.5.refs_7_.refs_3_ = f32[256,128]{1,0:T(8,128)S(1)} collective-permute-done((f32[256,128]{1,0:T(8,128)S(1)}, f32[256,128]{1,0:T(8,128)S(1)}, u32[]{:S(2)}, u32[]{:S(2)}) %collective-permute-start.5) | collective-permute-done | bytes 131104 | tf_op jit(solution)/shard_map/ppermute | solution.py:409
  17.8 0.1 pack_c.1
  17.9 0.0 copy-start.2
  17.9 3.5 %collective-permute-start.8 = (f32[128,128]{1,0:T(8,128)S(1)}, f32[128,128]{1,0:T(8,128)S(1)}, u32[]{:S(2)}, u32[]{:S(2)}) collective-permute-start(f32[128,128]{1,0:T(8,128)S(1)} %get-tuple-element.39), channel_id=1, source_target_pairs={{0,8},{8,16},{16,24},{24,0},{1,9},{9,17},{17,25},{25,1},{2,10},{10... | collective-permute-start | bytes 196616 | tf_op jit(solution)/shard_map/ppermute | solution.py:409
  21.4 0.0 collective-permute-start.9
  21.4 0.0 copy-done.1
  21.4 0.0 copy-done.2
  21.4 2.6 %inner.1 = (f32[8,192,128]{2,1,0:T(8,128)S(1)}, f32[2,128]{1,0:T(2,128)S(1)}) custom-call(f32[8,8]{1,0:T(8,128)S(1)} %copy-done.2, f32[8,192,128]{2,1,0:T(8,128)S(1)} %bitcast.10, f32[64,128]{1,0:T(8,128)S(1)} %get-tuple-element.26.refs_1_.scale_ref, f32[8,192,128]{2,1,0:T(8,128)S(1)} %bitcast.14, f32[64,128]{1,0:T(8,128)S(1)} %get-tuple-element.29.fr_ref, ...), custom_call_target="tpu_custom_call" | custom-call | tf_op jit(solution)/shard_map/inner/pallas_call | solution.py:510
  24.0 0.0 collective-permute-done.6.refs_8_.refs_10_
  24.0 0.0 collective-permute-done.7.refs_9_.refs_11_
  24.0 0.0 collective-permute-done.3.refs_5_
  24.1 1.2 %products.1 = (f32[7,192,128]{2,1,0:T(8,128)S(1)}, f32[2,128]{1,0:T(2,128)S(1)}, f32[64,128]{1,0:T(8,128)S(1)}, f32[64,128]{1,0:T(8,128)S(1)}) custom-call(f32[8,192,128]{2,1,0:T(8,128)S(1)} %bitcast.11, f32[64,128]{1,0:T(8,128)S(1)} %get-tuple-element.26.refs_1_.scale_ref, f32[8,192,128]{2,1,0:T(8,128)S(1)} %get-tuple-element.31.refs_2_, ...), custom_call_target="tpu_custom_call" | custom-call | tf_op jit(solution)/shard_map/products/pallas_call | solution.py:519
  25.3 1.0 %collective-permute-done.8.refs_4_ = f32[128,128]{1,0:T(8,128)S(1)} collective-permute-done((f32[128,128]{1,0:T(8,128)S(1)}, f32[128,128]{1,0:T(8,128)S(1)}, u32[]{:S(2)}, u32[]{:S(2)}) %collective-permute-start.8) | collective-permute-done | bytes 65568 | tf_op jit(solution)/shard_map/ppermute | solution.py:409
  26.3 0.0 collective-permute-done.9.refs_5_
  26.3 0.3 products_last.1
  26.6 12.9 %all_to_all.5.refs_0_ = f32[32,2,128]{2,1,0:T(2,128)S(1)} all-to-all(f32[32,2,128]{2,1,0:T(2,128)S(1)} %broadcast_in_dim.2), channel_id=1, replica_groups=mesh['loop'=4,'trans'=8] {'loop','trans'}, dimensions={0} | all-to-all | bytes 65536 | tf_op jit(solution)/shard_map/all_to_all | solution.py:538
  39.5 1.9 %combine.1 = (f32[8,192,128]{2,1,0:T(8,128)}, f32[8,8]{1,0:T(8,128)}, f32[8,8]{1,0:T(8,128)}) custom-call(f32[32,2,128]{2,1,0:T(2,128)S(1)} %all_to_all.5.refs_0_, f32[8,192,128]{2,1,0:T(8,128)S(1)} %bitcast.13, f32[7,192,128]{2,1,0:T(8,128)S(1)} %get-tuple-element.43.refs_8_.refs_2_, f32[1,192,128]{2,1,0:T(8,128)S(1)} %get-tuple-element.45.refs_3_), custom_call_target="tpu_custom_call" | custom-call | tf_op jit(solution)/shard_map/combine/pallas_call | solution.py:540
  (1 shorter events, 0.0 us)
Async XLA Ops:
  0.6 4.2 %copy-start = (f32[8,3,64,1,128]{4,3,2,1,0:T(1,128)S(1)}, f32[8,3,64,1,128]{4,3,2,1,0:T(1,128)}, u32[]{:S(2)}) copy-start(f32[8,3,64,1,128]{4,3,2,1,0:T(1,128)} %param.5) | copy-start | bytes 2359300
  1.8 10.4 %collective-permute-start.2 = (f32[576,128]{1,0:T(8,128)S(1)}, f32[576,128]{1,0:T(8,128)S(1)}, u32[]{:S(2)}, u32[]{:S(2)}) collective-permute-start(f32[576,128]{1,0:T(8,128)S(1)} %get-tuple-element.33), channel_id=1, source_target_pairs={{0,8},{8,0},{16,24},{24,16},{1,9},{9,1},{17,25},{25,17},{2,10},{10... | collective-permute-start | bytes 884744 | tf_op jit(solution)/shard_map/ppermute | solution.py:419
  5.3 3.7 %collective-permute-start = (f32[64,128]{1,0:T(8,128)S(1)}, f32[64,128]{1,0:T(8,128)S(1)}, u32[]{:S(2)}, u32[]{:S(2)}) collective-permute-start(f32[64,128]{1,0:T(8,128)S(1)} %get-tuple-element.27), channel_id=1, source_target_pairs={{0,1},{1,0},{2,3},{3,2},{4,5},{5,4},{6,7},{7,6},{8,9},{9,8},{10,11... | collective-permute-start | bytes 98312 | tf_op jit(solution)/shard_map/ppermute | solution.py:415
  5.4 3.7 %collective-permute-start.1 = (f32[64,128]{1,0:T(8,128)S(1)}, f32[64,128]{1,0:T(8,128)S(1)}, u32[]{:S(2)}, u32[]{:S(2)}) collective-permute-start(f32[64,128]{1,0:T(8,128)S(1)} %get-tuple-element.28), channel_id=1, source_target_pairs={{1,2},{2,1},{3,4},{4,3},{5,6},{6,5},{9,10},{10,9},{11,12},{12,11},... | collective-permute-start | bytes 98312 | tf_op jit(solution)/shard_map/ppermute | solution.py:415
  6.0 11.0 %collective-permute-start.4 = (f32[256,128]{1,0:T(8,128)S(1)}, f32[256,128]{1,0:T(8,128)S(1)}, u32[]{:S(2)}, u32[]{:S(2)}) collective-permute-start(f32[256,128]{1,0:T(8,128)S(1)} %get-tuple-element.36), channel_id=1, source_target_pairs={{0,8},{8,16},{16,24},{24,0},{1,9},{9,17},{17,25},{25,1},{2,10},{10... | collective-permute-start | bytes 393224 | tf_op jit(solution)/shard_map/ppermute | solution.py:409
  6.2 11.7 %collective-permute-start.5 = (f32[256,128]{1,0:T(8,128)S(1)}, f32[256,128]{1,0:T(8,128)S(1)}, u32[]{:S(2)}, u32[]{:S(2)}) collective-permute-start(f32[256,128]{1,0:T(8,128)S(1)} %get-tuple-element.37), channel_id=1, source_target_pairs={{0,24},{8,0},{16,8},{24,16},{1,25},{9,1},{17,9},{25,17},{2,26},{10... | collective-permute-start | bytes 393224 | tf_op jit(solution)/shard_map/ppermute | solution.py:409
  12.2 9.2 %copy-start.1 = (f32[8,3,64,1,128]{4,3,2,1,0:T(1,128)S(1)}, f32[8,3,64,1,128]{4,3,2,1,0:T(1,128)}, u32[]{:S(2)}) copy-start(f32[8,3,64,1,128]{4,3,2,1,0:T(1,128)} %param.6) | copy-start | bytes 2359300
  12.3 11.8 %collective-permute-start.3 = (f32[384,128]{1,0:T(8,128)S(1)}, f32[384,128]{1,0:T(8,128)S(1)}, u32[]{:S(2)}, u32[]{:S(2)}) collective-permute-start(f32[384,128]{1,0:T(8,128)S(1)} %relay.1), channel_id=1, source_target_pairs={{0,16},{8,24},{16,0},{24,8},{1,17},{9,25},{17,1},{25,9},{2,18},{10... | collective-permute-start | bytes 589832 | tf_op jit(solution)/shard_map/ppermute | solution.py:424
  14.1 9.9 %collective-permute-start.6 = (f32[264,128]{1,0:T(8,128)S(1)}, f32[264,128]{1,0:T(8,128)S(1)}, u32[]{:S(2)}, u32[]{:S(2)}) collective-permute-start(f32[264,128]{1,0:T(8,128)S(1)} %get-tuple-element.34.refs_1_), channel_id=1, source_target_pairs={{0,8},{8,16},{16,24},{24,0},{1,9},{9,17},{17,25},{25,1},{2,10},{10... | collective-permute-start | bytes 405512 | tf_op jit(solution)/shard_map/ppermute | solution.py:409
  16.3 7.7 %collective-permute-start.7 = (f32[264,128]{1,0:T(8,128)S(1)}, f32[264,128]{1,0:T(8,128)S(1)}, u32[]{:S(2)}, u32[]{:S(2)}) collective-permute-start(f32[264,128]{1,0:T(8,128)S(1)} %get-tuple-element.35.refs_2_), channel_id=1, source_target_pairs={{0,24},{8,0},{16,8},{24,16},{1,25},{9,1},{17,9},{25,17},{2,26},{10... | collective-permute-start | bytes 405512 | tf_op jit(solution)/shard_map/ppermute | solution.py:409
  17.9 3.5 %copy-start.2 = (f32[8,8]{1,0:T(8,128)S(1)}, f32[8,8]{1,0:T(8,128)}, u32[]{:S(2)}) copy-start(f32[8,8]{1,0:T(8,128)} %coup_ref.1) | copy-start | bytes 772
  17.9 8.4 %collective-permute-start.8 = (f32[128,128]{1,0:T(8,128)S(1)}, f32[128,128]{1,0:T(8,128)S(1)}, u32[]{:S(2)}, u32[]{:S(2)}) collective-permute-start(f32[128,128]{1,0:T(8,128)S(1)} %get-tuple-element.39), channel_id=1, source_target_pairs={{0,8},{8,16},{16,24},{24,0},{1,9},{9,17},{17,25},{25,1},{2,10},{10... | collective-permute-start | bytes 196616 | tf_op jit(solution)/shard_map/ppermute | solution.py:409
  21.4 4.9 %collective-permute-start.9 = (f32[128,128]{1,0:T(8,128)S(1)}, f32[128,128]{1,0:T(8,128)S(1)}, u32[]{:S(2)}, u32[]{:S(2)}) collective-permute-start(f32[128,128]{1,0:T(8,128)S(1)} %get-tuple-element.40), channel_id=1, source_target_pairs={{0,24},{8,0},{16,8},{24,16},{1,25},{9,1},{17,9},{25,17},{2,26},{10... | collective-permute-start | bytes 196616 | tf_op jit(solution)/shard_map/ppermute | solution.py:409

commit v11 on v10

--- a/solution.py
+++ b/solution.py
@@ -82,7 +82,8 @@
             x_ref[pl.ds((3 * m + c) * nz, nz), :] = v_ref[b, pl.ds(c * nz, nz), :] * scale
 
 
-def relay_kernel(nz, x_ref, after_f_ref, after_b_ref, y_ref):
+def relay_kernel(nz, x_ref, *refs):
+    y_ref = refs[-1]
     odd = odd_loop()
     count = x_ref.shape[0] // (3 * nz)
 
@@ -104,7 +105,7 @@
             store(m, forward_pair(*comps(m)))
 
 
-def edge_kernel(cut, v_ref, scale_ref, near_ref, far_ref, fwd_ref, bwd_ref):
+def edge_kernel(cut, v_ref, scale_ref, near_ref, far_ref, x_ref):
     scale = scale_ref[...]
     nz = scale.shape[0]
     lane = lane_ids(scale.shape)
@@ -120,7 +121,8 @@
     near_ref[...] = jnp.where(even, right, left)
     far_ref[...] = jnp.where(even, left, right)
     for m, b in enumerate(range(*cut)):
-        packed(v_ref, b, scale, fwd_ref, bwd_ref, 2 * m)
+        for c in range(3):
+            x_ref[pl.ds((3 * m + c) * nz, nz), :] = v_ref[b, pl.ds(c * nz, nz), :] * scale
 
 
 def turned(x):
@@ -128,7 +130,9 @@
     return jnp.concatenate([x, pad], axis=0).T
 
 
-def corner_kernel(begin, end, v_ref, scale_ref, near_ref, far_ref, fwd_ref, bwd_ref, fr_ref, fl_ref):
+def corner_kernel(
+    begin, end, v_ref, scale_ref, near_ref, far_ref, after_ref, fwd_ref, bwd_ref, fr_ref, fl_ref
+):
     scale = scale_ref[...]
     for b in range(begin, end):
         packed(v_ref, b, scale, fwd_ref, bwd_ref, 2 * (b - begin))
@@ -143,7 +147,7 @@
     bwd_ref[rows, :] = turned(from_left)[2 * nb : 3 * nb, :]
 
 
-def more_kernel(begin, end, v_ref, scale_ref, fwd_a_ref, bwd_a_ref, fwd_ref, bwd_ref):
+def more_kernel(begin, end, v_ref, scale_ref, after_ref, fwd_ref, bwd_ref):
     scale = scale_ref[...]
     for b in range(begin, end):
         packed(v_ref, b, scale, fwd_ref, bwd_ref, 2 * (b - begin))
@@ -439,7 +443,7 @@
     plane = jax.ShapeDtypeStruct((nz, nt), f32)
     pay_shape = jax.ShapeDtypeStruct((2, nt), f32)
     assert lax.axis_size("loop") % 2 == 0 and lax.axis_size("trans") % 2 == 0
-    marks = (0, nb * 3 // 8, nb * 5 // 8, nb - 1, nb)
+    marks = (0, nb // 4, nb // 2, nb - 1, nb)
     cut_r, cut_a, cut_b, cut_c = zip(marks[:-1], marks[1:])
 
     def planes(n, more=0):
@@ -465,47 +469,51 @@
         name="first",
     )(*(pltpu.with_memory_space_constraint(x, pltpu.HBM) for x in (v, mat, permittivity)))
     x_r = swap(x_r)
-    near, far, fwd_a, bwd_a = pl.pallas_call(
+    near, far, x_a = pl.pallas_call(
         lambda *refs: edge_kernel(cut_a, *refs),
-        out_shape=(plane, plane, planes(size_a), planes(size_a)),
+        out_shape=(plane, plane, planes(size_a * 3 // 2)),
         in_specs=[vm, vm],
-        out_specs=(vm,) * 4,
+        out_specs=(vm,) * 3,
         compiler_params=params,
         cost_estimate=free,
         name="edges",
     )(v, scale)
     near, far = trans_swaps(near, far)
-    fwd_a, bwd_a = shift(fwd_a, 1), shift(bwd_a, -1)
+    x_a = swap(x_a)
+    def relay_pair(x, size, name, *after):
+        return pl.pallas_call(
+            lambda *refs: relay_kernel(nz, *refs),
+            out_shape=planes(size),
+            in_specs=[vm] + [hbm] * len(after),
+            out_specs=vm,
+            compiler_params=params,
+            cost_estimate=free,
+            name=name,
+        )(x, *after)
+
+    pair_r = relay_pair(x_r, size_r, "relay", near, far)
+    y_r = relay(pair_r)
     own_f, own_b, from_left, from_right = pl.pallas_call(
         lambda *refs: corner_kernel(*cut_b, *refs),
         out_shape=(planes(size_b, nb), planes(size_b, nb), plane, plane),
-        in_specs=[vm] * 4,
+        in_specs=[vm] * 4 + [hbm],
         out_specs=(vm,) * 4,
         compiler_params=params,
         cost_estimate=free,
         name="pack_b",
-    )(v, scale, near, far)
+    )(v, scale, near, far, pair_r)
     fwd_b, bwd_b = shift(own_f, 1), shift(own_b, -1)
-    y_r = relay(
-        pl.pallas_call(
-            lambda *refs: relay_kernel(nz, *refs),
-            out_shape=planes(size_r),
-            in_specs=[vm, hbm, hbm],
-            out_specs=vm,
-            compiler_params=params,
-            cost_estimate=free,
-            name="relay",
-        )(x_r, own_f, own_b)
-    )
+    pair_a = relay_pair(x_a, size_a, "relay_a", pair_r)
+    y_a = relay(pair_a)
     fwd_c, bwd_c = pl.pallas_call(
         lambda *refs: more_kernel(*cut_c, *refs),
         out_shape=(planes(size_c), planes(size_c)),
-        in_specs=[vm, vm, hbm, hbm],
+        in_specs=[vm, vm, hbm],
         out_specs=(vm, vm),
         compiler_params=params,
         cost_estimate=free,
         name="pack_c",
-    )(v, scale, fwd_a, bwd_a)
+    )(v, scale, pair_a)
     fwd_c, bwd_c = shift(fwd_c, 1), shift(bwd_c, -1)
     inner, pay = pl.pallas_call(
         inner_kernel,
@@ -517,14 +525,14 @@
         name="inner",
     )(coupling_prev, v, scale, q, from_left, from_right)
     w_ab, pay, columns_f, columns_b = pl.pallas_call(
-        lambda *refs: sum_kernel(((*cut_r, True), (*cut_a, False), (*cut_b, False)), 0, *refs),
+        lambda *refs: sum_kernel(((*cut_r, True), (*cut_a, True), (*cut_b, False)), 0, *refs),
         out_shape=(works(cut_b[1]), pay_shape, plane, plane),
         in_specs=[vm] * 12,
         out_specs=(vm,) * 4,
         compiler_params=params,
         cost_estimate=free,
         name="products",
-    )(v, scale, inner, pay, x_r, y_r, fwd_a, bwd_a, fwd_b, bwd_b, fwd_b, bwd_b)
+    )(v, scale, inner, pay, x_r, y_r, x_a, y_a, fwd_b, bwd_b, fwd_b, bwd_b)
     w_c, pay = pl.pallas_call(
         lambda *refs: sum_kernel(((*cut_c, False),), cut_c[0], *refs),
         out_shape=(works(cut_c[1] - cut_c[0]), pay_shape),

time: 41.6 us -> 43.4 us (1.043)
  waiting for transfers between devices: 4.83 us -> 9.45 us
  blocking collectives: 12.9 us -> 10.7 us
  starting transfers between devices: 15 us -> 14.3 us
    ppermute x1 -> x2, waiting for transfers between devices: 0.01 us -> 5.02 us  [relay(): lax.ppermute(x, 'loop', [(i, (i + (-2 if i % 2 else 2)) % count) for i in...]
    all_to_all x1, blocking collectives: 12.9 us -> 10.7 us  [local(): pay = lax.all_to_all(pay, ('loop', 'trans'), 0, 0)]
    ppermute x6 -> x4, waiting for transfers between devices: 1.74 us -> 0.01 us  [shift(): lax.ppermute(x, 'loop', [(i, (i + loop_by) % count) for i in range(count)])]
    ppermute x6 -> x4, starting transfers between devices: 9.4 us -> 8.35 us  [shift(): lax.ppermute(x, 'loop', [(i, (i + loop_by) % count) for i in range(count)])]
    ppermute x1 -> x2, waiting for transfers between devices: 3.08 us -> 3.89 us  [swap(): lax.ppermute(x, 'loop', [(i, i ^ 1) for i in range(lax.axis_size('loop'))])]
    ppermute x1, waiting for transfers between devices: 0.01 us -> 0.53 us  [trans_swaps(): lax.ppermute(near, 'trans', [(t, t ^ 1) for t in range(count)])]
    ppermute x1 -> x2, starting transfers between devices: 1.84 us -> 2.09 us  [relay(): lax.ppermute(x, 'loop', [(i, (i + (-2 if i % 2 else 2)) % count) for i in...]
    ppermute x1 -> x2, starting transfers between devices: 3 us -> 3.15 us  [swap(): lax.ppermute(x, 'loop', [(i, i ^ 1) for i in range(lax.axis_size('loop'))])]
where the time goes in v11:
time: 43.4 us; the launch traced here: 43.2 us
  starting transfers between devices  14.3 us (33%)
  blocking collectives  10.7 us (25%)
  waiting for transfers between devices  9.45 us (22%)
  Pallas kernels  8.02 us (18%)
  between operations  0.76 us (2%)
    all_to_all x1, blocking collectives, local(): pay = lax.all_to_all(pay, ('loop', 'trans'), 0, 0)  10.7 us
    ppermute x4, starting transfers between devices, shift(): lax.ppermute(x, 'loop', [(i, (i + loop_by) % count) for i in range(count)])  8.35 us
    ppermute x2, waiting for transfers between devices, relay(): lax.ppermute(x, 'loop', [(i, (i + (-2 if i % 2 else 2)) % count) for i in...  5.02 us
    ppermute x2, waiting for transfers between devices, swap(): lax.ppermute(x, 'loop', [(i, i ^ 1) for i in range(lax.axis_size('loop'))])  3.89 us
    ppermute x2, starting transfers between devices, swap(): lax.ppermute(x, 'loop', [(i, i ^ 1) for i in range(lax.axis_size('loop'))])  3.15 us
    pallas_call x1, Pallas kernels, local(): pl.pallas_call(inner_kernel, out_shape=(works(nb), pay_shape), in_specs=[...  2.65 us
    ppermute x2, starting transfers between devices, relay(): lax.ppermute(x, 'loop', [(i, (i + (-2 if i % 2 else 2)) % count) for i in...  2.09 us
    pallas_call x1, Pallas kernels, local(): pl.pallas_call(lambda *refs: last_kernel(count, *refs), out_shape=(works(...  1.9 us
  transfers between devices with their start and end apart: 10, of which 3 were waited for; matrix products, arithmetic and copies ran while one was open for 0% of the time, Pallas kernels for 11%

profile of v11, /device:TPU:0, one launch (start us, length us, event | category | flops | bytes accessed | tf_op | source)
XLA Modules:
  0.0 43.2 jit_solution(964824187970127338)
XLA Ops:
  0.6 0.0 copy-start
  0.6 1.1 %first.1 = (f32[384,128]{1,0:T(8,128)S(1)}, f32[64,128]{1,0:T(8,128)S(1)}) custom-call(f32[8,192,128]{2,1,0:T(8,128)} %bitcast.6, s32[64,128]{1,0:T(8,128)} %bitcast.15, f32[4]{0:T(128)} %refs_2_.1), custom_call_target="tpu_custom_call" | custom-call | tf_op jit(solution)/shard_map/first/pallas_call | solution.py:456
  1.7 3.0 %collective-permute-start.2 = (f32[384,128]{1,0:T(8,128)S(1)}, f32[384,128]{1,0:T(8,128)S(1)}, u32[]{:S(2)}, u32[]{:S(2)}) collective-permute-start(f32[384,128]{1,0:T(8,128)S(1)} %get-tuple-element.28), channel_id=1, source_target_pairs={{0,8},{8,0},{16,24},{24,16},{1,9},{9,1},{17,25},{25,17},{2,10},{10... | collective-permute-start | bytes 589832 | tf_op jit(solution)/shard_map/ppermute | solution.py:423
  4.7 0.0 copy-done
  4.7 0.5 %edges.1 = (f32[64,128]{1,0:T(8,128)S(1)}, f32[64,128]{1,0:T(8,128)S(1)}, f32[384,128]{1,0:T(8,128)S(1)}) custom-call(f32[8,192,128]{2,1,0:T(8,128)S(1)} %bitcast.7, f32[64,128]{1,0:T(8,128)S(1)} %get-tuple-element.25.refs_1_.scale_ref), custom_call_target="tpu_custom_call" | custom-call | tf_op jit(solution)/shard_map/edges/pallas_call | solution.py:472
  5.2 0.1 collective-permute-start.4
  5.4 0.0 collective-permute-start
  5.4 0.7 %collective-permute-start.1 = (f32[64,128]{1,0:T(8,128)S(1)}, f32[64,128]{1,0:T(8,128)S(1)}, u32[]{:S(2)}, u32[]{:S(2)}) collective-permute-start(f32[64,128]{1,0:T(8,128)S(1)} %get-tuple-element.27), channel_id=1, source_target_pairs={{1,2},{2,1},{3,4},{4,3},{5,6},{6,5},{9,10},{10,9},{11,12},{12,11},... | collective-permute-start | bytes 98312 | tf_op jit(solution)/shard_map/ppermute | solution.py:419
  6.0 0.5 %collective-permute-done.refs_1_.refs_2_ = f32[64,128]{1,0:T(8,128)S(1)} collective-permute-done((f32[64,128]{1,0:T(8,128)S(1)}, f32[64,128]{1,0:T(8,128)S(1)}, u32[]{:S(2)}, u32[]{:S(2)}) %collective-permute-start) | collective-permute-done | bytes 32800 | tf_op jit(solution)/shard_map/ppermute | solution.py:419
  6.6 0.0 collective-permute-done.1.refs_2_.refs_3_
  6.6 3.9 %collective-permute-done.2.refs_0_.refs_4_ = f32[384,128]{1,0:T(8,128)S(1)} collective-permute-done((f32[384,128]{1,0:T(8,128)S(1)}, f32[384,128]{1,0:T(8,128)S(1)}, u32[]{:S(2)}, u32[]{:S(2)}) %collective-permute-start.2) | collective-permute-done | bytes 196640 | tf_op jit(solution)/shard_map/ppermute | solution.py:423
  10.5 0.1 relay.1.refs_4_.refs_1_
  10.5 0.1 pack_b.1
  10.7 0.0 copy-start.1
  10.7 2.0 %collective-permute-start.6 = (f32[392,128]{1,0:T(8,128)S(1)}, f32[392,128]{1,0:T(8,128)S(1)}, u32[]{:S(2)}, u32[]{:S(2)}) collective-permute-start(f32[392,128]{1,0:T(8,128)S(1)} %get-tuple-element.34), channel_id=1, source_target_pairs={{0,8},{8,16},{16,24},{24,0},{1,9},{9,17},{17,25},{25,1},{2,10},{10... | collective-permute-start | bytes 602120 | tf_op jit(solution)/shard_map/ppermute | solution.py:413
  12.7 1.0 %collective-permute-start.7 = (f32[392,128]{1,0:T(8,128)S(1)}, f32[392,128]{1,0:T(8,128)S(1)}, u32[]{:S(2)}, u32[]{:S(2)}) collective-permute-start(f32[392,128]{1,0:T(8,128)S(1)} %get-tuple-element.35), channel_id=1, source_target_pairs={{0,24},{8,0},{16,8},{24,16},{1,25},{9,1},{17,9},{25,17},{2,26},{10... | collective-permute-start | bytes 602120 | tf_op jit(solution)/shard_map/ppermute | solution.py:413
  13.7 2.0 %collective-permute-start.3 = (f32[256,128]{1,0:T(8,128)S(1)}, f32[256,128]{1,0:T(8,128)S(1)}, u32[]{:S(2)}, u32[]{:S(2)}) collective-permute-start(f32[256,128]{1,0:T(8,128)S(1)} %relay.1.refs_4_.refs_1_), channel_id=1, source_target_pairs={{0,16},{8,24},{16,0},{24,8},{1,17},{9,25},{17,1},{25,9},{2,18},{10... | collective-permute-start | bytes 393224 | tf_op jit(solution)/shard_map/ppermute | solution.py:428
  15.7 0.0 collective-permute-done.4.refs_0_.refs_6_
  15.7 0.1 relay_a.1.refs_2_
  15.8 0.1 collective-permute-start.5
  15.9 0.1 pack_c.1
  16.0 0.0 copy-start.2
  16.0 1.3 %collective-permute-start.8 = (f32[128,128]{1,0:T(8,128)S(1)}, f32[128,128]{1,0:T(8,128)S(1)}, u32[]{:S(2)}, u32[]{:S(2)}) collective-permute-start(f32[128,128]{1,0:T(8,128)S(1)} %get-tuple-element.37), channel_id=1, source_target_pairs={{0,8},{8,16},{16,24},{24,0},{1,9},{9,17},{17,25},{25,1},{2,10},{10... | collective-permute-start | bytes 196616 | tf_op jit(solution)/shard_map/ppermute | solution.py:413
  17.3 5.0 %collective-permute-done.3.refs_5_ = f32[256,128]{1,0:T(8,128)S(1)} collective-permute-done((f32[256,128]{1,0:T(8,128)S(1)}, f32[256,128]{1,0:T(8,128)S(1)}, u32[]{:S(2)}, u32[]{:S(2)}) %collective-permute-start.3) | collective-permute-done | bytes 131104 | tf_op jit(solution)/shard_map/ppermute | solution.py:428
  22.4 4.0 %collective-permute-start.9 = (f32[128,128]{1,0:T(8,128)S(1)}, f32[128,128]{1,0:T(8,128)S(1)}, u32[]{:S(2)}, u32[]{:S(2)}) collective-permute-start(f32[128,128]{1,0:T(8,128)S(1)} %get-tuple-element.38), channel_id=1, source_target_pairs={{0,24},{8,0},{16,8},{24,16},{1,25},{9,1},{17,9},{25,17},{2,26},{10... | collective-permute-start | bytes 196616 | tf_op jit(solution)/shard_map/ppermute | solution.py:413
  26.3 0.0 copy-done.1
  26.3 0.0 copy-done.2
  26.3 2.7 %inner.1 = (f32[8,192,128]{2,1,0:T(8,128)S(1)}, f32[2,128]{1,0:T(2,128)S(1)}) custom-call(f32[8,8]{1,0:T(8,128)S(1)} %copy-done.2, f32[8,192,128]{2,1,0:T(8,128)S(1)} %bitcast.10, f32[64,128]{1,0:T(8,128)S(1)} %get-tuple-element.25.refs_1_.scale_ref, f32[8,192,128]{2,1,0:T(8,128)S(1)} %bitcast.14, f32[64,128]{1,0:T(8,128)S(1)} %get-tuple-element.29.fr_ref, ...), custom_call_target="tpu_custom_call" | custom-call | tf_op jit(solution)/shard_map/inner/pallas_call | solution.py:518
  29.0 0.0 collective-permute-done.5.refs_7_
  29.0 0.0 collective-permute-done.6.refs_8_.refs_10_
  29.0 0.0 collective-permute-done.7.refs_9_.refs_11_
  29.0 1.2 %products.1 = (f32[7,192,128]{2,1,0:T(8,128)S(1)}, f32[2,128]{1,0:T(2,128)S(1)}, f32[64,128]{1,0:T(8,128)S(1)}, f32[64,128]{1,0:T(8,128)S(1)}) custom-call(f32[8,192,128]{2,1,0:T(8,128)S(1)} %bitcast.11, f32[64,128]{1,0:T(8,128)S(1)} %get-tuple-element.25.refs_1_.scale_ref, f32[8,192,128]{2,1,0:T(8,128)S(1)} %get-tuple-element.31.refs_2_, ...), custom_call_target="tpu_custom_call" | custom-call | tf_op jit(solution)/shard_map/products/pallas_call | solution.py:527
  30.3 0.0 collective-permute-done.8.refs_4_
  30.3 0.0 collective-permute-done.9.refs_5_
  30.3 0.3 products_last.1
  30.6 10.7 %all_to_all.5.refs_0_ = f32[32,2,128]{2,1,0:T(2,128)S(1)} all-to-all(f32[32,2,128]{2,1,0:T(2,128)S(1)} %broadcast_in_dim.2), channel_id=1, replica_groups=mesh['loop'=4,'trans'=8] {'loop','trans'}, dimensions={0} | all-to-all | bytes 65536 | tf_op jit(solution)/shard_map/all_to_all | solution.py:546
  41.3 1.9 %combine.1 = (f32[8,192,128]{2,1,0:T(8,128)}, f32[8,8]{1,0:T(8,128)}, f32[8,8]{1,0:T(8,128)}) custom-call(f32[32,2,128]{2,1,0:T(2,128)S(1)} %all_to_all.5.refs_0_, f32[8,192,128]{2,1,0:T(8,128)S(1)} %bitcast.13, f32[7,192,128]{2,1,0:T(8,128)S(1)} %get-tuple-element.41.refs_8_.refs_2_, f32[1,192,128]{2,1,0:T(8,128)S(1)} %get-tuple-element.43.refs_3_), custom_call_target="tpu_custom_call" | custom-call | tf_op jit(solution)/shard_map/combine/pallas_call | solution.py:548
  (1 shorter events, 0.0 us)
Async XLA Ops:
  0.6 4.1 %copy-start = (f32[8,3,64,1,128]{4,3,2,1,0:T(1,128)S(1)}, f32[8,3,64,1,128]{4,3,2,1,0:T(1,128)}, u32[]{:S(2)}) copy-start(f32[8,3,64,1,128]{4,3,2,1,0:T(1,128)} %param.5) | copy-start | bytes 2359300
  1.7 8.7 %collective-permute-start.2 = (f32[384,128]{1,0:T(8,128)S(1)}, f32[384,128]{1,0:T(8,128)S(1)}, u32[]{:S(2)}, u32[]{:S(2)}) collective-permute-start(f32[384,128]{1,0:T(8,128)S(1)} %get-tuple-element.28), channel_id=1, source_target_pairs={{0,8},{8,0},{16,24},{24,16},{1,9},{9,1},{17,25},{25,17},{2,10},{10... | collective-permute-start | bytes 589832 | tf_op jit(solution)/shard_map/ppermute | solution.py:423
  5.2 10.5 %collective-permute-start.4 = (f32[384,128]{1,0:T(8,128)S(1)}, f32[384,128]{1,0:T(8,128)S(1)}, u32[]{:S(2)}, u32[]{:S(2)}) collective-permute-start(f32[384,128]{1,0:T(8,128)S(1)} %get-tuple-element.33), channel_id=1, source_target_pairs={{0,8},{8,0},{16,24},{24,16},{1,9},{9,1},{17,25},{25,17},{2,10},{10... | collective-permute-start | bytes 589832 | tf_op jit(solution)/shard_map/ppermute | solution.py:423
  5.4 1.2 %collective-permute-start = (f32[64,128]{1,0:T(8,128)S(1)}, f32[64,128]{1,0:T(8,128)S(1)}, u32[]{:S(2)}, u32[]{:S(2)}) collective-permute-start(f32[64,128]{1,0:T(8,128)S(1)} %get-tuple-element.26), channel_id=1, source_target_pairs={{0,1},{1,0},{2,3},{3,2},{4,5},{5,4},{6,7},{7,6},{8,9},{9,8},{10,11... | collective-permute-start | bytes 98312 | tf_op jit(solution)/shard_map/ppermute | solution.py:419
  5.4 1.2 %collective-permute-start.1 = (f32[64,128]{1,0:T(8,128)S(1)}, f32[64,128]{1,0:T(8,128)S(1)}, u32[]{:S(2)}, u32[]{:S(2)}) collective-permute-start(f32[64,128]{1,0:T(8,128)S(1)} %get-tuple-element.27), channel_id=1, source_target_pairs={{1,2},{2,1},{3,4},{4,3},{5,6},{6,5},{9,10},{10,9},{11,12},{12,11},... | collective-permute-start | bytes 98312 | tf_op jit(solution)/shard_map/ppermute | solution.py:419
  10.7 15.7 %copy-start.1 = (f32[8,3,64,1,128]{4,3,2,1,0:T(1,128)S(1)}, f32[8,3,64,1,128]{4,3,2,1,0:T(1,128)}, u32[]{:S(2)}) copy-start(f32[8,3,64,1,128]{4,3,2,1,0:T(1,128)} %param.6) | copy-start | bytes 2359300
  10.7 18.3 %collective-permute-start.6 = (f32[392,128]{1,0:T(8,128)S(1)}, f32[392,128]{1,0:T(8,128)S(1)}, u32[]{:S(2)}, u32[]{:S(2)}) collective-permute-start(f32[392,128]{1,0:T(8,128)S(1)} %get-tuple-element.34), channel_id=1, source_target_pairs={{0,8},{8,16},{16,24},{24,0},{1,9},{9,17},{17,25},{25,1},{2,10},{10... | collective-permute-start | bytes 602120 | tf_op jit(solution)/shard_map/ppermute | solution.py:413
  12.7 16.3 %collective-permute-start.7 = (f32[392,128]{1,0:T(8,128)S(1)}, f32[392,128]{1,0:T(8,128)S(1)}, u32[]{:S(2)}, u32[]{:S(2)}) collective-permute-start(f32[392,128]{1,0:T(8,128)S(1)} %get-tuple-element.35), channel_id=1, source_target_pairs={{0,24},{8,0},{16,8},{24,16},{1,25},{9,1},{17,9},{25,17},{2,26},{10... | collective-permute-start | bytes 602120 | tf_op jit(solution)/shard_map/ppermute | solution.py:413
  13.7 8.6 %collective-permute-start.3 = (f32[256,128]{1,0:T(8,128)S(1)}, f32[256,128]{1,0:T(8,128)S(1)}, u32[]{:S(2)}, u32[]{:S(2)}) collective-permute-start(f32[256,128]{1,0:T(8,128)S(1)} %relay.1.refs_4_.refs_1_), channel_id=1, source_target_pairs={{0,16},{8,24},{16,0},{24,8},{1,17},{9,25},{17,1},{25,9},{2,18},{10... | collective-permute-start | bytes 393224 | tf_op jit(solution)/shard_map/ppermute | solution.py:428
  15.8 13.2 %collective-permute-start.5 = (f32[256,128]{1,0:T(8,128)S(1)}, f32[256,128]{1,0:T(8,128)S(1)}, u32[]{:S(2)}, u32[]{:S(2)}) collective-permute-start(f32[256,128]{1,0:T(8,128)S(1)} %relay_a.1.refs_2_), channel_id=1, source_target_pairs={{0,16},{8,24},{16,0},{24,8},{1,17},{9,25},{17,1},{25,9},{2,18},{10... | collective-permute-start | bytes 393224 | tf_op jit(solution)/shard_map/ppermute | solution.py:428
  16.0 10.3 %copy-start.2 = (f32[8,8]{1,0:T(8,128)S(1)}, f32[8,8]{1,0:T(8,128)}, u32[]{:S(2)}) copy-start(f32[8,8]{1,0:T(8,128)} %coup_ref.1) | copy-start | bytes 772
  16.0 14.2 %collective-permute-start.8 = (f32[128,128]{1,0:T(8,128)S(1)}, f32[128,128]{1,0:T(8,128)S(1)}, u32[]{:S(2)}, u32[]{:S(2)}) collective-permute-start(f32[128,128]{1,0:T(8,128)S(1)} %get-tuple-element.37), channel_id=1, source_target_pairs={{0,8},{8,16},{16,24},{24,0},{1,9},{9,17},{17,25},{25,1},{2,10},{10... | collective-permute-start | bytes 196616 | tf_op jit(solution)/shard_map/ppermute | solution.py:413
  22.4 7.9 %collective-permute-start.9 = (f32[128,128]{1,0:T(8,128)S(1)}, f32[128,128]{1,0:T(8,128)S(1)}, u32[]{:S(2)}, u32[]{:S(2)}) collective-permute-start(f32[128,128]{1,0:T(8,128)S(1)} %get-tuple-element.38), channel_id=1, source_target_pairs={{0,24},{8,0},{16,8},{24,16},{1,25},{9,1},{17,9},{25,17},{2,26},{10... | collective-permute-start | bytes 196616 | tf_op jit(solution)/shard_map/ppermute | solution.py:413

commit v12 on v10

--- a/solution.py
+++ b/solution.py
@@ -439,7 +439,7 @@
     plane = jax.ShapeDtypeStruct((nz, nt), f32)
     pay_shape = jax.ShapeDtypeStruct((2, nt), f32)
     assert lax.axis_size("loop") % 2 == 0 and lax.axis_size("trans") % 2 == 0
-    marks = (0, nb * 3 // 8, nb * 5 // 8, nb - 1, nb)
+    marks = (0, nb // 2, nb * 3 // 4, nb - 1, nb)
     cut_r, cut_a, cut_b, cut_c = zip(marks[:-1], marks[1:])
 
     def planes(n, more=0):

time: 41.6 us -> 46.5 us (1.12)
  waiting for transfers between devices: 4.83 us -> 10.4 us
  starting transfers between devices: 15 us -> 14.5 us
    ppermute x1, waiting for transfers between devices: 3.08 us -> 7.25 us  [swap(): lax.ppermute(x, 'loop', [(i, i ^ 1) for i in range(lax.axis_size('loop'))])]
    ppermute x6, waiting for transfers between devices: 1.74 us -> 2.67 us  [shift(): lax.ppermute(x, 'loop', [(i, (i + loop_by) % count) for i in range(count)])]
    ppermute x1, waiting for transfers between devices: 0.01 us -> 0.52 us  [trans_swaps(): lax.ppermute(near, 'trans', [(t, t ^ 1) for t in range(count)])]
  transfers between devices with their start and end apart: 10 -> 10, of which waited for: 3 -> 4; matrix products, arithmetic and copies ran while one was open for 0% -> 0% of each run, Pallas kernels for 11% -> 10%
where the time goes in v12:
time: 46.5 us; the launch traced here: 46.4 us
  starting transfers between devices  14.5 us (31%)
  blocking collectives  12.5 us (27%)
  waiting for transfers between devices  10.4 us (22%)
  Pallas kernels  8.04 us (17%)
  between operations  0.76 us (2%)
    all_to_all x1, blocking collectives, local(): pay = lax.all_to_all(pay, ('loop', 'trans'), 0, 0)  12.5 us
    ppermute x6, starting transfers between devices, shift(): lax.ppermute(x, 'loop', [(i, (i + loop_by) % count) for i in range(count)])  8.98 us
    ppermute x1, waiting for transfers between devices, swap(): lax.ppermute(x, 'loop', [(i, i ^ 1) for i in range(lax.axis_size('loop'))])  7.25 us
    ppermute x1, starting transfers between devices, swap(): lax.ppermute(x, 'loop', [(i, i ^ 1) for i in range(lax.axis_size('loop'))])  3 us
    ppermute x6, waiting for transfers between devices, shift(): lax.ppermute(x, 'loop', [(i, (i + loop_by) % count) for i in range(count)])  2.67 us
    pallas_call x1, Pallas kernels, local(): pl.pallas_call(inner_kernel, out_shape=(works(nb), pay_shape), in_specs=[...  2.65 us
    pallas_call x1, Pallas kernels, local(): pl.pallas_call(lambda *refs: last_kernel(count, *refs), out_shape=(works(...  1.9 us
    ppermute x1, starting transfers between devices, relay(): lax.ppermute(x, 'loop', [(i, (i + (-2 if i % 2 else 2)) % count) for i in...  1.83 us
  transfers between devices with their start and end apart: 10, of which 4 were waited for; matrix products, arithmetic and copies ran while one was open for 0% of the time, Pallas kernels for 10%

profile of v12, /device:TPU:0, one launch (start us, length us, event | category | flops | bytes accessed | tf_op | source)
XLA Modules:
  0.0 46.4 jit_solution(18407372491429611480)
XLA Ops:
  0.6 0.0 copy-start
  0.6 1.2 %first.1 = (f32[768,128]{1,0:T(8,128)S(1)}, f32[64,128]{1,0:T(8,128)S(1)}) custom-call(f32[8,192,128]{2,1,0:T(8,128)} %bitcast.6, s32[64,128]{1,0:T(8,128)} %bitcast.15, f32[4]{0:T(128)} %refs_2_.1), custom_call_target="tpu_custom_call" | custom-call | tf_op jit(solution)/shard_map/first/pallas_call | solution.py:452
  1.8 3.0 %collective-permute-start.2 = (f32[768,128]{1,0:T(8,128)S(1)}, f32[768,128]{1,0:T(8,128)S(1)}, u32[]{:S(2)}, u32[]{:S(2)}) collective-permute-start(f32[768,128]{1,0:T(8,128)S(1)} %get-tuple-element.33), channel_id=1, source_target_pairs={{0,8},{8,0},{16,24},{24,16},{1,9},{9,1},{17,25},{25,17},{2,10},{10... | collective-permute-start | bytes 1179656 | tf_op jit(solution)/shard_map/ppermute | solution.py:419
  4.8 0.0 copy-done
  4.8 0.5 %edges.1 = (f32[64,128]{1,0:T(8,128)S(1)}, f32[64,128]{1,0:T(8,128)S(1)}, f32[256,128]{1,0:T(8,128)S(1)}, f32[256,128]{1,0:T(8,128)S(1)}) custom-call(f32[8,192,128]{2,1,0:T(8,128)S(1)} %bitcast.7, f32[64,128]{1,0:T(8,128)S(1)} %get-tuple-element.26.refs_1_.scale_ref), custom_call_target="tpu_custom_call" | custom-call | tf_op jit(solution)/shard_map/edges/pallas_call | solution.py:468
  5.3 0.1 collective-permute-start
  5.4 0.7 %collective-permute-start.1 = (f32[64,128]{1,0:T(8,128)S(1)}, f32[64,128]{1,0:T(8,128)S(1)}, u32[]{:S(2)}, u32[]{:S(2)}) collective-permute-start(f32[64,128]{1,0:T(8,128)S(1)} %get-tuple-element.28), channel_id=1, source_target_pairs={{1,2},{2,1},{3,4},{4,3},{5,6},{6,5},{9,10},{10,9},{11,12},{12,11},... | collective-permute-start | bytes 98312 | tf_op jit(solution)/shard_map/ppermute | solution.py:415
  6.1 0.5 %collective-permute-done.refs_2_ = f32[64,128]{1,0:T(8,128)S(1)} collective-permute-done((f32[64,128]{1,0:T(8,128)S(1)}, f32[64,128]{1,0:T(8,128)S(1)}, u32[]{:S(2)}, u32[]{:S(2)}) %collective-permute-start) | collective-permute-done | bytes 32800 | tf_op jit(solution)/shard_map/ppermute | solution.py:415
  6.6 0.0 collective-permute-done.1.refs_3_
  6.6 0.1 pack_b.1
  6.7 7.2 %collective-permute-done.2.refs_0_.refs_4_ = f32[768,128]{1,0:T(8,128)S(1)} collective-permute-done((f32[768,128]{1,0:T(8,128)S(1)}, f32[768,128]{1,0:T(8,128)S(1)}, u32[]{:S(2)}, u32[]{:S(2)}) %collective-permute-start.2) | collective-permute-done | bytes 393248 | tf_op jit(solution)/shard_map/ppermute | solution.py:419
  14.0 0.0 copy-start.1
  14.0 0.1 relay.1
  14.1 1.8 %collective-permute-start.3 = (f32[512,128]{1,0:T(8,128)S(1)}, f32[512,128]{1,0:T(8,128)S(1)}, u32[]{:S(2)}, u32[]{:S(2)}) collective-permute-start(f32[512,128]{1,0:T(8,128)S(1)} %relay.1), channel_id=1, source_target_pairs={{0,16},{8,24},{16,0},{24,8},{1,17},{9,25},{17,1},{25,9},{2,18},{10... | collective-permute-start | bytes 786440 | tf_op jit(solution)/shard_map/ppermute | solution.py:424
  15.9 1.4 %collective-permute-start.4 = (f32[256,128]{1,0:T(8,128)S(1)}, f32[256,128]{1,0:T(8,128)S(1)}, u32[]{:S(2)}, u32[]{:S(2)}) collective-permute-start(f32[256,128]{1,0:T(8,128)S(1)} %get-tuple-element.36), channel_id=1, source_target_pairs={{0,8},{8,16},{16,24},{24,0},{1,9},{9,17},{17,25},{25,1},{2,10},{10... | collective-permute-start | bytes 393224 | tf_op jit(solution)/shard_map/ppermute | solution.py:409
  17.3 1.5 %collective-permute-start.5 = (f32[256,128]{1,0:T(8,128)S(1)}, f32[256,128]{1,0:T(8,128)S(1)}, u32[]{:S(2)}, u32[]{:S(2)}) collective-permute-start(f32[256,128]{1,0:T(8,128)S(1)} %get-tuple-element.37), channel_id=1, source_target_pairs={{0,24},{8,0},{16,8},{24,16},{1,25},{9,1},{17,9},{25,17},{2,26},{10... | collective-permute-start | bytes 393224 | tf_op jit(solution)/shard_map/ppermute | solution.py:409
  18.8 0.5 %collective-permute-start.6 = (f32[136,128]{1,0:T(8,128)S(1)}, f32[136,128]{1,0:T(8,128)S(1)}, u32[]{:S(2)}, u32[]{:S(2)}) collective-permute-start(f32[136,128]{1,0:T(8,128)S(1)} %get-tuple-element.34.refs_1_), channel_id=1, source_target_pairs={{0,8},{8,16},{16,24},{24,0},{1,9},{9,17},{17,25},{25,1},{2,10},{10... | collective-permute-start | bytes 208904 | tf_op jit(solution)/shard_map/ppermute | solution.py:409
  19.3 2.4 %collective-permute-start.7 = (f32[136,128]{1,0:T(8,128)S(1)}, f32[136,128]{1,0:T(8,128)S(1)}, u32[]{:S(2)}, u32[]{:S(2)}) collective-permute-start(f32[136,128]{1,0:T(8,128)S(1)} %get-tuple-element.35.refs_2_), channel_id=1, source_target_pairs={{0,24},{8,0},{16,8},{24,16},{1,25},{9,1},{17,9},{25,17},{2,26},{10... | collective-permute-start | bytes 208904 | tf_op jit(solution)/shard_map/ppermute | solution.py:409
  21.7 1.5 %collective-permute-done.4.refs_6_.refs_2_ = f32[256,128]{1,0:T(8,128)S(1)} collective-permute-done((f32[256,128]{1,0:T(8,128)S(1)}, f32[256,128]{1,0:T(8,128)S(1)}, u32[]{:S(2)}, u32[]{:S(2)}) %collective-permute-start.4) | collective-permute-done | bytes 131104 | tf_op jit(solution)/shard_map/ppermute | solution.py:409
  23.3 1.1 %collective-permute-done.5.refs_7_.refs_3_ = f32[256,128]{1,0:T(8,128)S(1)} collective-permute-done((f32[256,128]{1,0:T(8,128)S(1)}, f32[256,128]{1,0:T(8,128)S(1)}, u32[]{:S(2)}, u32[]{:S(2)}) %collective-permute-start.5) | collective-permute-done | bytes 131104 | tf_op jit(solution)/shard_map/ppermute | solution.py:409
  24.4 0.1 pack_c.1
  24.5 0.0 copy-start.2
  24.5 1.7 %collective-permute-start.8 = (f32[128,128]{1,0:T(8,128)S(1)}, f32[128,128]{1,0:T(8,128)S(1)}, u32[]{:S(2)}, u32[]{:S(2)}) collective-permute-start(f32[128,128]{1,0:T(8,128)S(1)} %get-tuple-element.39), channel_id=1, source_target_pairs={{0,8},{8,16},{16,24},{24,0},{1,9},{9,17},{17,25},{25,1},{2,10},{10... | collective-permute-start | bytes 196616 | tf_op jit(solution)/shard_map/ppermute | solution.py:409
  26.2 1.5 %collective-permute-start.9 = (f32[128,128]{1,0:T(8,128)S(1)}, f32[128,128]{1,0:T(8,128)S(1)}, u32[]{:S(2)}, u32[]{:S(2)}) collective-permute-start(f32[128,128]{1,0:T(8,128)S(1)} %get-tuple-element.40), channel_id=1, source_target_pairs={{0,24},{8,0},{16,8},{24,16},{1,25},{9,1},{17,9},{25,17},{2,26},{10... | collective-permute-start | bytes 196616 | tf_op jit(solution)/shard_map/ppermute | solution.py:409
  27.6 0.0 copy-done.1
  27.6 0.0 copy-done.2
  27.6 2.6 %inner.1 = (f32[8,192,128]{2,1,0:T(8,128)S(1)}, f32[2,128]{1,0:T(2,128)S(1)}) custom-call(f32[8,8]{1,0:T(8,128)S(1)} %copy-done.2, f32[8,192,128]{2,1,0:T(8,128)S(1)} %bitcast.10, f32[64,128]{1,0:T(8,128)S(1)} %get-tuple-element.26.refs_1_.scale_ref, f32[8,192,128]{2,1,0:T(8,128)S(1)} %bitcast.14, f32[64,128]{1,0:T(8,128)S(1)} %get-tuple-element.29.fr_ref, ...), custom_call_target="tpu_custom_call" | custom-call | tf_op jit(solution)/shard_map/inner/pallas_call | solution.py:510
  30.3 0.0 collective-permute-done.6.refs_8_.refs_10_
  30.3 0.0 collective-permute-done.7.refs_9_.refs_11_
  30.3 0.0 collective-permute-done.3.refs_5_
  30.3 1.2 %products.1 = (f32[7,192,128]{2,1,0:T(8,128)S(1)}, f32[2,128]{1,0:T(2,128)S(1)}, f32[64,128]{1,0:T(8,128)S(1)}, f32[64,128]{1,0:T(8,128)S(1)}) custom-call(f32[8,192,128]{2,1,0:T(8,128)S(1)} %bitcast.11, f32[64,128]{1,0:T(8,128)S(1)} %get-tuple-element.26.refs_1_.scale_ref, f32[8,192,128]{2,1,0:T(8,128)S(1)} %get-tuple-element.31.refs_2_, ...), custom_call_target="tpu_custom_call" | custom-call | tf_op jit(solution)/shard_map/products/pallas_call | solution.py:519
  31.6 0.0 collective-permute-done.8.refs_4_
  31.6 0.0 collective-permute-done.9.refs_5_
  31.6 0.3 products_last.1
  31.9 12.5 %all_to_all.5.refs_0_ = f32[32,2,128]{2,1,0:T(2,128)S(1)} all-to-all(f32[32,2,128]{2,1,0:T(2,128)S(1)} %broadcast_in_dim.2), channel_id=1, replica_groups=mesh['loop'=4,'trans'=8] {'loop','trans'}, dimensions={0} | all-to-all | bytes 65536 | tf_op jit(solution)/shard_map/all_to_all | solution.py:538
  44.5 1.9 %combine.1 = (f32[8,192,128]{2,1,0:T(8,128)}, f32[8,8]{1,0:T(8,128)}, f32[8,8]{1,0:T(8,128)}) custom-call(f32[32,2,128]{2,1,0:T(2,128)S(1)} %all_to_all.5.refs_0_, f32[8,192,128]{2,1,0:T(8,128)S(1)} %bitcast.13, f32[7,192,128]{2,1,0:T(8,128)S(1)} %get-tuple-element.43.refs_8_.refs_2_, f32[1,192,128]{2,1,0:T(8,128)S(1)} %get-tuple-element.45.refs_3_), custom_call_target="tpu_custom_call" | custom-call | tf_op jit(solution)/shard_map/combine/pallas_call | solution.py:540
  (1 shorter events, 0.0 us)
Async XLA Ops:
  0.6 4.2 %copy-start = (f32[8,3,64,1,128]{4,3,2,1,0:T(1,128)S(1)}, f32[8,3,64,1,128]{4,3,2,1,0:T(1,128)}, u32[]{:S(2)}) copy-start(f32[8,3,64,1,128]{4,3,2,1,0:T(1,128)} %param.5) | copy-start | bytes 2359300
  1.8 12.1 %collective-permute-start.2 = (f32[768,128]{1,0:T(8,128)S(1)}, f32[768,128]{1,0:T(8,128)S(1)}, u32[]{:S(2)}, u32[]{:S(2)}) collective-permute-start(f32[768,128]{1,0:T(8,128)S(1)} %get-tuple-element.33), channel_id=1, source_target_pairs={{0,8},{8,0},{16,24},{24,16},{1,9},{9,1},{17,25},{25,17},{2,10},{10... | collective-permute-start | bytes 1179656 | tf_op jit(solution)/shard_map/ppermute | solution.py:419
  5.3 1.3 %collective-permute-start = (f32[64,128]{1,0:T(8,128)S(1)}, f32[64,128]{1,0:T(8,128)S(1)}, u32[]{:S(2)}, u32[]{:S(2)}) collective-permute-start(f32[64,128]{1,0:T(8,128)S(1)} %get-tuple-element.27), channel_id=1, source_target_pairs={{0,1},{1,0},{2,3},{3,2},{4,5},{5,4},{6,7},{7,6},{8,9},{9,8},{10,11... | collective-permute-start | bytes 98312 | tf_op jit(solution)/shard_map/ppermute | solution.py:415
  5.4 1.2 %collective-permute-start.1 = (f32[64,128]{1,0:T(8,128)S(1)}, f32[64,128]{1,0:T(8,128)S(1)}, u32[]{:S(2)}, u32[]{:S(2)}) collective-permute-start(f32[64,128]{1,0:T(8,128)S(1)} %get-tuple-element.28), channel_id=1, source_target_pairs={{1,2},{2,1},{3,4},{4,3},{5,6},{6,5},{9,10},{10,9},{11,12},{12,11},... | collective-permute-start | bytes 98312 | tf_op jit(solution)/shard_map/ppermute | solution.py:415
  14.0 13.7 %copy-start.1 = (f32[8,3,64,1,128]{4,3,2,1,0:T(1,128)S(1)}, f32[8,3,64,1,128]{4,3,2,1,0:T(1,128)}, u32[]{:S(2)}) copy-start(f32[8,3,64,1,128]{4,3,2,1,0:T(1,128)} %param.6) | copy-start | bytes 2359300
  14.1 16.2 %collective-permute-start.3 = (f32[512,128]{1,0:T(8,128)S(1)}, f32[512,128]{1,0:T(8,128)S(1)}, u32[]{:S(2)}, u32[]{:S(2)}) collective-permute-start(f32[512,128]{1,0:T(8,128)S(1)} %relay.1), channel_id=1, source_target_pairs={{0,16},{8,24},{16,0},{24,8},{1,17},{9,25},{17,1},{25,9},{2,18},{10... | collective-permute-start | bytes 786440 | tf_op jit(solution)/shard_map/ppermute | solution.py:424
  15.9 7.4 %collective-permute-start.4 = (f32[256,128]{1,0:T(8,128)S(1)}, f32[256,128]{1,0:T(8,128)S(1)}, u32[]{:S(2)}, u32[]{:S(2)}) collective-permute-start(f32[256,128]{1,0:T(8,128)S(1)} %get-tuple-element.36), channel_id=1, source_target_pairs={{0,8},{8,16},{16,24},{24,0},{1,9},{9,17},{17,25},{25,1},{2,10},{10... | collective-permute-start | bytes 393224 | tf_op jit(solution)/shard_map/ppermute | solution.py:409
  17.3 7.1 %collective-permute-start.5 = (f32[256,128]{1,0:T(8,128)S(1)}, f32[256,128]{1,0:T(8,128)S(1)}, u32[]{:S(2)}, u32[]{:S(2)}) collective-permute-start(f32[256,128]{1,0:T(8,128)S(1)} %get-tuple-element.37), channel_id=1, source_target_pairs={{0,24},{8,0},{16,8},{24,16},{1,25},{9,1},{17,9},{25,17},{2,26},{10... | collective-permute-start | bytes 393224 | tf_op jit(solution)/shard_map/ppermute | solution.py:409
  18.8 11.5 %collective-permute-start.6 = (f32[136,128]{1,0:T(8,128)S(1)}, f32[136,128]{1,0:T(8,128)S(1)}, u32[]{:S(2)}, u32[]{:S(2)}) collective-permute-start(f32[136,128]{1,0:T(8,128)S(1)} %get-tuple-element.34.refs_1_), channel_id=1, source_target_pairs={{0,8},{8,16},{16,24},{24,0},{1,9},{9,17},{17,25},{25,1},{2,10},{10... | collective-permute-start | bytes 208904 | tf_op jit(solution)/shard_map/ppermute | solution.py:409
  19.3 11.0 %collective-permute-start.7 = (f32[136,128]{1,0:T(8,128)S(1)}, f32[136,128]{1,0:T(8,128)S(1)}, u32[]{:S(2)}, u32[]{:S(2)}) collective-permute-start(f32[136,128]{1,0:T(8,128)S(1)} %get-tuple-element.35.refs_2_), channel_id=1, source_target_pairs={{0,24},{8,0},{16,8},{24,16},{1,25},{9,1},{17,9},{25,17},{2,26},{10... | collective-permute-start | bytes 208904 | tf_op jit(solution)/shard_map/ppermute | solution.py:409
  24.5 3.1 %copy-start.2 = (f32[8,8]{1,0:T(8,128)S(1)}, f32[8,8]{1,0:T(8,128)}, u32[]{:S(2)}) copy-start(f32[8,8]{1,0:T(8,128)} %coup_ref.1) | copy-start | bytes 772
  24.5 7.1 %collective-permute-start.8 = (f32[128,128]{1,0:T(8,128)S(1)}, f32[128,128]{1,0:T(8,128)S(1)}, u32[]{:S(2)}, u32[]{:S(2)}) collective-permute-start(f32[128,128]{1,0:T(8,128)S(1)} %get-tuple-element.39), channel_id=1, source_target_pairs={{0,8},{8,16},{16,24},{24,0},{1,9},{9,17},{17,25},{25,1},{2,10},{10... | collective-permute-start | bytes 196616 | tf_op jit(solution)/shard_map/ppermute | solution.py:409
  26.2 5.4 %collective-permute-start.9 = (f32[128,128]{1,0:T(8,128)S(1)}, f32[128,128]{1,0:T(8,128)S(1)}, u32[]{:S(2)}, u32[]{:S(2)}) collective-permute-start(f32[128,128]{1,0:T(8,128)S(1)} %get-tuple-element.40), channel_id=1, source_target_pairs={{0,24},{8,0},{16,8},{24,16},{1,25},{9,1},{17,9},{25,17},{2,26},{10... | collective-permute-start | bytes 196616 | tf_op jit(solution)/shard_map/ppermute | solution.py:409

commit v13 on v10

--- a/solution.py
+++ b/solution.py
@@ -158,7 +158,7 @@
     return jnp.where(low, a, b) + swapped
 
 
-def add_products(pairs, steps, group, pays, unroll=8):
+def add_products(pairs, steps, group, pays, unroll=24):
     shape = pays[0].shape
     lane, row = lane_ids(shape), row_ids(shape)
     zero = jnp.zeros(shape, jnp.float32)

time: 41.6 us -> 41.5 us (level)
  no operation moved by 1% of the time
where the time goes in v13:
time: 41.5 us; the launch traced here: 41.3 us
  starting transfers between devices  15 us (36%)
  blocking collectives  12.9 us (31%)
  Pallas kernels  7.83 us (19%)
  waiting for transfers between devices  4.88 us (12%)
  between operations  0.73 us (2%)
    all_to_all x1, blocking collectives, local(): pay = lax.all_to_all(pay, ('loop', 'trans'), 0, 0)  12.9 us
    ppermute x6, starting transfers between devices, shift(): lax.ppermute(x, 'loop', [(i, (i + loop_by) % count) for i in range(count)])  9.4 us
    ppermute x1, waiting for transfers between devices, swap(): lax.ppermute(x, 'loop', [(i, i ^ 1) for i in range(lax.axis_size('loop'))])  3.08 us
    ppermute x1, starting transfers between devices, swap(): lax.ppermute(x, 'loop', [(i, i ^ 1) for i in range(lax.axis_size('loop'))])  3 us
    pallas_call x1, Pallas kernels, local(): pl.pallas_call(inner_kernel, out_shape=(works(nb), pay_shape), in_specs=[...  2.56 us
    pallas_call x1, Pallas kernels, local(): pl.pallas_call(lambda *refs: last_kernel(count, *refs), out_shape=(works(...  1.9 us
    ppermute x1, starting transfers between devices, relay(): lax.ppermute(x, 'loop', [(i, (i + (-2 if i % 2 else 2)) % count) for i in...  1.84 us
    ppermute x6, waiting for transfers between devices, shift(): lax.ppermute(x, 'loop', [(i, (i + loop_by) % count) for i in range(count)])  1.79 us
  transfers between devices with their start and end apart: 10, of which 3 were waited for; matrix products, arithmetic and copies ran while one was open for 0% of the time, Pallas kernels for 11%

profile of v13, /device:TPU:0, one launch (start us, length us, event | category | flops | bytes accessed | tf_op | source)
XLA Modules:
  0.0 41.3 jit_solution(15266045146323804991)
XLA Ops:
  0.6 0.0 copy-start
  0.6 1.1 %first.1 = (f32[576,128]{1,0:T(8,128)S(1)}, f32[64,128]{1,0:T(8,128)S(1)}) custom-call(f32[8,192,128]{2,1,0:T(8,128)} %bitcast.6, s32[64,128]{1,0:T(8,128)} %bitcast.15, f32[4]{0:T(128)} %refs_2_.1), custom_call_target="tpu_custom_call" | custom-call | tf_op jit(solution)/shard_map/first/pallas_call | solution.py:452
  1.8 3.0 %collective-permute-start.2 = (f32[576,128]{1,0:T(8,128)S(1)}, f32[576,128]{1,0:T(8,128)S(1)}, u32[]{:S(2)}, u32[]{:S(2)}) collective-permute-start(f32[576,128]{1,0:T(8,128)S(1)} %get-tuple-element.33), channel_id=1, source_target_pairs={{0,8},{8,0},{16,24},{24,16},{1,9},{9,1},{17,25},{25,17},{2,10},{10... | collective-permute-start | bytes 884744 | tf_op jit(solution)/shard_map/ppermute | solution.py:419
  4.8 0.0 copy-done
  4.8 0.5 %edges.1 = (f32[64,128]{1,0:T(8,128)S(1)}, f32[64,128]{1,0:T(8,128)S(1)}, f32[256,128]{1,0:T(8,128)S(1)}, f32[256,128]{1,0:T(8,128)S(1)}) custom-call(f32[8,192,128]{2,1,0:T(8,128)S(1)} %bitcast.7, f32[64,128]{1,0:T(8,128)S(1)} %get-tuple-element.26.refs_1_.scale_ref), custom_call_target="tpu_custom_call" | custom-call | tf_op jit(solution)/shard_map/edges/pallas_call | solution.py:468
  5.3 0.1 collective-permute-start
  5.4 0.7 %collective-permute-start.1 = (f32[64,128]{1,0:T(8,128)S(1)}, f32[64,128]{1,0:T(8,128)S(1)}, u32[]{:S(2)}, u32[]{:S(2)}) collective-permute-start(f32[64,128]{1,0:T(8,128)S(1)} %get-tuple-element.28), channel_id=1, source_target_pairs={{1,2},{2,1},{3,4},{4,3},{5,6},{6,5},{9,10},{10,9},{11,12},{12,11},... | collective-permute-start | bytes 98312 | tf_op jit(solution)/shard_map/ppermute | solution.py:415
  6.0 0.1 collective-permute-start.4
  6.2 2.9 %collective-permute-start.5 = (f32[256,128]{1,0:T(8,128)S(1)}, f32[256,128]{1,0:T(8,128)S(1)}, u32[]{:S(2)}, u32[]{:S(2)}) collective-permute-start(f32[256,128]{1,0:T(8,128)S(1)} %get-tuple-element.37), channel_id=1, source_target_pairs={{0,24},{8,0},{16,8},{24,16},{1,25},{9,1},{17,9},{25,17},{2,26},{10... | collective-permute-start | bytes 393224 | tf_op jit(solution)/shard_map/ppermute | solution.py:409
  9.0 0.0 collective-permute-done.refs_2_
  9.0 0.0 collective-permute-done.1.refs_3_
  9.0 0.1 pack_b.1
  9.1 3.1 %collective-permute-done.2.refs_0_.refs_4_ = f32[576,128]{1,0:T(8,128)S(1)} collective-permute-done((f32[576,128]{1,0:T(8,128)S(1)}, f32[576,128]{1,0:T(8,128)S(1)}, u32[]{:S(2)}, u32[]{:S(2)}) %collective-permute-start.2) | collective-permute-done | bytes 294944 | tf_op jit(solution)/shard_map/ppermute | solution.py:419
  12.2 0.0 copy-start.1
  12.2 0.1 relay.1
  12.3 1.8 %collective-permute-start.3 = (f32[384,128]{1,0:T(8,128)S(1)}, f32[384,128]{1,0:T(8,128)S(1)}, u32[]{:S(2)}, u32[]{:S(2)}) collective-permute-start(f32[384,128]{1,0:T(8,128)S(1)} %relay.1), channel_id=1, source_target_pairs={{0,16},{8,24},{16,0},{24,8},{1,17},{9,25},{17,1},{25,9},{2,18},{10... | collective-permute-start | bytes 589832 | tf_op jit(solution)/shard_map/ppermute | solution.py:424
  14.1 2.2 %collective-permute-start.6 = (f32[264,128]{1,0:T(8,128)S(1)}, f32[264,128]{1,0:T(8,128)S(1)}, u32[]{:S(2)}, u32[]{:S(2)}) collective-permute-start(f32[264,128]{1,0:T(8,128)S(1)} %get-tuple-element.34.refs_1_), channel_id=1, source_target_pairs={{0,8},{8,16},{16,24},{24,0},{1,9},{9,17},{17,25},{25,1},{2,10},{10... | collective-permute-start | bytes 405512 | tf_op jit(solution)/shard_map/ppermute | solution.py:409
  16.3 0.8 %collective-permute-start.7 = (f32[264,128]{1,0:T(8,128)S(1)}, f32[264,128]{1,0:T(8,128)S(1)}, u32[]{:S(2)}, u32[]{:S(2)}) collective-permute-start(f32[264,128]{1,0:T(8,128)S(1)} %get-tuple-element.35.refs_2_), channel_id=1, source_target_pairs={{0,24},{8,0},{16,8},{24,16},{1,25},{9,1},{17,9},{25,17},{2,26},{10... | collective-permute-start | bytes 405512 | tf_op jit(solution)/shard_map/ppermute | solution.py:409
  17.1 0.0 collective-permute-done.4.refs_6_.refs_2_
  17.1 0.8 %collective-permute-done.5.refs_7_.refs_3_ = f32[256,128]{1,0:T(8,128)S(1)} collective-permute-done((f32[256,128]{1,0:T(8,128)S(1)}, f32[256,128]{1,0:T(8,128)S(1)}, u32[]{:S(2)}, u32[]{:S(2)}) %collective-permute-start.5) | collective-permute-done | bytes 131104 | tf_op jit(solution)/shard_map/ppermute | solution.py:409
  17.8 0.1 pack_c.1
  17.9 0.0 copy-start.2
  17.9 3.5 %collective-permute-start.8 = (f32[128,128]{1,0:T(8,128)S(1)}, f32[128,128]{1,0:T(8,128)S(1)}, u32[]{:S(2)}, u32[]{:S(2)}) collective-permute-start(f32[128,128]{1,0:T(8,128)S(1)} %get-tuple-element.39), channel_id=1, source_target_pairs={{0,8},{8,16},{16,24},{24,0},{1,9},{9,17},{17,25},{25,1},{2,10},{10... | collective-permute-start | bytes 196616 | tf_op jit(solution)/shard_map/ppermute | solution.py:409
  21.4 0.0 collective-permute-start.9
  21.4 0.0 copy-done.1
  21.4 0.0 copy-done.2
  21.4 2.6 %inner.1 = (f32[8,192,128]{2,1,0:T(8,128)S(1)}, f32[2,128]{1,0:T(2,128)S(1)}) custom-call(f32[8,8]{1,0:T(8,128)S(1)} %copy-done.2, f32[8,192,128]{2,1,0:T(8,128)S(1)} %bitcast.10, f32[64,128]{1,0:T(8,128)S(1)} %get-tuple-element.26.refs_1_.scale_ref, f32[8,192,128]{2,1,0:T(8,128)S(1)} %bitcast.14, f32[64,128]{1,0:T(8,128)S(1)} %get-tuple-element.29.fr_ref, ...), custom_call_target="tpu_custom_call" | custom-call | tf_op jit(solution)/shard_map/inner/pallas_call | solution.py:510
  24.0 0.0 collective-permute-done.6.refs_8_.refs_10_
  24.0 0.0 collective-permute-done.7.refs_9_.refs_11_
  24.0 0.0 collective-permute-done.3.refs_5_
  24.0 1.2 %products.1 = (f32[7,192,128]{2,1,0:T(8,128)S(1)}, f32[2,128]{1,0:T(2,128)S(1)}, f32[64,128]{1,0:T(8,128)S(1)}, f32[64,128]{1,0:T(8,128)S(1)}) custom-call(f32[8,192,128]{2,1,0:T(8,128)S(1)} %bitcast.11, f32[64,128]{1,0:T(8,128)S(1)} %get-tuple-element.26.refs_1_.scale_ref, f32[8,192,128]{2,1,0:T(8,128)S(1)} %get-tuple-element.31.refs_2_, ...), custom_call_target="tpu_custom_call" | custom-call | tf_op jit(solution)/shard_map/products/pallas_call | solution.py:519
  25.2 1.0 %collective-permute-done.8.refs_4_ = f32[128,128]{1,0:T(8,128)S(1)} collective-permute-done((f32[128,128]{1,0:T(8,128)S(1)}, f32[128,128]{1,0:T(8,128)S(1)}, u32[]{:S(2)}, u32[]{:S(2)}) %collective-permute-start.8) | collective-permute-done | bytes 65568 | tf_op jit(solution)/shard_map/ppermute | solution.py:409
  26.3 0.0 collective-permute-done.9.refs_5_
  26.3 0.3 products_last.1
  26.6 12.9 %all_to_all.5.refs_0_ = f32[32,2,128]{2,1,0:T(2,128)S(1)} all-to-all(f32[32,2,128]{2,1,0:T(2,128)S(1)} %broadcast_in_dim.2), channel_id=1, replica_groups=mesh['loop'=4,'trans'=8] {'loop','trans'}, dimensions={0} | all-to-all | bytes 65536 | tf_op jit(solution)/shard_map/all_to_all | solution.py:538
  39.4 1.9 %combine.1 = (f32[8,192,128]{2,1,0:T(8,128)}, f32[8,8]{1,0:T(8,128)}, f32[8,8]{1,0:T(8,128)}) custom-call(f32[32,2,128]{2,1,0:T(2,128)S(1)} %all_to_all.5.refs_0_, f32[8,192,128]{2,1,0:T(8,128)S(1)} %bitcast.13, f32[7,192,128]{2,1,0:T(8,128)S(1)} %get-tuple-element.43.refs_8_.refs_2_, f32[1,192,128]{2,1,0:T(8,128)S(1)} %get-tuple-element.45.refs_3_), custom_call_target="tpu_custom_call" | custom-call | tf_op jit(solution)/shard_map/combine/pallas_call | solution.py:540
  (1 shorter events, 0.0 us)
Async XLA Ops:
  0.6 4.2 %copy-start = (f32[8,3,64,1,128]{4,3,2,1,0:T(1,128)S(1)}, f32[8,3,64,1,128]{4,3,2,1,0:T(1,128)}, u32[]{:S(2)}) copy-start(f32[8,3,64,1,128]{4,3,2,1,0:T(1,128)} %param.5) | copy-start | bytes 2359300
  1.8 10.4 %collective-permute-start.2 = (f32[576,128]{1,0:T(8,128)S(1)}, f32[576,128]{1,0:T(8,128)S(1)}, u32[]{:S(2)}, u32[]{:S(2)}) collective-permute-start(f32[576,128]{1,0:T(8,128)S(1)} %get-tuple-element.33), channel_id=1, source_target_pairs={{0,8},{8,0},{16,24},{24,16},{1,9},{9,1},{17,25},{25,17},{2,10},{10... | collective-permute-start | bytes 884744 | tf_op jit(solution)/shard_map/ppermute | solution.py:419
  5.3 3.7 %collective-permute-start = (f32[64,128]{1,0:T(8,128)S(1)}, f32[64,128]{1,0:T(8,128)S(1)}, u32[]{:S(2)}, u32[]{:S(2)}) collective-permute-start(f32[64,128]{1,0:T(8,128)S(1)} %get-tuple-element.27), channel_id=1, source_target_pairs={{0,1},{1,0},{2,3},{3,2},{4,5},{5,4},{6,7},{7,6},{8,9},{9,8},{10,11... | collective-permute-start | bytes 98312 | tf_op jit(solution)/shard_map/ppermute | solution.py:415
  5.4 3.7 %collective-permute-start.1 = (f32[64,128]{1,0:T(8,128)S(1)}, f32[64,128]{1,0:T(8,128)S(1)}, u32[]{:S(2)}, u32[]{:S(2)}) collective-permute-start(f32[64,128]{1,0:T(8,128)S(1)} %get-tuple-element.28), channel_id=1, source_target_pairs={{1,2},{2,1},{3,4},{4,3},{5,6},{6,5},{9,10},{10,9},{11,12},{12,11},... | collective-permute-start | bytes 98312 | tf_op jit(solution)/shard_map/ppermute | solution.py:415
  6.0 11.0 %collective-permute-start.4 = (f32[256,128]{1,0:T(8,128)S(1)}, f32[256,128]{1,0:T(8,128)S(1)}, u32[]{:S(2)}, u32[]{:S(2)}) collective-permute-start(f32[256,128]{1,0:T(8,128)S(1)} %get-tuple-element.36), channel_id=1, source_target_pairs={{0,8},{8,16},{16,24},{24,0},{1,9},{9,17},{17,25},{25,1},{2,10},{10... | collective-permute-start | bytes 393224 | tf_op jit(solution)/shard_map/ppermute | solution.py:409
  6.2 11.7 %collective-permute-start.5 = (f32[256,128]{1,0:T(8,128)S(1)}, f32[256,128]{1,0:T(8,128)S(1)}, u32[]{:S(2)}, u32[]{:S(2)}) collective-permute-start(f32[256,128]{1,0:T(8,128)S(1)} %get-tuple-element.37), channel_id=1, source_target_pairs={{0,24},{8,0},{16,8},{24,16},{1,25},{9,1},{17,9},{25,17},{2,26},{10... | collective-permute-start | bytes 393224 | tf_op jit(solution)/shard_map/ppermute | solution.py:409
  12.2 9.2 %copy-start.1 = (f32[8,3,64,1,128]{4,3,2,1,0:T(1,128)S(1)}, f32[8,3,64,1,128]{4,3,2,1,0:T(1,128)}, u32[]{:S(2)}) copy-start(f32[8,3,64,1,128]{4,3,2,1,0:T(1,128)} %param.6) | copy-start | bytes 2359300
  12.3 11.7 %collective-permute-start.3 = (f32[384,128]{1,0:T(8,128)S(1)}, f32[384,128]{1,0:T(8,128)S(1)}, u32[]{:S(2)}, u32[]{:S(2)}) collective-permute-start(f32[384,128]{1,0:T(8,128)S(1)} %relay.1), channel_id=1, source_target_pairs={{0,16},{8,24},{16,0},{24,8},{1,17},{9,25},{17,1},{25,9},{2,18},{10... | collective-permute-start | bytes 589832 | tf_op jit(solution)/shard_map/ppermute | solution.py:424
  14.1 9.8 %collective-permute-start.6 = (f32[264,128]{1,0:T(8,128)S(1)}, f32[264,128]{1,0:T(8,128)S(1)}, u32[]{:S(2)}, u32[]{:S(2)}) collective-permute-start(f32[264,128]{1,0:T(8,128)S(1)} %get-tuple-element.34.refs_1_), channel_id=1, source_target_pairs={{0,8},{8,16},{16,24},{24,0},{1,9},{9,17},{17,25},{25,1},{2,10},{10... | collective-permute-start | bytes 405512 | tf_op jit(solution)/shard_map/ppermute | solution.py:409
  16.3 7.7 %collective-permute-start.7 = (f32[264,128]{1,0:T(8,128)S(1)}, f32[264,128]{1,0:T(8,128)S(1)}, u32[]{:S(2)}, u32[]{:S(2)}) collective-permute-start(f32[264,128]{1,0:T(8,128)S(1)} %get-tuple-element.35.refs_2_), channel_id=1, source_target_pairs={{0,24},{8,0},{16,8},{24,16},{1,25},{9,1},{17,9},{25,17},{2,26},{10... | collective-permute-start | bytes 405512 | tf_op jit(solution)/shard_map/ppermute | solution.py:409
  17.9 3.5 %copy-start.2 = (f32[8,8]{1,0:T(8,128)S(1)}, f32[8,8]{1,0:T(8,128)}, u32[]{:S(2)}) copy-start(f32[8,8]{1,0:T(8,128)} %coup_ref.1) | copy-start | bytes 772
  17.9 8.4 %collective-permute-start.8 = (f32[128,128]{1,0:T(8,128)S(1)}, f32[128,128]{1,0:T(8,128)S(1)}, u32[]{:S(2)}, u32[]{:S(2)}) collective-permute-start(f32[128,128]{1,0:T(8,128)S(1)} %get-tuple-element.39), channel_id=1, source_target_pairs={{0,8},{8,16},{16,24},{24,0},{1,9},{9,17},{17,25},{25,1},{2,10},{10... | collective-permute-start | bytes 196616 | tf_op jit(solution)/shard_map/ppermute | solution.py:409
  21.4 4.9 %collective-permute-start.9 = (f32[128,128]{1,0:T(8,128)S(1)}, f32[128,128]{1,0:T(8,128)S(1)}, u32[]{:S(2)}, u32[]{:S(2)}) collective-permute-start(f32[128,128]{1,0:T(8,128)S(1)} %get-tuple-element.40), channel_id=1, source_target_pairs={{0,24},{8,0},{16,8},{24,16},{1,25},{9,1},{17,9},{25,17},{2,26},{10... | collective-permute-start | bytes 196616 | tf_op jit(solution)/shard_map/ppermute | solution.py:409
